TPU v7x, 32 devices: a whole 2x2x4 slice. The times are simulated.
32 devices in a mesh: grp: 4 (over x, core), gx: 2 (over y), gy: 4 (over z).
Axes of the slice: x: 2, y: 2, z: 4, core: 2. Of those that a mesh axis runs over, the one named last changes fastest.
Arguments:
- fields: float32 [4, 5, 32, 128, 384], P('grp', None, 'gx', 'gy'), may hold values from -6 to 6
- closure_in: float32 [64, 5], replicated, may hold values from -2.5 to 2.5
- closure_bias: float32 [64], replicated, may hold values from -4 to 4
- closure_out: float32 [64], replicated, may hold values from -0.75 to 0.75
- master: float32 [17280], replicated, may hold values from -0.6 to 0.6
- momentum: float32 [17280], replicated, may hold values from -3 to 3
- sample_block: int32 [24], replicated, may hold values from 0 to 47
- sample_trainer: int32 [24], replicated, may hold values from 0 to 7, as said below
Outputs:
- new_fields: float32 [4, 5, 32, 128, 384], P('grp', None, 'gx', 'gy')
- new_master: float32 [17280], P(('grp', 'gx', 'gy'))
- new_momentum: float32 [17280], P(('grp', 'gx', 'gy'))
Inputs may be any that keep to these rules, and one draw needn't show every extreme that they name: `sample_trainer`: entry o names the trainer c = gx * 4 + gy of the last group that receives the cube of evolution device o. Every trainer receives at least 2 and at most 6 cubes, at most 4 from one evolution group; in every draw some trainer receives 6, 4 of them from one group.
All inputs are finite; a program needn't handle non-finite values.
Results may differ from a plain program's by a relative error of at most 0.0026.
The roundings to bfloat16 on the way count: a program that leaves them out, or rounds other values in their place, can miss the bound.
Values may be sent and summed in bfloat16 or wider, within the bound.
No kernel may reach another device: no remote copies, remote signals or barrier semaphores. Data moves between devices by JAX's collectives and lax.ppermute only.
A program may use at most 192 MiB of HBM per device.

v0:
```python
import functools

import jax
import jax.numpy as jnp
import numpy as np
from jax import lax
from jax.experimental import pallas as pl
from jax.experimental.pallas import tpu as pltpu
from jax.sharding import PartitionSpec as P

F = 5
CH = 64
HID = 64
SUB = 16
TCAP = 6
INNER = 3
CELLS = 4096
NPARAM = 17280
TAPS = 27
PAIRS = TCAP // 2
COLS = (SUB + 2) * 128
PATCH = 16 * F
STACK = 3 * PATCH

time_step = 0.1
base_viscosity = 0.02
viscosity_gain = 0.2
buoyancy = 0.5
inner_rate = 0.02
outer_rate = 0.01
momentum_decay = 0.9
norm_epsilon = 1e-06
highest = lax.Precision.HIGHEST


def patch_position(row):
    group, py, pz = row // 4, row // 2 % 2, row % 2
    ypos = py + 1 if group in (0, 1) else (3 if py == 0 else 0)
    zpos = pz + 1 if group in (0, 2) else (3 if pz == 0 else 0)
    return ypos - 1, zpos - 1


def selections():
    first = np.zeros((4, 256, STACK), np.float32)
    last = np.zeros((4, 256, STACK), np.float32)
    for cell in range(4):
        py, pz = cell // 2, cell % 2
        for kx in range(3):
            for channel in range(F):
                for row in range(16):
                    ypos, zpos = patch_position(row)
                    column = kx * PATCH + channel * 16 + row
                    dy, dz = ypos - py, zpos - pz
                    if abs(dy) <= 1 and abs(dz) <= 1:
                        tap = 9 * kx + 3 * (dy + 1) + dz + 1
                        first[cell, tap * F + channel, column] = 1.0
                        last[cell, channel * TAPS + 26 - tap, column] = 1.0
    return first, last


SELECT_FIRST, SELECT_LAST = selections()


def dot_rows(left, right):
    return jnp.dot(left, right, preferred_element_type=jnp.float32)


def dot_lanes(left, right):
    return lax.dot_general(left, right, (((1,), (1,)), ((), ())), preferred_element_type=jnp.float32)


def patch_masks():
    row = lax.broadcasted_iota(jnp.int32, (8, 128), 0)
    lane = lax.broadcasted_iota(jnp.int32, (8, 128), 1)
    return {
        "pz0": row % 2 == 0,
        "py0": row // 2 % 2 == 0,
        "centre": row < 4,
        "z_first": lane % 8 == 0,
        "z_last": lane % 8 == 7,
        "y_first": lane // 8 % 8 == 0,
        "y_last": lane // 8 % 8 == 7,
    }


def edge_shift(values, step, parity_zero, first, last, forward):
    before = jnp.where(first, 0.0, pltpu.roll(values, step, 1))
    after = jnp.where(last, 0.0, pltpu.roll(values, 128 - step, 1))
    if forward:
        return jnp.where(parity_zero, after, before)
    return jnp.where(parity_zero, before, after)


def patch_stack(rows, masks):
    both = rows + pltpu.roll(rows, 4, 0)
    z_edge = edge_shift(both, 1, masks["pz0"], masks["z_first"], masks["z_last"], True)
    upper = jnp.where(masks["centre"], both, z_edge)
    lower = edge_shift(upper, 8, masks["py0"], masks["y_first"], masks["y_last"], True)
    return upper, lower


def patch_fold(upper, lower, masks):
    def fold_z(values):
        moved = edge_shift(values, 1, masks["pz0"], masks["z_first"], masks["z_last"], False)
        return values + pltpu.roll(moved, 4, 0)

    shifted = edge_shift(fold_z(lower), 8, masks["py0"], masks["y_first"], masks["y_last"], False)
    return fold_z(upper) + shifted


def store_planes(ref, pair, x, channels):
    stacked = jnp.concatenate([part for both in channels for part in both], axis=0).astype(jnp.bfloat16)
    for kx in range(3):
        start = pl.multiple_of((x + 2 - kx) * 128, 128)
        ref[pair, kx * PATCH : (kx + 1) * PATCH, pl.ds(start, 128)] = stacked


def train_kernel(sources, *refs):
    (slots, first_ref, last_ref, weight_ref, select_first, select_last) = refs[:6]
    arrived = refs[6 : 6 + sources]
    fields_ref = refs[6 + sources]
    delta_first, delta_last, new_fields_ref = refs[7 + sources : 10 + sources]
    (
        cubes,
        table,
        targets,
        inputs,
        errors,
        hiddens,
        slopes,
        partial_out,
        big_first,
        big_last,
        big_last_t,
        grad_first,
        grad_last,
        now_first,
        now_last,
        slot_sems,
        field_sem,
    ) = refs[10 + sources :]

    field_copy = pltpu.make_async_copy(fields_ref, new_fields_ref, field_sem)
    field_copy.start()
    for slot in range(TCAP):
        for source in range(sources):

            @pl.when((slots[2, slot] == 1) & (slots[0, slot] == source))
            def _():
                pltpu.make_async_copy(
                    arrived[source].at[slots[1, slot]], cubes.at[slot], slot_sems.at[slot]
                ).start()

        @pl.when(slots[2, slot] == 0)
        def _():
            cubes[slot] = jnp.zeros((2 * SUB * F, 256), jnp.bfloat16)

    masks = patch_masks()
    errors[...] = jnp.zeros(errors.shape, errors.dtype)
    inputs[...] = jnp.zeros(inputs.shape, inputs.dtype)
    partial_out[:, :, :128] = jnp.zeros((PAIRS, STACK, 128), jnp.float32)
    partial_out[:, :, COLS - 128 :] = jnp.zeros((PAIRS, STACK, 128), jnp.float32)
    table[...] = jnp.zeros(table.shape, table.dtype)
    targets[...] = jnp.zeros(targets.shape, targets.dtype)
    start_first = first_ref[...].astype(jnp.bfloat16).astype(jnp.float32)
    start_last = last_ref[...].astype(jnp.bfloat16).astype(jnp.float32)
    now_first[...] = start_first
    now_last[...] = start_last

    for slot in range(TCAP):

        @pl.when(slots[2, slot] == 1)
        def _():
            pltpu.make_async_copy(arrived[0].at[0], cubes.at[slot], slot_sems.at[slot]).wait()

    low_lanes = lax.broadcasted_iota(jnp.int32, (SUB * F, 128), 1) < 64

    def spread_rows(pair, start, put):
        even = cubes[2 * pair, start : start + SUB * F, :].astype(jnp.float32)
        odd = cubes[2 * pair + 1, start : start + SUB * F, :].astype(jnp.float32)
        for half in range(2):
            left = even[:, half * 128 : (half + 1) * 128]
            right = odd[:, half * 128 : (half + 1) * 128]
            put(2 * half, jnp.where(low_lanes, left, pltpu.roll(right, 64, 1)))
            put(2 * half + 1, jnp.where(low_lanes, pltpu.roll(left, 64, 1), right))

    for pair in range(PAIRS):

        def put_input(cell, values):
            table[pl.ds(cell, SUB * F, 8), :] = values

        def put_target(cell, values):
            targets[pl.ds(pair * SUB * F * 8 + cell, SUB * F, 8), :] = values

        spread_rows(pair, 0, put_input)
        spread_rows(pair, SUB * F, put_target)

        def stack_plane(x, carry):
            base = pl.multiple_of(x * (F * 8), 8)
            rows = table[pl.ds(base, F * 8), :]
            channels = [patch_stack(rows[8 * c : 8 * c + 8], masks) for c in range(F)]
            store_planes(inputs, pair, x, channels)
            return carry

        lax.fori_loop(0, SUB, stack_plane, 0)

    def train_step(step, step_carry):
        first_now = now_first[...].astype(jnp.bfloat16)
        last_now = now_last[...].astype(jnp.bfloat16)
        for cell in range(4):
            rows = slice(cell * CH, (cell + 1) * CH)
            big_first[rows, :] = dot_rows(first_now, select_first[cell]).astype(jnp.bfloat16)
            big_last[rows, :] = dot_rows(last_now, select_last[cell]).astype(jnp.bfloat16)
        big_last_t[...] = big_last[...].T
        grad_first[...] = jnp.zeros(grad_first.shape, jnp.float32)
        grad_last[...] = jnp.zeros(grad_last.shape, jnp.float32)

        def forward(index, carry):
            pair = index // 8
            column = pl.multiple_of((index % 8) * 256 + 128, 128)
            pre = dot_rows(big_first[...], inputs[pair, :, pl.ds(column, 256)])
            sigmoid = 0.5 * jnp.tanh(0.5 * pre) + 0.5
            value = pre * sigmoid
            hidden = value.astype(jnp.bfloat16)
            hiddens[pair, :, pl.ds(column, 256)] = hidden
            slopes[pair, :, pl.ds(column, 256)] = sigmoid + value * (1.0 - sigmoid)
            partial_out[pair, :, pl.ds(column, 256)] = dot_rows(big_last_t[...], hidden)
            return carry

        lax.fori_loop(0, 8 * PAIRS, forward, 0)

        def error_plane(index, carry):
            pair = index // SUB
            x = index % SUB
            column = pl.multiple_of((x + 1) * 128, 128)
            total = (
                partial_out[pair, 0:PATCH, pl.ds(pl.multiple_of(column + 128, 128), 128)]
                + partial_out[pair, PATCH : 2 * PATCH, pl.ds(column, 128)]
                + partial_out[pair, 2 * PATCH :, pl.ds(pl.multiple_of(column - 128, 128), 128)]
            )
            wanted = targets[pl.ds(pl.multiple_of(index * (F * 8), 8), F * 8), :]
            weight = weight_ref[pair]
            channels = []
            for c in range(F):
                predicted = patch_fold(
                    total[16 * c : 16 * c + 8], total[16 * c + 8 : 16 * c + 16], masks
                )
                error = weight * (predicted - wanted[8 * c : 8 * c + 8])
                error = jnp.where(masks["centre"], error, 0.0)
                error = error.astype(jnp.bfloat16).astype(jnp.float32)
                channels.append(patch_stack(error, masks))
            store_planes(errors, pair, x, channels)
            return carry

        lax.fori_loop(0, SUB * PAIRS, error_plane, 0)

        def backward(index, carry):
            pair = index // 4
            column = pl.multiple_of((index % 4) * 512 + 128, 128)
            error_stack = errors[pair, :, pl.ds(column, 512)]
            hidden_grad = dot_rows(big_last[...], error_stack)
            pre_grad = (hidden_grad * slopes[pair, :, pl.ds(column, 512)]).astype(jnp.bfloat16)
            grad_first[...] += dot_lanes(pre_grad, inputs[pair, :, pl.ds(column, 512)])
            grad_last[...] += dot_lanes(hiddens[pair, :, pl.ds(column, 512)], error_stack)
            return carry

        lax.fori_loop(0, 4 * PAIRS, backward, 0)

        def folded(grad_ref, select_ref):
            total = jnp.zeros((CH, 256), jnp.float32)
            for cell in range(4):
                rest = grad_ref[cell * CH : (cell + 1) * CH, :]
                for _ in range(3):
                    part = rest.astype(jnp.bfloat16)
                    total = total + dot_lanes(part, select_ref[cell])
                    rest = rest - part.astype(jnp.float32)
            return total

        now_first[...] = now_first[...] - inner_rate * folded(grad_first, select_first)
        now_last[...] = now_last[...] - inner_rate * folded(grad_last, select_last)
        return step_carry

    lax.fori_loop(0, INNER, train_step, 0)
    delta_first[...] = start_first - now_first[...]
    delta_last[...] = start_last - now_last[...]
    field_copy.wait()


def train_cubes(slots, first, last, weights, arrived, fields):
    sources = len(arrived)
    vmem = pl.BlockSpec(memory_space=pltpu.VMEM)
    anywhere = pl.BlockSpec(memory_space=pl.ANY)
    return pl.pallas_call(
        functools.partial(train_kernel, sources),
        out_shape=(
            jax.ShapeDtypeStruct((CH, 256), jnp.float32),
            jax.ShapeDtypeStruct((CH, 256), jnp.float32),
            jax.ShapeDtypeStruct(fields.shape, fields.dtype),
        ),
        in_specs=[pl.BlockSpec(memory_space=pltpu.SMEM)] + [vmem] * 5 + [anywhere] * (sources + 1),
        out_specs=(vmem, vmem, anywhere),
        scratch_shapes=[
            pltpu.VMEM((TCAP, 2 * SUB * F, 256), jnp.bfloat16),
            pltpu.VMEM((SUB * F * 8, 128), jnp.float32),
            pltpu.VMEM((PAIRS * SUB * F * 8, 128), jnp.float32),
            pltpu.VMEM((PAIRS, STACK, COLS), jnp.bfloat16),
            pltpu.VMEM((PAIRS, STACK, COLS), jnp.bfloat16),
            pltpu.VMEM((PAIRS, 4 * CH, COLS), jnp.bfloat16),
            pltpu.VMEM((PAIRS, 4 * CH, COLS), jnp.float32),
            pltpu.VMEM((PAIRS, STACK, COLS), jnp.float32),
            pltpu.VMEM((4 * CH, STACK), jnp.bfloat16),
            pltpu.VMEM((4 * CH, STACK), jnp.bfloat16),
            pltpu.VMEM((STACK, 4 * CH), jnp.bfloat16),
            pltpu.VMEM((4 * CH, STACK), jnp.float32),
            pltpu.VMEM((4 * CH, STACK), jnp.float32),
            pltpu.VMEM((CH, 256), jnp.float32),
            pltpu.VMEM((CH, 256), jnp.float32),
            pltpu.SemaphoreType.DMA((TCAP,)),
            pltpu.SemaphoreType.DMA,
        ],
        compiler_params=pltpu.CompilerParams(vmem_limit_bytes=48 * 1024 * 1024),
        name="train_cubes",
    )(
        slots,
        first,
        last,
        weights,
        jnp.asarray(SELECT_FIRST, jnp.bfloat16),
        jnp.asarray(SELECT_LAST, jnp.bfloat16),
        *arrived,
        fields,
    )


def evolve_kernel(closure, fields, x_low, x_high, y_low, y_high, new_fields):
    x_cells, y_cells, z_cells = fields.shape[1:]
    row = lax.broadcasted_iota(jnp.int32, (y_cells, z_cells), 0)
    lane = lax.broadcasted_iota(jnp.int32, (y_cells, z_cells), 1)
    part = y_cells // 2

    def plane(x, carry):
        eddies = []
        for half in range(2):
            rows = pl.ds(half * part, part)
            cells = [fields[f, x, rows, :] for f in range(F)]

            def unit(h, total):
                pre = closure[F, h] + closure[0, h] * cells[0]
                for f in range(1, F):
                    pre = pre + closure[f, h] * cells[f]
                return total + closure[F + 1, h] * (pre + pre * jnp.tanh(pre))

            total = lax.fori_loop(0, HID, unit, jnp.zeros((part, z_cells), jnp.float32), unroll=4)
            soft = jnp.maximum(total, 0.0) + jnp.log1p(jnp.exp(-jnp.abs(total)))
            eddies.append(base_viscosity + viscosity_gain * soft)
        viscosity = jnp.concatenate(eddies, axis=0)
        centre = [fields[f, x] for f in range(F)]
        below = jnp.maximum(x - 1, 0)
        above = jnp.minimum(x + 1, x_cells - 1)
        for f in range(F):
            value = centre[f]
            west = jnp.where(x == 0, x_low[f, 0], fields[f, below])
            east = jnp.where(x == x_cells - 1, x_high[f, 0], fields[f, above])
            south = jnp.where(row == 0, y_low[f, pl.ds(x, 1), :], pltpu.roll(value, 1, 0))
            north = jnp.where(
                row == y_cells - 1, y_high[f, pl.ds(x, 1), :], pltpu.roll(value, y_cells - 1, 0)
            )
            lower = jnp.where(lane == 0, 0.0, pltpu.roll(value, 1, 1))
            upper = jnp.where(lane == z_cells - 1, 0.0, pltpu.roll(value, z_cells - 1, 1))
            laplacian = east + west + north + south + upper + lower - 6.0 * value
            advection = (
                centre[0] * (east - west) + centre[1] * (north - south) + centre[2] * (upper - lower)
            )
            tendency = viscosity * laplacian - 0.5 * advection
            if f == 2:
                tendency = tendency + buoyancy * centre[3]
            new_fields[f, x] = value + time_step * tendency
        return carry

    lax.fori_loop(0, x_cells, plane, 0)


def evolve(closure, fields, x_low, x_high, y_low, y_high):
    vmem = pl.BlockSpec(memory_space=pltpu.VMEM)
    return pl.pallas_call(
        evolve_kernel,
        out_shape=jax.ShapeDtypeStruct(fields.shape, fields.dtype),
        in_specs=[pl.BlockSpec(memory_space=pltpu.SMEM)] + [vmem] * 5,
        out_specs=vmem,
        compiler_params=pltpu.CompilerParams(vmem_limit_bytes=48 * 1024 * 1024),
        name="evolve_brick",
    )(closure, fields, x_low, x_high, y_low, y_high)


def cube_tendency(padded, closure_in, closure_bias, closure_out):
    centre = padded[:, 1:-1, 1:-1, 1:-1]
    east, west = padded[:, 2:, 1:-1, 1:-1], padded[:, :-2, 1:-1, 1:-1]
    north, south = padded[:, 1:-1, 2:, 1:-1], padded[:, 1:-1, :-2, 1:-1]
    upper, lower = padded[:, 1:-1, 1:-1, 2:], padded[:, 1:-1, 1:-1, :-2]
    laplacian = east + west + north + south + upper + lower - 6.0 * centre
    advection = centre[0] * (east - west) + centre[1] * (north - south) + centre[2] * (upper - lower)
    columns = centre.reshape(F, CELLS)
    hidden = jax.nn.silu(jnp.dot(closure_in, columns, precision=highest) + closure_bias[:, None])
    soft = jax.nn.softplus(jnp.dot(closure_out, hidden, precision=highest))
    viscosity = base_viscosity + viscosity_gain * soft.reshape(SUB, SUB, SUB)
    tendency = viscosity * laplacian - 0.5 * advection
    return tendency.at[2].add(buoyancy * centre[3])


def patch_rows(cube):
    half = SUB // 2
    split = cube.astype(jnp.bfloat16).reshape(F, SUB, half, 2, half, 2)
    return jnp.transpose(split, (1, 0, 3, 5, 2, 4)).reshape(SUB * F, 256)


def slot_lists(sample_trainer, column, trainers):
    owner_ids = jnp.arange(sample_trainer.shape[0], dtype=jnp.int32)
    same_trainer = sample_trainer[:, None] == sample_trainer[None, :]
    earlier = owner_ids[None, :] < owner_ids[:, None]
    rank_all = jnp.sum((same_trainer & earlier).astype(jnp.int32), axis=1)
    mine_mask = sample_trainer == column
    slot_ids = jnp.arange(TCAP, dtype=jnp.int32)
    chosen = mine_mask[None, :] & (rank_all[None, :] == slot_ids[:, None])
    slot_owner = jnp.sum(jnp.where(chosen, owner_ids[None, :], 0), axis=1)
    slot_valid = jnp.any(chosen, axis=1)
    sample_count = jnp.maximum(jnp.sum(mine_mask.astype(jnp.int32)), 1)
    shift = jnp.mod(column - slot_owner % trainers, trainers)
    table = jnp.stack([shift, slot_owner // trainers, slot_valid.astype(jnp.int32)])
    slot_weight = jnp.where(slot_valid, 1.0 / (sample_count.astype(jnp.float32) * CELLS), 0.0)
    weights = jnp.repeat(2.0 * slot_weight, 64).reshape(PAIRS, 1, 128)
    return table.astype(jnp.int32), jnp.broadcast_to(weights, (PAIRS, 8, 128))


def on_device(
    fields, closure_in, closure_bias, closure_out, master, momentum, sample_block, sample_trainer
):
    group_count = lax.axis_size("grp")
    x_devices = lax.axis_size("gx")
    y_devices = lax.axis_size("gy")
    trainers = x_devices * y_devices
    my_group = lax.axis_index("grp")
    my_column = lax.axis_index("gx") * y_devices + lax.axis_index("gy")
    is_trainer = my_group == group_count - 1
    everyone = ("grp", "gx", "gy")
    first_trainer = (group_count - 1) * trainers
    brick = fields[0]
    x_cells, y_cells, z_cells = brick.shape[1:]

    def neighbours(values_low, values_high, axis):
        count = lax.axis_size(axis)
        from_low = lax.ppermute(values_high, axis, [(i, (i + 1) % count) for i in range(count)])
        from_high = lax.ppermute(values_low, axis, [((i + 1) % count, i) for i in range(count)])
        return from_low, from_high

    x_low, x_high = neighbours(brick[:, :1], brick[:, -1:], "gx")
    y_low, y_high = neighbours(brick[:, :, 0], brick[:, :, -1], "gy")

    sim_group = jnp.minimum(my_group, group_count - 2)
    block_id = sample_block[sim_group * trainers + my_column]
    y_blocks = y_cells // SUB
    z_blocks = z_cells // SUB
    x_start = block_id // (y_blocks * z_blocks) * SUB
    y_start = block_id // z_blocks % y_blocks * SUB
    z_start = block_id % z_blocks * SUB
    walled = jnp.pad(brick, ((0, 0), (1, 1), (1, 1), (1, 1)))
    core = lax.dynamic_slice(walled, (0, x_start, y_start, z_start), (F, SUB + 2, SUB + 2, SUB + 2))

    def side(values, starts, shape):
        pads = [(0, 0)] + [(1, 1)] * (values.ndim - 1)
        return lax.dynamic_slice(jnp.pad(values, pads), (0,) + starts, (F,) + shape)

    span = SUB + 2
    place = lax.broadcasted_iota(jnp.int32, (1, span, span, span), 1) + x_start
    across = lax.broadcasted_iota(jnp.int32, (1, span, span, span), 2) + y_start
    core = jnp.where(
        place == 0, side(x_low[:, 0], (y_start, z_start), (span, span))[:, None], core
    )
    core = jnp.where(
        place == x_cells + 1, side(x_high[:, 0], (y_start, z_start), (span, span))[:, None], core
    )
    core = jnp.where(
        across == 0, side(y_low, (x_start, z_start), (span, span))[:, :, None], core
    )
    core = jnp.where(
        across == y_cells + 1, side(y_high, (x_start, z_start), (span, span))[:, :, None], core
    )
    change = cube_tendency(core, closure_in, closure_bias, closure_out)
    payload = jnp.concatenate([patch_rows(core[:, 1:-1, 1:-1, 1:-1]), patch_rows(change)], axis=0)

    landed = jnp.stack(
        [
            lax.ppermute(
                payload,
                everyone,
                [(g * trainers + c, first_trainer + c) for c in range(trainers)],
            )
            for g in range(group_count - 1)
        ]
    )
    arrived = [landed]
    for shift in range(1, trainers):
        pairs = [
            (first_trainer + c, first_trainer + (c + shift) % trainers) for c in range(trainers)
        ]
        arrived.append(lax.ppermute(landed, everyone, pairs))

    slots, weights = slot_lists(sample_trainer, my_column, trainers)
    first_count = CH * TAPS * F
    first = jnp.pad(master[:first_count].reshape(CH, TAPS * F), ((0, 0), (0, 256 - TAPS * F)))
    last = jnp.pad(master[first_count:].reshape(TAPS * F, CH).T, ((0, 0), (0, 256 - TAPS * F)))
    closure = jnp.concatenate(
        [0.5 * closure_in.T, 0.5 * closure_bias[None], closure_out[None]], axis=0
    )

    def train_here():
        delta_first, delta_last, new_brick = train_cubes(
            slots, first, last, weights, arrived, brick
        )
        delta = jnp.concatenate(
            [delta_first[:, : TAPS * F].reshape(-1), delta_last[:, : TAPS * F].T.reshape(-1)]
        )
        return delta, new_brick

    def evolve_here():
        new_brick = evolve(closure, brick, x_low, x_high, y_low, y_high)
        return jnp.zeros((NPARAM,), jnp.float32), new_brick

    delta, new_brick = lax.cond(is_trainer, train_here, evolve_here)

    part_size = NPARAM // trainers
    total = jnp.zeros((NPARAM,), jnp.float32)
    mine = lax.dynamic_slice_in_dim(delta, my_column * part_size, part_size)
    for shift in range(1, trainers):
        pairs = [
            (first_trainer + c, first_trainer + (c + shift) % trainers) for c in range(trainers)
        ]
        target = (my_column + shift) % trainers
        piece = lax.dynamic_slice_in_dim(delta, target * part_size, part_size)
        mine = mine + lax.ppermute(piece, everyone, pairs)
    total = lax.dynamic_update_slice_in_dim(total, mine, my_column * part_size, 0)
    for shift in range(1, trainers):
        pairs = [
            (first_trainer + c, first_trainer + (c + shift) % trainers) for c in range(trainers)
        ]
        source = (my_column - shift) % trainers
        total = lax.dynamic_update_slice_in_dim(
            total, lax.ppermute(mine, everyone, pairs), source * part_size, 0
        )
    final = jnp.where(is_trainer, total, 0.0)
    for g in range(group_count - 1):
        pairs = [(first_trainer + c, g * trainers + c) for c in range(trainers)]
        final = final + lax.ppermute(total, everyone, pairs)

    share_size = NPARAM // (group_count * trainers)
    share_start = (my_group * trainers + my_column) * share_size
    momentum_share = lax.dynamic_slice_in_dim(momentum, share_start, share_size)
    master_share = lax.dynamic_slice_in_dim(master, share_start, share_size)
    inverse = 1.0 / jnp.sqrt(jnp.sum(final * final) / NPARAM + norm_epsilon)
    delta_share = lax.dynamic_slice_in_dim(final, share_start, share_size)
    new_momentum = momentum_decay * momentum_share + delta_share * inverse
    new_master = master_share - outer_rate * new_momentum
    return (new_brick[None], new_master, new_momentum)


def solution(mesh):
    in_specs = (P("grp", None, "gx", "gy", None), P(), P(), P(), P(), P(), P(), P())
    out_specs = (P("grp", None, "gx", "gy", None), P(("grp", "gx", "gy")), P(("grp", "gx", "gy")))
    return jax.shard_map(
        on_device, mesh=mesh, in_specs=in_specs, out_specs=out_specs, check_vma=False
    )
```

profile of v0, /device:TPU:0, one launch (start us, length us, event | category | flops | bytes accessed | tf_op | source)
XLA Modules:
  0.0 240.4 jit_solution(3725964702858066709)
XLA Ops:
  0.6 4.4 %copy.81 = f32[1,5,16,32,384]{4,2,1,3,0:T(8,128)S(1)} copy(f32[1,5,16,32,384]{4,3,2,1,0:T(8,128)} %param.14) | data formatting | bytes 7864320 | tf_op args[0]
  5.4 3.0 %collective-permute-start.1 = (f32[5,1,32,384]{3,1,0,2:T(1,128)S(1)}, f32[5,1,32,384]{3,1,0,2:T(1,128)S(1)}, u32[]{:S(2)}, u32[]{:S(2)}) collective-permute-start(f32[5,1,32,384]{3,1,0,2:T(1,128)S(1)} %get-tuple-element.262), channel_id=1, source_target_pairs={{4,0},{0,4},{5,1},{1,5},{6,2},{2,6},{7,3},{3,7},{12,8},{8,12},{13,... | collective-permute-start | bytes 737288 | tf_op jit(solution)/shard_map/ppermute | solution.py:452
  8.5 2.1 collective-permute-start.2
  10.6 2.1 collective-permute-start.3
  16.6 0.6 convert_reduce_fusion.1
  18.0 1.7 collective-permute-done
  19.8 1.9 fusion.4
  23.0 1.0 fusion
  24.0 0.9 fusion.5
  25.1 1.1 multiply_subtract_fusion
  26.6 0.7 copy.72
  27.3 0.8 reshape.250
  28.3 0.7 copy.68
  29.0 0.8 reshape.247
  29.9 2.2 collective-permute-start.4
  32.1 0.7 collective-permute-start.5
  32.8 0.7 collective-permute-start.6
  33.5 0.8 collective-permute-done.4
  34.3 0.7 collective-permute-start.10
  35.0 0.7 collective-permute-start.11
  35.8 0.7 collective-permute-start.12
  36.4 0.7 collective-permute-start.13
  37.1 0.7 collective-permute-start.7
  37.8 0.7 collective-permute-start.8
  38.5 0.9 collective-permute-start.9
  40.4 41.3 %conditional.1 = (f32[17280]{0:T(1024)S(1)}, f32[1,5,16,32,384]{4,3,2,1,0:T(8,128)}) conditional(s32[]{:T(128)} %convert_element_type.42, (f32[7,64]{1,0:T(8,128)S(1)}, f32[5,16,32,384]{3,1,0,2:T(8,128)}, f32[5,1,32,384]{3,1,0,2:T(1,128)S(1)}, f32[5,1,32,384]{3,1,0,2:T(1,128)S(1)}, f32[5,16,384]{2,1,0:T(8,128)S(1)}, ...), branch_computations={%region_4.5_spmd, %region_5.6_spmd.clone} | conditional | flops 17294 | bytes 36230608 | solution.py:528
  40.4 3.3 %copy.73.fields = f32[5,16,32,384]{3,2,1,0:T(8,128)S(1)} copy(f32[5,16,32,384]{3,1,0,2:T(8,128)} %get-tuple-element.233) | data formatting | bytes 7864320 | tf_op jit(solution)/shard_map
  43.8 37.9 %evolve_brick.1 = f32[5,16,32,384]{3,2,1,0:T(8,128)} custom-call(f32[7,64]{1,0:T(8,128)S(1)} %get-tuple-element.105.closure, f32[5,16,32,384]{3,2,1,0:T(8,128)S(1)} %copy.73.fields, f32[5,1,32,384]{3,2,1,0:T(8,128)S(1)} %copy.74.x_low, f32[5,1,32,384]{3,2,1,0:T(8,128)S(1)} %copy.75.x_high, f32[5,16,384]{2,1,0:T(8,128)S(1)} %get-tuple-element.109.y_low, ...), custom_call_target="tpu_custom_call" | custom-call | tf_op jit(solution)/shard_map/cond/branch_0_fun/evolve_brick/pallas_call | solution.py:385
  81.8 0.7 collective-permute-start.14
  82.5 0.7 collective-permute-start.15
  83.2 0.7 collective-permute-start.16
  83.8 0.7 collective-permute-start.17
  84.5 0.7 collective-permute-start.18
  85.2 0.7 collective-permute-start.19
  85.9 0.7 collective-permute-start.20
  86.8 0.7 collective-permute-start.21
  87.5 0.7 collective-permute-start.22
  88.2 0.7 collective-permute-start.23
  88.9 0.7 collective-permute-start.24
  89.5 0.7 collective-permute-start.25
  90.2 0.7 collective-permute-start.26
  90.9 0.7 collective-permute-start.27
  94.1 1.3 collective-permute-start.28
  95.4 0.7 collective-permute-start.29
  96.0 0.7 collective-permute-start.30
  96.7 140.9 %collective-permute-done.28 = f32[17280]{0:T(1024)S(1)} collective-permute-done((f32[17280]{0:T(1024)S(1)}, f32[17280]{0:T(1024)S(1)}, u32[]{:S(2)}, u32[]{:S(2)}) %collective-permute-start.28) | collective-permute-done | bytes 69152 | tf_op jit(solution)/shard_map/ppermute | solution.py:552
  237.7 0.6 multiply_reduce_fusion
  239.0 1.4 multiply_subtract_fusion.1
  (95 shorter events, 6.9 us)
Async XLA Ops:
  5.0 3.5 %copy-start.3 = (f32[1,5,16,32,384]{4,2,1,3,0:T(8,128)}, f32[1,5,16,32,384]{4,2,1,3,0:T(8,128)S(1)}, u32[]{:S(2)}) copy-start(f32[1,5,16,32,384]{4,2,1,3,0:T(8,128)S(1)} %copy.81) | copy-start | bytes 11796484
  5.0 7.7 %copy-start.17 = (s32[24]{0:T(128)S(1)}, s32[24]{0:T(128)}, u32[]{:S(2)}) copy-start(s32[24]{0:T(128)} %param.20) | copy-start | bytes 292
  5.0 11.5 %copy-start.16 = (s32[24]{0:T(128)S(1)}, s32[24]{0:T(128)}, u32[]{:S(2)}) copy-start(s32[24]{0:T(128)} %param.21) | copy-start | bytes 292
  5.4 12.4 %collective-permute-start.1 = (f32[5,1,32,384]{3,1,0,2:T(1,128)S(1)}, f32[5,1,32,384]{3,1,0,2:T(1,128)S(1)}, u32[]{:S(2)}, u32[]{:S(2)}) collective-permute-start(f32[5,1,32,384]{3,1,0,2:T(1,128)S(1)} %get-tuple-element.262), channel_id=1, source_target_pairs={{4,0},{0,4},{5,1},{1,5},{6,2},{2,6},{7,3},{3,7},{12,8},{8,12},{13,... | collective-permute-start | bytes 737288 | tf_op jit(solution)/shard_map/ppermute | solution.py:452
  8.4 11.2 %collective-permute-start = (f32[5,1,32,384]{3,1,0,2:T(1,128)S(1)}, f32[5,1,32,384]{3,1,0,2:T(1,128)S(1)}, u32[]{:S(2)}, u32[]{:S(2)}) collective-permute-start(f32[5,1,32,384]{3,1,0,2:T(1,128)S(1)} %get-tuple-element.263), channel_id=1, source_target_pairs={{0,4},{4,0},{1,5},{5,1},{2,6},{6,2},{3,7},{7,3},{8,12},{12,8},{9,1... | collective-permute-start | bytes 737288 | tf_op jit(solution)/shard_map/ppermute | solution.py:451
  8.5 9.1 %collective-permute-start.2 = (f32[5,16,384]{2,1,0:T(8,128)S(1)}, f32[5,16,384]{2,1,0:T(8,128)S(1)}, u32[]{:S(2)}, u32[]{:S(2)}) collective-permute-start(f32[5,16,384]{2,1,0:T(8,128)S(1)} %get-tuple-element.261), channel_id=1, source_target_pairs={{0,1},{1,2},{2,3},{3,0},{4,5},{5,6},{6,7},{7,4},{8,9},{9,10},{10,1... | collective-permute-start | bytes 368648 | tf_op jit(solution)/shard_map/ppermute | solution.py:451
  10.6 7.1 %collective-permute-start.3 = (f32[5,16,384]{2,1,0:T(8,128)S(1)}, f32[5,16,384]{2,1,0:T(8,128)S(1)}, u32[]{:S(2)}, u32[]{:S(2)}) collective-permute-start(f32[5,16,384]{2,1,0:T(8,128)S(1)} %get-tuple-element.260), channel_id=1, source_target_pairs={{1,0},{2,1},{3,2},{0,3},{5,4},{6,5},{7,6},{4,7},{9,8},{10,9},{11,1... | collective-permute-start | bytes 368648 | tf_op jit(solution)/shard_map/ppermute | solution.py:452
  22.3 0.7 copy-start.13
  22.3 0.7 copy-start.14
  22.5 1.5 copy-start.15
  28.3 11.8 %copy-start.12 = (f32[17280]{0:T(1024)S(1)}, f32[17280]{0:T(1024)}, u32[]{:S(2)}) copy-start(f32[17280]{0:T(1024)} %param.18) | copy-start | bytes 207364
  29.9 4.3 %collective-permute-start.4 = (bf16[160,256]{1,0:T(8,128)(2,1)S(1)}, bf16[160,256]{1,0:T(8,128)(2,1)S(1)}, u32[]{:S(2)}, u32[]{:S(2)}) collective-permute-start(bf16[160,256]{1,0:T(8,128)(2,1)S(1)} %constant_dynamic-update-slice_fusion), channel_id=1, source_target_pairs={{0,24},{1,25},{2,26},{3,27},{4,28},{5,29},{6,30},{7,31}} | collective-permute-start | bytes 245768 | tf_op jit(solution)/shard_map/ppermute | solution.py:492
  32.1 2.1 collective-permute-start.5
  32.8 1.5 collective-permute-start.6
  34.3 3.5 %collective-permute-start.10 = (bf16[3,160,256]{2,1,0:T(8,128)(2,1)S(1)}, bf16[3,160,256]{2,1,0:T(8,128)(2,1)S(1)}, u32[]{:S(2)}, u32[]{:S(2)}) collective-permute-start(bf16[3,160,256]{2,1,0:T(8,128)(2,1)S(1)} %pad_maximum_fusion.1), channel_id=1, source_target_pairs={{24,28},{25,29},{26,30},{27,31},{28,24},{29,25},{30,26},{31,27}} | collective-permute-start | bytes 737288 | tf_op jit(solution)/shard_map/ppermute | solution.py:505
  35.0 3.6 %collective-permute-start.11 = (bf16[3,160,256]{2,1,0:T(8,128)(2,1)S(1)}, bf16[3,160,256]{2,1,0:T(8,128)(2,1)S(1)}, u32[]{:S(2)}, u32[]{:S(2)}) collective-permute-start(bf16[3,160,256]{2,1,0:T(8,128)(2,1)S(1)} %pad_maximum_fusion.1), channel_id=1, source_target_pairs={{24,29},{25,30},{26,31},{27,24},{28,25},{29,26},{30,27},{31,28}} | collective-permute-start | bytes 737288 | tf_op jit(solution)/shard_map/ppermute | solution.py:505
  35.8 4.6 %collective-permute-start.12 = (bf16[3,160,256]{2,1,0:T(8,128)(2,1)S(1)}, bf16[3,160,256]{2,1,0:T(8,128)(2,1)S(1)}, u32[]{:S(2)}, u32[]{:S(2)}) collective-permute-start(bf16[3,160,256]{2,1,0:T(8,128)(2,1)S(1)} %pad_maximum_fusion.1), channel_id=1, source_target_pairs={{24,30},{25,31},{26,24},{27,25},{28,26},{29,27},{30,28},{31,29}} | collective-permute-start | bytes 737288 | tf_op jit(solution)/shard_map/ppermute | solution.py:505
  36.4 3.9 %collective-permute-start.13 = (bf16[3,160,256]{2,1,0:T(8,128)(2,1)S(1)}, bf16[3,160,256]{2,1,0:T(8,128)(2,1)S(1)}, u32[]{:S(2)}, u32[]{:S(2)}) collective-permute-start(bf16[3,160,256]{2,1,0:T(8,128)(2,1)S(1)} %pad_maximum_fusion.1), channel_id=1, source_target_pairs={{24,31},{25,24},{26,25},{27,26},{28,27},{29,28},{30,29},{31,30}} | collective-permute-start | bytes 737288 | tf_op jit(solution)/shard_map/ppermute | solution.py:505
  37.1 3.2 %collective-permute-start.7 = (bf16[3,160,256]{2,1,0:T(8,128)(2,1)S(1)}, bf16[3,160,256]{2,1,0:T(8,128)(2,1)S(1)}, u32[]{:S(2)}, u32[]{:S(2)}) collective-permute-start(bf16[3,160,256]{2,1,0:T(8,128)(2,1)S(1)} %pad_maximum_fusion.1), channel_id=1, source_target_pairs={{24,25},{25,26},{26,27},{27,28},{28,29},{29,30},{30,31},{31,24}} | collective-permute-start | bytes 737288 | tf_op jit(solution)/shard_map/ppermute | solution.py:505
  37.8 2.6 %collective-permute-start.8 = (bf16[3,160,256]{2,1,0:T(8,128)(2,1)S(1)}, bf16[3,160,256]{2,1,0:T(8,128)(2,1)S(1)}, u32[]{:S(2)}, u32[]{:S(2)}) collective-permute-start(bf16[3,160,256]{2,1,0:T(8,128)(2,1)S(1)} %pad_maximum_fusion.1), channel_id=1, source_target_pairs={{24,26},{25,27},{26,28},{27,29},{28,30},{29,31},{30,24},{31,25}} | collective-permute-start | bytes 737288 | tf_op jit(solution)/shard_map/ppermute | solution.py:505
  38.5 1.9 collective-permute-start.9
  81.8 3.4 %collective-permute-start.14 = (f32[2160]{0:T(1024)S(1)}, f32[2160]{0:T(1024)S(1)}, u32[]{:S(2)}, u32[]{:S(2)}) collective-permute-start(f32[2160]{0:T(1024)S(1)} %get-tuple-element.267), channel_id=1, source_target_pairs={{24,25},{25,26},{26,27},{27,28},{28,29},{29,30},{30,31},{31,24}} | collective-permute-start | bytes 25928 | tf_op jit(solution)/shard_map/ppermute | solution.py:539
  82.5 3.4 %collective-permute-start.15 = (f32[2160]{0:T(1024)S(1)}, f32[2160]{0:T(1024)S(1)}, u32[]{:S(2)}, u32[]{:S(2)}) collective-permute-start(f32[2160]{0:T(1024)S(1)} %get-tuple-element.273), channel_id=1, source_target_pairs={{24,26},{25,27},{26,28},{27,29},{28,30},{29,31},{30,24},{31,25}} | collective-permute-start | bytes 25928 | tf_op jit(solution)/shard_map/ppermute | solution.py:539
  83.2 3.4 %collective-permute-start.16 = (f32[2160]{0:T(1024)S(1)}, f32[2160]{0:T(1024)S(1)}, u32[]{:S(2)}, u32[]{:S(2)}) collective-permute-start(f32[2160]{0:T(1024)S(1)} %get-tuple-element.272), channel_id=1, source_target_pairs={{24,27},{25,28},{26,29},{27,30},{28,31},{29,24},{30,25},{31,26}} | collective-permute-start | bytes 25928 | tf_op jit(solution)/shard_map/ppermute | solution.py:539
  83.8 2.7 %collective-permute-start.17 = (f32[2160]{0:T(1024)S(1)}, f32[2160]{0:T(1024)S(1)}, u32[]{:S(2)}, u32[]{:S(2)}) collective-permute-start(f32[2160]{0:T(1024)S(1)} %get-tuple-element.271), channel_id=1, source_target_pairs={{24,28},{25,29},{26,30},{27,31},{28,24},{29,25},{30,26},{31,27}} | collective-permute-start | bytes 25928 | tf_op jit(solution)/shard_map/ppermute | solution.py:539
  84.5 2.1 collective-permute-start.18
  85.2 1.4 collective-permute-start.19
  85.9 0.7 collective-permute-start.20
  86.8 3.4 %collective-permute-start.21 = (f32[2160]{0:T(1024)S(1)}, f32[2160]{0:T(1024)S(1)}, u32[]{:S(2)}, u32[]{:S(2)}) collective-permute-start(f32[2160]{0:T(1024)S(1)} %get-tuple-element.257), channel_id=1, source_target_pairs={{24,25},{25,26},{26,27},{27,28},{28,29},{29,30},{30,31},{31,24}} | collective-permute-start | bytes 25928 | tf_op jit(solution)/shard_map/ppermute | solution.py:547
  87.5 3.4 %collective-permute-start.22 = (f32[2160]{0:T(1024)S(1)}, f32[2160]{0:T(1024)S(1)}, u32[]{:S(2)}, u32[]{:S(2)}) collective-permute-start(f32[2160]{0:T(1024)S(1)} %get-tuple-element.257), channel_id=1, source_target_pairs={{24,26},{25,27},{26,28},{27,29},{28,30},{29,31},{30,24},{31,25}} | collective-permute-start | bytes 25928 | tf_op jit(solution)/shard_map/ppermute | solution.py:547
  88.2 4.1 %collective-permute-start.23 = (f32[2160]{0:T(1024)S(1)}, f32[2160]{0:T(1024)S(1)}, u32[]{:S(2)}, u32[]{:S(2)}) collective-permute-start(f32[2160]{0:T(1024)S(1)} %get-tuple-element.257), channel_id=1, source_target_pairs={{24,27},{25,28},{26,29},{27,30},{28,31},{29,24},{30,25},{31,26}} | collective-permute-start | bytes 25928 | tf_op jit(solution)/shard_map/ppermute | solution.py:547
  88.9 3.8 %collective-permute-start.24 = (f32[2160]{0:T(1024)S(1)}, f32[2160]{0:T(1024)S(1)}, u32[]{:S(2)}, u32[]{:S(2)}) collective-permute-start(f32[2160]{0:T(1024)S(1)} %get-tuple-element.257), channel_id=1, source_target_pairs={{24,28},{25,29},{26,30},{27,31},{28,24},{29,25},{30,26},{31,27}} | collective-permute-start | bytes 25928 | tf_op jit(solution)/shard_map/ppermute | solution.py:547
  89.5 3.5 %collective-permute-start.25 = (f32[2160]{0:T(1024)S(1)}, f32[2160]{0:T(1024)S(1)}, u32[]{:S(2)}, u32[]{:S(2)}) collective-permute-start(f32[2160]{0:T(1024)S(1)} %get-tuple-element.257), channel_id=1, source_target_pairs={{24,29},{25,30},{26,31},{27,24},{28,25},{29,26},{30,27},{31,28}} | collective-permute-start | bytes 25928 | tf_op jit(solution)/shard_map/ppermute | solution.py:547
  90.2 3.2 %collective-permute-start.26 = (f32[2160]{0:T(1024)S(1)}, f32[2160]{0:T(1024)S(1)}, u32[]{:S(2)}, u32[]{:S(2)}) collective-permute-start(f32[2160]{0:T(1024)S(1)} %get-tuple-element.257), channel_id=1, source_target_pairs={{24,30},{25,31},{26,24},{27,25},{28,26},{29,27},{30,28},{31,29}} | collective-permute-start | bytes 25928 | tf_op jit(solution)/shard_map/ppermute | solution.py:547
  90.9 2.8 %collective-permute-start.27 = (f32[2160]{0:T(1024)S(1)}, f32[2160]{0:T(1024)S(1)}, u32[]{:S(2)}, u32[]{:S(2)}) collective-permute-start(f32[2160]{0:T(1024)S(1)} %get-tuple-element.257), channel_id=1, source_target_pairs={{24,31},{25,24},{26,25},{27,26},{28,27},{29,28},{30,29},{31,30}} | collective-permute-start | bytes 25928 | tf_op jit(solution)/shard_map/ppermute | solution.py:547
  94.1 143.6 %collective-permute-start.28 = (f32[17280]{0:T(1024)S(1)}, f32[17280]{0:T(1024)S(1)}, u32[]{:S(2)}, u32[]{:S(2)}) collective-permute-start(f32[17280]{0:T(1024)S(1)} %dynamic_update_slice.31), channel_id=1, source_target_pairs={{24,0},{25,1},{26,2},{27,3},{28,4},{29,5},{30,6},{31,7}} | collective-permute-start | bytes 207368 | tf_op jit(solution)/shard_map/ppermute | solution.py:552
  95.4 142.3 %collective-permute-start.29 = (f32[17280]{0:T(1024)S(1)}, f32[17280]{0:T(1024)S(1)}, u32[]{:S(2)}, u32[]{:S(2)}) collective-permute-start(f32[17280]{0:T(1024)S(1)} %dynamic_update_slice.31), channel_id=1, source_target_pairs={{24,8},{25,9},{26,10},{27,11},{28,12},{29,13},{30,14},{31,15}} | collective-permute-start | bytes 207368 | tf_op jit(solution)/shard_map/ppermute | solution.py:552
  96.0 141.6 %collective-permute-start.30 = (f32[17280]{0:T(1024)S(1)}, f32[17280]{0:T(1024)S(1)}, u32[]{:S(2)}, u32[]{:S(2)}) collective-permute-start(f32[17280]{0:T(1024)S(1)} %dynamic_update_slice.31), channel_id=1, source_target_pairs={{24,16},{25,17},{26,18},{27,19},{28,20},{29,21},{30,22},{31,23}} | collective-permute-start | bytes 207368 | tf_op jit(solution)/shard_map/ppermute | solution.py:552
where the time goes:
time: 242 us; the launch traced here: 240 us
  waiting for transfers between devices  143 us (59%)
  Pallas kernels  37.9 us (16%)
  starting transfers between devices  27.6 us (11%)
  local copies, waits for them, and re-layouts  16.7 us (7%)
  other arithmetic  6.56 us (3%)
  between operations  6.28 us (3%)
    ppermute x3, waiting for transfers between devices, on_device(): final = final + lax.ppermute(total, everyone, pairs)  141 us
    pallas_call x1, Pallas kernels, evolve(): pl.pallas_call(evolve_kernel, out_shape=jax.ShapeDtypeStruct(fields.shape...  37.9 us
    ppermute x2, starting transfers between devices, neighbours(): lax.ppermute(values_low, axis, [((i + 1) % count, i) for i in range(count)])  5.12 us
    ppermute x7, starting transfers between devices, on_device(): arrived.append(lax.ppermute(landed, everyone, pairs))  4.91 us
  transfers between devices with their start and end apart: 31, of which 3 were waited for; matrix products, arithmetic and copies ran while one was open for 2% of the time, Pallas kernels for 0%

commit v1 on v0

--- a/solution.py
+++ b/solution.py
@@ -202,7 +202,7 @@
             store_planes(inputs, pair, x, channels)
             return carry
 
-        lax.fori_loop(0, SUB, stack_plane, 0)
+        lax.fori_loop(0, SUB, stack_plane, 0, unroll=8)
 
     def train_step(step, step_carry):
         first_now = now_first[...].astype(jnp.bfloat16)
@@ -227,7 +227,7 @@
             partial_out[pair, :, pl.ds(column, 256)] = dot_rows(big_last_t[...], hidden)
             return carry
 
-        lax.fori_loop(0, 8 * PAIRS, forward, 0)
+        lax.fori_loop(0, 8 * PAIRS, forward, 0, unroll=2)
 
         def error_plane(index, carry):
             pair = index // SUB
@@ -252,7 +252,7 @@
             store_planes(errors, pair, x, channels)
             return carry
 
-        lax.fori_loop(0, SUB * PAIRS, error_plane, 0)
+        lax.fori_loop(0, SUB * PAIRS, error_plane, 0, unroll=8)
 
         def backward(index, carry):
             pair = index // 4
@@ -267,14 +267,15 @@
         lax.fori_loop(0, 4 * PAIRS, backward, 0)
 
         def folded(grad_ref, select_ref):
-            total = jnp.zeros((CH, 256), jnp.float32)
+            total = jnp.zeros((3 * CH, 256), jnp.float32)
             for cell in range(4):
                 rest = grad_ref[cell * CH : (cell + 1) * CH, :]
+                parts = []
                 for _ in range(3):
-                    part = rest.astype(jnp.bfloat16)
-                    total = total + dot_lanes(part, select_ref[cell])
-                    rest = rest - part.astype(jnp.float32)
-            return total
+                    parts.append(rest.astype(jnp.bfloat16))
+                    rest = rest - parts[-1].astype(jnp.float32)
+                total = total + dot_lanes(jnp.concatenate(parts, axis=0), select_ref[cell])
+            return total[:CH] + total[CH : 2 * CH] + total[2 * CH :]
 
         now_first[...] = now_first[...] - inner_rate * folded(grad_first, select_first)
         now_last[...] = now_last[...] - inner_rate * folded(grad_last, select_last)
@@ -413,7 +414,13 @@
     return jnp.transpose(split, (1, 0, 3, 5, 2, 4)).reshape(SUB * F, 256)
 
 
-def slot_lists(sample_trainer, column, trainers):
+def doubling_steps(x_devices, y_devices):
+    along_y = [1 << bit for bit in reversed(range(y_devices.bit_length() - 1))]
+    along_x = [y_devices << bit for bit in reversed(range(x_devices.bit_length() - 1))]
+    return along_y + along_x
+
+
+def slot_lists(sample_trainer, column, trainers, groups, steps):
     owner_ids = jnp.arange(sample_trainer.shape[0], dtype=jnp.int32)
     same_trainer = sample_trainer[:, None] == sample_trainer[None, :]
     earlier = owner_ids[None, :] < owner_ids[:, None]
@@ -424,8 +431,12 @@
     slot_owner = jnp.sum(jnp.where(chosen, owner_ids[None, :], 0), axis=1)
     slot_valid = jnp.any(chosen, axis=1)
     sample_count = jnp.maximum(jnp.sum(mine_mask.astype(jnp.int32)), 1)
-    shift = jnp.mod(column - slot_owner % trainers, trainers)
-    table = jnp.stack([shift, slot_owner // trainers, slot_valid.astype(jnp.int32)])
+    apart = jnp.bitwise_xor(slot_owner % trainers, column)
+    place = jnp.zeros_like(apart)
+    for order, distance in enumerate(steps[:-1]):
+        place = place + (apart // distance % 2) * (1 << order)
+    half = apart // steps[-1] % 2
+    table = jnp.stack([half, place * groups + slot_owner // trainers, slot_valid.astype(jnp.int32)])
     slot_weight = jnp.where(slot_valid, 1.0 / (sample_count.astype(jnp.float32) * CELLS), 0.0)
     weights = jnp.repeat(2.0 * slot_weight, 64).reshape(PAIRS, 1, 128)
     return table.astype(jnp.int32), jnp.broadcast_to(weights, (PAIRS, 8, 128))
@@ -487,6 +498,9 @@
     change = cube_tendency(core, closure_in, closure_bias, closure_out)
     payload = jnp.concatenate([patch_rows(core[:, 1:-1, 1:-1, 1:-1]), patch_rows(change)], axis=0)
 
+    def swap(distance):
+        return [(first_trainer + c, first_trainer + (c ^ distance)) for c in range(trainers)]
+
     landed = jnp.stack(
         [
             lax.ppermute(
@@ -497,14 +511,13 @@
             for g in range(group_count - 1)
         ]
     )
-    arrived = [landed]
-    for shift in range(1, trainers):
-        pairs = [
-            (first_trainer + c, first_trainer + (c + shift) % trainers) for c in range(trainers)
-        ]
-        arrived.append(lax.ppermute(landed, everyone, pairs))
-
-    slots, weights = slot_lists(sample_trainer, my_column, trainers)
+    steps = doubling_steps(x_devices, y_devices)
+    held = landed
+    for distance in steps[:-1]:
+        held = jnp.concatenate([held, lax.ppermute(held, everyone, swap(distance))], axis=0)
+    arrived = [held, lax.ppermute(held, everyone, swap(steps[-1]))]
+
+    slots, weights = slot_lists(sample_trainer, my_column, trainers, group_count - 1, steps)
     first_count = CH * TAPS * F
     first = jnp.pad(master[:first_count].reshape(CH, TAPS * F), ((0, 0), (0, 256 - TAPS * F)))
     last = jnp.pad(master[first_count:].reshape(TAPS * F, CH).T, ((0, 0), (0, 256 - TAPS * F)))
@@ -527,25 +540,9 @@
 
     delta, new_brick = lax.cond(is_trainer, train_here, evolve_here)
 
-    part_size = NPARAM // trainers
-    total = jnp.zeros((NPARAM,), jnp.float32)
-    mine = lax.dynamic_slice_in_dim(delta, my_column * part_size, part_size)
-    for shift in range(1, trainers):
-        pairs = [
-            (first_trainer + c, first_trainer + (c + shift) % trainers) for c in range(trainers)
-        ]
-        target = (my_column + shift) % trainers
-        piece = lax.dynamic_slice_in_dim(delta, target * part_size, part_size)
-        mine = mine + lax.ppermute(piece, everyone, pairs)
-    total = lax.dynamic_update_slice_in_dim(total, mine, my_column * part_size, 0)
-    for shift in range(1, trainers):
-        pairs = [
-            (first_trainer + c, first_trainer + (c + shift) % trainers) for c in range(trainers)
-        ]
-        source = (my_column - shift) % trainers
-        total = lax.dynamic_update_slice_in_dim(
-            total, lax.ppermute(mine, everyone, pairs), source * part_size, 0
-        )
+    total = delta
+    for distance in steps:
+        total = total + lax.ppermute(total, everyone, swap(distance))
     final = jnp.where(is_trainer, total, 0.0)
     for g in range(group_count - 1):
         pairs = [(first_trainer + c, g * trainers + c) for c in range(trainers)]

time: 242 us -> 191 us (0.79)
  waiting for transfers between devices: 143 us -> 105 us
  starting transfers between devices: 27.6 us -> 17.6 us
    ppermute x3, waiting for transfers between devices: 141 us -> 103 us  [on_device(): final = final + lax.ppermute(total, everyone, pairs)]
    ppermute x21 -> x6, starting transfers between devices: 14.2 us -> 4.21 us  [the longest x3 1.98 us: on_device(): total = total + lax.ppermute(total, everyone, swap(distance))]
    unnamed x16 -> x32, local copies, waits for them, and re-layouts: 4.53 us -> 5.67 us
  transfers between devices with their start and end apart: 31 -> 16, of which waited for: 3 -> 3; matrix products, arithmetic and copies ran while one was open for 2% -> 1% of each run, Pallas kernels for 0% -> 0%
where the time goes in v1:
time: 191 us; the launch traced here: 190 us
  waiting for transfers between devices  105 us (55%)
  Pallas kernels  37.9 us (20%)
  starting transfers between devices  17.6 us (9%)
  local copies, waits for them, and re-layouts  15.4 us (8%)
  other arithmetic  6.15 us (3%)
  between operations  5.91 us (3%)
    ppermute x3, waiting for transfers between devices, on_device(): final = final + lax.ppermute(total, everyone, pairs)  103 us
    pallas_call x1, Pallas kernels, evolve(): pl.pallas_call(evolve_kernel, out_shape=jax.ShapeDtypeStruct(fields.shape...  37.9 us
    unnamed x32, local copies, waits for them, and re-layouts  5.67 us
    ppermute x2, starting transfers between devices, neighbours(): lax.ppermute(values_low, axis, [((i + 1) % count, i) for i in range(count)])  5.12 us
  transfers between devices with their start and end apart: 16, of which 3 were waited for; matrix products, arithmetic and copies ran while one was open for 1% of the time, Pallas kernels for 0%

profile of v1, /device:TPU:0, one launch (start us, length us, event | category | flops | bytes accessed | tf_op | source)
XLA Modules:
  0.0 190.0 jit_solution(9959397715220213594)
XLA Ops:
  0.6 4.4 %copy.81 = f32[1,5,16,32,384]{4,2,1,3,0:T(8,128)S(1)} copy(f32[1,5,16,32,384]{4,3,2,1,0:T(8,128)} %param.14) | data formatting | bytes 7864320 | tf_op args[0]
  5.1 0.3 fusion.30
  5.4 3.0 %collective-permute-start.1 = (f32[5,1,32,384]{3,1,0,2:T(1,128)S(1)}, f32[5,1,32,384]{3,1,0,2:T(1,128)S(1)}, u32[]{:S(2)}, u32[]{:S(2)}) collective-permute-start(f32[5,1,32,384]{3,1,0,2:T(1,128)S(1)} %get-tuple-element.200), channel_id=1, source_target_pairs={{4,0},{0,4},{5,1},{1,5},{6,2},{2,6},{7,3},{3,7},{12,8},{8,12},{13,... | collective-permute-start | bytes 737288 | tf_op jit(solution)/shard_map/ppermute | solution.py:463
  8.5 2.1 %collective-permute-start.2 = (f32[5,16,384]{2,1,0:T(8,128)S(1)}, f32[5,16,384]{2,1,0:T(8,128)S(1)}, u32[]{:S(2)}, u32[]{:S(2)}) collective-permute-start(f32[5,16,384]{2,1,0:T(8,128)S(1)} %get-tuple-element.199), channel_id=1, source_target_pairs={{0,1},{1,2},{2,3},{3,0},{4,5},{5,6},{6,7},{7,4},{8,9},{9,10},{10,1... | collective-permute-start | bytes 368648 | tf_op jit(solution)/shard_map/ppermute | solution.py:462
  10.6 2.1 %collective-permute-start.3 = (f32[5,16,384]{2,1,0:T(8,128)S(1)}, f32[5,16,384]{2,1,0:T(8,128)S(1)}, u32[]{:S(2)}, u32[]{:S(2)}) collective-permute-start(f32[5,16,384]{2,1,0:T(8,128)S(1)} %get-tuple-element.198), channel_id=1, source_target_pairs={{1,0},{2,1},{3,2},{0,3},{5,4},{6,5},{7,6},{4,7},{9,8},{10,9},{11,1... | collective-permute-start | bytes 368648 | tf_op jit(solution)/shard_map/ppermute | solution.py:463
  12.7 0.6 dynamic_slice.30
  16.6 0.6 convert_reduce_fusion.1
  17.2 0.2 convert_reduce_fusion
  17.7 0.4 copy-done.6
  18.1 0.1 copy-done.8
  18.4 1.3 collective-permute-done
  19.8 0.5 copy-done.4
  20.4 1.6 fusion.4
  22.0 0.2 slice.136
  22.2 0.2 slice_bitcast_fusion.3
  22.4 0.2 slice.168
  22.6 0.2 copy.69
  22.8 0.3 reshape.387
  23.2 1.0 fusion
  24.3 0.9 fusion.5
  25.3 1.1 multiply_subtract_fusion
  26.6 0.2 copy.71
  26.8 0.7 copy.72
  27.5 0.8 reshape.389
  28.4 0.2 copy.67
  28.6 0.7 copy.68
  29.3 0.9 reshape.386
  30.2 2.2 %collective-permute-start.4 = (bf16[160,256]{1,0:T(8,128)(2,1)S(1)}, bf16[160,256]{1,0:T(8,128)(2,1)S(1)}, u32[]{:S(2)}, u32[]{:S(2)}) collective-permute-start(bf16[160,256]{1,0:T(8,128)(2,1)S(1)} %constant_dynamic-update-slice_fusion), channel_id=1, source_target_pairs={{0,24},{1,25},{2,26},{3,27},{4,28},{5,29},{6,30},{7,31}} | collective-permute-start | bytes 245768 | tf_op jit(solution)/shard_map/ppermute | solution.py:506
  32.4 0.7 collective-permute-start.5
  33.1 0.7 collective-permute-start.6
  33.8 0.1 fusion.18
  33.9 0.7 collective-permute-done.4
  34.6 0.7 collective-permute-start.7
  36.2 0.8 collective-permute-start.8
  37.2 0.7 collective-permute-start.9
  37.9 0.1 select_reduce_fusion
  38.1 41.5 %conditional.1 = (f32[17280]{0:T(1024)S(1)}, f32[1,5,16,32,384]{4,3,2,1,0:T(8,128)}) conditional(s32[]{:T(128)} %convert_element_type.42, (f32[7,64]{1,0:T(8,128)S(1)}, f32[5,16,32,384]{3,1,0,2:T(8,128)}, f32[5,1,32,384]{3,1,0,2:T(1,128)S(1)}, f32[5,1,32,384]{3,1,0,2:T(1,128)S(1)}, f32[5,16,384]{2,1,0:T(8,128)S(1)}, ...), branch_computations={%region_4.5_spmd, %region_5.6_spmd.clone} | conditional | flops 17294 | bytes 28366062 | solution.py:541
  38.3 3.3 %copy.73.fields = f32[5,16,32,384]{3,2,1,0:T(8,128)S(1)} copy(f32[5,16,32,384]{3,1,0,2:T(8,128)} %get-tuple-element.179) | data formatting | bytes 7864320 | tf_op jit(solution)/shard_map
  41.7 37.9 %evolve_brick.1 = f32[5,16,32,384]{3,2,1,0:T(8,128)} custom-call(f32[7,64]{1,0:T(8,128)S(1)} %get-tuple-element.87.closure, f32[5,16,32,384]{3,2,1,0:T(8,128)S(1)} %copy.73.fields, f32[5,1,32,384]{3,2,1,0:T(8,128)S(1)} %copy.74.x_low, f32[5,1,32,384]{3,2,1,0:T(8,128)S(1)} %copy.75.x_high, f32[5,16,384]{2,1,0:T(8,128)S(1)} %get-tuple-element.91.y_low, ...), custom_call_target="tpu_custom_call" | custom-call | tf_op jit(solution)/shard_map/cond/branch_0_fun/evolve_brick/pallas_call | solution.py:386
  79.7 0.7 collective-permute-start.10
  80.3 0.7 collective-permute-start.11
  81.0 0.7 collective-permute-start.12
  81.7 1.3 collective-permute-start.13
  83.0 0.7 collective-permute-start.14
  83.7 0.7 collective-permute-start.15
  84.4 102.9 %collective-permute-done.13 = f32[17280]{0:T(1024)S(1)} collective-permute-done((f32[17280]{0:T(1024)S(1)}, f32[17280]{0:T(1024)S(1)}, u32[]{:S(2)}, u32[]{:S(2)}) %collective-permute-start.13) | collective-permute-done | bytes 69152 | tf_op jit(solution)/shard_map/ppermute | solution.py:549
  187.3 0.6 multiply_reduce_fusion
  188.7 1.4 multiply_subtract_fusion.1
  (76 shorter events, 1.5 us)
Async XLA Ops:
  5.0 3.5 %copy-start.3 = (f32[1,5,16,32,384]{4,2,1,3,0:T(8,128)}, f32[1,5,16,32,384]{4,2,1,3,0:T(8,128)S(1)}, u32[]{:S(2)}) copy-start(f32[1,5,16,32,384]{4,2,1,3,0:T(8,128)S(1)} %copy.81) | copy-start | bytes 11796484
  5.0 7.7 %copy-start.15 = (s32[24]{0:T(128)S(1)}, s32[24]{0:T(128)}, u32[]{:S(2)}) copy-start(s32[24]{0:T(128)} %param.20) | copy-start | bytes 292
  5.0 11.5 %copy-start.14 = (s32[24]{0:T(128)S(1)}, s32[24]{0:T(128)}, u32[]{:S(2)}) copy-start(s32[24]{0:T(128)} %param.21) | copy-start | bytes 292
  5.4 12.8 %collective-permute-start.1 = (f32[5,1,32,384]{3,1,0,2:T(1,128)S(1)}, f32[5,1,32,384]{3,1,0,2:T(1,128)S(1)}, u32[]{:S(2)}, u32[]{:S(2)}) collective-permute-start(f32[5,1,32,384]{3,1,0,2:T(1,128)S(1)} %get-tuple-element.200), channel_id=1, source_target_pairs={{4,0},{0,4},{5,1},{1,5},{6,2},{2,6},{7,3},{3,7},{12,8},{8,12},{13,... | collective-permute-start | bytes 737288 | tf_op jit(solution)/shard_map/ppermute | solution.py:463
  8.4 11.2 %collective-permute-start = (f32[5,1,32,384]{3,1,0,2:T(1,128)S(1)}, f32[5,1,32,384]{3,1,0,2:T(1,128)S(1)}, u32[]{:S(2)}, u32[]{:S(2)}) collective-permute-start(f32[5,1,32,384]{3,1,0,2:T(1,128)S(1)} %get-tuple-element.201), channel_id=1, source_target_pairs={{0,4},{4,0},{1,5},{5,1},{2,6},{6,2},{3,7},{7,3},{8,12},{12,8},{9,1... | collective-permute-start | bytes 737288 | tf_op jit(solution)/shard_map/ppermute | solution.py:462
  8.5 8.9 %collective-permute-start.2 = (f32[5,16,384]{2,1,0:T(8,128)S(1)}, f32[5,16,384]{2,1,0:T(8,128)S(1)}, u32[]{:S(2)}, u32[]{:S(2)}) collective-permute-start(f32[5,16,384]{2,1,0:T(8,128)S(1)} %get-tuple-element.199), channel_id=1, source_target_pairs={{0,1},{1,2},{2,3},{3,0},{4,5},{5,6},{6,7},{7,4},{8,9},{9,10},{10,1... | collective-permute-start | bytes 368648 | tf_op jit(solution)/shard_map/ppermute | solution.py:462
  10.6 7.0 %collective-permute-start.3 = (f32[5,16,384]{2,1,0:T(8,128)S(1)}, f32[5,16,384]{2,1,0:T(8,128)S(1)}, u32[]{:S(2)}, u32[]{:S(2)}) collective-permute-start(f32[5,16,384]{2,1,0:T(8,128)S(1)} %get-tuple-element.198), channel_id=1, source_target_pairs={{1,0},{2,1},{3,2},{0,3},{5,4},{6,5},{7,6},{4,7},{9,8},{10,9},{11,1... | collective-permute-start | bytes 368648 | tf_op jit(solution)/shard_map/ppermute | solution.py:463
  17.5 0.7 copy-start.6
  17.6 0.6 copy-start.8
  19.7 0.7 copy-start.4
  22.5 0.7 copy-start.11
  22.5 0.7 copy-start.12
  22.8 1.5 copy-start.13
  28.6 7.3 %copy-start.10 = (f32[17280]{0:T(1024)S(1)}, f32[17280]{0:T(1024)}, u32[]{:S(2)}) copy-start(f32[17280]{0:T(1024)} %param.18) | copy-start | bytes 207364
  30.2 4.3 %collective-permute-start.4 = (bf16[160,256]{1,0:T(8,128)(2,1)S(1)}, bf16[160,256]{1,0:T(8,128)(2,1)S(1)}, u32[]{:S(2)}, u32[]{:S(2)}) collective-permute-start(bf16[160,256]{1,0:T(8,128)(2,1)S(1)} %constant_dynamic-update-slice_fusion), channel_id=1, source_target_pairs={{0,24},{1,25},{2,26},{3,27},{4,28},{5,29},{6,30},{7,31}} | collective-permute-start | bytes 245768 | tf_op jit(solution)/shard_map/ppermute | solution.py:506
  32.4 2.1 %collective-permute-start.5 = (bf16[160,256]{1,0:T(8,128)(2,1)S(1)}, bf16[160,256]{1,0:T(8,128)(2,1)S(1)}, u32[]{:S(2)}, u32[]{:S(2)}) collective-permute-start(bf16[160,256]{1,0:T(8,128)(2,1)S(1)} %constant_dynamic-update-slice_fusion), channel_id=1, source_target_pairs={{8,24},{9,25},{10,26},{11,27},{12,28},{13,29},{14,30},{15,31}} | collective-permute-start | bytes 245768 | tf_op jit(solution)/shard_map/ppermute | solution.py:506
  33.1 1.5 collective-permute-start.6
  34.6 1.5 collective-permute-start.7
  36.2 1.9 %copy-start.5 = (f32[5,1,32,384]{3,1,0,2:T(1,128)S(1)}, f32[5,1,32,384]{3,1,0,2:T(1,128)}, u32[]{:S(2)}) copy-start(f32[5,1,32,384]{3,1,0,2:T(1,128)} %copy-done.4) | copy-start | bytes 737284
  36.2 1.9 %copy-start.7 = (f32[5,16,384]{2,1,0:T(8,128)S(1)}, f32[5,16,384]{2,1,0:T(8,128)}, u32[]{:S(2)}) copy-start(f32[5,16,384]{2,1,0:T(8,128)} %copy-done.6) | copy-start | bytes 368644
  36.2 1.9 %copy-start.9 = (f32[5,16,384]{2,1,0:T(8,128)S(1)}, f32[5,16,384]{2,1,0:T(8,128)}, u32[]{:S(2)}) copy-start(f32[5,16,384]{2,1,0:T(8,128)} %copy-done.8) | copy-start | bytes 368644
  36.2 0.9 collective-permute-start.8
  37.2 0.9 collective-permute-start.9
  79.7 0.7 collective-permute-start.10
  80.3 0.7 collective-permute-start.11
  81.0 0.7 collective-permute-start.12
  81.7 105.6 %collective-permute-start.13 = (f32[17280]{0:T(1024)S(1)}, f32[17280]{0:T(1024)S(1)}, u32[]{:S(2)}, u32[]{:S(2)}) collective-permute-start(f32[17280]{0:T(1024)S(1)} %add.286), channel_id=1, source_target_pairs={{24,0},{25,1},{26,2},{27,3},{28,4},{29,5},{30,6},{31,7}} | collective-permute-start | bytes 207368 | tf_op jit(solution)/shard_map/ppermute | solution.py:549
  83.0 104.3 %collective-permute-start.14 = (f32[17280]{0:T(1024)S(1)}, f32[17280]{0:T(1024)S(1)}, u32[]{:S(2)}, u32[]{:S(2)}) collective-permute-start(f32[17280]{0:T(1024)S(1)} %add.286), channel_id=1, source_target_pairs={{24,8},{25,9},{26,10},{27,11},{28,12},{29,13},{30,14},{31,15}} | collective-permute-start | bytes 207368 | tf_op jit(solution)/shard_map/ppermute | solution.py:549
  83.7 103.6 %collective-permute-start.15 = (f32[17280]{0:T(1024)S(1)}, f32[17280]{0:T(1024)S(1)}, u32[]{:S(2)}, u32[]{:S(2)}) collective-permute-start(f32[17280]{0:T(1024)S(1)} %add.286), channel_id=1, source_target_pairs={{24,16},{25,17},{26,18},{27,19},{28,20},{29,21},{30,22},{31,23}} | collective-permute-start | bytes 207368 | tf_op jit(solution)/shard_map/ppermute | solution.py:549

commit v2 on v1

v2 whole, which is shorter than its diff:
```python
import functools

import jax
import jax.numpy as jnp
import numpy as np
from jax import lax
from jax.experimental import pallas as pl
from jax.experimental.pallas import tpu as pltpu
from jax.sharding import PartitionSpec as P

F = 5
CH = 64
HID = 64
SUB = 16
TCAP = 6
INNER = 3
CELLS = 4096
NPARAM = 17280
TAPS = 27
PAIRS = TCAP // 2
COLS = (SUB + 2) * 128
PATCH = 16 * F
STACK = 3 * PATCH

time_step = 0.1
base_viscosity = 0.02
viscosity_gain = 0.2
buoyancy = 0.5
inner_rate = 0.02
outer_rate = 0.01
momentum_decay = 0.9
norm_epsilon = 1e-06


def patch_position(row):
    group, py, pz = row // 4, row // 2 % 2, row % 2
    ypos = py + 1 if group in (0, 1) else (3 if py == 0 else 0)
    zpos = pz + 1 if group in (0, 2) else (3 if pz == 0 else 0)
    return ypos - 1, zpos - 1


def selections():
    first = np.zeros((4, 256, STACK), np.float32)
    last = np.zeros((4, 256, STACK), np.float32)
    for cell in range(4):
        py, pz = cell // 2, cell % 2
        for kx in range(3):
            for channel in range(F):
                for row in range(16):
                    ypos, zpos = patch_position(row)
                    column = kx * PATCH + channel * 16 + row
                    dy, dz = ypos - py, zpos - pz
                    if abs(dy) <= 1 and abs(dz) <= 1:
                        tap = 9 * kx + 3 * (dy + 1) + dz + 1
                        first[cell, tap * F + channel, column] = 1.0
                        last[cell, channel * TAPS + 26 - tap, column] = 1.0
    return first, last


SELECT_FIRST, SELECT_LAST = selections()


def dot_rows(left, right):
    return jnp.dot(left, right, preferred_element_type=jnp.float32)


def dot_lanes(left, right):
    return lax.dot_general(left, right, (((1,), (1,)), ((), ())), preferred_element_type=jnp.float32)


def patch_masks():
    row = lax.broadcasted_iota(jnp.int32, (8, 128), 0)
    lane = lax.broadcasted_iota(jnp.int32, (8, 128), 1)
    return {
        "pz0": row % 2 == 0,
        "py0": row // 2 % 2 == 0,
        "centre": row < 4,
        "z_first": lane % 8 == 0,
        "z_last": lane % 8 == 7,
        "y_first": lane // 8 % 8 == 0,
        "y_last": lane // 8 % 8 == 7,
    }


def edge_shift(values, step, parity_zero, first, last, forward):
    before = jnp.where(first, 0.0, pltpu.roll(values, step, 1))
    after = jnp.where(last, 0.0, pltpu.roll(values, 128 - step, 1))
    if forward:
        return jnp.where(parity_zero, after, before)
    return jnp.where(parity_zero, before, after)


def patch_stack(rows, masks):
    both = rows + pltpu.roll(rows, 4, 0)
    z_edge = edge_shift(both, 1, masks["pz0"], masks["z_first"], masks["z_last"], True)
    upper = jnp.where(masks["centre"], both, z_edge)
    lower = edge_shift(upper, 8, masks["py0"], masks["y_first"], masks["y_last"], True)
    return upper, lower


def patch_fold(upper, lower, masks):
    def fold_z(values):
        moved = edge_shift(values, 1, masks["pz0"], masks["z_first"], masks["z_last"], False)
        return values + pltpu.roll(moved, 4, 0)

    shifted = edge_shift(fold_z(lower), 8, masks["py0"], masks["y_first"], masks["y_last"], False)
    return fold_z(upper) + shifted


def store_planes(ref, pair, x, channels):
    stacked = jnp.concatenate([part for both in channels for part in both], axis=0).astype(jnp.bfloat16)
    for kx in range(3):
        start = pl.multiple_of((x + 2 - kx) * 128, 128)
        ref[pair, kx * PATCH : (kx + 1) * PATCH, pl.ds(start, 128)] = stacked


def train_kernel(steps, *refs):
    (trainer_of, place, first_ref, last_ref, select_first, select_last) = refs[:6]
    arrived_inputs, arrived_targets = refs[6:8], refs[8:10]
    fields_ref = refs[10]
    delta_first, delta_last, new_fields_ref = refs[11:14]
    (
        slots,
        cubes,
        table,
        targets,
        inputs,
        errors,
        hiddens,
        pre_grads,
        slopes,
        partial_out,
        big_first,
        big_last,
        big_last_t,
        now_first,
        now_last,
        slot_sems,
        field_sem,
    ) = refs[14:]

    field_copy = pltpu.make_async_copy(fields_ref, new_fields_ref, field_sem)
    field_copy.start()

    groups = place[3]
    trainers = trainer_of.shape[0] // groups
    column = place[1] * place[4] + place[2]

    def visit(owner, count):
        mine = trainer_of[owner] == column

        @pl.when(mine)
        def _():
            source = lax.rem(owner, trainers)
            entry = jnp.int32(0)
            for order, distance in enumerate(steps[:-1]):
                entry = entry + apart(source, column, distance) * (1 << order)
            slots[0, count] = apart(source, column, steps[-1])
            slots[1, count] = entry * groups + lax.div(owner, trainers)

        return count + jnp.where(mine, 1, 0)

    count = lax.fori_loop(0, trainer_of.shape[0], visit, jnp.int32(0))

    def fetch(slot, wait):
        for kind, arrived in enumerate((arrived_inputs, arrived_targets)):
            for half in range(2):

                @pl.when((slot < count) & (slots[0, slot] == half))
                def _():
                    copy = pltpu.make_async_copy(
                        arrived[half].at[slots[1, slot]], cubes.at[kind, slot], slot_sems.at[kind, slot]
                    )
                    copy.wait() if wait else copy.start()

    for slot in range(TCAP):
        fetch(slot, False)

        @pl.when(slot >= count)
        def _():
            cubes[:, slot] = jnp.zeros((2, SUB * F, 256), jnp.bfloat16)

    masks = patch_masks()
    for ref in (errors, inputs):
        ref[:, :PATCH, 128:256] = jnp.zeros((PAIRS, PATCH, 128), jnp.bfloat16)
        ref[:, 2 * PATCH :, COLS - 256 : COLS - 128] = jnp.zeros((PAIRS, PATCH, 128), jnp.bfloat16)
    partial_out[:, :, :128] = jnp.zeros((PAIRS, STACK, 128), jnp.float32)
    partial_out[:, :, COLS - 128 :] = jnp.zeros((PAIRS, STACK, 128), jnp.float32)
    table[...] = jnp.zeros(table.shape, table.dtype)
    targets[...] = jnp.zeros(targets.shape, targets.dtype)
    lane = lax.broadcasted_iota(jnp.int32, (8, 128), 1)
    full_weight = 2.0 * (1.0 / (jnp.full((8, 128), count, jnp.int32).astype(jnp.float32) * CELLS))
    weights = [
        jnp.where(lane // 64 + 2 * pair < count, full_weight, 0.0) for pair in range(PAIRS)
    ]
    start_first = first_ref[...].astype(jnp.bfloat16).astype(jnp.float32)
    start_last = last_ref[...].astype(jnp.bfloat16).astype(jnp.float32)
    now_first[...] = start_first
    now_last[...] = start_last

    for slot in range(TCAP):
        fetch(slot, True)

    low_lanes = lax.broadcasted_iota(jnp.int32, (SUB * F, 128), 1) < 64

    def spread_rows(pair, kind, put):
        even = cubes[kind, 2 * pair].astype(jnp.float32)
        odd = cubes[kind, 2 * pair + 1].astype(jnp.float32)
        for half in range(2):
            left = even[:, half * 128 : (half + 1) * 128]
            right = odd[:, half * 128 : (half + 1) * 128]
            put(2 * half, jnp.where(low_lanes, left, pltpu.roll(right, 64, 1)))
            put(2 * half + 1, jnp.where(low_lanes, pltpu.roll(left, 64, 1), right))

    for pair in range(PAIRS):

        def put_input(cell, values):
            table[pl.ds(cell, SUB * F, 8), :] = values

        def put_target(cell, values):
            targets[pl.ds(pair * SUB * F * 8 + cell, SUB * F, 8), :] = values

        spread_rows(pair, 0, put_input)
        spread_rows(pair, 1, put_target)

        def stack_plane(x, carry):
            channels = [
                patch_stack(table[pl.ds(pl.multiple_of((c * SUB + x) * 8, 8), 8), :], masks)
                for c in range(F)
            ]
            store_planes(inputs, pair, x, channels)
            return carry

        lax.fori_loop(0, SUB, stack_plane, 0, unroll=8)

    def train_step(step, step_carry):
        first_now = now_first[...].astype(jnp.bfloat16)
        last_now = now_last[...].astype(jnp.bfloat16)
        for cell in range(4):
            rows = slice(cell * CH, (cell + 1) * CH)
            big_first[rows, :] = dot_rows(first_now, select_first[cell]).astype(jnp.bfloat16)
            big_last[rows, :] = dot_rows(last_now, select_last[cell]).astype(jnp.bfloat16)
        big_last_t[...] = big_last[...].T
        def forward(index, carry):
            pair = index // 4
            column = pl.multiple_of((index % 4) * 512 + 128, 128)
            pre = dot_rows(big_first[...], inputs[pair, :, pl.ds(column, 512)])
            sigmoid = 0.5 * jnp.tanh(0.5 * pre) + 0.5
            value = pre * sigmoid
            hidden = value.astype(jnp.bfloat16)
            hiddens[pair, :, pl.ds(column, 512)] = hidden
            slopes[pair, :, pl.ds(column, 512)] = sigmoid + value * (1.0 - sigmoid)
            partial_out[pair, :, pl.ds(column, 512)] = dot_rows(big_last_t[...], hidden)
            return carry

        lax.fori_loop(0, 4 * PAIRS, forward, 0, unroll=2)

        def error_plane(index, carry):
            pair = index // SUB
            x = index % SUB
            column = pl.multiple_of((x + 1) * 128, 128)
            total = (
                partial_out[pair, 0:PATCH, pl.ds(pl.multiple_of(column + 128, 128), 128)]
                + partial_out[pair, PATCH : 2 * PATCH, pl.ds(column, 128)]
                + partial_out[pair, 2 * PATCH :, pl.ds(pl.multiple_of(column - 128, 128), 128)]
            )
            weight = jnp.where(pair == 0, weights[0], jnp.where(pair == 1, weights[1], weights[2]))
            channels = []
            for c in range(F):
                predicted = patch_fold(
                    total[16 * c : 16 * c + 8], total[16 * c + 8 : 16 * c + 16], masks
                )
                row = pl.multiple_of(((pair * F + c) * SUB + x) * 8, 8)
                error = weight * (predicted - targets[pl.ds(row, 8), :])
                error = jnp.where(masks["centre"], error, 0.0)
                error = error.astype(jnp.bfloat16).astype(jnp.float32)
                channels.append(patch_stack(error, masks))
            store_planes(errors, pair, x, channels)
            return carry

        lax.fori_loop(0, SUB * PAIRS, error_plane, 0, unroll=8)

        def backward(index, carry):
            pair = index // 4
            column = pl.multiple_of((index % 4) * 512 + 128, 128)
            hidden_grad = dot_rows(big_last[...], errors[pair, :, pl.ds(column, 512)])
            slope = slopes[pair, :, pl.ds(column, 512)]
            pre_grads[pair, :, pl.ds(column, 512)] = (hidden_grad * slope).astype(jnp.bfloat16)
            return carry

        lax.fori_loop(0, 4 * PAIRS, backward, 0, unroll=2)
        body = slice(128, COLS - 128)
        grad_first = jnp.zeros((4 * CH, STACK), jnp.float32)
        grad_last = jnp.zeros((4 * CH, STACK), jnp.float32)
        for pair in range(PAIRS):
            grad_first += dot_lanes(pre_grads[pair, :, body], inputs[pair, :, body])
            grad_last += dot_lanes(hiddens[pair, :, body], errors[pair, :, body])

        def folded(grad, select_ref):
            total = jnp.zeros((3 * CH, 256), jnp.float32)
            for cell in range(4):
                rest = grad[cell * CH : (cell + 1) * CH, :]
                parts = []
                for _ in range(3):
                    parts.append(rest.astype(jnp.bfloat16))
                    rest = rest - parts[-1].astype(jnp.float32)
                total = total + dot_lanes(jnp.concatenate(parts, axis=0), select_ref[cell])
            return total[:CH] + total[CH : 2 * CH] + total[2 * CH :]

        now_first[...] = now_first[...] - inner_rate * folded(grad_first, select_first)
        now_last[...] = now_last[...] - inner_rate * folded(grad_last, select_last)
        return step_carry

    lax.fori_loop(0, INNER, train_step, 0)
    delta_first[...] = start_first - now_first[...]
    delta_last[...] = start_last - now_last[...]
    field_copy.wait()


def apart(left, right, distance):
    return jnp.where(lax.rem(lax.div(left, distance), 2) == lax.rem(lax.div(right, distance), 2), 0, 1)


def train_cubes(trainer_of, place, first, last, arrived_inputs, arrived_targets, fields, steps):
    vmem = pl.BlockSpec(memory_space=pltpu.VMEM)
    smem = pl.BlockSpec(memory_space=pltpu.SMEM)
    anywhere = pl.BlockSpec(memory_space=pl.ANY)
    hbm = pl.BlockSpec(memory_space=pltpu.HBM)
    return pl.pallas_call(
        functools.partial(train_kernel, steps),
        out_shape=(
            jax.ShapeDtypeStruct((CH, 256), jnp.float32),
            jax.ShapeDtypeStruct((CH, 256), jnp.float32),
            jax.ShapeDtypeStruct(fields.shape, fields.dtype),
        ),
        in_specs=[smem] * 2 + [vmem] * 4 + [anywhere] * 4 + [hbm],
        out_specs=(vmem, vmem, hbm),
        scratch_shapes=[
            pltpu.SMEM((2, TCAP), jnp.int32),
            pltpu.VMEM((2, TCAP, SUB * F, 256), jnp.bfloat16),
            pltpu.VMEM((SUB * F * 8, 128), jnp.float32),
            pltpu.VMEM((PAIRS * SUB * F * 8, 128), jnp.float32),
            pltpu.VMEM((PAIRS, STACK, COLS), jnp.bfloat16),
            pltpu.VMEM((PAIRS, STACK, COLS), jnp.bfloat16),
            pltpu.VMEM((PAIRS, 4 * CH, COLS), jnp.bfloat16),
            pltpu.VMEM((PAIRS, 4 * CH, COLS), jnp.bfloat16),
            pltpu.VMEM((PAIRS, 4 * CH, COLS), jnp.float32),
            pltpu.VMEM((PAIRS, STACK, COLS), jnp.float32),
            pltpu.VMEM((4 * CH, STACK), jnp.bfloat16),
            pltpu.VMEM((4 * CH, STACK), jnp.bfloat16),
            pltpu.VMEM((STACK, 4 * CH), jnp.bfloat16),
            pltpu.VMEM((CH, 256), jnp.float32),
            pltpu.VMEM((CH, 256), jnp.float32),
            pltpu.SemaphoreType.DMA((2, TCAP)),
            pltpu.SemaphoreType.DMA,
        ],
        compiler_params=pltpu.CompilerParams(vmem_limit_bytes=48 * 1024 * 1024),
        name="train_cubes",
    )(
        trainer_of,
        place,
        first,
        last,
        jnp.asarray(SELECT_FIRST, jnp.bfloat16),
        jnp.asarray(SELECT_LAST, jnp.bfloat16),
        *arrived_inputs,
        *arrived_targets,
        fields,
    )


def viscosity_of(cells, closure_in, closure_bias, closure_out):
    halves = [0.5 * value for value in cells]

    def unit(h, total):
        half = 0.5 * closure_bias[h] + closure_in[h, 0] * halves[0]
        for f in range(1, F):
            half = half + closure_in[h, f] * halves[f]
        return total + closure_out[h] * (half + half * jnp.tanh(half))

    total = lax.fori_loop(0, HID, unit, jnp.zeros(cells[0].shape, jnp.float32), unroll=4)
    soft = jnp.maximum(total, 0.0) + jnp.log1p(jnp.exp(-jnp.abs(total)))
    return base_viscosity + viscosity_gain * soft


def evolve_kernel(
    closure_in, closure_bias, closure_out, fields, x_low, x_high, y_low, y_high, new_fields
):
    x_cells, y_cells, z_cells = fields.shape[1:]
    row = lax.broadcasted_iota(jnp.int32, (y_cells, z_cells), 0)
    lane = lax.broadcasted_iota(jnp.int32, (y_cells, z_cells), 1)
    part = y_cells // 2

    def plane(x, carry):
        eddies = []
        for half in range(2):
            rows = pl.ds(half * part, part)
            cells = [fields[f, x, rows, :] for f in range(F)]
            eddies.append(viscosity_of(cells, closure_in, closure_bias, closure_out))
        viscosity = jnp.concatenate(eddies, axis=0)
        centre = [fields[f, x] for f in range(F)]
        below = jnp.maximum(x - 1, 0)
        above = jnp.minimum(x + 1, x_cells - 1)
        for f in range(F):
            value = centre[f]
            west = jnp.where(x == 0, x_low[f], fields[f, below])
            east = jnp.where(x == x_cells - 1, x_high[f], fields[f, above])
            south = jnp.where(row == 0, y_low[f, pl.ds(x, 1), :], pltpu.roll(value, 1, 0))
            north = jnp.where(
                row == y_cells - 1, y_high[f, pl.ds(x, 1), :], pltpu.roll(value, y_cells - 1, 0)
            )
            lower = jnp.where(lane == 0, 0.0, pltpu.roll(value, 1, 1))
            upper = jnp.where(lane == z_cells - 1, 0.0, pltpu.roll(value, z_cells - 1, 1))
            laplacian = east + west + north + south + upper + lower - 6.0 * value
            advection = (
                centre[0] * (east - west) + centre[1] * (north - south) + centre[2] * (upper - lower)
            )
            tendency = viscosity * laplacian - 0.5 * advection
            if f == 2:
                tendency = tendency + buoyancy * centre[3]
            new_fields[f, x] = value + time_step * tendency
        return carry

    lax.fori_loop(0, x_cells, plane, 0)


def evolve(closure_in, closure_bias, closure_out, fields, x_low, x_high, y_low, y_high):
    vmem = pl.BlockSpec(memory_space=pltpu.VMEM)
    return pl.pallas_call(
        evolve_kernel,
        out_shape=jax.ShapeDtypeStruct(fields.shape, fields.dtype),
        in_specs=[pl.BlockSpec(memory_space=pltpu.SMEM)] * 3 + [vmem] * 5,
        out_specs=vmem,
        compiler_params=pltpu.CompilerParams(vmem_limit_bytes=48 * 1024 * 1024),
        name="evolve_brick",
    )(closure_in, closure_bias, closure_out, fields, x_low, x_high, y_low, y_high)


def cell_order():
    order = np.zeros((256, 256), np.float32)
    for y in range(SUB):
        for z in range(SUB):
            order[y * SUB + z, (y % 2 * 2 + z % 2) * 64 + y // 2 * 8 + z // 2] = 1.0
    return order


CELL_ORDER = cell_order()


def corner_of(sample_block, place, x_step, y_step, y_cells, z_cells):
    x_devices, y_devices = place[5], place[4]
    gx = lax.rem(place[1] + x_step + x_devices, x_devices)
    gy = lax.rem(place[2] + y_step + y_devices, y_devices)
    group = jnp.minimum(place[0], place[3] - 1)
    block = sample_block[(group * x_devices + gx) * y_devices + gy]
    z_blocks = z_cells // SUB
    return lax.rem(lax.div(block, z_blocks), y_cells // SUB) * SUB, lax.rem(block, z_blocks) * SUB


def sample_kernel(
    y_cells,
    z_cells,
    sample_block,
    place,
    order,
    brick,
    centre,
    lower,
    upper,
    own_rows,
    faces,
    row_for_low,
    row_for_high,
    payload,
    windows,
    sems,
):
    rows_of_x = y_cells
    rows_of_field = SUB * y_cells
    window_rows = F * rows_of_field
    copies = [
        pltpu.make_async_copy(
            brick.at[:, pl.ds(w * 128, 128)], windows.at[pl.ds(w * window_rows, window_rows)], sems.at[w]
        )
        for w in range(z_cells // 128)
    ]
    for copy in copies:
        copy.start()
    for copy in copies:
        copy.wait()

    def corner(x_step, y_step):
        return corner_of(sample_block, place, x_step, y_step, y_cells, z_cells)

    def piece(row, count, stride, z, lane_start):
        values = windows[pl.ds(lax.div(z, 128) * window_rows + row, count, stride), :]
        return pltpu.roll(values, lax.rem(lane_start - lax.rem(z, 128) + 256, 128), 1)

    lane = lax.broadcasted_iota(jnp.int32, (SUB, 128), 1)
    y_start, z_start = corner(0, 0)
    z_below = jnp.maximum(z_start - 1, 0)
    z_above = jnp.minimum(z_start + SUB, z_cells - 1)
    for field in range(F):
        for half in range(2):
            inside = jnp.zeros((SUB, 128), jnp.float32)
            below = jnp.zeros((SUB, 128), jnp.float32)
            above = jnp.zeros((SUB, 128), jnp.float32)
            for step in range(8):
                row = field * rows_of_field + y_start + half * 8 + step
                first = step * SUB
                inside = jnp.where(lane // SUB == step, piece(row, SUB, rows_of_x, z_start, first), inside)
                below = jnp.where(lane == first, piece(row, SUB, rows_of_x, z_below, first), below)
                last = first + SUB - 1
                above = jnp.where(lane == last, piece(row, SUB, rows_of_x, z_above, last), above)
            below = jnp.where(z_start == 0, 0.0, below)
            above = jnp.where(z_start + SUB == z_cells, 0.0, above)
            at = (slice(field * SUB, (field + 1) * SUB), slice(half * 128, (half + 1) * 128))
            centre[at] = inside
            lower[at] = jnp.where(lane % SUB == 0, below, pltpu.roll(inside, 1, 1))
            upper[at] = jnp.where(lane % SUB == SUB - 1, above, pltpu.roll(inside, 127, 1))

    def y_row(y, z):
        total = jnp.zeros((SUB, 128), jnp.float32)
        for field in range(F):
            part = piece(field * rows_of_field + y, SUB, rows_of_x, z, field * SUB)
            total = jnp.where(lane // SUB == field, part, total)
        return total

    own_rows[0] = y_row(jnp.maximum(y_start - 1, 0), z_start)
    own_rows[1] = y_row(jnp.minimum(y_start + SUB, y_cells - 1), z_start)
    row_for_low[...] = y_row(0, corner(0, -1)[1])
    row_for_high[...] = y_row(y_cells - 1, corner(0, 1)[1])
    lane = lane[:8]
    for face, (x, step) in enumerate(((0, -1), (SUB - 1, 1))):
        y_there, z_there = corner(step, 0)
        for half in range(2):
            total = jnp.zeros((8, 128), jnp.float32)
            for step in range(8):
                row = x * rows_of_x + y_there + half * 8 + step
                part = piece(row, 8, rows_of_field, z_there, step * SUB)
                total = jnp.where(lane // SUB == step, part, total)
            faces[face, :, half * 128 : (half + 1) * 128] = total
    payload[...] = dot_rows(centre[...].astype(jnp.bfloat16), order[...]).astype(jnp.bfloat16)


def sample_cube(sample_block, place, brick):
    fields, x_cells, y_cells, z_cells = brick.shape
    vmem = pl.BlockSpec(memory_space=pltpu.VMEM)
    smem = pl.BlockSpec(memory_space=pltpu.SMEM)
    rows = fields * x_cells * y_cells
    cube = jax.ShapeDtypeStruct((F * SUB, 256), jnp.float32)
    line = jax.ShapeDtypeStruct((SUB, 128), jnp.float32)
    return pl.pallas_call(
        functools.partial(sample_kernel, y_cells, z_cells),
        out_shape=(
            cube,
            cube,
            cube,
            jax.ShapeDtypeStruct((2, SUB, 128), jnp.float32),
            jax.ShapeDtypeStruct((2, 8, 256), jnp.float32),
            line,
            line,
            jax.ShapeDtypeStruct((F * SUB, 256), jnp.bfloat16),
        ),
        in_specs=[smem, smem, vmem, pl.BlockSpec(memory_space=pltpu.HBM)],
        out_specs=(vmem,) * 8,
        scratch_shapes=[
            pltpu.VMEM((z_cells // 128 * rows + 4 * x_cells * y_cells, 128), jnp.float32),
            pltpu.SemaphoreType.DMA((z_cells // 128,)),
        ],
        compiler_params=pltpu.CompilerParams(vmem_limit_bytes=48 * 1024 * 1024),
        name="sample_cube",
    )(sample_block, place, jnp.asarray(CELL_ORDER, jnp.bfloat16), brick.reshape(rows, z_cells))


def change_kernel(
    y_cells,
    z_cells,
    sample_block,
    place,
    closure_in,
    closure_bias,
    closure_out,
    order,
    centre,
    lower,
    upper,
    own_rows,
    face_low,
    face_high,
    row_low,
    row_high,
    payload,
):
    y_start = corner_of(sample_block, place, 0, 0, y_cells, z_cells)[0]
    row = lax.broadcasted_iota(jnp.int32, (SUB, 256), 0)
    lane = lax.broadcasted_iota(jnp.int32, (SUB, 256), 1)
    south_row = jnp.where(y_start == 0, row_low[...], own_rows[0])
    north_row = jnp.where(y_start + SUB == y_cells, row_high[...], own_rows[1])
    cells = [centre[f * SUB : (f + 1) * SUB, :] for f in range(F)]
    viscosity = viscosity_of(cells, closure_in, closure_bias, closure_out)
    changes = []
    for f in range(F):
        value = cells[f]
        west = jnp.where(row == 0, face_low[f : f + 1, :], pltpu.roll(value, 1, 0))
        east = jnp.where(row == SUB - 1, face_high[f : f + 1, :], pltpu.roll(value, SUB - 1, 0))
        edge = pltpu.roll(south_row, (128 - f * SUB) % 128, 1)
        south = jnp.where(lane < SUB, jnp.concatenate([edge, edge], 1), pltpu.roll(value, SUB, 1))
        edge = pltpu.roll(north_row, 112 - f * SUB, 1)
        north = jnp.where(
            lane >= 256 - SUB, jnp.concatenate([edge, edge], 1), pltpu.roll(value, 256 - SUB, 1)
        )
        down = lower[f * SUB : (f + 1) * SUB, :]
        up = upper[f * SUB : (f + 1) * SUB, :]
        laplacian = east + west + north + south + up + down - 6.0 * value
        advection = cells[0] * (east - west) + cells[1] * (north - south) + cells[2] * (up - down)
        change = viscosity * laplacian - 0.5 * advection
        if f == 2:
            change = change + buoyancy * cells[3]
        changes.append(change)
    changes = jnp.concatenate(changes, axis=0).astype(jnp.bfloat16)
    payload[...] = dot_rows(changes, order[...]).astype(jnp.bfloat16)


def cube_change(sample_block, place, closure, cube, halo, y_cells, z_cells):
    vmem = pl.BlockSpec(memory_space=pltpu.VMEM)
    smem = pl.BlockSpec(memory_space=pltpu.SMEM)
    return pl.pallas_call(
        functools.partial(change_kernel, y_cells, z_cells),
        out_shape=jax.ShapeDtypeStruct((F * SUB, 256), jnp.bfloat16),
        in_specs=[smem] * 5 + [vmem] * 9,
        out_specs=vmem,
        name="cube_change",
    )(sample_block, place, *closure, jnp.asarray(CELL_ORDER, jnp.bfloat16), *cube, *halo)


def doubling_steps(x_devices, y_devices):
    along_y = [1 << bit for bit in reversed(range(y_devices.bit_length() - 1))]
    along_x = [y_devices << bit for bit in reversed(range(x_devices.bit_length() - 1))]
    return along_y + along_x


def on_device(
    fields, closure_in, closure_bias, closure_out, master, momentum, sample_block, sample_trainer
):
    group_count = lax.axis_size("grp")
    x_devices = lax.axis_size("gx")
    y_devices = lax.axis_size("gy")
    trainers = x_devices * y_devices
    my_group = lax.axis_index("grp")
    my_column = lax.axis_index("gx") * y_devices + lax.axis_index("gy")
    is_trainer = my_group == group_count - 1
    everyone = ("grp", "gx", "gy")
    sim_groups = group_count - 1
    first_trainer = sim_groups * trainers
    brick = fields[0]
    y_cells, z_cells = brick.shape[2:]
    closure = (closure_in, closure_bias, closure_out)
    place = jnp.stack(
        [
            my_group,
            lax.axis_index("gx"),
            lax.axis_index("gy"),
            jnp.int32(sim_groups),
            jnp.int32(y_devices),
            jnp.int32(x_devices),
        ]
    ).astype(jnp.int32)

    def neighbours(for_low, for_high, along_x):
        def pairs(step):
            found = []
            for g in range(sim_groups):
                for c in range(trainers):
                    gx, gy = c // y_devices, c % y_devices
                    if along_x:
                        gx = (gx + step) % x_devices
                    else:
                        gy = (gy + step) % y_devices
                    found.append((g * trainers + c, (g * x_devices + gx) * y_devices + gy))
            return found

        if (x_devices if along_x else y_devices) == 2:
            both = lax.ppermute(jnp.stack([for_high, for_low]), everyone, pairs(1))
            return both[0], both[1]
        from_low = lax.ppermute(for_high, everyone, pairs(1))
        return from_low, lax.ppermute(for_low, everyone, pairs(-1))

    def swap(distance):
        return [(first_trainer + c, first_trainer + (c ^ distance)) for c in range(trainers)]

    steps = doubling_steps(x_devices, y_devices)

    def to_trainers(payload):
        return jnp.stack(
            [
                lax.ppermute(
                    payload,
                    everyone,
                    [(g * trainers + c, first_trainer + c) for c in range(trainers)],
                )
                for g in range(sim_groups)
            ]
        )

    def among_trainers(held):
        for distance in steps[:-1]:
            held = jnp.concatenate([held, lax.ppermute(held, everyone, swap(distance))], axis=0)
        return [held, lax.ppermute(held, everyone, swap(steps[-1]))]

    *cube, faces, row_for_low, row_for_high, sent_inputs = sample_cube(sample_block, place, brick)
    face_halo = neighbours(faces[0], faces[1], True)
    row_halo = neighbours(row_for_low, row_for_high, False)
    landed_inputs = to_trainers(sent_inputs)
    sent_targets = cube_change(
        sample_block, place, closure, cube, (*face_halo, *row_halo), y_cells, z_cells
    )
    landed_targets = to_trainers(sent_targets)
    edges = (brick[:, 0], brick[:, -1], brick[:, :, 0], brick[:, :, -1])
    *edges, landed_targets = lax.optimization_barrier((*edges, landed_targets))
    halo = (*neighbours(edges[0], edges[1], True), *neighbours(edges[2], edges[3], False))
    arrived_inputs = among_trainers(landed_inputs)
    arrived_targets = among_trainers(landed_targets)

    first_count = CH * TAPS * F
    first = jnp.pad(master[:first_count].reshape(CH, TAPS * F), ((0, 0), (0, 256 - TAPS * F)))
    last = jnp.pad(master[first_count:].reshape(TAPS * F, CH).T, ((0, 0), (0, 256 - TAPS * F)))

    def train_here():
        delta_first, delta_last, new_brick = train_cubes(
            sample_trainer, place, first, last, arrived_inputs, arrived_targets, brick, steps
        )
        delta = jnp.concatenate(
            [delta_first[:, : TAPS * F].reshape(-1), delta_last[:, : TAPS * F].T.reshape(-1)]
        )
        return delta, new_brick

    def evolve_here():
        new_brick = evolve(*closure, brick, *halo)
        return jnp.zeros((NPARAM,), jnp.float32), new_brick

    delta, new_brick = lax.cond(is_trainer, train_here, evolve_here)

    total = delta
    for distance in steps:
        total = total + lax.ppermute(total, everyone, swap(distance))
    final = jnp.where(is_trainer, total, 0.0)
    for g in range(sim_groups):
        pairs = [(first_trainer + c, g * trainers + c) for c in range(trainers)]
        final = final + lax.ppermute(total, everyone, pairs)

    share_size = NPARAM // (group_count * trainers)
    share_start = (my_group * trainers + my_column) * share_size
    momentum_share = lax.dynamic_slice_in_dim(momentum, share_start, share_size)
    master_share = lax.dynamic_slice_in_dim(master, share_start, share_size)
    inverse = 1.0 / jnp.sqrt(jnp.sum(final * final) / NPARAM + norm_epsilon)
    delta_share = lax.dynamic_slice_in_dim(final, share_start, share_size)
    new_momentum = momentum_decay * momentum_share + delta_share * inverse
    new_master = master_share - outer_rate * new_momentum
    return (new_brick[None], new_master, new_momentum)


def solution(mesh):
    in_specs = (P("grp", None, "gx", "gy", None), P(), P(), P(), P(), P(), P(), P())
    out_specs = (P("grp", None, "gx", "gy", None), P(("grp", "gx", "gy")), P(("grp", "gx", "gy")))
    return jax.shard_map(
        on_device, mesh=mesh, in_specs=in_specs, out_specs=out_specs, check_vma=False
    )
```

time: 191 us -> 222 us (1.16)
  starting transfers between devices: 17.6 us -> 39.6 us
  Pallas kernels: 37.9 us -> 54.1 us
  waiting for transfers between devices: 105 us -> 113 us
  local copies, waits for them, and re-layouts: 15.4 us -> 9.91 us
  between operations: 5.91 us -> 1.87 us
  other arithmetic: 6.15 us -> 2.17 us
    ppermute x10 -> x18, starting transfers between devices: 13 us -> 35 us  [the longest x6 9.59 us: to_trainers(): lax.ppermute(payload, everyone, [(g * trainers + c, first_trainer + c) fo...]
    pallas_call x1, Pallas kernels: 37.9 us -> 46.6 us  [evolve(): pl.pallas_call(evolve_kernel, out_shape=jax.ShapeDtypeStruct(fields.shape...]
    pallas_call x0 -> x2, Pallas kernels: none -> 7.49 us  [the longest x1 4.43 us: sample_cube(): pl.pallas_call(functools.partial(sample_kernel, y_cells, z_cells), out_sh...]
    ppermute x3, waiting for transfers between devices: 103 us -> 109 us  [on_device(): final = final + lax.ppermute(total, everyone, pairs)]
    another operation x4 -> x3, local copies, waits for them, and re-layouts: 3.37 us -> 0.19 us
    ppermute x10 -> x18, waiting for transfers between devices: 1.95 us -> 4.66 us  [the longest x2 2.06 us: neighbours(): return (from_low, lax.ppermute(for_low, everyone, pairs(-1)))]
    unnamed x32 -> x34, local copies, waits for them, and re-layouts: 5.67 us -> 6.1 us
  transfers between devices with their start and end apart: 16 -> 24, of which waited for: 3 -> 5; matrix products, arithmetic and copies ran while one was open for 1% -> 2% of each run, Pallas kernels for 0% -> 1%
where the time goes in v2:
time: 222 us; the launch traced here: 221 us
  waiting for transfers between devices  113 us (51%)
  Pallas kernels  54.1 us (24%)
  starting transfers between devices  39.6 us (18%)
  local copies, waits for them, and re-layouts  9.91 us (4%)
    ppermute x3, waiting for transfers between devices, on_device(): final = final + lax.ppermute(total, everyone, pairs)  109 us
    pallas_call x1, Pallas kernels, evolve(): pl.pallas_call(evolve_kernel, out_shape=jax.ShapeDtypeStruct(fields.shape...  46.6 us
    ppermute x6, starting transfers between devices, to_trainers(): lax.ppermute(payload, everyone, [(g * trainers + c, first_trainer + c) fo...  9.59 us
    ppermute x2, starting transfers between devices, neighbours(): return (from_low, lax.ppermute(for_low, everyone, pairs(-1)))  8.53 us
    ppermute x2, starting transfers between devices, neighbours(): from_low = lax.ppermute(for_high, everyone, pairs(1))  6.97 us
    unnamed x34, local copies, waits for them, and re-layouts  6.1 us
    ppermute x2, starting transfers between devices, neighbours(): both = lax.ppermute(jnp.stack([for_high, for_low]), everyone, pairs(1))  5.84 us
  transfers between devices with their start and end apart: 24, of which 5 were waited for; matrix products, arithmetic and copies ran while one was open for 2% of the time, Pallas kernels for 1%

profile of v2, /device:TPU:0, one launch (start us, length us, event | category | flops | bytes accessed | tf_op | source)
XLA Modules:
  0.0 221.1 jit_solution(2016722870126332930)
XLA Ops:
  0.8 0.9 copy-done
  1.7 0.7 copy-done.7
  2.3 4.4 %sample_cube.1 = (f32[80,256]{1,0:T(8,128)S(1)}, f32[80,256]{1,0:T(8,128)S(1)}, f32[80,256]{1,0:T(8,128)S(1)}, f32[2,16,128]{2,1,0:T(8,128)S(1)}, f32[2,8,256]{2...) custom-call(s32[24]{0:T(128)S(1)} %copy-done.7, s32[6]{0:T(128)S(1)} %stack.51.place, ...), custom_call_target="tpu_custom_call" | custom-call | tf_op jit(solution)/shard_map/sample_cube/pallas_call | solution.py:553
  6.8 0.6 copy-done.3
  7.4 0.6 copy-done.4
  8.0 0.6 copy-done.5
  8.6 0.6 copy-done.6
  9.3 0.8 collective-permute-start.11
  10.0 0.7 collective-permute-start.10
  10.7 5.5 %collective-permute-start.9 = (bf16[80,256]{1,0:T(8,128)(2,1)S(1)}, bf16[80,256]{1,0:T(8,128)(2,1)S(1)}, u32[]{:S(2)}, u32[]{:S(2)}) collective-permute-start(bf16[80,256]{1,0:T(8,128)(2,1)S(1)} %get-tuple-element.90), channel_id=1, source_target_pairs={{0,24},{1,25},{2,26},{3,27},{4,28},{5,29},{6,30},{7,31}} | collective-permute-start | bytes 122888 | tf_op jit(solution)/shard_map/ppermute | solution.py:697
  16.3 3.5 %collective-permute-start.1 = (f32[16,128]{1,0:T(8,128)S(1)}, f32[16,128]{1,0:T(8,128)S(1)}, u32[]{:S(2)}, u32[]{:S(2)}) collective-permute-start(f32[16,128]{1,0:T(8,128)S(1)} %get-tuple-element.84), channel_id=1, source_target_pairs={{0,1},{1,2},{2,3},{3,0},{4,5},{5,6},{6,7},{7,4},{8,9},{9,10},{10,1... | collective-permute-start | bytes 24584 | tf_op jit(solution)/shard_map/ppermute | solution.py:686
  19.8 3.4 %collective-permute-start = (f32[2,8,256]{2,1,0:T(8,128)S(1)}, f32[2,8,256]{2,1,0:T(8,128)S(1)}, u32[]{:S(2)}, u32[]{:S(2)}) collective-permute-start(f32[2,8,256]{2,1,0:T(8,128)S(1)} %pad_maximum_fusion.6), channel_id=1, source_target_pairs={{0,4},{1,5},{2,6},{3,7},{4,0},{5,1},{6,2},{7,3},{8,12},{9,13},{10,... | collective-permute-start | bytes 49160 | tf_op jit(solution)/shard_map/ppermute | solution.py:684
  23.2 1.7 fusion
  24.9 1.1 slice_bitcast_fusion.3
  26.0 0.7 copy_bitcast_fusion
  26.7 0.7 copy.26.closure_in
  27.4 4.1 %collective-permute-start.2 = (f32[16,128]{1,0:T(8,128)S(1)}, f32[16,128]{1,0:T(8,128)S(1)}, u32[]{:S(2)}, u32[]{:S(2)}) collective-permute-start(f32[16,128]{1,0:T(8,128)S(1)} %get-tuple-element.85), channel_id=1, source_target_pairs={{0,3},{1,0},{2,1},{3,2},{4,7},{5,4},{6,5},{7,6},{8,11},{9,8},{10,9... | collective-permute-start | bytes 24584 | tf_op jit(solution)/shard_map/ppermute | solution.py:687
  31.6 0.6 slice_bitcast_fusion.5
  32.2 0.8 collective-permute-done.2.row_high
  33.0 0.6 copy-done.11
  33.5 3.1 %cube_change.1 = bf16[80,256]{1,0:T(8,128)(2,1)} custom-call(s32[24]{0:T(128)} %sample_block.3, s32[6]{0:T(128)S(1)} %stack.51.place, f32[64,5]{1,0:T(8,128)} %copy.26.closure_in, f32[64]{0:T(128)S(1)} %copy-done.12, f32[64]{0:T(128)S(1)} %copy-done.13, bf16[256,256]{1,0:T(8,128)(2,1)} %constant.51.clone.order, f32[80,256]{1,0:T(8,128)} %copy-done.3, ...), custom_call_target="tpu_custom_call" | custom-call | tf_op jit(solution)/shard_map/cube_change/pallas_call | solution.py:628
  36.6 0.7 collective-permute-start.5
  37.3 0.7 collective-permute-start.4
  37.9 1.3 collective-permute-start.3
  39.3 0.7 collective-permute-start.12
  40.0 1.2 collective-permute-done.3
  41.2 0.7 collective-permute-start.15
  42.0 2.4 %collective-permute-start.6 = (f32[2,5,32,384]{3,2,1,0:T(8,128)S(1)}, f32[2,5,32,384]{3,2,1,0:T(8,128)S(1)}, u32[]{:S(2)}, u32[]{:S(2)}) collective-permute-start(f32[2,5,32,384]{3,2,1,0:T(8,128)S(1)} %pad_maximum_fusion.1), channel_id=1, source_target_pairs={{0,4},{1,5},{2,6},{3,7},{4,0},{5,1},{6,2},{7,3},{8,12},{9,13},{10,... | collective-permute-start | bytes 1474568 | tf_op jit(solution)/shard_map/ppermute | solution.py:684
  44.4 0.7 collective-permute-start.13
  45.2 0.7 collective-permute-start.16
  45.9 0.7 collective-permute-start.14
  46.7 0.7 collective-permute-start.17
  47.4 3.5 %collective-permute-start.7 = (f32[5,16,384]{2,1,0:T(8,128)}, f32[5,16,384]{2,1,0:T(8,128)S(1)}, u32[]{:S(2)}, u32[]{:S(2)}) collective-permute-start(f32[5,16,384]{2,1,0:T(8,128)} %get-tuple-element.88), channel_id=1, source_target_pairs={{0,1},{1,2},{2,3},{3,0},{4,5},{5,6},{6,7},{7,4},{8,9},{9,10},{10,1... | collective-permute-start | bytes 368648 | tf_op jit(solution)/shard_map/ppermute | solution.py:686
  50.9 4.4 %collective-permute-start.8 = (f32[5,16,384]{2,1,0:T(8,128)}, f32[5,16,384]{2,1,0:T(8,128)S(1)}, u32[]{:S(2)}, u32[]{:S(2)}) collective-permute-start(f32[5,16,384]{2,1,0:T(8,128)} %get-tuple-element.89), channel_id=1, source_target_pairs={{0,3},{1,0},{2,1},{3,2},{4,7},{5,4},{6,5},{7,6},{8,11},{9,8},{10,9... | collective-permute-start | bytes 368648 | tf_op jit(solution)/shard_map/ppermute | solution.py:687
  55.4 1.4 collective-permute-done.7
  56.8 1.3 collective-permute-done.8
  58.1 46.8 %conditional.1 = (f32[17280]{0:T(1024)S(1)}, f32[1,5,16,32,384]{4,3,2,1,0:T(8,128)}) conditional(s32[]{:T(128)} %convert_element_type.6, (f32[64,5]{0,1:T(8,128)S(1)}, f32[64]{0:T(128)S(1)}, f32[64]{0:T(128)S(1)}, f32[5,16,32,384]{3,2,1,0:T(8,128)}, f32[2,5,32,384]{3,2,1,0:T(8,128)S(1)}, /*index=5*/f32[2,5,32,384]{3,2,1,0:T(8,128)S(1)}, ...), branch_computations={%region_0.1_spmd, %region_1.2_spmd.clone} | conditional | flops 17280 | bytes 4754512 | solution.py:742
  58.1 0.1 copy.27.closure_in
  58.3 46.6 %evolve_brick.1 = f32[5,16,32,384]{3,2,1,0:T(8,128)} custom-call(f32[64,5]{1,0:T(8,128)S(1)} %copy.27.closure_in, f32[64]{0:T(128)S(1)} %get-tuple-element.40.closure_bias, f32[64]{0:T(128)S(1)} %get-tuple-element.41.closure_out, f32[5,16,32,384]{3,2,1,0:T(8,128)} %get-tuple-element.42.fields, f32[5,32,384]{2,1,0:T(8,128)S(1)} %get-tuple-element.165.x_low, ...), custom_call_target="tpu_custom_call" | custom-call | tf_op jit(solution)/shard_map/cond/branch_0_fun/evolve_brick/pallas_call | solution.py:429
  104.9 0.7 collective-permute-start.18
  105.6 0.7 collective-permute-start.19
  106.3 0.7 collective-permute-start.20
  107.0 0.7 collective-permute-start.23
  107.7 0.7 collective-permute-start.22
  108.4 1.3 collective-permute-start.21
  109.7 108.7 %collective-permute-done.21 = f32[17280]{0:T(1024)S(1)} collective-permute-done((f32[17280]{0:T(1024)S(1)}, f32[17280]{0:T(1024)S(1)}, u32[]{:S(2)}, u32[]{:S(2)}) %collective-permute-start.21) | collective-permute-done | bytes 69152 | tf_op jit(solution)/shard_map/ppermute | solution.py:750
  218.4 0.6 multiply_reduce_fusion
  219.7 1.4 multiply_subtract_fusion
  (61 shorter events, 0.6 us)
Async XLA Ops:
  0.6 26.1 %copy-start.9 = (f32[64,5]{0,1:T(8,128)S(1)}, f32[64,5]{0,1:T(8,128)}, u32[]{:S(2)}) copy-start(f32[64,5]{0,1:T(8,128)} %param.15) | copy-start | bytes 3844
  0.6 32.9 %copy-start.13 = (f32[64]{0:T(128)S(1)}, f32[64]{0:T(128)}, u32[]{:S(2)}) copy-start(f32[64]{0:T(128)} %closure_out.1) | copy-start | bytes 772
  0.7 32.9 %copy-start.12 = (f32[64]{0:T(128)S(1)}, f32[64]{0:T(128)}, u32[]{:S(2)}) copy-start(f32[64]{0:T(128)} %closure_bias.1) | copy-start | bytes 772
  0.8 0.9 copy-start
  1.7 0.7 copy-start.7
  6.8 0.6 copy-start.3
  7.4 0.6 copy-start.4
  8.0 0.6 copy-start.5
  8.6 0.6 copy-start.6
  9.2 46.0 %copy-start.8 = (f32[17280]{0:T(1024)S(1)}, f32[17280]{0:T(1024)}, u32[]{:S(2)}) copy-start(f32[17280]{0:T(1024)} %param.18) | copy-start | bytes 207364
  9.2 48.9 %copy-start.14 = (s32[24]{0:T(128)S(1)}, s32[24]{0:T(128)}, u32[]{:S(2)}) copy-start(s32[24]{0:T(128)} %param.21) | copy-start | bytes 292
  9.3 28.7 %collective-permute-start.11 = (bf16[80,256]{1,0:T(8,128)(2,1)S(1)}, bf16[80,256]{1,0:T(8,128)(2,1)S(1)}, u32[]{:S(2)}, u32[]{:S(2)}) collective-permute-start(bf16[80,256]{1,0:T(8,128)(2,1)S(1)} %get-tuple-element.90), channel_id=1, source_target_pairs={{16,24},{17,25},{18,26},{19,27},{20,28},{21,29},{22,30},{23,31}} | collective-permute-start | bytes 122888 | tf_op jit(solution)/shard_map/ppermute | solution.py:697
  10.0 29.2 %collective-permute-start.10 = (bf16[80,256]{1,0:T(8,128)(2,1)S(1)}, bf16[80,256]{1,0:T(8,128)(2,1)S(1)}, u32[]{:S(2)}, u32[]{:S(2)}) collective-permute-start(bf16[80,256]{1,0:T(8,128)(2,1)S(1)} %get-tuple-element.90), channel_id=1, source_target_pairs={{8,24},{9,25},{10,26},{11,27},{12,28},{13,29},{14,30},{15,31}} | collective-permute-start | bytes 122888 | tf_op jit(solution)/shard_map/ppermute | solution.py:697
  10.7 28.5 %collective-permute-start.9 = (bf16[80,256]{1,0:T(8,128)(2,1)S(1)}, bf16[80,256]{1,0:T(8,128)(2,1)S(1)}, u32[]{:S(2)}, u32[]{:S(2)}) collective-permute-start(bf16[80,256]{1,0:T(8,128)(2,1)S(1)} %get-tuple-element.90), channel_id=1, source_target_pairs={{0,24},{1,25},{2,26},{3,27},{4,28},{5,29},{6,30},{7,31}} | collective-permute-start | bytes 122888 | tf_op jit(solution)/shard_map/ppermute | solution.py:697
  16.3 15.9 %collective-permute-start.1 = (f32[16,128]{1,0:T(8,128)S(1)}, f32[16,128]{1,0:T(8,128)S(1)}, u32[]{:S(2)}, u32[]{:S(2)}) collective-permute-start(f32[16,128]{1,0:T(8,128)S(1)} %get-tuple-element.84), channel_id=1, source_target_pairs={{0,1},{1,2},{2,3},{3,0},{4,5},{5,6},{6,7},{7,4},{8,9},{9,10},{10,1... | collective-permute-start | bytes 24584 | tf_op jit(solution)/shard_map/ppermute | solution.py:686
  19.8 7.6 %collective-permute-start = (f32[2,8,256]{2,1,0:T(8,128)S(1)}, f32[2,8,256]{2,1,0:T(8,128)S(1)}, u32[]{:S(2)}, u32[]{:S(2)}) collective-permute-start(f32[2,8,256]{2,1,0:T(8,128)S(1)} %pad_maximum_fusion.6), channel_id=1, source_target_pairs={{0,4},{1,5},{2,6},{3,7},{4,0},{5,1},{6,2},{7,3},{8,12},{9,13},{10,... | collective-permute-start | bytes 49160 | tf_op jit(solution)/shard_map/ppermute | solution.py:684
  27.4 5.5 %collective-permute-start.2 = (f32[16,128]{1,0:T(8,128)S(1)}, f32[16,128]{1,0:T(8,128)S(1)}, u32[]{:S(2)}, u32[]{:S(2)}) collective-permute-start(f32[16,128]{1,0:T(8,128)S(1)} %get-tuple-element.85), channel_id=1, source_target_pairs={{0,3},{1,0},{2,1},{3,2},{4,7},{5,4},{6,5},{7,6},{8,11},{9,8},{10,9... | collective-permute-start | bytes 24584 | tf_op jit(solution)/shard_map/ppermute | solution.py:687
  32.2 0.8 copy-start.10
  32.9 0.6 copy-start.11
  36.6 3.4 %collective-permute-start.5 = (bf16[80,256]{1,0:T(8,128)(2,1)}, bf16[80,256]{1,0:T(8,128)(2,1)S(1)}, u32[]{:S(2)}, u32[]{:S(2)}) collective-permute-start(bf16[80,256]{1,0:T(8,128)(2,1)} %cube_change.1), channel_id=1, source_target_pairs={{16,24},{17,25},{18,26},{19,27},{20,28},{21,29},{22,30},{23,31}} | collective-permute-start | bytes 122888 | tf_op jit(solution)/shard_map/ppermute | solution.py:697
  37.3 2.8 %collective-permute-start.4 = (bf16[80,256]{1,0:T(8,128)(2,1)}, bf16[80,256]{1,0:T(8,128)(2,1)S(1)}, u32[]{:S(2)}, u32[]{:S(2)}) collective-permute-start(bf16[80,256]{1,0:T(8,128)(2,1)} %cube_change.1), channel_id=1, source_target_pairs={{8,24},{9,25},{10,26},{11,27},{12,28},{13,29},{14,30},{15,31}} | collective-permute-start | bytes 122888 | tf_op jit(solution)/shard_map/ppermute | solution.py:697
  37.9 3.3 %collective-permute-start.3 = (bf16[80,256]{1,0:T(8,128)(2,1)}, bf16[80,256]{1,0:T(8,128)(2,1)S(1)}, u32[]{:S(2)}, u32[]{:S(2)}) collective-permute-start(bf16[80,256]{1,0:T(8,128)(2,1)} %cube_change.1), channel_id=1, source_target_pairs={{0,24},{1,25},{2,26},{3,27},{4,28},{5,29},{6,30},{7,31}} | collective-permute-start | bytes 122888 | tf_op jit(solution)/shard_map/ppermute | solution.py:697
  39.3 5.1 %collective-permute-start.12 = (bf16[3,80,256]{2,1,0:T(8,128)(2,1)S(1)}, bf16[3,80,256]{2,1,0:T(8,128)(2,1)S(1)}, u32[]{:S(2)}, u32[]{:S(2)}) collective-permute-start(bf16[3,80,256]{2,1,0:T(8,128)(2,1)S(1)} %pad_maximum_fusion.5), channel_id=1, source_target_pairs={{24,26},{25,27},{26,24},{27,25},{28,30},{29,31},{30,28},{31,29}} | collective-permute-start | bytes 368648 | tf_op jit(solution)/shard_map/ppermute | solution.py:708
  41.2 3.9 %collective-permute-start.15 = (bf16[3,80,256]{2,1,0:T(8,128)(2,1)S(1)}, bf16[3,80,256]{2,1,0:T(8,128)(2,1)S(1)}, u32[]{:S(2)}, u32[]{:S(2)}) collective-permute-start(bf16[3,80,256]{2,1,0:T(8,128)(2,1)S(1)} %pad_maximum_fusion.4), channel_id=1, source_target_pairs={{24,26},{25,27},{26,24},{27,25},{28,30},{29,31},{30,28},{31,29}} | collective-permute-start | bytes 368648 | tf_op jit(solution)/shard_map/ppermute | solution.py:708
  42.0 16.1 %collective-permute-start.6 = (f32[2,5,32,384]{3,2,1,0:T(8,128)S(1)}, f32[2,5,32,384]{3,2,1,0:T(8,128)S(1)}, u32[]{:S(2)}, u32[]{:S(2)}) collective-permute-start(f32[2,5,32,384]{3,2,1,0:T(8,128)S(1)} %pad_maximum_fusion.1), channel_id=1, source_target_pairs={{0,4},{1,5},{2,6},{3,7},{4,0},{5,1},{6,2},{7,3},{8,12},{9,13},{10,... | collective-permute-start | bytes 1474568 | tf_op jit(solution)/shard_map/ppermute | solution.py:684
  44.4 1.5 collective-permute-start.13
  45.2 1.5 collective-permute-start.16
  45.9 12.2 %collective-permute-start.14 = (bf16[12,80,256]{2,1,0:T(8,128)(2,1)S(1)}, bf16[12,80,256]{2,1,0:T(8,128)(2,1)S(1)}, u32[]{:S(2)}, u32[]{:S(2)}) collective-permute-start(bf16[12,80,256]{2,1,0:T(8,128)(2,1)S(1)} %constant_dynamic-update-slice_fusion), channel_id=1, source_target_pairs={{24,28},{25,29},{26,30},{27,31},{28,24},{29,25},{30,26},{31,27}} | collective-permute-start | bytes 1474568 | tf_op jit(solution)/shard_map/ppermute | solution.py:709
  46.7 11.4 %collective-permute-start.17 = (bf16[12,80,256]{2,1,0:T(8,128)(2,1)S(1)}, bf16[12,80,256]{2,1,0:T(8,128)(2,1)S(1)}, u32[]{:S(2)}, u32[]{:S(2)}) collective-permute-start(bf16[12,80,256]{2,1,0:T(8,128)(2,1)S(1)} %constant_dynamic-update-slice_fusion.5), channel_id=1, source_target_pairs={{24,28},{25,29},{26,30},{27,31},{28,24},{29,25},{30,26},{31,27}} | collective-permute-start | bytes 1474568 | tf_op jit(solution)/shard_map/ppermute | solution.py:709
  47.4 9.4 %collective-permute-start.7 = (f32[5,16,384]{2,1,0:T(8,128)}, f32[5,16,384]{2,1,0:T(8,128)S(1)}, u32[]{:S(2)}, u32[]{:S(2)}) collective-permute-start(f32[5,16,384]{2,1,0:T(8,128)} %get-tuple-element.88), channel_id=1, source_target_pairs={{0,1},{1,2},{2,3},{3,0},{4,5},{5,6},{6,7},{7,4},{8,9},{9,10},{10,1... | collective-permute-start | bytes 368648 | tf_op jit(solution)/shard_map/ppermute | solution.py:686
  50.9 7.2 %collective-permute-start.8 = (f32[5,16,384]{2,1,0:T(8,128)}, f32[5,16,384]{2,1,0:T(8,128)S(1)}, u32[]{:S(2)}, u32[]{:S(2)}) collective-permute-start(f32[5,16,384]{2,1,0:T(8,128)} %get-tuple-element.89), channel_id=1, source_target_pairs={{0,3},{1,0},{2,1},{3,2},{4,7},{5,4},{6,5},{7,6},{8,11},{9,8},{10,9... | collective-permute-start | bytes 368648 | tf_op jit(solution)/shard_map/ppermute | solution.py:687
  104.9 0.7 collective-permute-start.18
  105.6 0.7 collective-permute-start.19
  106.3 0.7 collective-permute-start.20
  107.0 2.7 %collective-permute-start.23 = (f32[17280]{0:T(1024)S(1)}, f32[17280]{0:T(1024)S(1)}, u32[]{:S(2)}, u32[]{:S(2)}) collective-permute-start(f32[17280]{0:T(1024)S(1)} %add.44), channel_id=1, source_target_pairs={{24,16},{25,17},{26,18},{27,19},{28,20},{29,21},{30,22},{31,23}} | collective-permute-start | bytes 207368 | tf_op jit(solution)/shard_map/ppermute | solution.py:750
  107.7 2.0 collective-permute-start.22
  108.4 110.0 %collective-permute-start.21 = (f32[17280]{0:T(1024)S(1)}, f32[17280]{0:T(1024)S(1)}, u32[]{:S(2)}, u32[]{:S(2)}) collective-permute-start(f32[17280]{0:T(1024)S(1)} %add.44), channel_id=1, source_target_pairs={{24,0},{25,1},{26,2},{27,3},{28,4},{29,5},{30,6},{31,7}} | collective-permute-start | bytes 207368 | tf_op jit(solution)/shard_map/ppermute | solution.py:750

commit v3 on v2

--- a/solution.py
+++ b/solution.py
@@ -116,9 +116,9 @@
 
 def train_kernel(steps, *refs):
     (trainer_of, place, first_ref, last_ref, select_first, select_last) = refs[:6]
-    arrived_inputs, arrived_targets = refs[6:8], refs[8:10]
-    fields_ref = refs[10]
-    delta_first, delta_last, new_fields_ref = refs[11:14]
+    arrived = refs[6:8]
+    fields_ref = refs[8]
+    delta_first, delta_last, new_fields_ref = refs[9:12]
     (
         slots,
         cubes,
@@ -133,11 +133,14 @@
         big_first,
         big_last,
         big_last_t,
+        raw,
+        grad_first,
+        grad_last,
         now_first,
         now_last,
         slot_sems,
         field_sem,
-    ) = refs[14:]
+    ) = refs[12:]
 
     field_copy = pltpu.make_async_copy(fields_ref, new_fields_ref, field_sem)
     field_copy.start()
@@ -163,22 +166,21 @@
     count = lax.fori_loop(0, trainer_of.shape[0], visit, jnp.int32(0))
 
     def fetch(slot, wait):
-        for kind, arrived in enumerate((arrived_inputs, arrived_targets)):
-            for half in range(2):
-
-                @pl.when((slot < count) & (slots[0, slot] == half))
-                def _():
-                    copy = pltpu.make_async_copy(
-                        arrived[half].at[slots[1, slot]], cubes.at[kind, slot], slot_sems.at[kind, slot]
-                    )
-                    copy.wait() if wait else copy.start()
+        for half in range(2):
+
+            @pl.when((slot < count) & (slots[0, slot] == half))
+            def _():
+                copy = pltpu.make_async_copy(
+                    arrived[half].at[slots[1, slot]], cubes.at[slot], slot_sems.at[slot]
+                )
+                copy.wait() if wait else copy.start()
 
     for slot in range(TCAP):
         fetch(slot, False)
 
         @pl.when(slot >= count)
         def _():
-            cubes[:, slot] = jnp.zeros((2, SUB * F, 256), jnp.bfloat16)
+            cubes[slot] = jnp.zeros((2 * SUB * F, 256), jnp.bfloat16)
 
     masks = patch_masks()
     for ref in (errors, inputs):
@@ -204,8 +206,9 @@
     low_lanes = lax.broadcasted_iota(jnp.int32, (SUB * F, 128), 1) < 64
 
     def spread_rows(pair, kind, put):
-        even = cubes[kind, 2 * pair].astype(jnp.float32)
-        odd = cubes[kind, 2 * pair + 1].astype(jnp.float32)
+        rows = slice(kind * SUB * F, (kind + 1) * SUB * F)
+        even = cubes[2 * pair, rows, :].astype(jnp.float32)
+        odd = cubes[2 * pair + 1, rows, :].astype(jnp.float32)
         for half in range(2):
             left = even[:, half * 128 : (half + 1) * 128]
             right = odd[:, half * 128 : (half + 1) * 128]
@@ -241,19 +244,41 @@
             big_first[rows, :] = dot_rows(first_now, select_first[cell]).astype(jnp.bfloat16)
             big_last[rows, :] = dot_rows(last_now, select_last[cell]).astype(jnp.bfloat16)
         big_last_t[...] = big_last[...].T
+        def tile_of(index):
+            return index // 8, pl.ds(pl.multiple_of((index % 8) * 256 + 128, 128), 256)
+
+        def first_layer(index):
+            pair, columns = tile_of(index)
+            raw[index % 2] = dot_rows(big_first[...], inputs[pair, :, columns])
+
+        def activate(index):
+            pair, columns = tile_of(index)
+            for part in range(8):
+                rows = slice(part * 32, (part + 1) * 32)
+                half = 0.5 * raw[index % 2, rows, :]
+                curve = jnp.tanh(half)
+                value = half + half * curve
+                hiddens[pair, rows, columns] = value.astype(jnp.bfloat16)
+                slopes[pair, rows, columns] = (0.5 + 0.5 * curve) + value * (0.5 - 0.5 * curve)
+
+        def last_layer(index):
+            pair, columns = tile_of(index)
+            partial_out[pair, :, columns] = dot_rows(big_last_t[...], hiddens[pair, :, columns])
+
         def forward(index, carry):
-            pair = index // 4
-            column = pl.multiple_of((index % 4) * 512 + 128, 128)
-            pre = dot_rows(big_first[...], inputs[pair, :, pl.ds(column, 512)])
-            sigmoid = 0.5 * jnp.tanh(0.5 * pre) + 0.5
-            value = pre * sigmoid
-            hidden = value.astype(jnp.bfloat16)
-            hiddens[pair, :, pl.ds(column, 512)] = hidden
-            slopes[pair, :, pl.ds(column, 512)] = sigmoid + value * (1.0 - sigmoid)
-            partial_out[pair, :, pl.ds(column, 512)] = dot_rows(big_last_t[...], hidden)
+            last_layer(index - 2)
+            activate(index - 1)
+            first_layer(index)
             return carry
 
-        lax.fori_loop(0, 4 * PAIRS, forward, 0, unroll=2)
+        tiles = 8 * PAIRS
+        first_layer(0)
+        activate(0)
+        first_layer(1)
+        lax.fori_loop(2, tiles, forward, 0)
+        last_layer(tiles - 2)
+        activate(tiles - 1)
+        last_layer(tiles - 1)
 
         def error_plane(index, carry):
             pair = index // SUB
@@ -280,21 +305,38 @@
 
         lax.fori_loop(0, SUB * PAIRS, error_plane, 0, unroll=8)
 
+        grad_first[...] = jnp.zeros(grad_first.shape, jnp.float32)
+        grad_last[...] = jnp.zeros(grad_last.shape, jnp.float32)
+
+        def hidden_layer(index):
+            pair, columns = tile_of(index)
+            raw[index % 2] = dot_rows(big_last[...], errors[pair, :, columns])
+
+        def scale(index):
+            pair, columns = tile_of(index)
+            for part in range(8):
+                rows = slice(part * 32, (part + 1) * 32)
+                product = raw[index % 2, rows, :] * slopes[pair, rows, columns]
+                pre_grads[pair, rows, columns] = product.astype(jnp.bfloat16)
+
+        def gradients(index):
+            pair, columns = tile_of(index)
+            grad_first[...] += dot_lanes(pre_grads[pair, :, columns], inputs[pair, :, columns])
+            grad_last[...] += dot_lanes(hiddens[pair, :, columns], errors[pair, :, columns])
+
         def backward(index, carry):
-            pair = index // 4
-            column = pl.multiple_of((index % 4) * 512 + 128, 128)
-            hidden_grad = dot_rows(big_last[...], errors[pair, :, pl.ds(column, 512)])
-            slope = slopes[pair, :, pl.ds(column, 512)]
-            pre_grads[pair, :, pl.ds(column, 512)] = (hidden_grad * slope).astype(jnp.bfloat16)
+            gradients(index - 2)
+            scale(index - 1)
+            hidden_layer(index)
             return carry
 
-        lax.fori_loop(0, 4 * PAIRS, backward, 0, unroll=2)
-        body = slice(128, COLS - 128)
-        grad_first = jnp.zeros((4 * CH, STACK), jnp.float32)
-        grad_last = jnp.zeros((4 * CH, STACK), jnp.float32)
-        for pair in range(PAIRS):
-            grad_first += dot_lanes(pre_grads[pair, :, body], inputs[pair, :, body])
-            grad_last += dot_lanes(hiddens[pair, :, body], errors[pair, :, body])
+        hidden_layer(0)
+        scale(0)
+        hidden_layer(1)
+        lax.fori_loop(2, tiles, backward, 0)
+        gradients(tiles - 2)
+        scale(tiles - 1)
+        gradients(tiles - 1)
 
         def folded(grad, select_ref):
             total = jnp.zeros((3 * CH, 256), jnp.float32)
@@ -321,7 +363,7 @@
     return jnp.where(lax.rem(lax.div(left, distance), 2) == lax.rem(lax.div(right, distance), 2), 0, 1)
 
 
-def train_cubes(trainer_of, place, first, last, arrived_inputs, arrived_targets, fields, steps):
+def train_cubes(trainer_of, place, first, last, arrived, fields, steps):
     vmem = pl.BlockSpec(memory_space=pltpu.VMEM)
     smem = pl.BlockSpec(memory_space=pltpu.SMEM)
     anywhere = pl.BlockSpec(memory_space=pl.ANY)
@@ -333,11 +375,11 @@
             jax.ShapeDtypeStruct((CH, 256), jnp.float32),
             jax.ShapeDtypeStruct(fields.shape, fields.dtype),
         ),
-        in_specs=[smem] * 2 + [vmem] * 4 + [anywhere] * 4 + [hbm],
+        in_specs=[smem] * 2 + [vmem] * 4 + [anywhere] * 2 + [hbm],
         out_specs=(vmem, vmem, hbm),
         scratch_shapes=[
             pltpu.SMEM((2, TCAP), jnp.int32),
-            pltpu.VMEM((2, TCAP, SUB * F, 256), jnp.bfloat16),
+            pltpu.VMEM((TCAP, 2 * SUB * F, 256), jnp.bfloat16),
             pltpu.VMEM((SUB * F * 8, 128), jnp.float32),
             pltpu.VMEM((PAIRS * SUB * F * 8, 128), jnp.float32),
             pltpu.VMEM((PAIRS, STACK, COLS), jnp.bfloat16),
@@ -349,9 +391,12 @@
             pltpu.VMEM((4 * CH, STACK), jnp.bfloat16),
             pltpu.VMEM((4 * CH, STACK), jnp.bfloat16),
             pltpu.VMEM((STACK, 4 * CH), jnp.bfloat16),
+            pltpu.VMEM((2, 4 * CH, 256), jnp.float32),
+            pltpu.VMEM((4 * CH, STACK), jnp.float32),
+            pltpu.VMEM((4 * CH, STACK), jnp.float32),
             pltpu.VMEM((CH, 256), jnp.float32),
             pltpu.VMEM((CH, 256), jnp.float32),
-            pltpu.SemaphoreType.DMA((2, TCAP)),
+            pltpu.SemaphoreType.DMA((TCAP,)),
             pltpu.SemaphoreType.DMA,
         ],
         compiler_params=pltpu.CompilerParams(vmem_limit_bytes=48 * 1024 * 1024),
@@ -363,29 +408,24 @@
         last,
         jnp.asarray(SELECT_FIRST, jnp.bfloat16),
         jnp.asarray(SELECT_LAST, jnp.bfloat16),
-        *arrived_inputs,
-        *arrived_targets,
+        *arrived,
         fields,
     )
 
 
-def viscosity_of(cells, closure_in, closure_bias, closure_out):
-    halves = [0.5 * value for value in cells]
-
+def viscosity_of(cells, closure):
     def unit(h, total):
-        half = 0.5 * closure_bias[h] + closure_in[h, 0] * halves[0]
+        half = closure[F, h] + closure[0, h] * cells[0]
         for f in range(1, F):
-            half = half + closure_in[h, f] * halves[f]
-        return total + closure_out[h] * (half + half * jnp.tanh(half))
+            half = half + closure[f, h] * cells[f]
+        return total + closure[F + 1, h] * (half + half * jnp.tanh(half))
 
     total = lax.fori_loop(0, HID, unit, jnp.zeros(cells[0].shape, jnp.float32), unroll=4)
     soft = jnp.maximum(total, 0.0) + jnp.log1p(jnp.exp(-jnp.abs(total)))
     return base_viscosity + viscosity_gain * soft
 
 
-def evolve_kernel(
-    closure_in, closure_bias, closure_out, fields, x_low, x_high, y_low, y_high, new_fields
-):
+def evolve_kernel(closure, fields, x_halo, y_low, y_high, new_fields):
     x_cells, y_cells, z_cells = fields.shape[1:]
     row = lax.broadcasted_iota(jnp.int32, (y_cells, z_cells), 0)
     lane = lax.broadcasted_iota(jnp.int32, (y_cells, z_cells), 1)
@@ -396,15 +436,15 @@
         for half in range(2):
             rows = pl.ds(half * part, part)
             cells = [fields[f, x, rows, :] for f in range(F)]
-            eddies.append(viscosity_of(cells, closure_in, closure_bias, closure_out))
+            eddies.append(viscosity_of(cells, closure))
         viscosity = jnp.concatenate(eddies, axis=0)
         centre = [fields[f, x] for f in range(F)]
         below = jnp.maximum(x - 1, 0)
         above = jnp.minimum(x + 1, x_cells - 1)
         for f in range(F):
             value = centre[f]
-            west = jnp.where(x == 0, x_low[f], fields[f, below])
-            east = jnp.where(x == x_cells - 1, x_high[f], fields[f, above])
+            west = jnp.where(x == 0, x_halo[1, f], fields[f, below])
+            east = jnp.where(x == x_cells - 1, x_halo[0, f], fields[f, above])
             south = jnp.where(row == 0, y_low[f, pl.ds(x, 1), :], pltpu.roll(value, 1, 0))
             north = jnp.where(
                 row == y_cells - 1, y_high[f, pl.ds(x, 1), :], pltpu.roll(value, y_cells - 1, 0)
@@ -424,16 +464,16 @@
     lax.fori_loop(0, x_cells, plane, 0)
 
 
-def evolve(closure_in, closure_bias, closure_out, fields, x_low, x_high, y_low, y_high):
+def evolve(closure, fields, x_halo, y_low, y_high):
     vmem = pl.BlockSpec(memory_space=pltpu.VMEM)
     return pl.pallas_call(
         evolve_kernel,
         out_shape=jax.ShapeDtypeStruct(fields.shape, fields.dtype),
-        in_specs=[pl.BlockSpec(memory_space=pltpu.SMEM)] * 3 + [vmem] * 5,
+        in_specs=[pl.BlockSpec(memory_space=pltpu.SMEM)] + [vmem] * 4,
         out_specs=vmem,
-        compiler_params=pltpu.CompilerParams(vmem_limit_bytes=48 * 1024 * 1024),
+        compiler_params=pltpu.CompilerParams(vmem_limit_bytes=16 * 1024 * 1024),
         name="evolve_brick",
-    )(closure_in, closure_bias, closure_out, fields, x_low, x_high, y_low, y_high)
+    )(closure, fields, x_halo, y_low, y_high)
 
 
 def cell_order():
@@ -462,7 +502,6 @@
     z_cells,
     sample_block,
     place,
-    order,
     brick,
     centre,
     lower,
@@ -471,9 +510,11 @@
     faces,
     row_for_low,
     row_for_high,
-    payload,
+    x_edges,
+    y_edges,
     windows,
     sems,
+    edge_sems,
 ):
     rows_of_x = y_cells
     rows_of_field = SUB * y_cells
@@ -484,7 +525,16 @@
         )
         for w in range(z_cells // 128)
     ]
-    for copy in copies:
+    edge_copies = [
+        pltpu.make_async_copy(
+            brick.at[pl.ds(f * rows_of_field + x * rows_of_x, rows_of_x)],
+            x_edges.at[side, f],
+            edge_sems.at[side, f],
+        )
+        for side, x in enumerate((0, SUB - 1))
+        for f in range(F)
+    ]
+    for copy in copies + edge_copies:
         copy.start()
     for copy in copies:
         copy.wait()
@@ -540,13 +590,22 @@
                 part = piece(row, 8, rows_of_field, z_there, step * SUB)
                 total = jnp.where(lane // SUB == step, part, total)
             faces[face, :, half * 128 : (half + 1) * 128] = total
-    payload[...] = dot_rows(centre[...].astype(jnp.bfloat16), order[...]).astype(jnp.bfloat16)
+    for side, y in enumerate((0, y_cells - 1)):
+        for field in range(F):
+            for w in range(z_cells // 128):
+                start = w * window_rows + field * rows_of_field + y
+                y_edges[side, field, :, w * 128 : (w + 1) * 128] = windows[
+                    pl.ds(start, SUB, rows_of_x), :
+                ]
+    for copy in edge_copies:
+        copy.wait()
 
 
 def sample_cube(sample_block, place, brick):
     fields, x_cells, y_cells, z_cells = brick.shape
     vmem = pl.BlockSpec(memory_space=pltpu.VMEM)
     smem = pl.BlockSpec(memory_space=pltpu.SMEM)
+    hbm = pl.BlockSpec(memory_space=pltpu.HBM)
     rows = fields * x_cells * y_cells
     cube = jax.ShapeDtypeStruct((F * SUB, 256), jnp.float32)
     line = jax.ShapeDtypeStruct((SUB, 128), jnp.float32)
@@ -560,17 +619,19 @@
             jax.ShapeDtypeStruct((2, 8, 256), jnp.float32),
             line,
             line,
-            jax.ShapeDtypeStruct((F * SUB, 256), jnp.bfloat16),
+            jax.ShapeDtypeStruct((2, fields, y_cells, z_cells), jnp.float32),
+            jax.ShapeDtypeStruct((2, fields, x_cells, z_cells), jnp.float32),
         ),
-        in_specs=[smem, smem, vmem, pl.BlockSpec(memory_space=pltpu.HBM)],
-        out_specs=(vmem,) * 8,
+        in_specs=[smem, smem, hbm],
+        out_specs=(vmem,) * 7 + (hbm, vmem),
         scratch_shapes=[
             pltpu.VMEM((z_cells // 128 * rows + 4 * x_cells * y_cells, 128), jnp.float32),
             pltpu.SemaphoreType.DMA((z_cells // 128,)),
+            pltpu.SemaphoreType.DMA((2, fields)),
         ],
-        compiler_params=pltpu.CompilerParams(vmem_limit_bytes=48 * 1024 * 1024),
+        compiler_params=pltpu.CompilerParams(vmem_limit_bytes=16 * 1024 * 1024),
         name="sample_cube",
-    )(sample_block, place, jnp.asarray(CELL_ORDER, jnp.bfloat16), brick.reshape(rows, z_cells))
+    )(sample_block, place, brick.reshape(rows, z_cells))
 
 
 def change_kernel(
@@ -578,16 +639,13 @@
     z_cells,
     sample_block,
     place,
-    closure_in,
-    closure_bias,
-    closure_out,
+    closure,
     order,
     centre,
     lower,
     upper,
     own_rows,
-    face_low,
-    face_high,
+    face_halo,
     row_low,
     row_high,
     payload,
@@ -598,12 +656,12 @@
     south_row = jnp.where(y_start == 0, row_low[...], own_rows[0])
     north_row = jnp.where(y_start + SUB == y_cells, row_high[...], own_rows[1])
     cells = [centre[f * SUB : (f + 1) * SUB, :] for f in range(F)]
-    viscosity = viscosity_of(cells, closure_in, closure_bias, closure_out)
+    viscosity = viscosity_of(cells, closure)
     changes = []
     for f in range(F):
         value = cells[f]
-        west = jnp.where(row == 0, face_low[f : f + 1, :], pltpu.roll(value, 1, 0))
-        east = jnp.where(row == SUB - 1, face_high[f : f + 1, :], pltpu.roll(value, SUB - 1, 0))
+        west = jnp.where(row == 0, face_halo[1, f : f + 1, :], pltpu.roll(value, 1, 0))
+        east = jnp.where(row == SUB - 1, face_halo[0, f : f + 1, :], pltpu.roll(value, SUB - 1, 0))
         edge = pltpu.roll(south_row, (128 - f * SUB) % 128, 1)
         south = jnp.where(lane < SUB, jnp.concatenate([edge, edge], 1), pltpu.roll(value, SUB, 1))
         edge = pltpu.roll(north_row, 112 - f * SUB, 1)
@@ -618,8 +676,8 @@
         if f == 2:
             change = change + buoyancy * cells[3]
         changes.append(change)
-    changes = jnp.concatenate(changes, axis=0).astype(jnp.bfloat16)
-    payload[...] = dot_rows(changes, order[...]).astype(jnp.bfloat16)
+    both = jnp.concatenate(cells + changes, axis=0).astype(jnp.bfloat16)
+    payload[...] = dot_rows(both, order[...]).astype(jnp.bfloat16)
 
 
 def cube_change(sample_block, place, closure, cube, halo, y_cells, z_cells):
@@ -627,11 +685,12 @@
     smem = pl.BlockSpec(memory_space=pltpu.SMEM)
     return pl.pallas_call(
         functools.partial(change_kernel, y_cells, z_cells),
-        out_shape=jax.ShapeDtypeStruct((F * SUB, 256), jnp.bfloat16),
-        in_specs=[smem] * 5 + [vmem] * 9,
+        out_shape=jax.ShapeDtypeStruct((2 * F * SUB, 256), jnp.bfloat16),
+        in_specs=[smem] * 3 + [vmem] * 8,
         out_specs=vmem,
+        compiler_params=pltpu.CompilerParams(vmem_limit_bytes=16 * 1024 * 1024),
         name="cube_change",
-    )(sample_block, place, *closure, jnp.asarray(CELL_ORDER, jnp.bfloat16), *cube, *halo)
+    )(sample_block, place, closure, jnp.asarray(CELL_ORDER, jnp.bfloat16), *cube, *halo)
 
 
 def doubling_steps(x_devices, y_devices):
@@ -655,7 +714,9 @@
     first_trainer = sim_groups * trainers
     brick = fields[0]
     y_cells, z_cells = brick.shape[2:]
-    closure = (closure_in, closure_bias, closure_out)
+    closure = jnp.concatenate(
+        [0.5 * closure_in.T, 0.5 * closure_bias[None], closure_out[None]], axis=0
+    )
     place = jnp.stack(
         [
             my_group,
@@ -667,24 +728,27 @@
         ]
     ).astype(jnp.int32)
 
-    def neighbours(for_low, for_high, along_x):
-        def pairs(step):
-            found = []
-            for g in range(sim_groups):
-                for c in range(trainers):
-                    gx, gy = c // y_devices, c % y_devices
-                    if along_x:
-                        gx = (gx + step) % x_devices
-                    else:
-                        gy = (gy + step) % y_devices
-                    found.append((g * trainers + c, (g * x_devices + gx) * y_devices + gy))
-            return found
-
-        if (x_devices if along_x else y_devices) == 2:
-            both = lax.ppermute(jnp.stack([for_high, for_low]), everyone, pairs(1))
-            return both[0], both[1]
-        from_low = lax.ppermute(for_high, everyone, pairs(1))
-        return from_low, lax.ppermute(for_low, everyone, pairs(-1))
+    def pairs(along_x, step):
+        found = []
+        for g in range(sim_groups):
+            for c in range(trainers):
+                gx, gy = c // y_devices, c % y_devices
+                if along_x:
+                    gx = (gx + step) % x_devices
+                else:
+                    gy = (gy + step) % y_devices
+                found.append((g * trainers + c, (g * x_devices + gx) * y_devices + gy))
+        return found
+
+    def x_neighbours(edges):
+        if x_devices == 2:
+            return lax.ppermute(edges, everyone, pairs(True, 1))
+        from_high = lax.ppermute(edges[0], everyone, pairs(True, -1))
+        return jnp.stack([from_high, lax.ppermute(edges[1], everyone, pairs(True, 1))])
+
+    def y_neighbours(for_low, for_high):
+        from_low = lax.ppermute(for_high, everyone, pairs(False, 1))
+        return from_low, lax.ppermute(for_low, everyone, pairs(False, -1))
 
     def swap(distance):
         return [(first_trainer + c, first_trainer + (c ^ distance)) for c in range(trainers)]
@@ -708,19 +772,15 @@
             held = jnp.concatenate([held, lax.ppermute(held, everyone, swap(distance))], axis=0)
         return [held, lax.ppermute(held, everyone, swap(steps[-1]))]
 
-    *cube, faces, row_for_low, row_for_high, sent_inputs = sample_cube(sample_block, place, brick)
-    face_halo = neighbours(faces[0], faces[1], True)
-    row_halo = neighbours(row_for_low, row_for_high, False)
-    landed_inputs = to_trainers(sent_inputs)
-    sent_targets = cube_change(
-        sample_block, place, closure, cube, (*face_halo, *row_halo), y_cells, z_cells
+    *cube, faces, row_for_low, row_for_high, x_edges, y_edges = sample_cube(
+        sample_block, place, brick
     )
-    landed_targets = to_trainers(sent_targets)
-    edges = (brick[:, 0], brick[:, -1], brick[:, :, 0], brick[:, :, -1])
-    *edges, landed_targets = lax.optimization_barrier((*edges, landed_targets))
-    halo = (*neighbours(edges[0], edges[1], True), *neighbours(edges[2], edges[3], False))
-    arrived_inputs = among_trainers(landed_inputs)
-    arrived_targets = among_trainers(landed_targets)
+    thin_halo = (x_neighbours(faces), *y_neighbours(row_for_low, row_for_high))
+    payload = cube_change(sample_block, place, closure, cube, thin_halo, y_cells, z_cells)
+    landed = to_trainers(payload)
+    x_edges, y_edges, landed = lax.optimization_barrier((x_edges, y_edges, landed))
+    halo = (x_neighbours(x_edges), *y_neighbours(y_edges[0], y_edges[1]))
+    arrived = among_trainers(landed)
 
     first_count = CH * TAPS * F
     first = jnp.pad(master[:first_count].reshape(CH, TAPS * F), ((0, 0), (0, 256 - TAPS * F)))
@@ -728,7 +788,7 @@
 
     def train_here():
         delta_first, delta_last, new_brick = train_cubes(
-            sample_trainer, place, first, last, arrived_inputs, arrived_targets, brick, steps
+            sample_trainer, place, first, last, arrived, brick, steps
         )
         delta = jnp.concatenate(
             [delta_first[:, : TAPS * F].reshape(-1), delta_last[:, : TAPS * F].T.reshape(-1)]
@@ -736,7 +796,7 @@
         return delta, new_brick
 
     def evolve_here():
-        new_brick = evolve(*closure, brick, *halo)
+        new_brick = evolve(closure, brick, *halo)
         return jnp.zeros((NPARAM,), jnp.float32), new_brick
 
     delta, new_brick = lax.cond(is_trainer, train_here, evolve_here)

time: 222 us -> 216 us (0.973)
  waiting for transfers between devices: 113 us -> 132 us
  local copies, waits for them, and re-layouts: 9.91 us -> 1.01 us
  starting transfers between devices: 39.6 us -> 31.3 us
  Pallas kernels: 54.1 us -> 46.3 us
    ppermute x3, waiting for transfers between devices: 109 us -> 122 us  [on_device(): final = final + lax.ppermute(total, everyone, pairs)]
    ppermute x6 -> x3, starting transfers between devices: 9.59 us -> 2.63 us  [to_trainers(): lax.ppermute(payload, everyone, [(g * trainers + c, first_trainer + c) fo...]
    pallas_call x1, Pallas kernels: 46.6 us -> 39.7 us  [evolve(): pl.pallas_call(evolve_kernel, out_shape=jax.ShapeDtypeStruct(fields.shape...]
    unnamed x34 -> x14, local copies, waits for them, and re-layouts: 6.1 us -> 0.72 us
    ppermute x6, waiting for transfers between devices: 3.44 us -> 8.16 us  [the longest x2 5.03 us: y_neighbours(): from_low = lax.ppermute(for_high, everyone, pairs(False, 1))]
  transfers between devices with their start and end apart: 24 -> 18, of which waited for: 5 -> 5; matrix products, arithmetic and copies ran while one was open for 2% -> 0% of each run, Pallas kernels for 1% -> 0%
where the time goes in v3:
time: 216 us; the launch traced here: 215 us
  waiting for transfers between devices  132 us (61%)
  Pallas kernels  46.3 us (21%)
  starting transfers between devices  31.3 us (14%)
    ppermute x3, waiting for transfers between devices, on_device(): final = final + lax.ppermute(total, everyone, pairs)  122 us
    pallas_call x1, Pallas kernels, evolve(): pl.pallas_call(evolve_kernel, out_shape=jax.ShapeDtypeStruct(fields.shape...  39.7 us
    ppermute x2, starting transfers between devices, y_neighbours(): return (from_low, lax.ppermute(for_low, everyone, pairs(False, -1)))  7.65 us
    ppermute x2, starting transfers between devices, x_neighbours(): return lax.ppermute(edges, everyone, pairs(True, 1))  7.28 us
    ppermute x2, starting transfers between devices, y_neighbours(): from_low = lax.ppermute(for_high, everyone, pairs(False, 1))  7.07 us
    pallas_call x1, Pallas kernels, sample_cube(): pl.pallas_call(functools.partial(sample_kernel, y_cells, z_cells), out_sh...  5.04 us
    ppermute x2, waiting for transfers between devices, y_neighbours(): from_low = lax.ppermute(for_high, everyone, pairs(False, 1))  5.03 us
  transfers between devices with their start and end apart: 18, of which 5 were waited for; matrix products, arithmetic and copies ran while one was open for 0% of the time, Pallas kernels for 0%

profile of v3, /device:TPU:0, one launch (start us, length us, event | category | flops | bytes accessed | tf_op | source)
XLA Modules:
  0.0 215.0 jit_solution(12857833295058965432)
XLA Ops:
  0.6 0.0 copy-start.2
  0.6 0.1 stack.27.place
  0.7 0.7 copy-done.3
  1.4 5.0 %sample_cube.1 = (f32[80,256]{1,0:T(8,128)S(1)}, f32[80,256]{1,0:T(8,128)S(1)}, f32[80,256]{1,0:T(8,128)S(1)}, f32[2,16,128]{2,1,0:T(8,128)S(1)}, f32[2,8,256]{2...) custom-call(s32[24]{0:T(128)S(1)} %copy-done.3, ...), custom_call_target="tpu_custom_call" | custom-call | tf_op jit(solution)/shard_map/sample_cube/pallas_call | solution.py:612
  6.5 4.9 %collective-permute-start.1 = (f32[16,128]{1,0:T(8,128)S(1)}, f32[16,128]{1,0:T(8,128)S(1)}, u32[]{:S(2)}, u32[]{:S(2)}) collective-permute-start(f32[16,128]{1,0:T(8,128)S(1)} %get-tuple-element.70), channel_id=1, source_target_pairs={{0,1},{1,2},{2,3},{3,0},{4,5},{5,6},{6,7},{7,4},{8,9},{9,10},{10,1... | collective-permute-start | bytes 24584 | tf_op jit(solution)/shard_map/ppermute | solution.py:750
  11.4 3.9 %collective-permute-start.2 = (f32[16,128]{1,0:T(8,128)S(1)}, f32[16,128]{1,0:T(8,128)S(1)}, u32[]{:S(2)}, u32[]{:S(2)}) collective-permute-start(f32[16,128]{1,0:T(8,128)S(1)} %get-tuple-element.71), channel_id=1, source_target_pairs={{0,3},{1,0},{2,1},{3,2},{4,7},{5,4},{6,5},{7,6},{8,11},{9,8},{10,9... | collective-permute-start | bytes 24584 | tf_op jit(solution)/shard_map/ppermute | solution.py:751
  15.3 3.6 %collective-permute-start = (f32[2,8,256]{2,1,0:T(8,128)S(1)}, f32[2,8,256]{2,1,0:T(8,128)S(1)}, u32[]{:S(2)}, u32[]{:S(2)}) collective-permute-start(f32[2,8,256]{2,1,0:T(8,128)S(1)} %get-tuple-element.69), channel_id=1, source_target_pairs={{0,4},{1,5},{2,6},{3,7},{4,0},{5,1},{6,2},{7,3},{8,12},{9,13},{10,... | collective-permute-start | bytes 49160 | tf_op jit(solution)/shard_map/ppermute | solution.py:745
  19.0 0.0 copy-done.7
  19.1 0.0 collective-permute-done.1.row_low
  19.1 0.0 collective-permute-done.2.row_high
  19.1 1.9 collective-permute-done.face_halo
  21.0 1.6 cube_change.1
  22.6 0.7 collective-permute-start.5
  23.3 0.7 collective-permute-start.4
  23.9 1.3 collective-permute-start.3
  25.2 0.0 collective-permute-done.5
  25.2 0.0 collective-permute-done.4
  25.3 2.0 collective-permute-done.3
  27.3 0.7 collective-permute-start.9
  28.0 0.0 collective-permute-done.9
  28.1 0.7 collective-permute-start.10
  28.8 0.0 collective-permute-done.10
  28.9 0.7 collective-permute-start.11
  29.6 3.6 %collective-permute-start.6 = (f32[2,5,32,384]{3,2,1,0:T(8,128)S(1)}, f32[2,5,32,384]{3,2,1,0:T(8,128)S(1)}, u32[]{:S(2)}, u32[]{:S(2)}) collective-permute-start(f32[2,5,32,384]{3,2,1,0:T(8,128)S(1)} %get-tuple-element.72), channel_id=1, source_target_pairs={{0,4},{1,5},{2,6},{3,7},{4,0},{5,1},{6,2},{7,3},{8,12},{9,13},{10,... | collective-permute-start | bytes 1474568 | tf_op jit(solution)/shard_map/ppermute | solution.py:745
  33.3 3.7 %collective-permute-start.8 = (f32[5,16,384]{2,1,0:T(8,128)S(1)}, f32[5,16,384]{2,1,0:T(8,128)S(1)}, u32[]{:S(2)}, u32[]{:S(2)}) collective-permute-start(f32[5,16,384]{2,1,0:T(8,128)S(1)} %get-tuple-element.121), channel_id=1, source_target_pairs={{0,3},{1,0},{2,1},{3,2},{4,7},{5,4},{6,5},{7,6},{8,11},{9,8},{10,9... | collective-permute-start | bytes 368648 | tf_op jit(solution)/shard_map/ppermute | solution.py:751
  37.0 2.1 collective-permute-start.7
  39.1 0.1 slice.40
  39.2 0.1 reshape.33
  39.3 1.2 collective-permute-done.8
  40.5 5.0 %collective-permute-done.7 = f32[5,16,384]{2,1,0:T(8,128)S(1)} collective-permute-done((f32[5,16,384]{2,1,0:T(8,128)S(1)}, f32[5,16,384]{2,1,0:T(8,128)S(1)}, u32[]{:S(2)}, u32[]{:S(2)}) %collective-permute-start.7) | collective-permute-done | bytes 122912 | tf_op jit(solution)/shard_map/ppermute | solution.py:750
  45.6 0.0 collective-permute-done.6
  45.6 0.0 collective-permute-done.11
  45.6 39.7 %conditional.1 = (f32[17280]{0:T(1024)S(1)}, f32[1,5,16,32,384]{4,3,2,1,0:T(8,128)}) conditional(s32[]{:T(128)} %convert_element_type.6, (f32[7,64]{1,0:T(8,128)S(1)}, f32[5,16,32,384]{3,2,1,0:T(8,128)}, f32[2,5,32,384]{3,2,1,0:T(8,128)S(1)}, f32[5,16,384]{2,1,0:T(8,128)S(1)}, f32[5,16,384]{2,1,0:T(8,128)S(1)}) %tuple.34, (s32[24]{0:T(128)}, ...), branch_computations={%region_0.1_spmd, %region_1.2_spmd.clone} | conditional | flops 17280 | bytes 4754512 | solution.py:802
  45.6 39.7 %evolve_brick.1 = f32[5,16,32,384]{3,2,1,0:T(8,128)} custom-call(f32[7,64]{1,0:T(8,128)S(1)} %get-tuple-element.29.closure, f32[5,16,32,384]{3,2,1,0:T(8,128)} %get-tuple-element.30.fields, f32[2,5,32,384]{3,2,1,0:T(8,128)S(1)} %get-tuple-element.31.x_halo, f32[5,16,384]{2,1,0:T(8,128)S(1)} %get-tuple-element.32.y_low, ...), custom_call_target="tpu_custom_call" | custom-call | tf_op jit(solution)/shard_map/cond/branch_0_fun/evolve_brick/pallas_call | solution.py:469
  85.3 0.7 collective-permute-start.12
  85.9 0.0 collective-permute-done.12
  86.0 0.7 collective-permute-start.13
  86.6 0.0 collective-permute-done.13
  86.7 0.7 collective-permute-start.14
  87.3 0.0 collective-permute-done.14
  87.4 0.7 collective-permute-start.17
  88.0 0.7 collective-permute-start.16
  88.7 1.3 collective-permute-start.15
  90.0 0.0 collective-permute-done.17
  90.0 0.0 collective-permute-done.16
  90.1 122.2 %collective-permute-done.15 = f32[17280]{0:T(1024)S(1)} collective-permute-done((f32[17280]{0:T(1024)S(1)}, f32[17280]{0:T(1024)S(1)}, u32[]{:S(2)}, u32[]{:S(2)}) %collective-permute-start.15) | collective-permute-done | bytes 69152 | tf_op jit(solution)/shard_map/ppermute | solution.py:810
  212.3 0.6 multiply_reduce_fusion
  213.6 1.4 multiply_subtract_fusion
  (22 shorter events, 0.2 us)
Async XLA Ops:
  0.6 20.4 %copy-start.2 = (bf16[256,256]{1,0:T(8,128)(2,1)S(1)}, bf16[256,256]{1,0:T(8,128)(2,1)}, u32[]{:S(2)}) copy-start(bf16[256,256]{1,0:T(8,128)(2,1)} %constant.54.clone.order) | copy-start | bytes 393220
  0.7 0.7 copy-start.3
  1.4 17.6 %copy-start.7 = (f32[64]{0:T(128)S(1)}, f32[64]{0:T(128)}, u32[]{:S(2)}) copy-start(f32[64]{0:T(128)} %param.15) | copy-start | bytes 772
  1.4 17.6 %copy-start.5 = (f32[64,5]{0,1:T(8,128)S(1)}, f32[64,5]{0,1:T(8,128)}, u32[]{:S(2)}) copy-start(f32[64,5]{0,1:T(8,128)} %param.14) | copy-start | bytes 3844
  1.4 17.6 %copy-start.6 = (f32[64]{0:T(128)S(1)}, f32[64]{0:T(128)}, u32[]{:S(2)}) copy-start(f32[64]{0:T(128)} %param.16) | copy-start | bytes 772
  1.4 37.7 %copy-start.4 = (f32[17280]{0:T(1024)S(1)}, f32[17280]{0:T(1024)}, u32[]{:S(2)}) copy-start(f32[17280]{0:T(1024)} %param.17) | copy-start | bytes 207364
  6.5 12.6 %collective-permute-start.1 = (f32[16,128]{1,0:T(8,128)S(1)}, f32[16,128]{1,0:T(8,128)S(1)}, u32[]{:S(2)}, u32[]{:S(2)}) collective-permute-start(f32[16,128]{1,0:T(8,128)S(1)} %get-tuple-element.70), channel_id=1, source_target_pairs={{0,1},{1,2},{2,3},{3,0},{4,5},{5,6},{6,7},{7,4},{8,9},{9,10},{10,1... | collective-permute-start | bytes 24584 | tf_op jit(solution)/shard_map/ppermute | solution.py:750
  11.4 7.7 %collective-permute-start.2 = (f32[16,128]{1,0:T(8,128)S(1)}, f32[16,128]{1,0:T(8,128)S(1)}, u32[]{:S(2)}, u32[]{:S(2)}) collective-permute-start(f32[16,128]{1,0:T(8,128)S(1)} %get-tuple-element.71), channel_id=1, source_target_pairs={{0,3},{1,0},{2,1},{3,2},{4,7},{5,4},{6,5},{7,6},{8,11},{9,8},{10,9... | collective-permute-start | bytes 24584 | tf_op jit(solution)/shard_map/ppermute | solution.py:751
  15.3 5.6 %collective-permute-start = (f32[2,8,256]{2,1,0:T(8,128)S(1)}, f32[2,8,256]{2,1,0:T(8,128)S(1)}, u32[]{:S(2)}, u32[]{:S(2)}) collective-permute-start(f32[2,8,256]{2,1,0:T(8,128)S(1)} %get-tuple-element.69), channel_id=1, source_target_pairs={{0,4},{1,5},{2,6},{3,7},{4,0},{5,1},{6,2},{7,3},{8,12},{9,13},{10,... | collective-permute-start | bytes 49160 | tf_op jit(solution)/shard_map/ppermute | solution.py:745
  22.6 2.7 %collective-permute-start.5 = (bf16[160,256]{1,0:T(8,128)(2,1)S(1)}, bf16[160,256]{1,0:T(8,128)(2,1)S(1)}, u32[]{:S(2)}, u32[]{:S(2)}) collective-permute-start(bf16[160,256]{1,0:T(8,128)(2,1)S(1)} %cube_change.1), channel_id=1, source_target_pairs={{16,24},{17,25},{18,26},{19,27},{20,28},{21,29},{22,30},{23,31}} | collective-permute-start | bytes 245768 | tf_op jit(solution)/shard_map/ppermute | solution.py:761
  23.3 2.0 collective-permute-start.4
  23.9 3.3 %collective-permute-start.3 = (bf16[160,256]{1,0:T(8,128)(2,1)S(1)}, bf16[160,256]{1,0:T(8,128)(2,1)S(1)}, u32[]{:S(2)}, u32[]{:S(2)}) collective-permute-start(bf16[160,256]{1,0:T(8,128)(2,1)S(1)} %cube_change.1), channel_id=1, source_target_pairs={{0,24},{1,25},{2,26},{3,27},{4,28},{5,29},{6,30},{7,31}} | collective-permute-start | bytes 245768 | tf_op jit(solution)/shard_map/ppermute | solution.py:761
  27.3 0.7 collective-permute-start.9
  28.1 0.8 collective-permute-start.10
  28.9 16.7 %collective-permute-start.11 = (bf16[12,160,256]{2,1,0:T(8,128)(2,1)S(1)}, bf16[12,160,256]{2,1,0:T(8,128)(2,1)S(1)}, u32[]{:S(2)}, u32[]{:S(2)}) collective-permute-start(bf16[12,160,256]{2,1,0:T(8,128)(2,1)S(1)} %constant_dynamic-update-slice_fusion), channel_id=1, source_target_pairs={{24,28},{25,29},{26,30},{27,31},{28,24},{29,25},{30,26},{31,27}} | collective-permute-start | bytes 2949128 | tf_op jit(solution)/shard_map/ppermute | solution.py:773
  29.6 16.0 %collective-permute-start.6 = (f32[2,5,32,384]{3,2,1,0:T(8,128)S(1)}, f32[2,5,32,384]{3,2,1,0:T(8,128)S(1)}, u32[]{:S(2)}, u32[]{:S(2)}) collective-permute-start(f32[2,5,32,384]{3,2,1,0:T(8,128)S(1)} %get-tuple-element.72), channel_id=1, source_target_pairs={{0,4},{1,5},{2,6},{3,7},{4,0},{5,1},{6,2},{7,3},{8,12},{9,13},{10,... | collective-permute-start | bytes 1474568 | tf_op jit(solution)/shard_map/ppermute | solution.py:745
  33.3 7.3 %collective-permute-start.8 = (f32[5,16,384]{2,1,0:T(8,128)S(1)}, f32[5,16,384]{2,1,0:T(8,128)S(1)}, u32[]{:S(2)}, u32[]{:S(2)}) collective-permute-start(f32[5,16,384]{2,1,0:T(8,128)S(1)} %get-tuple-element.121), channel_id=1, source_target_pairs={{0,3},{1,0},{2,1},{3,2},{4,7},{5,4},{6,5},{7,6},{8,11},{9,8},{10,9... | collective-permute-start | bytes 368648 | tf_op jit(solution)/shard_map/ppermute | solution.py:751
  37.0 8.6 %collective-permute-start.7 = (f32[5,16,384]{2,1,0:T(8,128)S(1)}, f32[5,16,384]{2,1,0:T(8,128)S(1)}, u32[]{:S(2)}, u32[]{:S(2)}) collective-permute-start(f32[5,16,384]{2,1,0:T(8,128)S(1)} %get-tuple-element.122), channel_id=1, source_target_pairs={{0,1},{1,2},{2,3},{3,0},{4,5},{5,6},{6,7},{7,4},{8,9},{9,10},{10,1... | collective-permute-start | bytes 368648 | tf_op jit(solution)/shard_map/ppermute | solution.py:750
  85.3 0.7 collective-permute-start.12
  86.0 0.7 collective-permute-start.13
  86.7 0.7 collective-permute-start.14
  87.4 2.7 %collective-permute-start.17 = (f32[17280]{0:T(1024)S(1)}, f32[17280]{0:T(1024)S(1)}, u32[]{:S(2)}, u32[]{:S(2)}) collective-permute-start(f32[17280]{0:T(1024)S(1)} %add.44), channel_id=1, source_target_pairs={{24,16},{25,17},{26,18},{27,19},{28,20},{29,21},{30,22},{31,23}} | collective-permute-start | bytes 207368 | tf_op jit(solution)/shard_map/ppermute | solution.py:810
  88.0 2.0 collective-permute-start.16
  88.7 123.5 %collective-permute-start.15 = (f32[17280]{0:T(1024)S(1)}, f32[17280]{0:T(1024)S(1)}, u32[]{:S(2)}, u32[]{:S(2)}) collective-permute-start(f32[17280]{0:T(1024)S(1)} %add.44), channel_id=1, source_target_pairs={{24,0},{25,1},{26,2},{27,3},{28,4},{29,5},{30,6},{31,7}} | collective-permute-start | bytes 207368 | tf_op jit(solution)/shard_map/ppermute | solution.py:810

commit v4 on v3

--- a/solution.py
+++ b/solution.py
@@ -138,12 +138,14 @@
         grad_last,
         now_first,
         now_last,
+        brick,
         slot_sems,
         field_sem,
     ) = refs[12:]
 
-    field_copy = pltpu.make_async_copy(fields_ref, new_fields_ref, field_sem)
-    field_copy.start()
+    field_in = pltpu.make_async_copy(fields_ref, brick, field_sem)
+    field_out = pltpu.make_async_copy(brick, new_fields_ref, field_sem)
+    field_in.start()
 
     groups = place[3]
     trainers = trainer_of.shape[0] // groups
@@ -235,6 +237,9 @@
             return carry
 
         lax.fori_loop(0, SUB, stack_plane, 0, unroll=8)
+
+    field_in.wait()
+    field_out.start()
 
     def train_step(step, step_carry):
         first_now = now_first[...].astype(jnp.bfloat16)
@@ -356,7 +361,7 @@
     lax.fori_loop(0, INNER, train_step, 0)
     delta_first[...] = start_first - now_first[...]
     delta_last[...] = start_last - now_last[...]
-    field_copy.wait()
+    field_out.wait()
 
 
 def apart(left, right, distance):
@@ -396,6 +401,7 @@
             pltpu.VMEM((4 * CH, STACK), jnp.float32),
             pltpu.VMEM((CH, 256), jnp.float32),
             pltpu.VMEM((CH, 256), jnp.float32),
+            pltpu.VMEM(fields.shape, fields.dtype),
             pltpu.SemaphoreType.DMA((TCAP,)),
             pltpu.SemaphoreType.DMA,
         ],
@@ -425,7 +431,8 @@
     return base_viscosity + viscosity_gain * soft
 
 
-def evolve_kernel(closure, fields, x_halo, y_low, y_high, new_fields):
+def evolve_kernel(closure, place, fields, x_halo, y_first, y_second, new_fields):
+    up_first = lax.rem(place[2], 2) == 0
     x_cells, y_cells, z_cells = fields.shape[1:]
     row = lax.broadcasted_iota(jnp.int32, (y_cells, z_cells), 0)
     lane = lax.broadcasted_iota(jnp.int32, (y_cells, z_cells), 1)
@@ -445,9 +452,14 @@
             value = centre[f]
             west = jnp.where(x == 0, x_halo[1, f], fields[f, below])
             east = jnp.where(x == x_cells - 1, x_halo[0, f], fields[f, above])
-            south = jnp.where(row == 0, y_low[f, pl.ds(x, 1), :], pltpu.roll(value, 1, 0))
+            first, second = y_first[f, pl.ds(x, 1), :], y_second[f, pl.ds(x, 1), :]
+            south = jnp.where(
+                row == 0, jnp.where(up_first, second, first), pltpu.roll(value, 1, 0)
+            )
             north = jnp.where(
-                row == y_cells - 1, y_high[f, pl.ds(x, 1), :], pltpu.roll(value, y_cells - 1, 0)
+                row == y_cells - 1,
+                jnp.where(up_first, first, second),
+                pltpu.roll(value, y_cells - 1, 0),
             )
             lower = jnp.where(lane == 0, 0.0, pltpu.roll(value, 1, 1))
             upper = jnp.where(lane == z_cells - 1, 0.0, pltpu.roll(value, z_cells - 1, 1))
@@ -464,16 +476,16 @@
     lax.fori_loop(0, x_cells, plane, 0)
 
 
-def evolve(closure, fields, x_halo, y_low, y_high):
+def evolve(closure, place, fields, x_halo, y_first, y_second):
     vmem = pl.BlockSpec(memory_space=pltpu.VMEM)
     return pl.pallas_call(
         evolve_kernel,
         out_shape=jax.ShapeDtypeStruct(fields.shape, fields.dtype),
-        in_specs=[pl.BlockSpec(memory_space=pltpu.SMEM)] + [vmem] * 4,
+        in_specs=[pl.BlockSpec(memory_space=pltpu.SMEM)] * 2 + [vmem] * 4,
         out_specs=vmem,
         compiler_params=pltpu.CompilerParams(vmem_limit_bytes=16 * 1024 * 1024),
         name="evolve_brick",
-    )(closure, fields, x_halo, y_low, y_high)
+    )(closure, place, fields, x_halo, y_first, y_second)
 
 
 def cell_order():
@@ -508,13 +520,12 @@
     upper,
     own_rows,
     faces,
-    row_for_low,
-    row_for_high,
+    row_for_first,
+    row_for_second,
     x_edges,
     y_edges,
     windows,
     sems,
-    edge_sems,
 ):
     rows_of_x = y_cells
     rows_of_field = SUB * y_cells
@@ -525,16 +536,7 @@
         )
         for w in range(z_cells // 128)
     ]
-    edge_copies = [
-        pltpu.make_async_copy(
-            brick.at[pl.ds(f * rows_of_field + x * rows_of_x, rows_of_x)],
-            x_edges.at[side, f],
-            edge_sems.at[side, f],
-        )
-        for side, x in enumerate((0, SUB - 1))
-        for f in range(F)
-    ]
-    for copy in copies + edge_copies:
+    for copy in copies:
         copy.start()
     for copy in copies:
         copy.wait()
@@ -578,8 +580,11 @@
 
     own_rows[0] = y_row(jnp.maximum(y_start - 1, 0), z_start)
     own_rows[1] = y_row(jnp.minimum(y_start + SUB, y_cells - 1), z_start)
-    row_for_low[...] = y_row(0, corner(0, -1)[1])
-    row_for_high[...] = y_row(y_cells - 1, corner(0, 1)[1])
+    up_first = lax.rem(place[2], 2) == 0
+    z_first = corner(0, jnp.where(up_first, 1, -1))[1]
+    z_second = corner(0, jnp.where(up_first, -1, 1))[1]
+    row_for_first[...] = y_row(jnp.where(up_first, y_cells - 1, 0), z_first)
+    row_for_second[...] = y_row(jnp.where(up_first, 0, y_cells - 1), z_second)
     lane = lane[:8]
     for face, (x, step) in enumerate(((0, -1), (SUB - 1, 1))):
         y_there, z_there = corner(step, 0)
@@ -590,15 +595,19 @@
                 part = piece(row, 8, rows_of_field, z_there, step * SUB)
                 total = jnp.where(lane // SUB == step, part, total)
             faces[face, :, half * 128 : (half + 1) * 128] = total
-    for side, y in enumerate((0, y_cells - 1)):
+    for side in range(2):
+        y = jnp.where(up_first == (side == 0), y_cells - 1, 0)
         for field in range(F):
             for w in range(z_cells // 128):
                 start = w * window_rows + field * rows_of_field + y
                 y_edges[side, field, :, w * 128 : (w + 1) * 128] = windows[
                     pl.ds(start, SUB, rows_of_x), :
                 ]
-    for copy in edge_copies:
-        copy.wait()
+    for side, x in enumerate((0, SUB - 1)):
+        for field in range(F):
+            for w in range(z_cells // 128):
+                start = w * window_rows + field * rows_of_field + x * rows_of_x
+                x_edges[side, field, :, w * 128 : (w + 1) * 128] = windows[pl.ds(start, rows_of_x), :]
 
 
 def sample_cube(sample_block, place, brick):
@@ -623,11 +632,10 @@
             jax.ShapeDtypeStruct((2, fields, x_cells, z_cells), jnp.float32),
         ),
         in_specs=[smem, smem, hbm],
-        out_specs=(vmem,) * 7 + (hbm, vmem),
+        out_specs=(vmem,) * 9,
         scratch_shapes=[
             pltpu.VMEM((z_cells // 128 * rows + 4 * x_cells * y_cells, 128), jnp.float32),
             pltpu.SemaphoreType.DMA((z_cells // 128,)),
-            pltpu.SemaphoreType.DMA((2, fields)),
         ],
         compiler_params=pltpu.CompilerParams(vmem_limit_bytes=16 * 1024 * 1024),
         name="sample_cube",
@@ -646,15 +654,18 @@
     upper,
     own_rows,
     face_halo,
-    row_low,
-    row_high,
+    row_first,
+    row_second,
     payload,
 ):
     y_start = corner_of(sample_block, place, 0, 0, y_cells, z_cells)[0]
     row = lax.broadcasted_iota(jnp.int32, (SUB, 256), 0)
     lane = lax.broadcasted_iota(jnp.int32, (SUB, 256), 1)
-    south_row = jnp.where(y_start == 0, row_low[...], own_rows[0])
-    north_row = jnp.where(y_start + SUB == y_cells, row_high[...], own_rows[1])
+    up_first = lax.rem(place[2], 2) == 0
+    row_low = jnp.where(up_first, row_second[...], row_first[...])
+    row_high = jnp.where(up_first, row_first[...], row_second[...])
+    south_row = jnp.where(y_start == 0, row_low, own_rows[0])
+    north_row = jnp.where(y_start + SUB == y_cells, row_high, own_rows[1])
     cells = [centre[f * SUB : (f + 1) * SUB, :] for f in range(F)]
     viscosity = viscosity_of(cells, closure)
     changes = []
@@ -728,27 +739,27 @@
         ]
     ).astype(jnp.int32)
 
-    def pairs(along_x, step):
+    def pairs(x_step, even_step):
         found = []
         for g in range(sim_groups):
             for c in range(trainers):
                 gx, gy = c // y_devices, c % y_devices
-                if along_x:
-                    gx = (gx + step) % x_devices
-                else:
-                    gy = (gy + step) % y_devices
+                gx = (gx + x_step) % x_devices
+                gy = (gy + (even_step if gy % 2 == 0 else -even_step)) % y_devices
                 found.append((g * trainers + c, (g * x_devices + gx) * y_devices + gy))
         return found
 
     def x_neighbours(edges):
         if x_devices == 2:
-            return lax.ppermute(edges, everyone, pairs(True, 1))
-        from_high = lax.ppermute(edges[0], everyone, pairs(True, -1))
-        return jnp.stack([from_high, lax.ppermute(edges[1], everyone, pairs(True, 1))])
-
-    def y_neighbours(for_low, for_high):
-        from_low = lax.ppermute(for_high, everyone, pairs(False, 1))
-        return from_low, lax.ppermute(for_low, everyone, pairs(False, -1))
+            return lax.ppermute(edges, everyone, pairs(1, 0))
+        from_high = lax.ppermute(edges[0], everyone, pairs(-1, 0))
+        return jnp.stack([from_high, lax.ppermute(edges[1], everyone, pairs(1, 0))])
+
+    def y_neighbours(for_first, for_second):
+        return (
+            lax.ppermute(for_first, everyone, pairs(0, 1)),
+            lax.ppermute(for_second, everyone, pairs(0, -1)),
+        )
 
     def swap(distance):
         return [(first_trainer + c, first_trainer + (c ^ distance)) for c in range(trainers)]
@@ -772,10 +783,10 @@
             held = jnp.concatenate([held, lax.ppermute(held, everyone, swap(distance))], axis=0)
         return [held, lax.ppermute(held, everyone, swap(steps[-1]))]
 
-    *cube, faces, row_for_low, row_for_high, x_edges, y_edges = sample_cube(
+    *cube, faces, row_for_first, row_for_second, x_edges, y_edges = sample_cube(
         sample_block, place, brick
     )
-    thin_halo = (x_neighbours(faces), *y_neighbours(row_for_low, row_for_high))
+    thin_halo = (x_neighbours(faces), *y_neighbours(row_for_first, row_for_second))
     payload = cube_change(sample_block, place, closure, cube, thin_halo, y_cells, z_cells)
     landed = to_trainers(payload)
     x_edges, y_edges, landed = lax.optimization_barrier((x_edges, y_edges, landed))
@@ -796,7 +807,7 @@
         return delta, new_brick
 
     def evolve_here():
-        new_brick = evolve(closure, brick, *halo)
+        new_brick = evolve(closure, place, brick, *halo)
         return jnp.zeros((NPARAM,), jnp.float32), new_brick
 
     delta, new_brick = lax.cond(is_trainer, train_here, evolve_here)

time: 216 us -> 181 us (0.84)
  waiting for transfers between devices: 132 us -> 98.2 us
    ppermute x3, waiting for transfers between devices: 122 us -> 89.3 us  [on_device(): final = final + lax.ppermute(total, everyone, pairs)]
where the time goes in v4:
time: 181 us; the launch traced here: 180 us
  waiting for transfers between devices  98.2 us (54%)
  Pallas kernels  46.2 us (26%)
  starting transfers between devices  30.7 us (17%)
  other arithmetic  2.15 us (1%)
    ppermute x3, waiting for transfers between devices, on_device(): final = final + lax.ppermute(total, everyone, pairs)  89.3 us
    pallas_call x1, Pallas kernels, evolve(): pl.pallas_call(evolve_kernel, out_shape=jax.ShapeDtypeStruct(fields.shape...  39.9 us
    ppermute x2, starting transfers between devices, y_neighbours(): lax.ppermute(for_second, everyone, pairs(0, -1))  7.64 us
    ppermute x2, starting transfers between devices, y_neighbours(): lax.ppermute(for_first, everyone, pairs(0, 1))  6.86 us
    ppermute x2, starting transfers between devices, x_neighbours(): return lax.ppermute(edges, everyone, pairs(1, 0))  6.85 us
    pallas_call x1, Pallas kernels, sample_cube(): pl.pallas_call(functools.partial(sample_kernel, y_cells, z_cells), out_sh...  4.75 us
  transfers between devices with their start and end apart: 18, of which 5 were waited for; matrix products, arithmetic and copies ran while one was open for 0% of the time, Pallas kernels for 0%

profile of v4, /device:TPU:0, one launch (start us, length us, event | category | flops | bytes accessed | tf_op | source)
XLA Modules:
  0.0 180.0 jit_solution(12230923691300655958)
XLA Ops:
  0.6 0.0 copy-start.2
  0.6 0.1 stack.27.place
  0.7 0.7 copy-done.3
  1.4 4.8 %sample_cube.1 = (f32[80,256]{1,0:T(8,128)S(1)}, f32[80,256]{1,0:T(8,128)S(1)}, f32[80,256]{1,0:T(8,128)S(1)}, f32[2,16,128]{2,1,0:T(8,128)S(1)}, f32[2,8,256]{2...) custom-call(s32[24]{0:T(128)S(1)} %copy-done.3, ...), custom_call_target="tpu_custom_call" | custom-call | tf_op jit(solution)/shard_map/sample_cube/pallas_call | solution.py:621
  6.2 4.9 %collective-permute-start.1 = (f32[16,128]{1,0:T(8,128)S(1)}, f32[16,128]{1,0:T(8,128)S(1)}, u32[]{:S(2)}, u32[]{:S(2)}) collective-permute-start(f32[16,128]{1,0:T(8,128)S(1)} %get-tuple-element.73), channel_id=1, source_target_pairs={{0,1},{1,0},{2,3},{3,2},{4,5},{5,4},{6,7},{7,6},{8,9},{9,8},{10,11... | collective-permute-start | bytes 24584 | tf_op jit(solution)/shard_map/ppermute | solution.py:760
  11.1 4.4 %collective-permute-start.2 = (f32[16,128]{1,0:T(8,128)S(1)}, f32[16,128]{1,0:T(8,128)S(1)}, u32[]{:S(2)}, u32[]{:S(2)}) collective-permute-start(f32[16,128]{1,0:T(8,128)S(1)} %get-tuple-element.74), channel_id=1, source_target_pairs={{0,3},{1,2},{2,1},{3,0},{4,7},{5,6},{6,5},{7,4},{8,11},{9,10},{10,... | collective-permute-start | bytes 24584 | tf_op jit(solution)/shard_map/ppermute | solution.py:761
  15.5 3.4 %collective-permute-start = (f32[2,8,256]{2,1,0:T(8,128)S(1)}, f32[2,8,256]{2,1,0:T(8,128)S(1)}, u32[]{:S(2)}, u32[]{:S(2)}) collective-permute-start(f32[2,8,256]{2,1,0:T(8,128)S(1)} %get-tuple-element.72), channel_id=1, source_target_pairs={{0,4},{1,5},{2,6},{3,7},{4,0},{5,1},{6,2},{7,3},{8,12},{9,13},{10,... | collective-permute-start | bytes 49160 | tf_op jit(solution)/shard_map/ppermute | solution.py:754
  19.0 0.0 copy-done.5
  19.0 0.0 collective-permute-done.1.row_first
  19.0 0.0 collective-permute-done.2.row_second
  19.0 2.1 %collective-permute-done.face_halo = f32[2,8,256]{2,1,0:T(8,128)S(1)} collective-permute-done((f32[2,8,256]{2,1,0:T(8,128)S(1)}, f32[2,8,256]{2,1,0:T(8,128)S(1)}, u32[]{:S(2)}, u32[]{:S(2)}) %collective-permute-start) | collective-permute-done | bytes 16416 | tf_op jit(solution)/shard_map/ppermute | solution.py:754
  21.1 1.6 cube_change.1
  22.7 0.7 collective-permute-start.5
  23.4 0.7 collective-permute-start.4
  24.1 1.3 collective-permute-start.3
  25.4 0.0 collective-permute-done.5
  25.4 0.0 collective-permute-done.4
  25.4 2.0 %collective-permute-done.3 = bf16[160,256]{1,0:T(8,128)(2,1)S(1)} collective-permute-done((bf16[160,256]{1,0:T(8,128)(2,1)S(1)}, bf16[160,256]{1,0:T(8,128)(2,1)S(1)}, u32[]{:S(2)}, u32[]{:S(2)}) %collective-permute-start.3) | collective-permute-done | bytes 81952 | tf_op jit(solution)/shard_map/ppermute | solution.py:772
  27.5 0.7 collective-permute-start.9
  28.1 0.0 collective-permute-done.9
  28.2 0.7 collective-permute-start.10
  29.0 0.0 collective-permute-done.10
  29.0 0.7 collective-permute-start.11
  29.7 3.4 %collective-permute-start.6 = (f32[2,5,32,384]{3,2,1,0:T(8,128)S(1)}, f32[2,5,32,384]{3,2,1,0:T(8,128)S(1)}, u32[]{:S(2)}, u32[]{:S(2)}) collective-permute-start(f32[2,5,32,384]{3,2,1,0:T(8,128)S(1)} %get-tuple-element.75), channel_id=1, source_target_pairs={{0,4},{1,5},{2,6},{3,7},{4,0},{5,1},{6,2},{7,3},{8,12},{9,13},{10,... | collective-permute-start | bytes 1474568 | tf_op jit(solution)/shard_map/ppermute | solution.py:754
  33.2 3.3 %collective-permute-start.8 = (f32[5,16,384]{2,1,0:T(8,128)S(1)}, f32[5,16,384]{2,1,0:T(8,128)S(1)}, u32[]{:S(2)}, u32[]{:S(2)}) collective-permute-start(f32[5,16,384]{2,1,0:T(8,128)S(1)} %get-tuple-element.124), channel_id=1, source_target_pairs={{0,3},{1,2},{2,1},{3,0},{4,7},{5,6},{6,5},{7,4},{8,11},{9,10},{10,... | collective-permute-start | bytes 368648 | tf_op jit(solution)/shard_map/ppermute | solution.py:761
  36.5 1.9 %collective-permute-start.7 = (f32[5,16,384]{2,1,0:T(8,128)S(1)}, f32[5,16,384]{2,1,0:T(8,128)S(1)}, u32[]{:S(2)}, u32[]{:S(2)}) collective-permute-start(f32[5,16,384]{2,1,0:T(8,128)S(1)} %get-tuple-element.125), channel_id=1, source_target_pairs={{0,1},{1,0},{2,3},{3,2},{4,5},{5,4},{6,7},{7,6},{8,9},{9,8},{10,11... | collective-permute-start | bytes 368648 | tf_op jit(solution)/shard_map/ppermute | solution.py:760
  38.4 0.1 slice.40
  38.5 0.1 reshape.33
  38.6 3.2 %collective-permute-done.8 = f32[5,16,384]{2,1,0:T(8,128)S(1)} collective-permute-done((f32[5,16,384]{2,1,0:T(8,128)S(1)}, f32[5,16,384]{2,1,0:T(8,128)S(1)}, u32[]{:S(2)}, u32[]{:S(2)}) %collective-permute-start.8) | collective-permute-done | bytes 122912 | tf_op jit(solution)/shard_map/ppermute | solution.py:761
  41.8 1.5 collective-permute-done.7
  43.2 0.0 collective-permute-done.6
  43.2 0.0 collective-permute-done.11
  43.2 39.9 %conditional.1 = (f32[17280]{0:T(1024)S(1)}, f32[1,5,16,32,384]{4,3,2,1,0:T(8,128)}) conditional(s32[]{:T(128)} %convert_element_type.6, (f32[7,64]{1,0:T(8,128)S(1)}, s32[6]{0:T(128)S(1)}, f32[5,16,32,384]{3,2,1,0:T(8,128)}, f32[2,5,32,384]{3,2,1,0:T(8,128)S(1)}, f32[5,16,384]{2,1,0:T(8,128)S(1)}, ...), branch_computations={%region_0.1_spmd, %region_1.2_spmd.clone} | conditional | flops 17280 | bytes 4754512 | solution.py:813
  43.2 39.9 %evolve_brick.1 = f32[5,16,32,384]{3,2,1,0:T(8,128)} custom-call(f32[7,64]{1,0:T(8,128)S(1)} %get-tuple-element.31.closure, s32[6]{0:T(128)S(1)} %get-tuple-element.32.place, f32[5,16,32,384]{3,2,1,0:T(8,128)} %get-tuple-element.33.fields, f32[2,5,32,384]{3,2,1,0:T(8,128)S(1)} %get-tuple-element.34.x_halo, f32[5,16,384]{2,1,0:T(8,128)S(1)} %get-tuple-element.35.y_first, ...), custom_call_target="tpu_custom_call" | custom-call | tf_op jit(solution)/shard_map/cond/branch_0_fun/evolve_brick/pallas_call | solution.py:481
  83.1 0.7 collective-permute-start.12
  83.8 0.0 collective-permute-done.12
  83.8 0.7 collective-permute-start.13
  84.5 0.0 collective-permute-done.13
  84.5 0.7 collective-permute-start.14
  85.2 0.0 collective-permute-done.14
  85.2 0.7 collective-permute-start.17
  85.9 0.7 collective-permute-start.16
  86.6 1.3 collective-permute-start.15
  87.9 0.0 collective-permute-done.17
  87.9 0.0 collective-permute-done.16
  87.9 89.3 %collective-permute-done.15 = f32[17280]{0:T(1024)S(1)} collective-permute-done((f32[17280]{0:T(1024)S(1)}, f32[17280]{0:T(1024)S(1)}, u32[]{:S(2)}, u32[]{:S(2)}) %collective-permute-start.15) | collective-permute-done | bytes 69152 | tf_op jit(solution)/shard_map/ppermute | solution.py:821
  177.3 0.6 multiply_reduce_fusion
  178.6 1.4 multiply_subtract_fusion
  (22 shorter events, 0.2 us)
Async XLA Ops:
  0.6 20.5 %copy-start.2 = (bf16[256,256]{1,0:T(8,128)(2,1)S(1)}, bf16[256,256]{1,0:T(8,128)(2,1)}, u32[]{:S(2)}) copy-start(bf16[256,256]{1,0:T(8,128)(2,1)} %constant.54.clone.order) | copy-start | bytes 393220
  0.7 0.7 copy-start.3
  1.4 17.5 %copy-start.7 = (f32[64]{0:T(128)S(1)}, f32[64]{0:T(128)}, u32[]{:S(2)}) copy-start(f32[64]{0:T(128)} %param.15) | copy-start | bytes 772
  1.4 17.6 %copy-start.5 = (f32[64,5]{0,1:T(8,128)S(1)}, f32[64,5]{0,1:T(8,128)}, u32[]{:S(2)}) copy-start(f32[64,5]{0,1:T(8,128)} %param.14) | copy-start | bytes 3844
  1.4 17.6 %copy-start.6 = (f32[64]{0:T(128)S(1)}, f32[64]{0:T(128)}, u32[]{:S(2)}) copy-start(f32[64]{0:T(128)} %param.16) | copy-start | bytes 772
  1.4 37.0 %copy-start.4 = (f32[17280]{0:T(1024)S(1)}, f32[17280]{0:T(1024)}, u32[]{:S(2)}) copy-start(f32[17280]{0:T(1024)} %param.17) | copy-start | bytes 207364
  6.2 12.8 %collective-permute-start.1 = (f32[16,128]{1,0:T(8,128)S(1)}, f32[16,128]{1,0:T(8,128)S(1)}, u32[]{:S(2)}, u32[]{:S(2)}) collective-permute-start(f32[16,128]{1,0:T(8,128)S(1)} %get-tuple-element.73), channel_id=1, source_target_pairs={{0,1},{1,0},{2,3},{3,2},{4,5},{5,4},{6,7},{7,6},{8,9},{9,8},{10,11... | collective-permute-start | bytes 24584 | tf_op jit(solution)/shard_map/ppermute | solution.py:760
  11.1 7.9 %collective-permute-start.2 = (f32[16,128]{1,0:T(8,128)S(1)}, f32[16,128]{1,0:T(8,128)S(1)}, u32[]{:S(2)}, u32[]{:S(2)}) collective-permute-start(f32[16,128]{1,0:T(8,128)S(1)} %get-tuple-element.74), channel_id=1, source_target_pairs={{0,3},{1,2},{2,1},{3,0},{4,7},{5,6},{6,5},{7,4},{8,11},{9,10},{10,... | collective-permute-start | bytes 24584 | tf_op jit(solution)/shard_map/ppermute | solution.py:761
  15.5 5.6 %collective-permute-start = (f32[2,8,256]{2,1,0:T(8,128)S(1)}, f32[2,8,256]{2,1,0:T(8,128)S(1)}, u32[]{:S(2)}, u32[]{:S(2)}) collective-permute-start(f32[2,8,256]{2,1,0:T(8,128)S(1)} %get-tuple-element.72), channel_id=1, source_target_pairs={{0,4},{1,5},{2,6},{3,7},{4,0},{5,1},{6,2},{7,3},{8,12},{9,13},{10,... | collective-permute-start | bytes 49160 | tf_op jit(solution)/shard_map/ppermute | solution.py:754
  22.7 2.7 %collective-permute-start.5 = (bf16[160,256]{1,0:T(8,128)(2,1)S(1)}, bf16[160,256]{1,0:T(8,128)(2,1)S(1)}, u32[]{:S(2)}, u32[]{:S(2)}) collective-permute-start(bf16[160,256]{1,0:T(8,128)(2,1)S(1)} %cube_change.1), channel_id=1, source_target_pairs={{16,24},{17,25},{18,26},{19,27},{20,28},{21,29},{22,30},{23,31}} | collective-permute-start | bytes 245768 | tf_op jit(solution)/shard_map/ppermute | solution.py:772
  23.4 2.0 %collective-permute-start.4 = (bf16[160,256]{1,0:T(8,128)(2,1)S(1)}, bf16[160,256]{1,0:T(8,128)(2,1)S(1)}, u32[]{:S(2)}, u32[]{:S(2)}) collective-permute-start(bf16[160,256]{1,0:T(8,128)(2,1)S(1)} %cube_change.1), channel_id=1, source_target_pairs={{8,24},{9,25},{10,26},{11,27},{12,28},{13,29},{14,30},{15,31}} | collective-permute-start | bytes 245768 | tf_op jit(solution)/shard_map/ppermute | solution.py:772
  24.1 3.3 %collective-permute-start.3 = (bf16[160,256]{1,0:T(8,128)(2,1)S(1)}, bf16[160,256]{1,0:T(8,128)(2,1)S(1)}, u32[]{:S(2)}, u32[]{:S(2)}) collective-permute-start(bf16[160,256]{1,0:T(8,128)(2,1)S(1)} %cube_change.1), channel_id=1, source_target_pairs={{0,24},{1,25},{2,26},{3,27},{4,28},{5,29},{6,30},{7,31}} | collective-permute-start | bytes 245768 | tf_op jit(solution)/shard_map/ppermute | solution.py:772
  27.5 0.7 collective-permute-start.9
  28.2 0.8 collective-permute-start.10
  29.0 14.2 %collective-permute-start.11 = (bf16[12,160,256]{2,1,0:T(8,128)(2,1)S(1)}, bf16[12,160,256]{2,1,0:T(8,128)(2,1)S(1)}, u32[]{:S(2)}, u32[]{:S(2)}) collective-permute-start(bf16[12,160,256]{2,1,0:T(8,128)(2,1)S(1)} %constant_dynamic-update-slice_fusion), channel_id=1, source_target_pairs={{24,28},{25,29},{26,30},{27,31},{28,24},{29,25},{30,26},{31,27}} | collective-permute-start | bytes 2949128 | tf_op jit(solution)/shard_map/ppermute | solution.py:784
  29.7 13.5 %collective-permute-start.6 = (f32[2,5,32,384]{3,2,1,0:T(8,128)S(1)}, f32[2,5,32,384]{3,2,1,0:T(8,128)S(1)}, u32[]{:S(2)}, u32[]{:S(2)}) collective-permute-start(f32[2,5,32,384]{3,2,1,0:T(8,128)S(1)} %get-tuple-element.75), channel_id=1, source_target_pairs={{0,4},{1,5},{2,6},{3,7},{4,0},{5,1},{6,2},{7,3},{8,12},{9,13},{10,... | collective-permute-start | bytes 1474568 | tf_op jit(solution)/shard_map/ppermute | solution.py:754
  33.2 8.6 %collective-permute-start.8 = (f32[5,16,384]{2,1,0:T(8,128)S(1)}, f32[5,16,384]{2,1,0:T(8,128)S(1)}, u32[]{:S(2)}, u32[]{:S(2)}) collective-permute-start(f32[5,16,384]{2,1,0:T(8,128)S(1)} %get-tuple-element.124), channel_id=1, source_target_pairs={{0,3},{1,2},{2,1},{3,0},{4,7},{5,6},{6,5},{7,4},{8,11},{9,10},{10,... | collective-permute-start | bytes 368648 | tf_op jit(solution)/shard_map/ppermute | solution.py:761
  36.5 6.8 %collective-permute-start.7 = (f32[5,16,384]{2,1,0:T(8,128)S(1)}, f32[5,16,384]{2,1,0:T(8,128)S(1)}, u32[]{:S(2)}, u32[]{:S(2)}) collective-permute-start(f32[5,16,384]{2,1,0:T(8,128)S(1)} %get-tuple-element.125), channel_id=1, source_target_pairs={{0,1},{1,0},{2,3},{3,2},{4,5},{5,4},{6,7},{7,6},{8,9},{9,8},{10,11... | collective-permute-start | bytes 368648 | tf_op jit(solution)/shard_map/ppermute | solution.py:760
  83.1 0.7 collective-permute-start.12
  83.8 0.7 collective-permute-start.13
  84.5 0.7 collective-permute-start.14
  85.2 2.7 %collective-permute-start.17 = (f32[17280]{0:T(1024)S(1)}, f32[17280]{0:T(1024)S(1)}, u32[]{:S(2)}, u32[]{:S(2)}) collective-permute-start(f32[17280]{0:T(1024)S(1)} %add.44), channel_id=1, source_target_pairs={{24,16},{25,17},{26,18},{27,19},{28,20},{29,21},{30,22},{31,23}} | collective-permute-start | bytes 207368 | tf_op jit(solution)/shard_map/ppermute | solution.py:821
  85.9 2.0 %collective-permute-start.16 = (f32[17280]{0:T(1024)S(1)}, f32[17280]{0:T(1024)S(1)}, u32[]{:S(2)}, u32[]{:S(2)}) collective-permute-start(f32[17280]{0:T(1024)S(1)} %add.44), channel_id=1, source_target_pairs={{24,8},{25,9},{26,10},{27,11},{28,12},{29,13},{30,14},{31,15}} | collective-permute-start | bytes 207368 | tf_op jit(solution)/shard_map/ppermute | solution.py:821
  86.6 90.7 %collective-permute-start.15 = (f32[17280]{0:T(1024)S(1)}, f32[17280]{0:T(1024)S(1)}, u32[]{:S(2)}, u32[]{:S(2)}) collective-permute-start(f32[17280]{0:T(1024)S(1)} %add.44), channel_id=1, source_target_pairs={{24,0},{25,1},{26,2},{27,3},{28,4},{29,5},{30,6},{31,7}} | collective-permute-start | bytes 207368 | tf_op jit(solution)/shard_map/ppermute | solution.py:821

commit v5 on v4

--- a/solution.py
+++ b/solution.py
@@ -115,7 +115,7 @@
 
 
 def train_kernel(steps, *refs):
-    (trainer_of, place, first_ref, last_ref, select_first, select_last) = refs[:6]
+    (trainer_of, place, first_ref, last_ref, far_first, far_last) = refs[:6]
     arrived = refs[6:8]
     fields_ref = refs[8]
     delta_first, delta_last, new_fields_ref = refs[9:12]
@@ -133,19 +133,22 @@
         big_first,
         big_last,
         big_last_t,
-        raw,
-        grad_first,
-        grad_last,
         now_first,
         now_last,
         brick,
+        select_first,
+        select_last,
         slot_sems,
         field_sem,
+        select_sems,
     ) = refs[12:]
 
     field_in = pltpu.make_async_copy(fields_ref, brick, field_sem)
     field_out = pltpu.make_async_copy(brick, new_fields_ref, field_sem)
-    field_in.start()
+    select_copies = [
+        pltpu.make_async_copy(far_first, select_first, select_sems.at[0]),
+        pltpu.make_async_copy(far_last, select_last, select_sems.at[1]),
+    ]
 
     groups = place[3]
     trainers = trainer_of.shape[0] // groups
@@ -179,6 +182,11 @@
 
     for slot in range(TCAP):
         fetch(slot, False)
+
+    for copy in select_copies:
+        copy.start()
+    field_in.start()
+    for slot in range(TCAP):
 
         @pl.when(slot >= count)
         def _():
@@ -238,6 +246,8 @@
 
         lax.fori_loop(0, SUB, stack_plane, 0, unroll=8)
 
+    for copy in select_copies:
+        copy.wait()
     field_in.wait()
     field_out.start()
 
@@ -252,38 +262,18 @@
         def tile_of(index):
             return index // 8, pl.ds(pl.multiple_of((index % 8) * 256 + 128, 128), 256)
 
-        def first_layer(index):
+        def forward(index, carry):
             pair, columns = tile_of(index)
-            raw[index % 2] = dot_rows(big_first[...], inputs[pair, :, columns])
-
-        def activate(index):
-            pair, columns = tile_of(index)
-            for part in range(8):
-                rows = slice(part * 32, (part + 1) * 32)
-                half = 0.5 * raw[index % 2, rows, :]
-                curve = jnp.tanh(half)
-                value = half + half * curve
-                hiddens[pair, rows, columns] = value.astype(jnp.bfloat16)
-                slopes[pair, rows, columns] = (0.5 + 0.5 * curve) + value * (0.5 - 0.5 * curve)
-
-        def last_layer(index):
-            pair, columns = tile_of(index)
-            partial_out[pair, :, columns] = dot_rows(big_last_t[...], hiddens[pair, :, columns])
-
-        def forward(index, carry):
-            last_layer(index - 2)
-            activate(index - 1)
-            first_layer(index)
+            half = 0.5 * dot_rows(big_first[...], inputs[pair, :, columns])
+            curve = jnp.tanh(half)
+            value = half + half * curve
+            hidden = value.astype(jnp.bfloat16)
+            hiddens[pair, :, columns] = hidden
+            slopes[pair, :, columns] = (0.5 + 0.5 * curve) + value * (0.5 - 0.5 * curve)
+            partial_out[pair, :, columns] = dot_rows(big_last_t[...], hidden)
             return carry
 
-        tiles = 8 * PAIRS
-        first_layer(0)
-        activate(0)
-        first_layer(1)
-        lax.fori_loop(2, tiles, forward, 0)
-        last_layer(tiles - 2)
-        activate(tiles - 1)
-        last_layer(tiles - 1)
+        lax.fori_loop(0, 8 * PAIRS, forward, 0, unroll=8)
 
         def error_plane(index, carry):
             pair = index // SUB
@@ -310,38 +300,19 @@
 
         lax.fori_loop(0, SUB * PAIRS, error_plane, 0, unroll=8)
 
-        grad_first[...] = jnp.zeros(grad_first.shape, jnp.float32)
-        grad_last[...] = jnp.zeros(grad_last.shape, jnp.float32)
-
-        def hidden_layer(index):
+        def backward(index, carry):
             pair, columns = tile_of(index)
-            raw[index % 2] = dot_rows(big_last[...], errors[pair, :, columns])
-
-        def scale(index):
-            pair, columns = tile_of(index)
-            for part in range(8):
-                rows = slice(part * 32, (part + 1) * 32)
-                product = raw[index % 2, rows, :] * slopes[pair, rows, columns]
-                pre_grads[pair, rows, columns] = product.astype(jnp.bfloat16)
-
-        def gradients(index):
-            pair, columns = tile_of(index)
-            grad_first[...] += dot_lanes(pre_grads[pair, :, columns], inputs[pair, :, columns])
-            grad_last[...] += dot_lanes(hiddens[pair, :, columns], errors[pair, :, columns])
-
-        def backward(index, carry):
-            gradients(index - 2)
-            scale(index - 1)
-            hidden_layer(index)
+            hidden_grad = dot_rows(big_last[...], errors[pair, :, columns])
+            pre_grads[pair, :, columns] = (hidden_grad * slopes[pair, :, columns]).astype(jnp.bfloat16)
             return carry
 
-        hidden_layer(0)
-        scale(0)
-        hidden_layer(1)
-        lax.fori_loop(2, tiles, backward, 0)
-        gradients(tiles - 2)
-        scale(tiles - 1)
-        gradients(tiles - 1)
+        lax.fori_loop(0, 8 * PAIRS, backward, 0, unroll=8)
+        body = slice(128, COLS - 128)
+        grad_first = jnp.zeros((4 * CH, STACK), jnp.float32)
+        grad_last = jnp.zeros((4 * CH, STACK), jnp.float32)
+        for pair in range(PAIRS):
+            grad_first += dot_lanes(pre_grads[pair, :, body], inputs[pair, :, body])
+            grad_last += dot_lanes(hiddens[pair, :, body], errors[pair, :, body])
 
         def folded(grad, select_ref):
             total = jnp.zeros((3 * CH, 256), jnp.float32)
@@ -380,7 +351,7 @@
             jax.ShapeDtypeStruct((CH, 256), jnp.float32),
             jax.ShapeDtypeStruct(fields.shape, fields.dtype),
         ),
-        in_specs=[smem] * 2 + [vmem] * 4 + [anywhere] * 2 + [hbm],
+        in_specs=[smem] * 2 + [vmem] * 2 + [hbm] * 2 + [anywhere] * 2 + [hbm],
         out_specs=(vmem, vmem, hbm),
         scratch_shapes=[
             pltpu.SMEM((2, TCAP), jnp.int32),
@@ -396,14 +367,14 @@
             pltpu.VMEM((4 * CH, STACK), jnp.bfloat16),
             pltpu.VMEM((4 * CH, STACK), jnp.bfloat16),
             pltpu.VMEM((STACK, 4 * CH), jnp.bfloat16),
-            pltpu.VMEM((2, 4 * CH, 256), jnp.float32),
-            pltpu.VMEM((4 * CH, STACK), jnp.float32),
-            pltpu.VMEM((4 * CH, STACK), jnp.float32),
             pltpu.VMEM((CH, 256), jnp.float32),
             pltpu.VMEM((CH, 256), jnp.float32),
             pltpu.VMEM(fields.shape, fields.dtype),
+            pltpu.VMEM((4, 256, STACK), jnp.bfloat16),
+            pltpu.VMEM((4, 256, STACK), jnp.bfloat16),
             pltpu.SemaphoreType.DMA((TCAP,)),
             pltpu.SemaphoreType.DMA,
+            pltpu.SemaphoreType.DMA((2,)),
         ],
         compiler_params=pltpu.CompilerParams(vmem_limit_bytes=48 * 1024 * 1024),
         name="train_cubes",
@@ -509,6 +480,12 @@
     return lax.rem(lax.div(block, z_blocks), y_cells // SUB) * SUB, lax.rem(block, z_blocks) * SUB
 
 
+def column_of(place, x_step, y_step):
+    gx = lax.rem(place[1] + x_step + place[5], place[5])
+    gy = lax.rem(place[2] + y_step + place[4], place[4])
+    return gx * place[4] + gy
+
+
 def sample_kernel(
     y_cells,
     z_cells,
@@ -519,9 +496,7 @@
     lower,
     upper,
     own_rows,
-    faces,
-    row_for_first,
-    row_for_second,
+    thin,
     x_edges,
     y_edges,
     windows,
@@ -580,21 +555,21 @@
 
     own_rows[0] = y_row(jnp.maximum(y_start - 1, 0), z_start)
     own_rows[1] = y_row(jnp.minimum(y_start + SUB, y_cells - 1), z_start)
-    up_first = lax.rem(place[2], 2) == 0
-    z_first = corner(0, jnp.where(up_first, 1, -1))[1]
-    z_second = corner(0, jnp.where(up_first, -1, 1))[1]
-    row_for_first[...] = y_row(jnp.where(up_first, y_cells - 1, 0), z_first)
-    row_for_second[...] = y_row(jnp.where(up_first, 0, y_cells - 1), z_second)
+    thin[...] = jnp.zeros(thin.shape, thin.dtype)
+    thin[column_of(place, 0, -1), :, :128] = y_row(0, corner(0, -1)[1])
+    thin[column_of(place, 0, 1), :, 128:] = y_row(y_cells - 1, corner(0, 1)[1])
     lane = lane[:8]
-    for face, (x, step) in enumerate(((0, -1), (SUB - 1, 1))):
-        y_there, z_there = corner(step, 0)
+    for face, (x, sign) in enumerate(((0, -1), (SUB - 1, 1))):
+        y_there, z_there = corner(sign, 0)
         for half in range(2):
             total = jnp.zeros((8, 128), jnp.float32)
             for step in range(8):
                 row = x * rows_of_x + y_there + half * 8 + step
                 part = piece(row, 8, rows_of_field, z_there, step * SUB)
                 total = jnp.where(lane // SUB == step, part, total)
-            faces[face, :, half * 128 : (half + 1) * 128] = total
+            at = (column_of(place, sign, 0), slice(face * 8, face * 8 + 8), slice(half * 128, half * 128 + 128))
+            thin[at] = total
+    up_first = lax.rem(place[2], 2) == 0
     for side in range(2):
         y = jnp.where(up_first == (side == 0), y_cells - 1, 0)
         for field in range(F):
@@ -610,14 +585,13 @@
                 x_edges[side, field, :, w * 128 : (w + 1) * 128] = windows[pl.ds(start, rows_of_x), :]
 
 
-def sample_cube(sample_block, place, brick):
+def sample_cube(sample_block, place, brick, columns):
     fields, x_cells, y_cells, z_cells = brick.shape
     vmem = pl.BlockSpec(memory_space=pltpu.VMEM)
     smem = pl.BlockSpec(memory_space=pltpu.SMEM)
     hbm = pl.BlockSpec(memory_space=pltpu.HBM)
     rows = fields * x_cells * y_cells
     cube = jax.ShapeDtypeStruct((F * SUB, 256), jnp.float32)
-    line = jax.ShapeDtypeStruct((SUB, 128), jnp.float32)
     return pl.pallas_call(
         functools.partial(sample_kernel, y_cells, z_cells),
         out_shape=(
@@ -625,14 +599,12 @@
             cube,
             cube,
             jax.ShapeDtypeStruct((2, SUB, 128), jnp.float32),
-            jax.ShapeDtypeStruct((2, 8, 256), jnp.float32),
-            line,
-            line,
+            jax.ShapeDtypeStruct((columns, SUB, 256), jnp.float32),
             jax.ShapeDtypeStruct((2, fields, y_cells, z_cells), jnp.float32),
             jax.ShapeDtypeStruct((2, fields, x_cells, z_cells), jnp.float32),
         ),
         in_specs=[smem, smem, hbm],
-        out_specs=(vmem,) * 9,
+        out_specs=(vmem,) * 7,
         scratch_shapes=[
             pltpu.VMEM((z_cells // 128 * rows + 4 * x_cells * y_cells, 128), jnp.float32),
             pltpu.SemaphoreType.DMA((z_cells // 128,)),
@@ -653,26 +625,23 @@
     lower,
     upper,
     own_rows,
-    face_halo,
-    row_first,
-    row_second,
+    thin,
     payload,
 ):
     y_start = corner_of(sample_block, place, 0, 0, y_cells, z_cells)[0]
     row = lax.broadcasted_iota(jnp.int32, (SUB, 256), 0)
     lane = lax.broadcasted_iota(jnp.int32, (SUB, 256), 1)
-    up_first = lax.rem(place[2], 2) == 0
-    row_low = jnp.where(up_first, row_second[...], row_first[...])
-    row_high = jnp.where(up_first, row_first[...], row_second[...])
-    south_row = jnp.where(y_start == 0, row_low, own_rows[0])
-    north_row = jnp.where(y_start + SUB == y_cells, row_high, own_rows[1])
+    south_row = jnp.where(y_start == 0, thin[column_of(place, 0, -1), :, 128:], own_rows[0])
+    north_row = jnp.where(y_start + SUB == y_cells, thin[column_of(place, 0, 1), :, :128], own_rows[1])
+    face_low = thin[column_of(place, -1, 0), 8:, :]
+    face_high = thin[column_of(place, 1, 0), :8, :]
     cells = [centre[f * SUB : (f + 1) * SUB, :] for f in range(F)]
     viscosity = viscosity_of(cells, closure)
     changes = []
     for f in range(F):
         value = cells[f]
-        west = jnp.where(row == 0, face_halo[1, f : f + 1, :], pltpu.roll(value, 1, 0))
-        east = jnp.where(row == SUB - 1, face_halo[0, f : f + 1, :], pltpu.roll(value, SUB - 1, 0))
+        west = jnp.where(row == 0, face_low[f : f + 1, :], pltpu.roll(value, 1, 0))
+        east = jnp.where(row == SUB - 1, face_high[f : f + 1, :], pltpu.roll(value, SUB - 1, 0))
         edge = pltpu.roll(south_row, (128 - f * SUB) % 128, 1)
         south = jnp.where(lane < SUB, jnp.concatenate([edge, edge], 1), pltpu.roll(value, SUB, 1))
         edge = pltpu.roll(north_row, 112 - f * SUB, 1)
@@ -691,17 +660,17 @@
     payload[...] = dot_rows(both, order[...]).astype(jnp.bfloat16)
 
 
-def cube_change(sample_block, place, closure, cube, halo, y_cells, z_cells):
+def cube_change(sample_block, place, closure, cube, thin, y_cells, z_cells):
     vmem = pl.BlockSpec(memory_space=pltpu.VMEM)
     smem = pl.BlockSpec(memory_space=pltpu.SMEM)
     return pl.pallas_call(
         functools.partial(change_kernel, y_cells, z_cells),
         out_shape=jax.ShapeDtypeStruct((2 * F * SUB, 256), jnp.bfloat16),
-        in_specs=[smem] * 3 + [vmem] * 8,
+        in_specs=[smem] * 3 + [vmem] * 6,
         out_specs=vmem,
         compiler_params=pltpu.CompilerParams(vmem_limit_bytes=16 * 1024 * 1024),
         name="cube_change",
-    )(sample_block, place, closure, jnp.asarray(CELL_ORDER, jnp.bfloat16), *cube, *halo)
+    )(sample_block, place, closure, jnp.asarray(CELL_ORDER, jnp.bfloat16), *cube, thin)
 
 
 def doubling_steps(x_devices, y_devices):
@@ -783,11 +752,9 @@
             held = jnp.concatenate([held, lax.ppermute(held, everyone, swap(distance))], axis=0)
         return [held, lax.ppermute(held, everyone, swap(steps[-1]))]
 
-    *cube, faces, row_for_first, row_for_second, x_edges, y_edges = sample_cube(
-        sample_block, place, brick
-    )
-    thin_halo = (x_neighbours(faces), *y_neighbours(row_for_first, row_for_second))
-    payload = cube_change(sample_block, place, closure, cube, thin_halo, y_cells, z_cells)
+    *cube, thin, x_edges, y_edges = sample_cube(sample_block, place, brick, trainers)
+    thin = lax.all_to_all(thin, ("gx", "gy"), split_axis=0, concat_axis=0, tiled=True)
+    payload = cube_change(sample_block, place, closure, cube, thin, y_cells, z_cells)
     landed = to_trainers(payload)
     x_edges, y_edges, landed = lax.optimization_barrier((x_edges, y_edges, landed))
     halo = (x_neighbours(x_edges), *y_neighbours(y_edges[0], y_edges[1]))
@@ -796,6 +763,8 @@
     first_count = CH * TAPS * F
     first = jnp.pad(master[:first_count].reshape(CH, TAPS * F), ((0, 0), (0, 256 - TAPS * F)))
     last = jnp.pad(master[first_count:].reshape(TAPS * F, CH).T, ((0, 0), (0, 256 - TAPS * F)))
+
+    first, last = lax.optimization_barrier((first, last))
 
     def train_here():
         delta_first, delta_last, new_brick = train_cubes(

time: 181 us -> 174 us (0.961)
  starting transfers between devices: 30.7 us -> 25.2 us
  waiting for transfers between devices: 98.2 us -> 95.4 us
    ppermute x3, waiting for transfers between devices: 89.3 us -> 80.7 us  [on_device(): final = final + lax.ppermute(total, everyone, pairs)]
    all_to_all x0 -> x1, waiting for transfers between devices: none -> 7.45 us  [on_device(): lax.all_to_all(thin, ('gx', 'gy'), split_axis=0, concat_axis=0, tiled=True)]
    all_to_all x0 -> x1, starting transfers between devices: none -> 7.3 us  [on_device(): lax.all_to_all(thin, ('gx', 'gy'), split_axis=0, concat_axis=0, tiled=True)]
    ppermute x2 -> x1, starting transfers between devices: 7.64 us -> 2.68 us  [y_neighbours(): lax.ppermute(for_second, everyone, pairs(0, -1))]
    ppermute x2 -> x1, starting transfers between devices: 6.86 us -> 1.94 us  [y_neighbours(): lax.ppermute(for_first, everyone, pairs(0, 1))]
    ppermute x2 -> x1, starting transfers between devices: 6.85 us -> 2.47 us  [x_neighbours(): return lax.ppermute(edges, everyone, pairs(1, 0))]
    ppermute x2 -> x1, waiting for transfers between devices: 2.11 us -> 0.01 us  [x_neighbours(): return lax.ppermute(edges, everyone, pairs(1, 0))]
    ppermute x2 -> x1, waiting for transfers between devices: 3.21 us -> 3.93 us  [y_neighbours(): lax.ppermute(for_second, everyone, pairs(0, -1))]
  transfers between devices with their start and end apart: 18 -> 16, of which waited for: 5 -> 5; matrix products, arithmetic and copies ran while one was open for 0% -> 1% of each run, Pallas kernels for 0% -> 0%
where the time goes in v5:
time: 174 us; the launch traced here: 173 us
  waiting for transfers between devices  95.4 us (55%)
  Pallas kernels  46.6 us (27%)
  starting transfers between devices  25.2 us (14%)
  other arithmetic  2.14 us (1%)
  local copies, waits for them, and re-layouts  1.9 us (1%)
    ppermute x3, waiting for transfers between devices, on_device(): final = final + lax.ppermute(total, everyone, pairs)  80.7 us
    pallas_call x1, Pallas kernels, evolve(): pl.pallas_call(evolve_kernel, out_shape=jax.ShapeDtypeStruct(fields.shape...  39.6 us
    all_to_all x1, waiting for transfers between devices, on_device(): lax.all_to_all(thin, ('gx', 'gy'), split_axis=0, concat_axis=0, tiled=True)  7.45 us
    all_to_all x1, starting transfers between devices, on_device(): lax.all_to_all(thin, ('gx', 'gy'), split_axis=0, concat_axis=0, tiled=True)  7.3 us
    pallas_call x1, Pallas kernels, sample_cube(): pl.pallas_call(functools.partial(sample_kernel, y_cells, z_cells), out_sh...  5.4 us
    ppermute x3, starting transfers between devices, to_trainers(): lax.ppermute(payload, everyone, [(g * trainers + c, first_trainer + c) fo...  4.05 us
    ppermute x1, waiting for transfers between devices, y_neighbours(): lax.ppermute(for_second, everyone, pairs(0, -1))  3.93 us
  transfers between devices with their start and end apart: 16, of which 5 were waited for; matrix products, arithmetic and copies ran while one was open for 1% of the time, Pallas kernels for 0%

profile of v5, /device:TPU:0, one launch (start us, length us, event | category | flops | bytes accessed | tf_op | source)
XLA Modules:
  0.0 172.9 jit_solution(8023774345469462493)
XLA Ops:
  0.6 0.0 copy-start.2
  0.6 0.1 stack.27.place
  0.7 0.7 copy-done.3
  1.4 0.0 copy-start.5
  1.4 0.0 copy-start.8
  1.4 5.4 %sample_cube.1 = (f32[80,256]{1,0:T(8,128)S(1)}, f32[80,256]{1,0:T(8,128)S(1)}, f32[80,256]{1,0:T(8,128)S(1)}, f32[2,16,128]{2,1,0:T(8,128)S(1)}, f32[8,16,256]{...) custom-call(s32[24]{0:T(128)S(1)} %copy-done.3, s32[6]{0:T(128)S(1)} %stack.27.place, ...), custom_call_target="tpu_custom_call" | custom-call | tf_op jit(solution)/shard_map/sample_cube/pallas_call | solution.py:595
  6.8 7.3 %all-to-all-start = ((f32[8,16,256]{2,1,0:T(8,128)}), f32[8,16,256]{2,1,0:T(8,128)S(1)}, u32[]{:S(2)}, u32[]{:S(2)}) async-start(f32[8,16,256]{2,1,0:T(8,128)} %get-tuple-element.72), calls=%async_computation | async-start | bytes 262144 | tf_op jit(solution)/shard_map/all_to_all | solution.py:756
  14.2 0.0 copy-done.7
  14.2 7.5 %all-to-all-done.thin = f32[8,16,256]{2,1,0:T(8,128)S(1)} async-done(((f32[8,16,256]{2,1,0:T(8,128)}), f32[8,16,256]{2,1,0:T(8,128)S(1)}, u32[]{:S(2)}, u32[]{:S(2)}) %all-to-all-start) | async-done | bytes 131104 | tf_op jit(solution)/shard_map/all_to_all | solution.py:756
  21.7 1.6 cube_change.1
  23.3 0.7 collective-permute-start.2
  23.9 0.7 collective-permute-start.1
  24.6 2.7 %collective-permute-start = (bf16[160,256]{1,0:T(8,128)(2,1)S(1)}, bf16[160,256]{1,0:T(8,128)(2,1)S(1)}, u32[]{:S(2)}, u32[]{:S(2)}) collective-permute-start(bf16[160,256]{1,0:T(8,128)(2,1)S(1)} %cube_change.1), channel_id=1, source_target_pairs={{0,24},{1,25},{2,26},{3,27},{4,28},{5,29},{6,30},{7,31}} | collective-permute-start | bytes 245768 | tf_op jit(solution)/shard_map/ppermute | solution.py:741
  27.3 0.0 collective-permute-done.2
  27.3 0.0 collective-permute-done.1
  27.4 2.0 %collective-permute-done = bf16[160,256]{1,0:T(8,128)(2,1)S(1)} collective-permute-done((bf16[160,256]{1,0:T(8,128)(2,1)S(1)}, bf16[160,256]{1,0:T(8,128)(2,1)S(1)}, u32[]{:S(2)}, u32[]{:S(2)}) %collective-permute-start) | collective-permute-done | bytes 81952 | tf_op jit(solution)/shard_map/ppermute | solution.py:741
  29.4 0.7 collective-permute-start.6
  30.1 0.0 collective-permute-done.6
  30.2 0.7 collective-permute-start.7
  30.9 0.0 collective-permute-done.7
  31.0 0.7 collective-permute-start.8
  31.7 2.5 %collective-permute-start.3 = (f32[2,5,32,384]{3,2,1,0:T(8,128)S(1)}, f32[2,5,32,384]{3,2,1,0:T(8,128)S(1)}, u32[]{:S(2)}, u32[]{:S(2)}) collective-permute-start(f32[2,5,32,384]{3,2,1,0:T(8,128)S(1)} %get-tuple-element.73), channel_id=1, source_target_pairs={{0,4},{1,5},{2,6},{3,7},{4,0},{5,1},{6,2},{7,3},{8,12},{9,13},{10,... | collective-permute-start | bytes 1474568 | tf_op jit(solution)/shard_map/ppermute | solution.py:723
  34.2 0.7 slice_bitcast_fusion.1
  34.8 2.7 %collective-permute-start.5 = (f32[5,16,384]{2,1,0:T(8,128)}, f32[5,16,384]{2,1,0:T(8,128)}, u32[]{:S(2)}, u32[]{:S(2)}) collective-permute-start(f32[5,16,384]{2,1,0:T(8,128)} %get-tuple-element.114), channel_id=1, source_target_pairs={{0,3},{1,2},{2,1},{3,0},{4,7},{5,6},{6,5},{7,4},{8,11},{9,10},{10,... | collective-permute-start | bytes 368648 | tf_op jit(solution)/shard_map/ppermute | solution.py:730
  37.5 1.9 %collective-permute-start.4 = (f32[5,16,384]{2,1,0:T(8,128)S(1)}, f32[5,16,384]{2,1,0:T(8,128)}, u32[]{:S(2)}, u32[]{:S(2)}) collective-permute-start(f32[5,16,384]{2,1,0:T(8,128)S(1)} %get-tuple-element.115), channel_id=1, source_target_pairs={{0,1},{1,0},{2,3},{3,2},{4,5},{5,4},{6,7},{7,6},{8,9},{9,8},{10,11... | collective-permute-start | bytes 368648 | tf_op jit(solution)/shard_map/ppermute | solution.py:729
  39.5 0.1 fusion
  39.6 0.1 reshape.33
  39.6 0.2 slice.39
  39.9 3.9 %collective-permute-done.5 = f32[5,16,384]{2,1,0:T(8,128)} collective-permute-done((f32[5,16,384]{2,1,0:T(8,128)}, f32[5,16,384]{2,1,0:T(8,128)}, u32[]{:S(2)}, u32[]{:S(2)}) %collective-permute-start.5) | collective-permute-done | bytes 122912 | tf_op jit(solution)/shard_map/ppermute | solution.py:730
  43.8 1.2 collective-permute-done.4
  45.1 0.0 collective-permute-done.3
  45.1 0.0 collective-permute-done.8
  45.1 39.6 %conditional.1 = (f32[17280]{0:T(1024)S(1)}, f32[1,5,16,32,384]{4,3,2,1,0:T(8,128)}) conditional(s32[]{:T(128)} %convert_element_type.6, (f32[7,64]{1,0:T(8,128)S(1)}, s32[6]{0:T(128)S(1)}, f32[5,16,32,384]{3,2,1,0:T(8,128)}, f32[2,5,32,384]{3,2,1,0:T(8,128)S(1)}, f32[5,16,384]{2,1,0:T(8,128)}, /*index=5*/f32[5,16,384]{2,1,0:T(8,128)}) %tuple.37, ...), branch_computations={%region_0.1_spmd, %region_1.2_spmd.clone} | conditional | flops 17280 | bytes 4478024 | solution.py:782
  45.1 39.6 %evolve_brick.1 = f32[5,16,32,384]{3,2,1,0:T(8,128)} custom-call(f32[7,64]{1,0:T(8,128)S(1)} %get-tuple-element.31.closure, s32[6]{0:T(128)S(1)} %get-tuple-element.32.place, f32[5,16,32,384]{3,2,1,0:T(8,128)} %get-tuple-element.33.fields, f32[2,5,32,384]{3,2,1,0:T(8,128)S(1)} %get-tuple-element.34.x_halo, f32[5,16,384]{2,1,0:T(8,128)} %get-tuple-element.35.y_first, ...), custom_call_target="tpu_custom_call" | custom-call | tf_op jit(solution)/shard_map/cond/branch_0_fun/evolve_brick/pallas_call | solution.py:452
  84.7 0.7 collective-permute-start.9
  85.4 0.0 collective-permute-done.9
  85.4 0.7 collective-permute-start.10
  86.1 0.0 collective-permute-done.10
  86.1 0.7 collective-permute-start.11
  86.8 0.0 collective-permute-done.11
  86.8 0.7 collective-permute-start.14
  87.5 0.7 collective-permute-start.13
  88.2 1.3 collective-permute-start.12
  89.5 0.0 collective-permute-done.14
  89.5 0.0 collective-permute-done.13
  89.5 80.7 %collective-permute-done.12 = f32[17280]{0:T(1024)S(1)} collective-permute-done((f32[17280]{0:T(1024)S(1)}, f32[17280]{0:T(1024)S(1)}, u32[]{:S(2)}, u32[]{:S(2)}) %collective-permute-start.12) | collective-permute-done | bytes 69152 | tf_op jit(solution)/shard_map/ppermute | solution.py:790
  170.2 0.6 multiply_reduce_fusion
  171.5 1.4 multiply_subtract_fusion
  (25 shorter events, 0.2 us)
Async XLA Ops:
  0.6 21.0 %copy-start.2 = (bf16[256,256]{1,0:T(8,128)(2,1)S(1)}, bf16[256,256]{1,0:T(8,128)(2,1)}, u32[]{:S(2)}) copy-start(bf16[256,256]{1,0:T(8,128)(2,1)} %constant.54.clone.order) | copy-start | bytes 393220
  0.7 0.7 copy-start.3
  1.4 12.7 %copy-start.6 = (f32[64,5]{0,1:T(8,128)S(1)}, f32[64,5]{0,1:T(8,128)}, u32[]{:S(2)}) copy-start(f32[64,5]{0,1:T(8,128)} %param.14) | copy-start | bytes 3844
  1.4 12.8 %copy-start.9 = (f32[64]{0:T(128)S(1)}, f32[64]{0:T(128)}, u32[]{:S(2)}) copy-start(f32[64]{0:T(128)} %param.15) | copy-start | bytes 772
  1.4 12.8 %copy-start.7 = (f32[64]{0:T(128)S(1)}, f32[64]{0:T(128)}, u32[]{:S(2)}) copy-start(f32[64]{0:T(128)} %param.16) | copy-start | bytes 772
  1.4 20.3 %copy-start.4 = (s32[24]{0:T(128)S(1)}, s32[24]{0:T(128)}, u32[]{:S(2)}) copy-start(s32[24]{0:T(128)} %sample_block.3) | copy-start | bytes 292
  1.4 38.1 %copy-start.5 = (f32[17280]{0:T(1024)S(1)}, f32[17280]{0:T(1024)}, u32[]{:S(2)}) copy-start(f32[17280]{0:T(1024)} %param.17) | copy-start | bytes 207364
  1.4 43.7 %copy-start.8 = (s32[24]{0:T(128)S(1)}, s32[24]{0:T(128)}, u32[]{:S(2)}) copy-start(s32[24]{0:T(128)} %param.20) | copy-start | bytes 292
  6.8 14.8 %all-to-all-start = ((f32[8,16,256]{2,1,0:T(8,128)}), f32[8,16,256]{2,1,0:T(8,128)S(1)}, u32[]{:S(2)}, u32[]{:S(2)}) async-start(f32[8,16,256]{2,1,0:T(8,128)} %get-tuple-element.72), calls=%async_computation | async-start | bytes 262144 | tf_op jit(solution)/shard_map/all_to_all | solution.py:756
  23.3 4.1 %collective-permute-start.2 = (bf16[160,256]{1,0:T(8,128)(2,1)S(1)}, bf16[160,256]{1,0:T(8,128)(2,1)S(1)}, u32[]{:S(2)}, u32[]{:S(2)}) collective-permute-start(bf16[160,256]{1,0:T(8,128)(2,1)S(1)} %cube_change.1), channel_id=1, source_target_pairs={{16,24},{17,25},{18,26},{19,27},{20,28},{21,29},{22,30},{23,31}} | collective-permute-start | bytes 245768 | tf_op jit(solution)/shard_map/ppermute | solution.py:741
  23.9 3.4 %collective-permute-start.1 = (bf16[160,256]{1,0:T(8,128)(2,1)S(1)}, bf16[160,256]{1,0:T(8,128)(2,1)S(1)}, u32[]{:S(2)}, u32[]{:S(2)}) collective-permute-start(bf16[160,256]{1,0:T(8,128)(2,1)S(1)} %cube_change.1), channel_id=1, source_target_pairs={{8,24},{9,25},{10,26},{11,27},{12,28},{13,29},{14,30},{15,31}} | collective-permute-start | bytes 245768 | tf_op jit(solution)/shard_map/ppermute | solution.py:741
  24.6 4.8 %collective-permute-start = (bf16[160,256]{1,0:T(8,128)(2,1)S(1)}, bf16[160,256]{1,0:T(8,128)(2,1)S(1)}, u32[]{:S(2)}, u32[]{:S(2)}) collective-permute-start(bf16[160,256]{1,0:T(8,128)(2,1)S(1)} %cube_change.1), channel_id=1, source_target_pairs={{0,24},{1,25},{2,26},{3,27},{4,28},{5,29},{6,30},{7,31}} | collective-permute-start | bytes 245768 | tf_op jit(solution)/shard_map/ppermute | solution.py:741
  29.4 0.7 collective-permute-start.6
  30.2 0.8 collective-permute-start.7
  31.0 14.1 %collective-permute-start.8 = (bf16[12,160,256]{2,1,0:T(8,128)(2,1)S(1)}, bf16[12,160,256]{2,1,0:T(8,128)(2,1)S(1)}, u32[]{:S(2)}, u32[]{:S(2)}) collective-permute-start(bf16[12,160,256]{2,1,0:T(8,128)(2,1)S(1)} %constant_dynamic-update-slice_fusion), channel_id=1, source_target_pairs={{24,28},{25,29},{26,30},{27,31},{28,24},{29,25},{30,26},{31,27}} | collective-permute-start | bytes 2949128 | tf_op jit(solution)/shard_map/ppermute | solution.py:753
  31.7 13.4 %collective-permute-start.3 = (f32[2,5,32,384]{3,2,1,0:T(8,128)S(1)}, f32[2,5,32,384]{3,2,1,0:T(8,128)S(1)}, u32[]{:S(2)}, u32[]{:S(2)}) collective-permute-start(f32[2,5,32,384]{3,2,1,0:T(8,128)S(1)} %get-tuple-element.73), channel_id=1, source_target_pairs={{0,4},{1,5},{2,6},{3,7},{4,0},{5,1},{6,2},{7,3},{8,12},{9,13},{10,... | collective-permute-start | bytes 1474568 | tf_op jit(solution)/shard_map/ppermute | solution.py:723
  34.8 9.0 %collective-permute-start.5 = (f32[5,16,384]{2,1,0:T(8,128)}, f32[5,16,384]{2,1,0:T(8,128)}, u32[]{:S(2)}, u32[]{:S(2)}) collective-permute-start(f32[5,16,384]{2,1,0:T(8,128)} %get-tuple-element.114), channel_id=1, source_target_pairs={{0,3},{1,2},{2,1},{3,0},{4,7},{5,6},{6,5},{7,4},{8,11},{9,10},{10,... | collective-permute-start | bytes 368648 | tf_op jit(solution)/shard_map/ppermute | solution.py:730
  37.5 7.5 %collective-permute-start.4 = (f32[5,16,384]{2,1,0:T(8,128)S(1)}, f32[5,16,384]{2,1,0:T(8,128)}, u32[]{:S(2)}, u32[]{:S(2)}) collective-permute-start(f32[5,16,384]{2,1,0:T(8,128)S(1)} %get-tuple-element.115), channel_id=1, source_target_pairs={{0,1},{1,0},{2,3},{3,2},{4,5},{5,4},{6,7},{7,6},{8,9},{9,8},{10,11... | collective-permute-start | bytes 368648 | tf_op jit(solution)/shard_map/ppermute | solution.py:729
  84.7 0.7 collective-permute-start.9
  85.4 0.7 collective-permute-start.10
  86.1 0.7 collective-permute-start.11
  86.8 2.7 %collective-permute-start.14 = (f32[17280]{0:T(1024)S(1)}, f32[17280]{0:T(1024)S(1)}, u32[]{:S(2)}, u32[]{:S(2)}) collective-permute-start(f32[17280]{0:T(1024)S(1)} %add.44), channel_id=1, source_target_pairs={{24,16},{25,17},{26,18},{27,19},{28,20},{29,21},{30,22},{31,23}} | collective-permute-start | bytes 207368 | tf_op jit(solution)/shard_map/ppermute | solution.py:790
  87.5 2.0 %collective-permute-start.13 = (f32[17280]{0:T(1024)S(1)}, f32[17280]{0:T(1024)S(1)}, u32[]{:S(2)}, u32[]{:S(2)}) collective-permute-start(f32[17280]{0:T(1024)S(1)} %add.44), channel_id=1, source_target_pairs={{24,8},{25,9},{26,10},{27,11},{28,12},{29,13},{30,14},{31,15}} | collective-permute-start | bytes 207368 | tf_op jit(solution)/shard_map/ppermute | solution.py:790
  88.2 82.0 %collective-permute-start.12 = (f32[17280]{0:T(1024)S(1)}, f32[17280]{0:T(1024)S(1)}, u32[]{:S(2)}, u32[]{:S(2)}) collective-permute-start(f32[17280]{0:T(1024)S(1)} %add.44), channel_id=1, source_target_pairs={{24,0},{25,1},{26,2},{27,3},{28,4},{29,5},{30,6},{31,7}} | collective-permute-start | bytes 207368 | tf_op jit(solution)/shard_map/ppermute | solution.py:790

commit v6 on v5

--- a/solution.py
+++ b/solution.py
@@ -60,6 +60,59 @@
 SELECT_FIRST, SELECT_LAST = selections()
 
 
+def column_of(place, x_step, y_step):
+    gx = lax.rem(place[1] + x_step + place[5], place[5])
+    gy = lax.rem(place[2] + y_step + place[4], place[4])
+    return gx * place[4] + gy
+
+
+def xor_of(left, right, size):
+    total = jnp.int32(0)
+    for bit in range(size.bit_length() - 1):
+        one, other = lax.rem(lax.div(left, 1 << bit), 2), lax.rem(lax.div(right, 1 << bit), 2)
+        total = total + jnp.where(one == other, 0, 1 << bit)
+    return total
+
+
+def owner_apart(owner, place, y_devices, x_devices):
+    trainers = x_devices * y_devices
+    column = lax.rem(owner, trainers)
+    y_apart = xor_of(lax.rem(column, y_devices), place[2], y_devices)
+    x_apart = xor_of(lax.div(column, y_devices), place[1], x_devices)
+    return lax.div(owner, trainers), y_apart, x_apart
+
+
+def pick_kernel(y_devices, x_devices, apart, trainer_of, place, *refs):
+    near, chosen = refs[:y_devices], refs[y_devices]
+    wanted = xor_of(place[1], apart, x_devices) * y_devices + place[2]
+
+    def visit(owner, count):
+        group, y_apart, x_apart = owner_apart(owner, place, y_devices, x_devices)
+        mine = (trainer_of[owner] == wanted) & (x_apart == 0)
+        for source in range(y_devices):
+
+            @pl.when(mine & (y_apart == source))
+            def _():
+                chosen[count] = near[source][group]
+
+        return count + jnp.where(mine, 1, 0)
+
+    lax.fori_loop(0, trainer_of.shape[0], visit, jnp.int32(0))
+
+
+def pick_cubes(trainer_of, place, near, y_devices, x_devices, apart):
+    vmem = pl.BlockSpec(memory_space=pltpu.VMEM)
+    smem = pl.BlockSpec(memory_space=pltpu.SMEM)
+    return pl.pallas_call(
+        functools.partial(pick_kernel, y_devices, x_devices, apart),
+        out_shape=jax.ShapeDtypeStruct((TCAP, *near[0].shape[1:]), near[0].dtype),
+        in_specs=[smem, smem] + [vmem] * len(near),
+        out_specs=vmem,
+        compiler_params=pltpu.CompilerParams(vmem_limit_bytes=16 * 1024 * 1024),
+        name="pick_cubes",
+    )(trainer_of, place, *near)
+
+
 def dot_rows(left, right):
     return jnp.dot(left, right, preferred_element_type=jnp.float32)
 
@@ -114,13 +167,15 @@
         ref[pair, kx * PATCH : (kx + 1) * PATCH, pl.ds(start, 128)] = stacked
 
 
-def train_kernel(steps, *refs):
+def train_kernel(y_devices, x_devices, *refs):
+    sources = y_devices + x_devices - 1
     (trainer_of, place, first_ref, last_ref, far_first, far_last) = refs[:6]
-    arrived = refs[6:8]
-    fields_ref = refs[8]
-    delta_first, delta_last, new_fields_ref = refs[9:12]
+    arrived = refs[6 : 6 + sources]
+    fields_ref = refs[6 + sources]
+    delta_first, delta_last, new_fields_ref = refs[7 + sources : 10 + sources]
     (
         slots,
+        picked,
         cubes,
         table,
         targets,
@@ -133,6 +188,9 @@
         big_first,
         big_last,
         big_last_t,
+        raw,
+        grad_first,
+        grad_last,
         now_first,
         now_last,
         brick,
@@ -141,7 +199,7 @@
         slot_sems,
         field_sem,
         select_sems,
-    ) = refs[12:]
+    ) = refs[10 + sources :]
 
     field_in = pltpu.make_async_copy(fields_ref, brick, field_sem)
     field_out = pltpu.make_async_copy(brick, new_fields_ref, field_sem)
@@ -151,32 +209,31 @@
     ]
 
     groups = place[3]
-    trainers = trainer_of.shape[0] // groups
-    column = place[1] * place[4] + place[2]
+    for other in range(x_devices):
+        picked[other] = 0
 
     def visit(owner, count):
-        mine = trainer_of[owner] == column
+        mine = trainer_of[owner] == column_of(place, 0, 0)
 
         @pl.when(mine)
         def _():
-            source = lax.rem(owner, trainers)
-            entry = jnp.int32(0)
-            for order, distance in enumerate(steps[:-1]):
-                entry = entry + apart(source, column, distance) * (1 << order)
-            slots[0, count] = apart(source, column, steps[-1])
-            slots[1, count] = entry * groups + lax.div(owner, trainers)
+            group, y_apart, x_apart = owner_apart(owner, place, y_devices, x_devices)
+            near = x_apart == 0
+            slots[0, count] = jnp.where(near, y_apart, y_devices - 1 + x_apart)
+            slots[1, count] = jnp.where(near, group, picked[x_apart])
+            picked[x_apart] = picked[x_apart] + 1
 
         return count + jnp.where(mine, 1, 0)
 
     count = lax.fori_loop(0, trainer_of.shape[0], visit, jnp.int32(0))
 
     def fetch(slot, wait):
-        for half in range(2):
-
-            @pl.when((slot < count) & (slots[0, slot] == half))
+        for source in range(sources):
+
+            @pl.when((slot < count) & (slots[0, slot] == source))
             def _():
                 copy = pltpu.make_async_copy(
-                    arrived[half].at[slots[1, slot]], cubes.at[slot], slot_sems.at[slot]
+                    arrived[source].at[slots[1, slot]], cubes.at[slot], slot_sems.at[slot]
                 )
                 copy.wait() if wait else copy.start()
 
@@ -262,18 +319,30 @@
         def tile_of(index):
             return index // 8, pl.ds(pl.multiple_of((index % 8) * 256 + 128, 128), 256)
 
-        def forward(index, carry):
+        def first_layer(index, carry):
             pair, columns = tile_of(index)
-            half = 0.5 * dot_rows(big_first[...], inputs[pair, :, columns])
-            curve = jnp.tanh(half)
-            value = half + half * curve
-            hidden = value.astype(jnp.bfloat16)
-            hiddens[pair, :, columns] = hidden
-            slopes[pair, :, columns] = (0.5 + 0.5 * curve) + value * (0.5 - 0.5 * curve)
-            partial_out[pair, :, columns] = dot_rows(big_last_t[...], hidden)
+            raw[pair, :, columns] = dot_rows(big_first[...], inputs[pair, :, columns])
             return carry
 
-        lax.fori_loop(0, 8 * PAIRS, forward, 0, unroll=8)
+        def activate(index, carry):
+            pair, columns = tile_of(index)
+            for part in range(4):
+                rows = slice(part * 64, (part + 1) * 64)
+                half = 0.5 * raw[pair, rows, columns]
+                curve = jnp.tanh(half)
+                value = half + half * curve
+                hiddens[pair, rows, columns] = value.astype(jnp.bfloat16)
+                slopes[pair, rows, columns] = (0.5 + 0.5 * curve) + value * (0.5 - 0.5 * curve)
+            return carry
+
+        def last_layer(index, carry):
+            pair, columns = tile_of(index)
+            partial_out[pair, :, columns] = dot_rows(big_last_t[...], hiddens[pair, :, columns])
+            return carry
+
+        lax.fori_loop(0, 8 * PAIRS, first_layer, 0, unroll=4)
+        lax.fori_loop(0, 8 * PAIRS, activate, 0, unroll=2)
+        lax.fori_loop(0, 8 * PAIRS, last_layer, 0, unroll=4)
 
         def error_plane(index, carry):
             pair = index // SUB
@@ -300,19 +369,31 @@
 
         lax.fori_loop(0, SUB * PAIRS, error_plane, 0, unroll=8)
 
-        def backward(index, carry):
+        def hidden_layer(index, carry):
             pair, columns = tile_of(index)
-            hidden_grad = dot_rows(big_last[...], errors[pair, :, columns])
-            pre_grads[pair, :, columns] = (hidden_grad * slopes[pair, :, columns]).astype(jnp.bfloat16)
+            raw[pair, :, columns] = dot_rows(big_last[...], errors[pair, :, columns])
             return carry
 
-        lax.fori_loop(0, 8 * PAIRS, backward, 0, unroll=8)
+        def scale(index, carry):
+            pair, columns = tile_of(index)
+            for part in range(4):
+                rows = slice(part * 64, (part + 1) * 64)
+                product = raw[pair, rows, columns] * slopes[pair, rows, columns]
+                pre_grads[pair, rows, columns] = product.astype(jnp.bfloat16)
+            return carry
+
+        lax.fori_loop(0, 8 * PAIRS, hidden_layer, 0, unroll=4)
+        lax.fori_loop(0, 8 * PAIRS, scale, 0, unroll=2)
         body = slice(128, COLS - 128)
-        grad_first = jnp.zeros((4 * CH, STACK), jnp.float32)
-        grad_last = jnp.zeros((4 * CH, STACK), jnp.float32)
-        for pair in range(PAIRS):
-            grad_first += dot_lanes(pre_grads[pair, :, body], inputs[pair, :, body])
-            grad_last += dot_lanes(hiddens[pair, :, body], errors[pair, :, body])
+        grad_first[...] = jnp.zeros(grad_first.shape, jnp.float32)
+        grad_last[...] = jnp.zeros(grad_last.shape, jnp.float32)
+
+        def gradients(pair, carry):
+            grad_first[...] += dot_lanes(pre_grads[pair, :, body], inputs[pair, :, body])
+            grad_last[...] += dot_lanes(hiddens[pair, :, body], errors[pair, :, body])
+            return carry
+
+        lax.fori_loop(0, PAIRS, gradients, 0)
 
         def folded(grad, select_ref):
             total = jnp.zeros((3 * CH, 256), jnp.float32)
@@ -335,26 +416,23 @@
     field_out.wait()
 
 
-def apart(left, right, distance):
-    return jnp.where(lax.rem(lax.div(left, distance), 2) == lax.rem(lax.div(right, distance), 2), 0, 1)
-
-
-def train_cubes(trainer_of, place, first, last, arrived, fields, steps):
+def train_cubes(trainer_of, place, first, last, arrived, fields, y_devices, x_devices):
     vmem = pl.BlockSpec(memory_space=pltpu.VMEM)
     smem = pl.BlockSpec(memory_space=pltpu.SMEM)
     anywhere = pl.BlockSpec(memory_space=pl.ANY)
     hbm = pl.BlockSpec(memory_space=pltpu.HBM)
     return pl.pallas_call(
-        functools.partial(train_kernel, steps),
+        functools.partial(train_kernel, y_devices, x_devices),
         out_shape=(
             jax.ShapeDtypeStruct((CH, 256), jnp.float32),
             jax.ShapeDtypeStruct((CH, 256), jnp.float32),
             jax.ShapeDtypeStruct(fields.shape, fields.dtype),
         ),
-        in_specs=[smem] * 2 + [vmem] * 2 + [hbm] * 2 + [anywhere] * 2 + [hbm],
+        in_specs=[smem] * 2 + [vmem] * 2 + [hbm] * 2 + [anywhere] * len(arrived) + [hbm],
         out_specs=(vmem, vmem, hbm),
         scratch_shapes=[
             pltpu.SMEM((2, TCAP), jnp.int32),
+            pltpu.SMEM((x_devices,), jnp.int32),
             pltpu.VMEM((TCAP, 2 * SUB * F, 256), jnp.bfloat16),
             pltpu.VMEM((SUB * F * 8, 128), jnp.float32),
             pltpu.VMEM((PAIRS * SUB * F * 8, 128), jnp.float32),
@@ -367,6 +445,9 @@
             pltpu.VMEM((4 * CH, STACK), jnp.bfloat16),
             pltpu.VMEM((4 * CH, STACK), jnp.bfloat16),
             pltpu.VMEM((STACK, 4 * CH), jnp.bfloat16),
+            pltpu.VMEM((PAIRS, 4 * CH, COLS), jnp.float32),
+            pltpu.VMEM((4 * CH, STACK), jnp.float32),
+            pltpu.VMEM((4 * CH, STACK), jnp.float32),
             pltpu.VMEM((CH, 256), jnp.float32),
             pltpu.VMEM((CH, 256), jnp.float32),
             pltpu.VMEM(fields.shape, fields.dtype),
@@ -478,12 +559,6 @@
     block = sample_block[(group * x_devices + gx) * y_devices + gy]
     z_blocks = z_cells // SUB
     return lax.rem(lax.div(block, z_blocks), y_cells // SUB) * SUB, lax.rem(block, z_blocks) * SUB
-
-
-def column_of(place, x_step, y_step):
-    gx = lax.rem(place[1] + x_step + place[5], place[5])
-    gy = lax.rem(place[2] + y_step + place[4], place[4])
-    return gx * place[4] + gy
 
 
 def sample_kernel(
@@ -673,12 +748,6 @@
     )(sample_block, place, closure, jnp.asarray(CELL_ORDER, jnp.bfloat16), *cube, thin)
 
 
-def doubling_steps(x_devices, y_devices):
-    along_y = [1 << bit for bit in reversed(range(y_devices.bit_length() - 1))]
-    along_x = [y_devices << bit for bit in reversed(range(x_devices.bit_length() - 1))]
-    return along_y + along_x
-
-
 def on_device(
     fields, closure_in, closure_bias, closure_out, master, momentum, sample_block, sample_trainer
 ):
@@ -733,8 +802,6 @@
     def swap(distance):
         return [(first_trainer + c, first_trainer + (c ^ distance)) for c in range(trainers)]
 
-    steps = doubling_steps(x_devices, y_devices)
-
     def to_trainers(payload):
         return jnp.stack(
             [
@@ -747,10 +814,11 @@
             ]
         )
 
-    def among_trainers(held):
-        for distance in steps[:-1]:
-            held = jnp.concatenate([held, lax.ppermute(held, everyone, swap(distance))], axis=0)
-        return [held, lax.ppermute(held, everyone, swap(steps[-1]))]
+    def from_line(held):
+        return [lax.ppermute(held, everyone, swap(apart)) for apart in range(1, y_devices)]
+
+    def across(apart, held):
+        return lax.ppermute(held, everyone, swap(apart * y_devices))
 
     *cube, thin, x_edges, y_edges = sample_cube(sample_block, place, brick, trainers)
     thin = lax.all_to_all(thin, ("gx", "gy"), split_axis=0, concat_axis=0, tiled=True)
@@ -758,7 +826,12 @@
     landed = to_trainers(payload)
     x_edges, y_edges, landed = lax.optimization_barrier((x_edges, y_edges, landed))
     halo = (x_neighbours(x_edges), *y_neighbours(y_edges[0], y_edges[1]))
-    arrived = among_trainers(landed)
+    near = [landed, *from_line(landed)]
+    far = [
+        across(apart, pick_cubes(sample_trainer, place, near, y_devices, x_devices, apart))
+        for apart in range(1, x_devices)
+    ]
+    arrived = [*near, *far]
 
     first_count = CH * TAPS * F
     first = jnp.pad(master[:first_count].reshape(CH, TAPS * F), ((0, 0), (0, 256 - TAPS * F)))
@@ -768,7 +841,7 @@
 
     def train_here():
         delta_first, delta_last, new_brick = train_cubes(
-            sample_trainer, place, first, last, arrived, brick, steps
+            sample_trainer, place, first, last, arrived, brick, y_devices, x_devices
         )
         delta = jnp.concatenate(
             [delta_first[:, : TAPS * F].reshape(-1), delta_last[:, : TAPS * F].T.reshape(-1)]
@@ -781,9 +854,8 @@
 
     delta, new_brick = lax.cond(is_trainer, train_here, evolve_here)
 
-    total = delta
-    for distance in steps:
-        total = total + lax.ppermute(total, everyone, swap(distance))
+    line = sum(from_line(delta), delta)
+    total = sum((across(apart, line) for apart in range(1, x_devices)), line)
     final = jnp.where(is_trainer, total, 0.0)
     for g in range(sim_groups):
         pairs = [(first_trainer + c, g * trainers + c) for c in range(trainers)]

time: 174 us -> 169 us (0.971)
  waiting for transfers between devices: 95.4 us -> 87.5 us
  Pallas kernels: 46.6 us -> 48.4 us
    ppermute x3, waiting for transfers between devices: 80.7 us -> 72.9 us  [on_device(): final = final + lax.ppermute(total, everyone, pairs)]
    pallas_call x0 -> x1, Pallas kernels: none -> 1.78 us  [pick_cubes(): pl.pallas_call(functools.partial(pick_kernel, y_devices, x_devices, apart...]
    ppermute x6 -> x8, starting transfers between devices: 4.09 us -> 5.38 us  [the longest x6 4.02 us: from_line(): lax.ppermute(held, everyone, swap(apart))]
  transfers between devices with their start and end apart: 16 -> 18, of which waited for: 5 -> 5; matrix products, arithmetic and copies ran while one was open for 1% -> 1% of each run, Pallas kernels for 0% -> 1%
where the time goes in v6:
time: 169 us; the launch traced here: 168 us
  waiting for transfers between devices  87.5 us (52%)
  Pallas kernels  48.4 us (29%)
  starting transfers between devices  26.4 us (16%)
  other arithmetic  2.09 us (1%)
  local copies, waits for them, and re-layouts  1.82 us (1%)
  between operations  1.7 us (1%)
    ppermute x3, waiting for transfers between devices, on_device(): final = final + lax.ppermute(total, everyone, pairs)  72.9 us
    pallas_call x1, Pallas kernels, evolve(): pl.pallas_call(evolve_kernel, out_shape=jax.ShapeDtypeStruct(fields.shape...  39.6 us
    all_to_all x1, waiting for transfers between devices, on_device(): lax.all_to_all(thin, ('gx', 'gy'), split_axis=0, concat_axis=0, tiled=True)  7.45 us
    all_to_all x1, starting transfers between devices, on_device(): lax.all_to_all(thin, ('gx', 'gy'), split_axis=0, concat_axis=0, tiled=True)  7.3 us
    pallas_call x1, Pallas kernels, sample_cube(): pl.pallas_call(functools.partial(sample_kernel, y_cells, z_cells), out_sh...  5.4 us
    ppermute x3, starting transfers between devices, to_trainers(): lax.ppermute(payload, everyone, [(g * trainers + c, first_trainer + c) fo...  4.05 us
    ppermute x6, starting transfers between devices, from_line(): lax.ppermute(held, everyone, swap(apart))  4.02 us
    ppermute x1, waiting for transfers between devices, y_neighbours(): lax.ppermute(for_second, everyone, pairs(0, -1))  3.94 us
  transfers between devices with their start and end apart: 18, of which 5 were waited for; matrix products, arithmetic and copies ran while one was open for 1% of the time, Pallas kernels for 1%

profile of v6, /device:TPU:0, one launch (start us, length us, event | category | flops | bytes accessed | tf_op | source)
XLA Modules:
  0.0 168.0 jit_solution(9422717217729713498)
XLA Ops:
  0.6 0.0 copy-start.2
  0.6 0.1 stack.27.place
  0.7 0.7 copy-done.3
  1.4 0.0 copy-start.4
  1.4 5.4 %sample_cube.1 = (f32[80,256]{1,0:T(8,128)S(1)}, f32[80,256]{1,0:T(8,128)S(1)}, f32[80,256]{1,0:T(8,128)S(1)}, f32[2,16,128]{2,1,0:T(8,128)S(1)}, f32[8,16,256]{...) custom-call(s32[24]{0:T(128)S(1)} %copy-done.3, s32[6]{0:T(128)S(1)} %stack.27.place, ...), custom_call_target="tpu_custom_call" | custom-call | tf_op jit(solution)/shard_map/sample_cube/pallas_call | solution.py:670
  6.8 7.3 %all-to-all-start = ((f32[8,16,256]{2,1,0:T(8,128)}), f32[8,16,256]{2,1,0:T(8,128)S(1)}, u32[]{:S(2)}, u32[]{:S(2)}) async-start(f32[8,16,256]{2,1,0:T(8,128)} %get-tuple-element.81), calls=%async_computation | async-start | bytes 262144 | tf_op jit(solution)/shard_map/all_to_all | solution.py:824
  14.2 7.5 %all-to-all-done.thin = f32[8,16,256]{2,1,0:T(8,128)S(1)} async-done(((f32[8,16,256]{2,1,0:T(8,128)}), f32[8,16,256]{2,1,0:T(8,128)S(1)}, u32[]{:S(2)}, u32[]{:S(2)}) %all-to-all-start) | async-done | bytes 131104 | tf_op jit(solution)/shard_map/all_to_all | solution.py:824
  21.6 1.6 cube_change.1
  23.2 0.7 collective-permute-start.2
  23.9 0.7 collective-permute-start.1
  24.6 2.7 %collective-permute-start = (bf16[160,256]{1,0:T(8,128)(2,1)S(1)}, bf16[160,256]{1,0:T(8,128)(2,1)S(1)}, u32[]{:S(2)}, u32[]{:S(2)}) collective-permute-start(bf16[160,256]{1,0:T(8,128)(2,1)S(1)} %cube_change.1), channel_id=1, source_target_pairs={{0,24},{1,25},{2,26},{3,27},{4,28},{5,29},{6,30},{7,31}} | collective-permute-start | bytes 245768 | tf_op jit(solution)/shard_map/ppermute | solution.py:808
  27.3 0.0 collective-permute-done.2
  27.3 0.0 collective-permute-done.1
  27.3 2.0 %collective-permute-done = bf16[160,256]{1,0:T(8,128)(2,1)S(1)} collective-permute-done((bf16[160,256]{1,0:T(8,128)(2,1)S(1)}, bf16[160,256]{1,0:T(8,128)(2,1)S(1)}, u32[]{:S(2)}, u32[]{:S(2)}) %collective-permute-start) | collective-permute-done | bytes 81952 | tf_op jit(solution)/shard_map/ppermute | solution.py:808
  29.4 0.7 collective-permute-start.8
  30.1 0.7 collective-permute-start.7
  30.8 0.7 collective-permute-start.6
  31.4 2.5 %collective-permute-start.3 = (f32[2,5,32,384]{3,2,1,0:T(8,128)S(1)}, f32[2,5,32,384]{3,2,1,0:T(8,128)S(1)}, u32[]{:S(2)}, u32[]{:S(2)}) collective-permute-start(f32[2,5,32,384]{3,2,1,0:T(8,128)S(1)} %get-tuple-element.82), channel_id=1, source_target_pairs={{0,4},{1,5},{2,6},{3,7},{4,0},{5,1},{6,2},{7,3},{8,12},{9,13},{10,... | collective-permute-start | bytes 1474568 | tf_op jit(solution)/shard_map/ppermute | solution.py:792
  33.9 0.0 collective-permute-done.8.refs_3_
  33.9 0.0 collective-permute-done.6.refs_1_
  34.0 1.8 %pick_cubes.1 = bf16[6,160,256]{2,1,0:T(8,128)(2,1)S(1)} custom-call(s32[24]{0:T(128)S(1)} %copy-done.6, s32[6]{0:T(128)S(1)} %stack.27.place, bf16[3,160,256]{2,1,0:T(8,128)(2,1)S(1)} %pad_maximum_fusion.1.refs_0_, bf16[3,160,256]{2,1,0:T(8,128)(2,1)S(1)} %collective-permute-done.6.refs_1_, bf16[3,160,256]{2,1,0:T(8,128)(2,1)S(1)} %collective-permute-done.7.refs_2_, ...), custom_call_target="tpu_custom_call" | custom-call | tf_op jit(solution)/shard_map/pick_cubes/pallas_call | solution.py:106
  35.8 0.7 collective-permute-start.9
  36.5 0.7 slice_bitcast_fusion.1
  37.1 2.7 %collective-permute-start.5 = (f32[5,16,384]{2,1,0:T(8,128)}, f32[5,16,384]{2,1,0:T(8,128)}, u32[]{:S(2)}, u32[]{:S(2)}) collective-permute-start(f32[5,16,384]{2,1,0:T(8,128)} %get-tuple-element.130), channel_id=1, source_target_pairs={{0,3},{1,2},{2,1},{3,0},{4,7},{5,6},{6,5},{7,4},{8,11},{9,10},{10,... | collective-permute-start | bytes 368648 | tf_op jit(solution)/shard_map/ppermute | solution.py:799
  39.8 1.9 %collective-permute-start.4 = (f32[5,16,384]{2,1,0:T(8,128)S(1)}, f32[5,16,384]{2,1,0:T(8,128)}, u32[]{:S(2)}, u32[]{:S(2)}) collective-permute-start(f32[5,16,384]{2,1,0:T(8,128)S(1)} %get-tuple-element.131), channel_id=1, source_target_pairs={{0,1},{1,0},{2,3},{3,2},{4,5},{5,4},{6,7},{7,6},{8,9},{9,8},{10,11... | collective-permute-start | bytes 368648 | tf_op jit(solution)/shard_map/ppermute | solution.py:798
  41.8 0.1 fusion
  41.8 0.1 reshape.33
  41.9 0.2 slice.39
  42.2 3.9 %collective-permute-done.5 = f32[5,16,384]{2,1,0:T(8,128)} collective-permute-done((f32[5,16,384]{2,1,0:T(8,128)}, f32[5,16,384]{2,1,0:T(8,128)}, u32[]{:S(2)}, u32[]{:S(2)}) %collective-permute-start.5) | collective-permute-done | bytes 122912 | tf_op jit(solution)/shard_map/ppermute | solution.py:799
  46.1 1.2 collective-permute-done.4
  47.3 0.0 collective-permute-done.3
  47.3 0.0 collective-permute-done.9
  47.3 39.6 %conditional.1 = (f32[17280]{0:T(1024)S(1)}, f32[1,5,16,32,384]{4,3,2,1,0:T(8,128)}) conditional(s32[]{:T(128)} %convert_element_type.6, (f32[7,64]{1,0:T(8,128)S(1)}, s32[6]{0:T(128)S(1)}, f32[5,16,32,384]{3,2,1,0:T(8,128)}, f32[2,5,32,384]{3,2,1,0:T(8,128)S(1)}, f32[5,16,384]{2,1,0:T(8,128)}, /*index=5*/f32[5,16,384]{2,1,0:T(8,128)}) %tuple.37, ...), branch_computations={%region_0.1_spmd, %region_1.2_spmd.clone} | conditional | flops 17280 | bytes 4478024 | solution.py:855
  47.4 39.6 %evolve_brick.1 = f32[5,16,32,384]{3,2,1,0:T(8,128)} custom-call(f32[7,64]{1,0:T(8,128)S(1)} %get-tuple-element.37.closure, s32[6]{0:T(128)S(1)} %get-tuple-element.38.place, f32[5,16,32,384]{3,2,1,0:T(8,128)} %get-tuple-element.39.fields, f32[2,5,32,384]{3,2,1,0:T(8,128)S(1)} %get-tuple-element.40.x_halo, f32[5,16,384]{2,1,0:T(8,128)} %get-tuple-element.41.y_first, ...), custom_call_target="tpu_custom_call" | custom-call | tf_op jit(solution)/shard_map/cond/branch_0_fun/evolve_brick/pallas_call | solution.py:533
  87.0 0.7 collective-permute-start.12
  87.7 0.7 collective-permute-start.11
  88.3 0.7 collective-permute-start.10
  89.0 0.0 collective-permute-done.11
  89.0 0.0 collective-permute-done.10
  89.1 0.7 collective-permute-start.13
  89.7 0.0 collective-permute-done.13
  89.8 0.7 collective-permute-start.16
  90.4 0.7 collective-permute-start.15
  91.1 1.3 collective-permute-start.14
  92.4 0.0 collective-permute-done.15
  92.4 72.9 %collective-permute-done.14 = f32[17280]{0:T(1024)S(1)} collective-permute-done((f32[17280]{0:T(1024)S(1)}, f32[17280]{0:T(1024)S(1)}, u32[]{:S(2)}, u32[]{:S(2)}) %collective-permute-start.14) | collective-permute-done | bytes 69152 | tf_op jit(solution)/shard_map/ppermute | solution.py:862
  165.3 0.6 multiply_reduce_fusion
  166.6 1.4 multiply_subtract_fusion
  (23 shorter events, 0.1 us)
Async XLA Ops:
  0.6 21.0 %copy-start.2 = (bf16[256,256]{1,0:T(8,128)(2,1)S(1)}, bf16[256,256]{1,0:T(8,128)(2,1)}, u32[]{:S(2)}) copy-start(bf16[256,256]{1,0:T(8,128)(2,1)} %constant.54.clone.order) | copy-start | bytes 393220
  0.7 0.7 copy-start.3
  1.4 12.7 %copy-start.5 = (f32[64,5]{0,1:T(8,128)S(1)}, f32[64,5]{0,1:T(8,128)}, u32[]{:S(2)}) copy-start(f32[64,5]{0,1:T(8,128)} %param.14) | copy-start | bytes 3844
  1.4 12.7 %copy-start.8 = (f32[64]{0:T(128)S(1)}, f32[64]{0:T(128)}, u32[]{:S(2)}) copy-start(f32[64]{0:T(128)} %param.15) | copy-start | bytes 772
  1.4 12.8 %copy-start.7 = (f32[64]{0:T(128)S(1)}, f32[64]{0:T(128)}, u32[]{:S(2)}) copy-start(f32[64]{0:T(128)} %param.16) | copy-start | bytes 772
  1.4 32.6 %copy-start.6 = (s32[24]{0:T(128)S(1)}, s32[24]{0:T(128)}, u32[]{:S(2)}) copy-start(s32[24]{0:T(128)} %trainer_of.1) | copy-start | bytes 292
  1.4 40.4 %copy-start.4 = (f32[17280]{0:T(1024)S(1)}, f32[17280]{0:T(1024)}, u32[]{:S(2)}) copy-start(f32[17280]{0:T(1024)} %param.17) | copy-start | bytes 207364
  6.8 14.8 %all-to-all-start = ((f32[8,16,256]{2,1,0:T(8,128)}), f32[8,16,256]{2,1,0:T(8,128)S(1)}, u32[]{:S(2)}, u32[]{:S(2)}) async-start(f32[8,16,256]{2,1,0:T(8,128)} %get-tuple-element.81), calls=%async_computation | async-start | bytes 262144 | tf_op jit(solution)/shard_map/all_to_all | solution.py:824
  23.2 4.1 %collective-permute-start.2 = (bf16[160,256]{1,0:T(8,128)(2,1)S(1)}, bf16[160,256]{1,0:T(8,128)(2,1)S(1)}, u32[]{:S(2)}, u32[]{:S(2)}) collective-permute-start(bf16[160,256]{1,0:T(8,128)(2,1)S(1)} %cube_change.1), channel_id=1, source_target_pairs={{16,24},{17,25},{18,26},{19,27},{20,28},{21,29},{22,30},{23,31}} | collective-permute-start | bytes 245768 | tf_op jit(solution)/shard_map/ppermute | solution.py:808
  23.9 3.4 %collective-permute-start.1 = (bf16[160,256]{1,0:T(8,128)(2,1)S(1)}, bf16[160,256]{1,0:T(8,128)(2,1)S(1)}, u32[]{:S(2)}, u32[]{:S(2)}) collective-permute-start(bf16[160,256]{1,0:T(8,128)(2,1)S(1)} %cube_change.1), channel_id=1, source_target_pairs={{8,24},{9,25},{10,26},{11,27},{12,28},{13,29},{14,30},{15,31}} | collective-permute-start | bytes 245768 | tf_op jit(solution)/shard_map/ppermute | solution.py:808
  24.6 4.8 %collective-permute-start = (bf16[160,256]{1,0:T(8,128)(2,1)S(1)}, bf16[160,256]{1,0:T(8,128)(2,1)S(1)}, u32[]{:S(2)}, u32[]{:S(2)}) collective-permute-start(bf16[160,256]{1,0:T(8,128)(2,1)S(1)} %cube_change.1), channel_id=1, source_target_pairs={{0,24},{1,25},{2,26},{3,27},{4,28},{5,29},{6,30},{7,31}} | collective-permute-start | bytes 245768 | tf_op jit(solution)/shard_map/ppermute | solution.py:808
  29.4 4.5 %collective-permute-start.8 = (bf16[3,160,256]{2,1,0:T(8,128)(2,1)S(1)}, bf16[3,160,256]{2,1,0:T(8,128)(2,1)S(1)}, u32[]{:S(2)}, u32[]{:S(2)}) collective-permute-start(bf16[3,160,256]{2,1,0:T(8,128)(2,1)S(1)} %pad_maximum_fusion.1.refs_0_), channel_id=1, source_target_pairs={{24,27},{25,26},{26,25},{27,24},{28,31},{29,30},{30,29},{31,28}} | collective-permute-start | bytes 737288 | tf_op jit(solution)/shard_map/ppermute | solution.py:818
  30.1 3.9 %collective-permute-start.7 = (bf16[3,160,256]{2,1,0:T(8,128)(2,1)S(1)}, bf16[3,160,256]{2,1,0:T(8,128)(2,1)S(1)}, u32[]{:S(2)}, u32[]{:S(2)}) collective-permute-start(bf16[3,160,256]{2,1,0:T(8,128)(2,1)S(1)} %pad_maximum_fusion.1.refs_0_), channel_id=1, source_target_pairs={{24,26},{25,27},{26,24},{27,25},{28,30},{29,31},{30,28},{31,29}} | collective-permute-start | bytes 737288 | tf_op jit(solution)/shard_map/ppermute | solution.py:818
  30.8 3.2 %collective-permute-start.6 = (bf16[3,160,256]{2,1,0:T(8,128)(2,1)S(1)}, bf16[3,160,256]{2,1,0:T(8,128)(2,1)S(1)}, u32[]{:S(2)}, u32[]{:S(2)}) collective-permute-start(bf16[3,160,256]{2,1,0:T(8,128)(2,1)S(1)} %pad_maximum_fusion.1.refs_0_), channel_id=1, source_target_pairs={{24,25},{25,24},{26,27},{27,26},{28,29},{29,28},{30,31},{31,30}} | collective-permute-start | bytes 737288 | tf_op jit(solution)/shard_map/ppermute | solution.py:818
  31.4 15.9 %collective-permute-start.3 = (f32[2,5,32,384]{3,2,1,0:T(8,128)S(1)}, f32[2,5,32,384]{3,2,1,0:T(8,128)S(1)}, u32[]{:S(2)}, u32[]{:S(2)}) collective-permute-start(f32[2,5,32,384]{3,2,1,0:T(8,128)S(1)} %get-tuple-element.82), channel_id=1, source_target_pairs={{0,4},{1,5},{2,6},{3,7},{4,0},{5,1},{6,2},{7,3},{8,12},{9,13},{10,... | collective-permute-start | bytes 1474568 | tf_op jit(solution)/shard_map/ppermute | solution.py:792
  35.8 11.6 %collective-permute-start.9 = (bf16[6,160,256]{2,1,0:T(8,128)(2,1)S(1)}, bf16[6,160,256]{2,1,0:T(8,128)(2,1)S(1)}, u32[]{:S(2)}, u32[]{:S(2)}) collective-permute-start(bf16[6,160,256]{2,1,0:T(8,128)(2,1)S(1)} %pick_cubes.1), channel_id=1, source_target_pairs={{24,28},{25,29},{26,30},{27,31},{28,24},{29,25},{30,26},{31,27}} | collective-permute-start | bytes 1474568 | tf_op jit(solution)/shard_map/ppermute | solution.py:821
  37.1 9.0 %collective-permute-start.5 = (f32[5,16,384]{2,1,0:T(8,128)}, f32[5,16,384]{2,1,0:T(8,128)}, u32[]{:S(2)}, u32[]{:S(2)}) collective-permute-start(f32[5,16,384]{2,1,0:T(8,128)} %get-tuple-element.130), channel_id=1, source_target_pairs={{0,3},{1,2},{2,1},{3,0},{4,7},{5,6},{6,5},{7,4},{8,11},{9,10},{10,... | collective-permute-start | bytes 368648 | tf_op jit(solution)/shard_map/ppermute | solution.py:799
  39.8 7.5 %collective-permute-start.4 = (f32[5,16,384]{2,1,0:T(8,128)S(1)}, f32[5,16,384]{2,1,0:T(8,128)}, u32[]{:S(2)}, u32[]{:S(2)}) collective-permute-start(f32[5,16,384]{2,1,0:T(8,128)S(1)} %get-tuple-element.131), channel_id=1, source_target_pairs={{0,1},{1,0},{2,3},{3,2},{4,5},{5,4},{6,7},{7,6},{8,9},{9,8},{10,11... | collective-permute-start | bytes 368648 | tf_op jit(solution)/shard_map/ppermute | solution.py:798
  87.0 2.0 %collective-permute-start.12 = (f32[17280]{0:T(1024)S(1)}, f32[17280]{0:T(1024)S(1)}, u32[]{:S(2)}, u32[]{:S(2)}) collective-permute-start(f32[17280]{0:T(1024)S(1)} %get-tuple-element.88), channel_id=1, source_target_pairs={{24,27},{25,26},{26,25},{27,24},{28,31},{29,30},{30,29},{31,28}} | collective-permute-start | bytes 207368 | tf_op jit(solution)/shard_map/ppermute | solution.py:818
  87.7 1.4 collective-permute-start.11
  88.3 0.7 collective-permute-start.10
  89.1 0.7 collective-permute-start.13
  89.8 2.7 %collective-permute-start.16 = (f32[17280]{0:T(1024)S(1)}, f32[17280]{0:T(1024)S(1)}, u32[]{:S(2)}, u32[]{:S(2)}) collective-permute-start(f32[17280]{0:T(1024)S(1)} %add.48), channel_id=1, source_target_pairs={{24,16},{25,17},{26,18},{27,19},{28,20},{29,21},{30,22},{31,23}} | collective-permute-start | bytes 207368 | tf_op jit(solution)/shard_map/ppermute | solution.py:862
  90.4 2.0 %collective-permute-start.15 = (f32[17280]{0:T(1024)S(1)}, f32[17280]{0:T(1024)S(1)}, u32[]{:S(2)}, u32[]{:S(2)}) collective-permute-start(f32[17280]{0:T(1024)S(1)} %add.48), channel_id=1, source_target_pairs={{24,8},{25,9},{26,10},{27,11},{28,12},{29,13},{30,14},{31,15}} | collective-permute-start | bytes 207368 | tf_op jit(solution)/shard_map/ppermute | solution.py:862
  91.1 74.2 %collective-permute-start.14 = (f32[17280]{0:T(1024)S(1)}, f32[17280]{0:T(1024)S(1)}, u32[]{:S(2)}, u32[]{:S(2)}) collective-permute-start(f32[17280]{0:T(1024)S(1)} %add.48), channel_id=1, source_target_pairs={{24,0},{25,1},{26,2},{27,3},{28,4},{29,5},{30,6},{31,7}} | collective-permute-start | bytes 207368 | tf_op jit(solution)/shard_map/ppermute | solution.py:862

commit v7 on v6

--- a/solution.py
+++ b/solution.py
@@ -160,11 +160,11 @@
     return fold_z(upper) + shifted
 
 
-def store_planes(ref, pair, x, channels):
+def store_planes(ref, x, channels):
     stacked = jnp.concatenate([part for both in channels for part in both], axis=0).astype(jnp.bfloat16)
     for kx in range(3):
         start = pl.multiple_of((x + 2 - kx) * 128, 128)
-        ref[pair, kx * PATCH : (kx + 1) * PATCH, pl.ds(start, 128)] = stacked
+        ref[kx * PATCH : (kx + 1) * PATCH, pl.ds(start, 128)] = stacked
 
 
 def train_kernel(y_devices, x_devices, *refs):
@@ -178,17 +178,9 @@
         picked,
         cubes,
         table,
-        targets,
-        inputs,
-        errors,
-        hiddens,
-        pre_grads,
-        slopes,
-        partial_out,
         big_first,
         big_last,
         big_last_t,
-        raw,
         grad_first,
         grad_last,
         now_first,
@@ -199,7 +191,11 @@
         slot_sems,
         field_sem,
         select_sems,
+        *pair_refs,
     ) = refs[10 + sources :]
+    targets, inputs, errors, hiddens, pre_grads, slopes, partial_out, raw = [
+        pair_refs[kind * PAIRS : (kind + 1) * PAIRS] for kind in range(8)
+    ]
 
     field_in = pltpu.make_async_copy(fields_ref, brick, field_sem)
     field_out = pltpu.make_async_copy(brick, new_fields_ref, field_sem)
@@ -250,13 +246,14 @@
             cubes[slot] = jnp.zeros((2 * SUB * F, 256), jnp.bfloat16)
 
     masks = patch_masks()
-    for ref in (errors, inputs):
-        ref[:, :PATCH, 128:256] = jnp.zeros((PAIRS, PATCH, 128), jnp.bfloat16)
-        ref[:, 2 * PATCH :, COLS - 256 : COLS - 128] = jnp.zeros((PAIRS, PATCH, 128), jnp.bfloat16)
-    partial_out[:, :, :128] = jnp.zeros((PAIRS, STACK, 128), jnp.float32)
-    partial_out[:, :, COLS - 128 :] = jnp.zeros((PAIRS, STACK, 128), jnp.float32)
-    table[...] = jnp.zeros(table.shape, table.dtype)
-    targets[...] = jnp.zeros(targets.shape, targets.dtype)
+    for ref in (*errors, *inputs):
+        ref[:PATCH, 128:256] = jnp.zeros((PATCH, 128), jnp.bfloat16)
+        ref[2 * PATCH :, COLS - 256 : COLS - 128] = jnp.zeros((PATCH, 128), jnp.bfloat16)
+    for ref in partial_out:
+        ref[:, :128] = jnp.zeros((STACK, 128), jnp.float32)
+        ref[:, COLS - 128 :] = jnp.zeros((STACK, 128), jnp.float32)
+    for ref in (table, *targets):
+        ref[...] = jnp.zeros(ref.shape, ref.dtype)
     lane = lax.broadcasted_iota(jnp.int32, (8, 128), 1)
     full_weight = 2.0 * (1.0 / (jnp.full((8, 128), count, jnp.int32).astype(jnp.float32) * CELLS))
     weights = [
@@ -288,7 +285,7 @@
             table[pl.ds(cell, SUB * F, 8), :] = values
 
         def put_target(cell, values):
-            targets[pl.ds(pair * SUB * F * 8 + cell, SUB * F, 8), :] = values
+            targets[pair][pl.ds(cell, SUB * F, 8), :] = values
 
         spread_rows(pair, 0, put_input)
         spread_rows(pair, 1, put_target)
@@ -298,7 +295,7 @@
                 patch_stack(table[pl.ds(pl.multiple_of((c * SUB + x) * 8, 8), 8), :], masks)
                 for c in range(F)
             ]
-            store_planes(inputs, pair, x, channels)
+            store_planes(inputs[pair], x, channels)
             return carry
 
         lax.fori_loop(0, SUB, stack_plane, 0, unroll=8)
@@ -313,87 +310,82 @@
         last_now = now_last[...].astype(jnp.bfloat16)
         for cell in range(4):
             rows = slice(cell * CH, (cell + 1) * CH)
-            big_first[rows, :] = dot_rows(first_now, select_first[cell]).astype(jnp.bfloat16)
-            big_last[rows, :] = dot_rows(last_now, select_last[cell]).astype(jnp.bfloat16)
-        big_last_t[...] = big_last[...].T
-        def tile_of(index):
-            return index // 8, pl.ds(pl.multiple_of((index % 8) * 256 + 128, 128), 256)
-
-        def first_layer(index, carry):
-            pair, columns = tile_of(index)
-            raw[pair, :, columns] = dot_rows(big_first[...], inputs[pair, :, columns])
-            return carry
-
-        def activate(index, carry):
-            pair, columns = tile_of(index)
-            for part in range(4):
-                rows = slice(part * 64, (part + 1) * 64)
-                half = 0.5 * raw[pair, rows, columns]
-                curve = jnp.tanh(half)
-                value = half + half * curve
-                hiddens[pair, rows, columns] = value.astype(jnp.bfloat16)
-                slopes[pair, rows, columns] = (0.5 + 0.5 * curve) + value * (0.5 - 0.5 * curve)
-            return carry
-
-        def last_layer(index, carry):
-            pair, columns = tile_of(index)
-            partial_out[pair, :, columns] = dot_rows(big_last_t[...], hiddens[pair, :, columns])
-            return carry
-
-        lax.fori_loop(0, 8 * PAIRS, first_layer, 0, unroll=4)
-        lax.fori_loop(0, 8 * PAIRS, activate, 0, unroll=2)
-        lax.fori_loop(0, 8 * PAIRS, last_layer, 0, unroll=4)
-
-        def error_plane(index, carry):
-            pair = index // SUB
-            x = index % SUB
-            column = pl.multiple_of((x + 1) * 128, 128)
-            total = (
-                partial_out[pair, 0:PATCH, pl.ds(pl.multiple_of(column + 128, 128), 128)]
-                + partial_out[pair, PATCH : 2 * PATCH, pl.ds(column, 128)]
-                + partial_out[pair, 2 * PATCH :, pl.ds(pl.multiple_of(column - 128, 128), 128)]
-            )
-            weight = jnp.where(pair == 0, weights[0], jnp.where(pair == 1, weights[1], weights[2]))
-            channels = []
-            for c in range(F):
-                predicted = patch_fold(
-                    total[16 * c : 16 * c + 8], total[16 * c + 8 : 16 * c + 16], masks
-                )
-                row = pl.multiple_of(((pair * F + c) * SUB + x) * 8, 8)
-                error = weight * (predicted - targets[pl.ds(row, 8), :])
-                error = jnp.where(masks["centre"], error, 0.0)
-                error = error.astype(jnp.bfloat16).astype(jnp.float32)
-                channels.append(patch_stack(error, masks))
-            store_planes(errors, pair, x, channels)
-            return carry
-
-        lax.fori_loop(0, SUB * PAIRS, error_plane, 0, unroll=8)
-
-        def hidden_layer(index, carry):
-            pair, columns = tile_of(index)
-            raw[pair, :, columns] = dot_rows(big_last[...], errors[pair, :, columns])
-            return carry
-
-        def scale(index, carry):
-            pair, columns = tile_of(index)
-            for part in range(4):
-                rows = slice(part * 64, (part + 1) * 64)
-                product = raw[pair, rows, columns] * slopes[pair, rows, columns]
-                pre_grads[pair, rows, columns] = product.astype(jnp.bfloat16)
-            return carry
-
-        lax.fori_loop(0, 8 * PAIRS, hidden_layer, 0, unroll=4)
-        lax.fori_loop(0, 8 * PAIRS, scale, 0, unroll=2)
-        body = slice(128, COLS - 128)
+            big_first[rows, :] = (0.5 * dot_rows(first_now, select_first[cell])).astype(jnp.bfloat16)
+            spread_last = dot_rows(last_now, select_last[cell])
+            big_last[rows, :] = (0.5 * spread_last).astype(jnp.bfloat16)
+            big_last_t[:, rows] = spread_last.T.astype(jnp.bfloat16)
         grad_first[...] = jnp.zeros(grad_first.shape, jnp.float32)
         grad_last[...] = jnp.zeros(grad_last.shape, jnp.float32)
 
-        def gradients(pair, carry):
-            grad_first[...] += dot_lanes(pre_grads[pair, :, body], inputs[pair, :, body])
-            grad_last[...] += dot_lanes(hiddens[pair, :, body], errors[pair, :, body])
-            return carry
-
-        lax.fori_loop(0, PAIRS, gradients, 0)
+        def columns_of(quarter):
+            return pl.ds(pl.multiple_of(quarter * 512 + 128, 128), 512)
+
+        def first_layer(pair, quarter):
+            columns = columns_of(quarter)
+            raw[pair][:, columns] = dot_rows(big_first[...], inputs[pair][:, columns])
+
+        def activate(pair, quarter):
+            columns = columns_of(quarter)
+            for part in range(8):
+                rows = slice(part * 32, (part + 1) * 32)
+                half = raw[pair][rows, columns]
+                curve = jnp.tanh(half)
+                above = 1.0 + curve
+                value = half * above
+                hiddens[pair][rows, columns] = value.astype(jnp.bfloat16)
+                slopes[pair][rows, columns] = above + value * (1.0 - curve)
+
+        def last_layer(pair, quarter):
+            columns = columns_of(quarter)
+            partial_out[pair][:, columns] = dot_rows(big_last_t[...], hiddens[pair][:, columns])
+
+        def find_errors(pair, quarter):
+            for plane in range(4):
+                x = quarter * 4 + plane
+                column = pl.multiple_of((x + 1) * 128, 128)
+                total = (
+                    partial_out[pair][0:PATCH, pl.ds(pl.multiple_of(column + 128, 128), 128)]
+                    + partial_out[pair][PATCH : 2 * PATCH, pl.ds(column, 128)]
+                    + partial_out[pair][2 * PATCH :, pl.ds(pl.multiple_of(column - 128, 128), 128)]
+                )
+                channels = []
+                for c in range(F):
+                    predicted = patch_fold(
+                        total[16 * c : 16 * c + 8], total[16 * c + 8 : 16 * c + 16], masks
+                    )
+                    row = pl.multiple_of((c * SUB + x) * 8, 8)
+                    error = weights[pair] * (predicted - targets[pair][pl.ds(row, 8), :])
+                    error = jnp.where(masks["centre"], error, 0.0)
+                    error = error.astype(jnp.bfloat16).astype(jnp.float32)
+                    channels.append(patch_stack(error, masks))
+                store_planes(errors[pair], x, channels)
+
+        def hidden_layer(pair, quarter):
+            columns = columns_of(quarter)
+            raw[pair][:, columns] = dot_rows(big_last[...], errors[pair][:, columns])
+
+        def scale(pair, quarter):
+            columns = columns_of(quarter)
+            for part in range(8):
+                rows = slice(part * 32, (part + 1) * 32)
+                product = raw[pair][rows, columns] * slopes[pair][rows, columns]
+                pre_grads[pair][rows, columns] = product.astype(jnp.bfloat16)
+
+        def gradients(pair, quarter):
+            columns = columns_of(quarter)
+            grad_first[...] += dot_lanes(pre_grads[pair][:, columns], inputs[pair][:, columns])
+            grad_last[...] += dot_lanes(hiddens[pair][:, columns], errors[pair][:, columns])
+
+        stages = (first_layer, activate, last_layer, find_errors, hidden_layer, scale, gradients)
+        for turn in range(len(stages) + PAIRS - 1):
+
+            def run(quarter, carry):
+                for pair in range(PAIRS):
+                    if 0 <= turn - pair < len(stages):
+                        stages[turn - pair](pair, quarter)
+                return carry
+
+            lax.fori_loop(0, 4, run, 0)
 
         def folded(grad, select_ref):
             total = jnp.zeros((3 * CH, 256), jnp.float32)
@@ -435,17 +427,9 @@
             pltpu.SMEM((x_devices,), jnp.int32),
             pltpu.VMEM((TCAP, 2 * SUB * F, 256), jnp.bfloat16),
             pltpu.VMEM((SUB * F * 8, 128), jnp.float32),
-            pltpu.VMEM((PAIRS * SUB * F * 8, 128), jnp.float32),
-            pltpu.VMEM((PAIRS, STACK, COLS), jnp.bfloat16),
-            pltpu.VMEM((PAIRS, STACK, COLS), jnp.bfloat16),
-            pltpu.VMEM((PAIRS, 4 * CH, COLS), jnp.bfloat16),
-            pltpu.VMEM((PAIRS, 4 * CH, COLS), jnp.bfloat16),
-            pltpu.VMEM((PAIRS, 4 * CH, COLS), jnp.float32),
-            pltpu.VMEM((PAIRS, STACK, COLS), jnp.float32),
             pltpu.VMEM((4 * CH, STACK), jnp.bfloat16),
             pltpu.VMEM((4 * CH, STACK), jnp.bfloat16),
             pltpu.VMEM((STACK, 4 * CH), jnp.bfloat16),
-            pltpu.VMEM((PAIRS, 4 * CH, COLS), jnp.float32),
             pltpu.VMEM((4 * CH, STACK), jnp.float32),
             pltpu.VMEM((4 * CH, STACK), jnp.float32),
             pltpu.VMEM((CH, 256), jnp.float32),
@@ -456,8 +440,14 @@
             pltpu.SemaphoreType.DMA((TCAP,)),
             pltpu.SemaphoreType.DMA,
             pltpu.SemaphoreType.DMA((2,)),
-        ],
-        compiler_params=pltpu.CompilerParams(vmem_limit_bytes=48 * 1024 * 1024),
+        ]
+        + [pltpu.VMEM((SUB * F * 8, 128), jnp.float32)] * PAIRS
+        + [pltpu.VMEM((STACK, COLS), jnp.bfloat16)] * (2 * PAIRS)
+        + [pltpu.VMEM((4 * CH, COLS), jnp.bfloat16)] * (2 * PAIRS)
+        + [pltpu.VMEM((4 * CH, COLS), jnp.float32)] * PAIRS
+        + [pltpu.VMEM((STACK, COLS), jnp.float32)] * PAIRS
+        + [pltpu.VMEM((4 * CH, COLS), jnp.float32)] * PAIRS,
+        compiler_params=pltpu.CompilerParams(vmem_limit_bytes=52 * 1024 * 1024),
         name="train_cubes",
     )(
         trainer_of,

time: 169 us -> 136 us (0.80)
  waiting for transfers between devices: 87.5 us -> 54.6 us
    ppermute x3, waiting for transfers between devices: 72.9 us -> 39.9 us  [on_device(): final = final + lax.ppermute(total, everyone, pairs)]
where the time goes in v7:
time: 136 us; the launch traced here: 135 us
  waiting for transfers between devices  54.6 us (40%)
  Pallas kernels  48.4 us (36%)
  starting transfers between devices  26.4 us (19%)
  other arithmetic  2.09 us (2%)
  local copies, waits for them, and re-layouts  1.82 us (1%)
  between operations  1.7 us (1%)
    ppermute x3, waiting for transfers between devices, on_device(): final = final + lax.ppermute(total, everyone, pairs)  39.9 us
    pallas_call x1, Pallas kernels, evolve(): pl.pallas_call(evolve_kernel, out_shape=jax.ShapeDtypeStruct(fields.shape...  39.6 us
    all_to_all x1, waiting for transfers between devices, on_device(): lax.all_to_all(thin, ('gx', 'gy'), split_axis=0, concat_axis=0, tiled=True)  7.45 us
    all_to_all x1, starting transfers between devices, on_device(): lax.all_to_all(thin, ('gx', 'gy'), split_axis=0, concat_axis=0, tiled=True)  7.3 us
    pallas_call x1, Pallas kernels, sample_cube(): pl.pallas_call(functools.partial(sample_kernel, y_cells, z_cells), out_sh...  5.39 us
    ppermute x3, starting transfers between devices, to_trainers(): lax.ppermute(payload, everyone, [(g * trainers + c, first_trainer + c) fo...  4.05 us
    ppermute x6, starting transfers between devices, from_line(): lax.ppermute(held, everyone, swap(apart))  4.02 us
    ppermute x1, waiting for transfers between devices, y_neighbours(): lax.ppermute(for_second, everyone, pairs(0, -1))  3.93 us
  transfers between devices with their start and end apart: 18, of which 5 were waited for; matrix products, arithmetic and copies ran while one was open for 1% of the time, Pallas kernels for 1%

profile of v7, /device:TPU:0, one launch (start us, length us, event | category | flops | bytes accessed | tf_op | source)
XLA Modules:
  0.0 135.0 jit_solution(604529514822254157)
XLA Ops:
  0.6 0.0 copy-start.2
  0.6 0.1 stack.27.place
  0.7 0.7 copy-done.3
  1.4 0.0 copy-start.4
  1.4 5.4 %sample_cube.1 = (f32[80,256]{1,0:T(8,128)S(1)}, f32[80,256]{1,0:T(8,128)S(1)}, f32[80,256]{1,0:T(8,128)S(1)}, f32[2,16,128]{2,1,0:T(8,128)S(1)}, f32[8,16,256]{...) custom-call(s32[24]{0:T(128)S(1)} %copy-done.3, s32[6]{0:T(128)S(1)} %stack.27.place, ...), custom_call_target="tpu_custom_call" | custom-call | tf_op jit(solution)/shard_map/sample_cube/pallas_call | solution.py:660
  6.8 7.3 %all-to-all-start = ((f32[8,16,256]{2,1,0:T(8,128)}), f32[8,16,256]{2,1,0:T(8,128)S(1)}, u32[]{:S(2)}, u32[]{:S(2)}) async-start(f32[8,16,256]{2,1,0:T(8,128)} %get-tuple-element.81), calls=%async_computation | async-start | bytes 262144 | tf_op jit(solution)/shard_map/all_to_all | solution.py:814
  14.2 7.5 %all-to-all-done.thin = f32[8,16,256]{2,1,0:T(8,128)S(1)} async-done(((f32[8,16,256]{2,1,0:T(8,128)}), f32[8,16,256]{2,1,0:T(8,128)S(1)}, u32[]{:S(2)}, u32[]{:S(2)}) %all-to-all-start) | async-done | bytes 131104 | tf_op jit(solution)/shard_map/all_to_all | solution.py:814
  21.6 1.6 %cube_change.1 = bf16[160,256]{1,0:T(8,128)(2,1)S(1)} custom-call(s32[24]{0:T(128)S(1)} %copy-done.3, s32[6]{0:T(128)S(1)} %stack.27.place, f32[7,64]{1,0:T(8,128)S(1)} %pad_maximum_fusion.2.closure, bf16[256,256]{1,0:T(8,128)(2,1)S(1)} %copy-done.2, f32[80,256]{1,0:T(8,128)S(1)} %get-tuple-element.77.centre, f32[80,256]{1,0:T(8,128)S(1)} %get-tuple-element.78.lower, ...), custom_call_target="tpu_custom_call" | custom-call | tf_op jit(solution)/shard_map/cube_change/pallas_call | solution.py:731
  23.2 0.7 collective-permute-start.2
  23.9 0.7 collective-permute-start.1
  24.6 2.7 %collective-permute-start = (bf16[160,256]{1,0:T(8,128)(2,1)S(1)}, bf16[160,256]{1,0:T(8,128)(2,1)S(1)}, u32[]{:S(2)}, u32[]{:S(2)}) collective-permute-start(bf16[160,256]{1,0:T(8,128)(2,1)S(1)} %cube_change.1), channel_id=1, source_target_pairs={{0,24},{1,25},{2,26},{3,27},{4,28},{5,29},{6,30},{7,31}} | collective-permute-start | bytes 245768 | tf_op jit(solution)/shard_map/ppermute | solution.py:798
  27.3 0.0 collective-permute-done.2
  27.3 0.0 collective-permute-done.1
  27.3 2.0 %collective-permute-done = bf16[160,256]{1,0:T(8,128)(2,1)S(1)} collective-permute-done((bf16[160,256]{1,0:T(8,128)(2,1)S(1)}, bf16[160,256]{1,0:T(8,128)(2,1)S(1)}, u32[]{:S(2)}, u32[]{:S(2)}) %collective-permute-start) | collective-permute-done | bytes 81952 | tf_op jit(solution)/shard_map/ppermute | solution.py:798
  29.4 0.7 collective-permute-start.8
  30.1 0.7 collective-permute-start.7
  30.8 0.7 collective-permute-start.6
  31.4 2.5 %collective-permute-start.3 = (f32[2,5,32,384]{3,2,1,0:T(8,128)S(1)}, f32[2,5,32,384]{3,2,1,0:T(8,128)S(1)}, u32[]{:S(2)}, u32[]{:S(2)}) collective-permute-start(f32[2,5,32,384]{3,2,1,0:T(8,128)S(1)} %get-tuple-element.82), channel_id=1, source_target_pairs={{0,4},{1,5},{2,6},{3,7},{4,0},{5,1},{6,2},{7,3},{8,12},{9,13},{10,... | collective-permute-start | bytes 1474568 | tf_op jit(solution)/shard_map/ppermute | solution.py:782
  33.9 0.0 collective-permute-done.8.refs_3_
  33.9 0.0 collective-permute-done.7.refs_2_
  33.9 0.0 collective-permute-done.6.refs_1_
  34.0 1.8 %pick_cubes.1 = bf16[6,160,256]{2,1,0:T(8,128)(2,1)S(1)} custom-call(s32[24]{0:T(128)S(1)} %copy-done.6, s32[6]{0:T(128)S(1)} %stack.27.place, bf16[3,160,256]{2,1,0:T(8,128)(2,1)S(1)} %pad_maximum_fusion.1.refs_0_, bf16[3,160,256]{2,1,0:T(8,128)(2,1)S(1)} %collective-permute-done.6.refs_1_, bf16[3,160,256]{2,1,0:T(8,128)(2,1)S(1)} %collective-permute-done.7.refs_2_, ...), custom_call_target="tpu_custom_call" | custom-call | tf_op jit(solution)/shard_map/pick_cubes/pallas_call | solution.py:106
  35.7 0.7 collective-permute-start.9
  36.4 0.7 slice_bitcast_fusion.1
  37.1 2.7 %collective-permute-start.5 = (f32[5,16,384]{2,1,0:T(8,128)}, f32[5,16,384]{2,1,0:T(8,128)}, u32[]{:S(2)}, u32[]{:S(2)}) collective-permute-start(f32[5,16,384]{2,1,0:T(8,128)} %get-tuple-element.130), channel_id=1, source_target_pairs={{0,3},{1,2},{2,1},{3,0},{4,7},{5,6},{6,5},{7,4},{8,11},{9,10},{10,... | collective-permute-start | bytes 368648 | tf_op jit(solution)/shard_map/ppermute | solution.py:789
  39.8 1.9 %collective-permute-start.4 = (f32[5,16,384]{2,1,0:T(8,128)S(1)}, f32[5,16,384]{2,1,0:T(8,128)}, u32[]{:S(2)}, u32[]{:S(2)}) collective-permute-start(f32[5,16,384]{2,1,0:T(8,128)S(1)} %get-tuple-element.131), channel_id=1, source_target_pairs={{0,1},{1,0},{2,3},{3,2},{4,5},{5,4},{6,7},{7,6},{8,9},{9,8},{10,11... | collective-permute-start | bytes 368648 | tf_op jit(solution)/shard_map/ppermute | solution.py:788
  41.8 0.1 fusion
  41.8 0.1 reshape.33
  41.9 0.2 slice.39
  42.2 3.9 %collective-permute-done.5 = f32[5,16,384]{2,1,0:T(8,128)} collective-permute-done((f32[5,16,384]{2,1,0:T(8,128)}, f32[5,16,384]{2,1,0:T(8,128)}, u32[]{:S(2)}, u32[]{:S(2)}) %collective-permute-start.5) | collective-permute-done | bytes 122912 | tf_op jit(solution)/shard_map/ppermute | solution.py:789
  46.1 1.2 collective-permute-done.4
  47.3 0.0 collective-permute-done.3
  47.3 0.0 collective-permute-done.9
  47.3 39.6 %conditional.1 = (f32[17280]{0:T(1024)S(1)}, f32[1,5,16,32,384]{4,3,2,1,0:T(8,128)}) conditional(s32[]{:T(128)} %convert_element_type.6, (f32[7,64]{1,0:T(8,128)S(1)}, s32[6]{0:T(128)S(1)}, f32[5,16,32,384]{3,2,1,0:T(8,128)}, f32[2,5,32,384]{3,2,1,0:T(8,128)S(1)}, f32[5,16,384]{2,1,0:T(8,128)}, /*index=5*/f32[5,16,384]{2,1,0:T(8,128)}) %tuple.37, ...), branch_computations={%region_0.1_spmd, %region_1.2_spmd.clone} | conditional | flops 17280 | bytes 4478024 | solution.py:845
  47.3 39.6 %evolve_brick.1 = f32[5,16,32,384]{3,2,1,0:T(8,128)} custom-call(f32[7,64]{1,0:T(8,128)S(1)} %get-tuple-element.37.closure, s32[6]{0:T(128)S(1)} %get-tuple-element.38.place, f32[5,16,32,384]{3,2,1,0:T(8,128)} %get-tuple-element.39.fields, f32[2,5,32,384]{3,2,1,0:T(8,128)S(1)} %get-tuple-element.40.x_halo, f32[5,16,384]{2,1,0:T(8,128)} %get-tuple-element.41.y_first, ...), custom_call_target="tpu_custom_call" | custom-call | tf_op jit(solution)/shard_map/cond/branch_0_fun/evolve_brick/pallas_call | solution.py:523
  87.0 0.7 collective-permute-start.12
  87.6 0.7 collective-permute-start.11
  88.3 0.7 collective-permute-start.10
  89.0 0.0 collective-permute-done.12
  89.0 0.0 collective-permute-done.10
  89.1 0.7 collective-permute-start.13
  89.8 0.7 collective-permute-start.16
  90.4 0.7 collective-permute-start.15
  91.1 1.3 collective-permute-start.14
  92.4 0.0 collective-permute-done.16
  92.4 39.9 %collective-permute-done.14 = f32[17280]{0:T(1024)S(1)} collective-permute-done((f32[17280]{0:T(1024)S(1)}, f32[17280]{0:T(1024)S(1)}, u32[]{:S(2)}, u32[]{:S(2)}) %collective-permute-start.14) | collective-permute-done | bytes 69152 | tf_op jit(solution)/shard_map/ppermute | solution.py:852
  132.3 0.6 multiply_reduce_fusion
  133.6 1.4 %multiply_subtract_fusion = (f32[540]{0:T(1024)}, f32[540]{0:T(1024)}) fusion(f32[17280]{0:T(1024)S(1)} %copy-done.4, s32[]{:T(128)S(6)} %select_n.13, f32[]{:T(128)S(6)} %sqrt.3, f32[17280]{0:T(1024)S(1)} %get-tuple-element.129, f32[17280]{0:T(1024)} %param.18), kind=kLoop, calls=%fused_computation.9 | loop fusion | flops 2700 | bytes 10808 | tf_op jit(solution)/shard_map/sub | solution.py:861
  (23 shorter events, 0.1 us)
Async XLA Ops:
  0.6 21.0 %copy-start.2 = (bf16[256,256]{1,0:T(8,128)(2,1)S(1)}, bf16[256,256]{1,0:T(8,128)(2,1)}, u32[]{:S(2)}) copy-start(bf16[256,256]{1,0:T(8,128)(2,1)} %constant.54.clone.order) | copy-start | bytes 393220
  0.7 0.7 copy-start.3
  1.4 12.7 %copy-start.5 = (f32[64,5]{0,1:T(8,128)S(1)}, f32[64,5]{0,1:T(8,128)}, u32[]{:S(2)}) copy-start(f32[64,5]{0,1:T(8,128)} %param.14) | copy-start | bytes 3844
  1.4 12.7 %copy-start.8 = (f32[64]{0:T(128)S(1)}, f32[64]{0:T(128)}, u32[]{:S(2)}) copy-start(f32[64]{0:T(128)} %param.15) | copy-start | bytes 772
  1.4 12.8 %copy-start.7 = (f32[64]{0:T(128)S(1)}, f32[64]{0:T(128)}, u32[]{:S(2)}) copy-start(f32[64]{0:T(128)} %param.16) | copy-start | bytes 772
  1.4 32.6 %copy-start.6 = (s32[24]{0:T(128)S(1)}, s32[24]{0:T(128)}, u32[]{:S(2)}) copy-start(s32[24]{0:T(128)} %trainer_of.1) | copy-start | bytes 292
  1.4 40.3 %copy-start.4 = (f32[17280]{0:T(1024)S(1)}, f32[17280]{0:T(1024)}, u32[]{:S(2)}) copy-start(f32[17280]{0:T(1024)} %param.17) | copy-start | bytes 207364
  6.8 14.8 %all-to-all-start = ((f32[8,16,256]{2,1,0:T(8,128)}), f32[8,16,256]{2,1,0:T(8,128)S(1)}, u32[]{:S(2)}, u32[]{:S(2)}) async-start(f32[8,16,256]{2,1,0:T(8,128)} %get-tuple-element.81), calls=%async_computation | async-start | bytes 262144 | tf_op jit(solution)/shard_map/all_to_all | solution.py:814
  23.2 4.1 %collective-permute-start.2 = (bf16[160,256]{1,0:T(8,128)(2,1)S(1)}, bf16[160,256]{1,0:T(8,128)(2,1)S(1)}, u32[]{:S(2)}, u32[]{:S(2)}) collective-permute-start(bf16[160,256]{1,0:T(8,128)(2,1)S(1)} %cube_change.1), channel_id=1, source_target_pairs={{16,24},{17,25},{18,26},{19,27},{20,28},{21,29},{22,30},{23,31}} | collective-permute-start | bytes 245768 | tf_op jit(solution)/shard_map/ppermute | solution.py:798
  23.9 3.4 %collective-permute-start.1 = (bf16[160,256]{1,0:T(8,128)(2,1)S(1)}, bf16[160,256]{1,0:T(8,128)(2,1)S(1)}, u32[]{:S(2)}, u32[]{:S(2)}) collective-permute-start(bf16[160,256]{1,0:T(8,128)(2,1)S(1)} %cube_change.1), channel_id=1, source_target_pairs={{8,24},{9,25},{10,26},{11,27},{12,28},{13,29},{14,30},{15,31}} | collective-permute-start | bytes 245768 | tf_op jit(solution)/shard_map/ppermute | solution.py:798
  24.6 4.8 %collective-permute-start = (bf16[160,256]{1,0:T(8,128)(2,1)S(1)}, bf16[160,256]{1,0:T(8,128)(2,1)S(1)}, u32[]{:S(2)}, u32[]{:S(2)}) collective-permute-start(bf16[160,256]{1,0:T(8,128)(2,1)S(1)} %cube_change.1), channel_id=1, source_target_pairs={{0,24},{1,25},{2,26},{3,27},{4,28},{5,29},{6,30},{7,31}} | collective-permute-start | bytes 245768 | tf_op jit(solution)/shard_map/ppermute | solution.py:798
  29.4 4.5 %collective-permute-start.8 = (bf16[3,160,256]{2,1,0:T(8,128)(2,1)S(1)}, bf16[3,160,256]{2,1,0:T(8,128)(2,1)S(1)}, u32[]{:S(2)}, u32[]{:S(2)}) collective-permute-start(bf16[3,160,256]{2,1,0:T(8,128)(2,1)S(1)} %pad_maximum_fusion.1.refs_0_), channel_id=1, source_target_pairs={{24,27},{25,26},{26,25},{27,24},{28,31},{29,30},{30,29},{31,28}} | collective-permute-start | bytes 737288 | tf_op jit(solution)/shard_map/ppermute | solution.py:808
  30.1 3.9 %collective-permute-start.7 = (bf16[3,160,256]{2,1,0:T(8,128)(2,1)S(1)}, bf16[3,160,256]{2,1,0:T(8,128)(2,1)S(1)}, u32[]{:S(2)}, u32[]{:S(2)}) collective-permute-start(bf16[3,160,256]{2,1,0:T(8,128)(2,1)S(1)} %pad_maximum_fusion.1.refs_0_), channel_id=1, source_target_pairs={{24,26},{25,27},{26,24},{27,25},{28,30},{29,31},{30,28},{31,29}} | collective-permute-start | bytes 737288 | tf_op jit(solution)/shard_map/ppermute | solution.py:808
  30.8 3.2 %collective-permute-start.6 = (bf16[3,160,256]{2,1,0:T(8,128)(2,1)S(1)}, bf16[3,160,256]{2,1,0:T(8,128)(2,1)S(1)}, u32[]{:S(2)}, u32[]{:S(2)}) collective-permute-start(bf16[3,160,256]{2,1,0:T(8,128)(2,1)S(1)} %pad_maximum_fusion.1.refs_0_), channel_id=1, source_target_pairs={{24,25},{25,24},{26,27},{27,26},{28,29},{29,28},{30,31},{31,30}} | collective-permute-start | bytes 737288 | tf_op jit(solution)/shard_map/ppermute | solution.py:808
  31.4 15.9 %collective-permute-start.3 = (f32[2,5,32,384]{3,2,1,0:T(8,128)S(1)}, f32[2,5,32,384]{3,2,1,0:T(8,128)S(1)}, u32[]{:S(2)}, u32[]{:S(2)}) collective-permute-start(f32[2,5,32,384]{3,2,1,0:T(8,128)S(1)} %get-tuple-element.82), channel_id=1, source_target_pairs={{0,4},{1,5},{2,6},{3,7},{4,0},{5,1},{6,2},{7,3},{8,12},{9,13},{10,... | collective-permute-start | bytes 1474568 | tf_op jit(solution)/shard_map/ppermute | solution.py:782
  35.7 11.6 %collective-permute-start.9 = (bf16[6,160,256]{2,1,0:T(8,128)(2,1)S(1)}, bf16[6,160,256]{2,1,0:T(8,128)(2,1)S(1)}, u32[]{:S(2)}, u32[]{:S(2)}) collective-permute-start(bf16[6,160,256]{2,1,0:T(8,128)(2,1)S(1)} %pick_cubes.1), channel_id=1, source_target_pairs={{24,28},{25,29},{26,30},{27,31},{28,24},{29,25},{30,26},{31,27}} | collective-permute-start | bytes 1474568 | tf_op jit(solution)/shard_map/ppermute | solution.py:811
  37.1 9.0 %collective-permute-start.5 = (f32[5,16,384]{2,1,0:T(8,128)}, f32[5,16,384]{2,1,0:T(8,128)}, u32[]{:S(2)}, u32[]{:S(2)}) collective-permute-start(f32[5,16,384]{2,1,0:T(8,128)} %get-tuple-element.130), channel_id=1, source_target_pairs={{0,3},{1,2},{2,1},{3,0},{4,7},{5,6},{6,5},{7,4},{8,11},{9,10},{10,... | collective-permute-start | bytes 368648 | tf_op jit(solution)/shard_map/ppermute | solution.py:789
  39.8 7.5 %collective-permute-start.4 = (f32[5,16,384]{2,1,0:T(8,128)S(1)}, f32[5,16,384]{2,1,0:T(8,128)}, u32[]{:S(2)}, u32[]{:S(2)}) collective-permute-start(f32[5,16,384]{2,1,0:T(8,128)S(1)} %get-tuple-element.131), channel_id=1, source_target_pairs={{0,1},{1,0},{2,3},{3,2},{4,5},{5,4},{6,7},{7,6},{8,9},{9,8},{10,11... | collective-permute-start | bytes 368648 | tf_op jit(solution)/shard_map/ppermute | solution.py:788
  87.0 2.0 %collective-permute-start.12 = (f32[17280]{0:T(1024)S(1)}, f32[17280]{0:T(1024)S(1)}, u32[]{:S(2)}, u32[]{:S(2)}) collective-permute-start(f32[17280]{0:T(1024)S(1)} %get-tuple-element.88), channel_id=1, source_target_pairs={{24,27},{25,26},{26,25},{27,24},{28,31},{29,30},{30,29},{31,28}} | collective-permute-start | bytes 207368 | tf_op jit(solution)/shard_map/ppermute | solution.py:808
  87.6 1.4 %collective-permute-start.11 = (f32[17280]{0:T(1024)S(1)}, f32[17280]{0:T(1024)S(1)}, u32[]{:S(2)}, u32[]{:S(2)}) collective-permute-start(f32[17280]{0:T(1024)S(1)} %get-tuple-element.88), channel_id=1, source_target_pairs={{24,26},{25,27},{26,24},{27,25},{28,30},{29,31},{30,28},{31,29}} | collective-permute-start | bytes 207368 | tf_op jit(solution)/shard_map/ppermute | solution.py:808
  88.3 0.7 collective-permute-start.10
  89.1 0.7 collective-permute-start.13
  89.8 2.7 %collective-permute-start.16 = (f32[17280]{0:T(1024)S(1)}, f32[17280]{0:T(1024)S(1)}, u32[]{:S(2)}, u32[]{:S(2)}) collective-permute-start(f32[17280]{0:T(1024)S(1)} %add.48), channel_id=1, source_target_pairs={{24,16},{25,17},{26,18},{27,19},{28,20},{29,21},{30,22},{31,23}} | collective-permute-start | bytes 207368 | tf_op jit(solution)/shard_map/ppermute | solution.py:852
  90.4 2.0 %collective-permute-start.15 = (f32[17280]{0:T(1024)S(1)}, f32[17280]{0:T(1024)S(1)}, u32[]{:S(2)}, u32[]{:S(2)}) collective-permute-start(f32[17280]{0:T(1024)S(1)} %add.48), channel_id=1, source_target_pairs={{24,8},{25,9},{26,10},{27,11},{28,12},{29,13},{30,14},{31,15}} | collective-permute-start | bytes 207368 | tf_op jit(solution)/shard_map/ppermute | solution.py:852
  91.1 41.2 %collective-permute-start.14 = (f32[17280]{0:T(1024)S(1)}, f32[17280]{0:T(1024)S(1)}, u32[]{:S(2)}, u32[]{:S(2)}) collective-permute-start(f32[17280]{0:T(1024)S(1)} %add.48), channel_id=1, source_target_pairs={{24,0},{25,1},{26,2},{27,3},{28,4},{29,5},{30,6},{31,7}} | collective-permute-start | bytes 207368 | tf_op jit(solution)/shard_map/ppermute | solution.py:852

commit v8 on v7

--- a/solution.py
+++ b/solution.py
@@ -34,8 +34,8 @@
 
 def patch_position(row):
     group, py, pz = row // 4, row // 2 % 2, row % 2
-    ypos = py + 1 if group in (0, 1) else (3 if py == 0 else 0)
-    zpos = pz + 1 if group in (0, 2) else (3 if pz == 0 else 0)
+    ypos = py + 1 if group in (0, 2) else (3 if py == 0 else 0)
+    zpos = pz + 1 if group in (0, 1) else (3 if pz == 0 else 0)
     return ypos - 1, zpos - 1
 
 
@@ -124,40 +124,35 @@
 def patch_masks():
     row = lax.broadcasted_iota(jnp.int32, (8, 128), 0)
     lane = lax.broadcasted_iota(jnp.int32, (8, 128), 1)
+    z, y = lane % 8, lane // 8 % 8
+    even_z, even_y = row % 2 == 0, row // 2 % 2 == 0
     return {
-        "pz0": row % 2 == 0,
-        "py0": row // 2 % 2 == 0,
         "centre": row < 4,
-        "z_first": lane % 8 == 0,
-        "z_last": lane % 8 == 7,
-        "y_first": lane // 8 % 8 == 0,
-        "y_last": lane // 8 % 8 == 7,
+        "even_z": even_z,
+        "even_y": even_y,
+        "gather_z": jnp.where(even_z, z, 7 - z) < 7,
+        "gather_y": jnp.where(even_y, y, 7 - y) < 7,
+        "scatter_z": jnp.where(even_z, z, 7 - z) > 0,
+        "scatter_y": jnp.where(even_y, y, 7 - y) > 0,
     }
 
 
-def edge_shift(values, step, parity_zero, first, last, forward):
-    before = jnp.where(first, 0.0, pltpu.roll(values, step, 1))
-    after = jnp.where(last, 0.0, pltpu.roll(values, 128 - step, 1))
-    if forward:
-        return jnp.where(parity_zero, after, before)
-    return jnp.where(parity_zero, before, after)
+def edge_shift(values, step, even, inside, gather):
+    before, after = pltpu.roll(values, step, 1), pltpu.roll(values, 128 - step, 1)
+    moved = jnp.where(even, after, before) if gather else jnp.where(even, before, after)
+    return jnp.where(inside, moved, 0.0)
 
 
 def patch_stack(rows, masks):
-    both = rows + pltpu.roll(rows, 4, 0)
-    z_edge = edge_shift(both, 1, masks["pz0"], masks["z_first"], masks["z_last"], True)
-    upper = jnp.where(masks["centre"], both, z_edge)
-    lower = edge_shift(upper, 8, masks["py0"], masks["y_first"], masks["y_last"], True)
-    return upper, lower
+    both = jnp.where(masks["centre"], rows, pltpu.roll(rows, 4, 0))
+    y_edge = edge_shift(both, 8, masks["even_y"], masks["gather_y"], True)
+    upper = jnp.where(masks["centre"], both, y_edge)
+    return upper, edge_shift(upper, 1, masks["even_z"], masks["gather_z"], True)
 
 
 def patch_fold(upper, lower, masks):
-    def fold_z(values):
-        moved = edge_shift(values, 1, masks["pz0"], masks["z_first"], masks["z_last"], False)
-        return values + pltpu.roll(moved, 4, 0)
-
-    shifted = edge_shift(fold_z(lower), 8, masks["py0"], masks["y_first"], masks["y_last"], False)
-    return fold_z(upper) + shifted
+    line = upper + edge_shift(lower, 1, masks["even_z"], masks["scatter_z"], False)
+    return line + pltpu.roll(edge_shift(line, 8, masks["even_y"], masks["scatter_y"], False), 4, 0)
 
 
 def store_planes(ref, x, channels):
@@ -177,7 +172,6 @@
         slots,
         picked,
         cubes,
-        table,
         big_first,
         big_last,
         big_last_t,
@@ -193,8 +187,8 @@
         select_sems,
         *pair_refs,
     ) = refs[10 + sources :]
-    targets, inputs, errors, hiddens, pre_grads, slopes, partial_out, raw = [
-        pair_refs[kind * PAIRS : (kind + 1) * PAIRS] for kind in range(8)
+    targets, tables, inputs, errors, hiddens, pre_grads, slopes, partial_out, raw = [
+        pair_refs[kind * PAIRS : (kind + 1) * PAIRS] for kind in range(9)
     ]
 
     field_in = pltpu.make_async_copy(fields_ref, brick, field_sem)
@@ -252,7 +246,7 @@
     for ref in partial_out:
         ref[:, :128] = jnp.zeros((STACK, 128), jnp.float32)
         ref[:, COLS - 128 :] = jnp.zeros((STACK, 128), jnp.float32)
-    for ref in (table, *targets):
+    for ref in (*tables, *targets):
         ref[...] = jnp.zeros(ref.shape, ref.dtype)
     lane = lax.broadcasted_iota(jnp.int32, (8, 128), 1)
     full_weight = 2.0 * (1.0 / (jnp.full((8, 128), count, jnp.int32).astype(jnp.float32) * CELLS))
@@ -260,7 +254,7 @@
         jnp.where(lane // 64 + 2 * pair < count, full_weight, 0.0) for pair in range(PAIRS)
     ]
     start_first = first_ref[...].astype(jnp.bfloat16).astype(jnp.float32)
-    start_last = last_ref[...].astype(jnp.bfloat16).astype(jnp.float32)
+    start_last = last_ref[...].T.astype(jnp.bfloat16).astype(jnp.float32)
     now_first[...] = start_first
     now_last[...] = start_last
 
@@ -282,7 +276,7 @@
     for pair in range(PAIRS):
 
         def put_input(cell, values):
-            table[pl.ds(cell, SUB * F, 8), :] = values
+            tables[pair][pl.ds(cell, SUB * F, 8), :] = values
 
         def put_target(cell, values):
             targets[pair][pl.ds(cell, SUB * F, 8), :] = values
@@ -290,15 +284,18 @@
         spread_rows(pair, 0, put_input)
         spread_rows(pair, 1, put_target)
 
-        def stack_plane(x, carry):
-            channels = [
-                patch_stack(table[pl.ds(pl.multiple_of((c * SUB + x) * 8, 8), 8), :], masks)
-                for c in range(F)
-            ]
-            store_planes(inputs[pair], x, channels)
-            return carry
-
-        lax.fori_loop(0, SUB, stack_plane, 0, unroll=8)
+    def stack_planes(quarter, carry):
+        for pair in range(PAIRS):
+            for plane in range(4):
+                x = quarter * 4 + plane
+                channels = [
+                    patch_stack(tables[pair][pl.ds(pl.multiple_of((c * SUB + x) * 8, 8), 8), :], masks)
+                    for c in range(F)
+                ]
+                store_planes(inputs[pair], x, channels)
+        return carry
+
+    lax.fori_loop(0, 4, stack_planes, 0)
 
     for copy in select_copies:
         copy.wait()
@@ -355,8 +352,6 @@
                     )
                     row = pl.multiple_of((c * SUB + x) * 8, 8)
                     error = weights[pair] * (predicted - targets[pair][pl.ds(row, 8), :])
-                    error = jnp.where(masks["centre"], error, 0.0)
-                    error = error.astype(jnp.bfloat16).astype(jnp.float32)
                     channels.append(patch_stack(error, masks))
                 store_planes(errors[pair], x, channels)
 
@@ -404,11 +399,11 @@
 
     lax.fori_loop(0, INNER, train_step, 0)
     delta_first[...] = start_first - now_first[...]
-    delta_last[...] = start_last - now_last[...]
+    delta_last[...] = (start_last - now_last[...]).T
     field_out.wait()
 
 
-def train_cubes(trainer_of, place, first, last, arrived, fields, y_devices, x_devices):
+def train_cubes(trainer_of, place, first, last, selects, arrived, fields, y_devices, x_devices):
     vmem = pl.BlockSpec(memory_space=pltpu.VMEM)
     smem = pl.BlockSpec(memory_space=pltpu.SMEM)
     anywhere = pl.BlockSpec(memory_space=pl.ANY)
@@ -417,7 +412,7 @@
         functools.partial(train_kernel, y_devices, x_devices),
         out_shape=(
             jax.ShapeDtypeStruct((CH, 256), jnp.float32),
-            jax.ShapeDtypeStruct((CH, 256), jnp.float32),
+            jax.ShapeDtypeStruct((256, CH), jnp.float32),
             jax.ShapeDtypeStruct(fields.shape, fields.dtype),
         ),
         in_specs=[smem] * 2 + [vmem] * 2 + [hbm] * 2 + [anywhere] * len(arrived) + [hbm],
@@ -426,7 +421,6 @@
             pltpu.SMEM((2, TCAP), jnp.int32),
             pltpu.SMEM((x_devices,), jnp.int32),
             pltpu.VMEM((TCAP, 2 * SUB * F, 256), jnp.bfloat16),
-            pltpu.VMEM((SUB * F * 8, 128), jnp.float32),
             pltpu.VMEM((4 * CH, STACK), jnp.bfloat16),
             pltpu.VMEM((4 * CH, STACK), jnp.bfloat16),
             pltpu.VMEM((STACK, 4 * CH), jnp.bfloat16),
@@ -441,7 +435,7 @@
             pltpu.SemaphoreType.DMA,
             pltpu.SemaphoreType.DMA((2,)),
         ]
-        + [pltpu.VMEM((SUB * F * 8, 128), jnp.float32)] * PAIRS
+        + [pltpu.VMEM((SUB * F * 8, 128), jnp.float32)] * (2 * PAIRS)
         + [pltpu.VMEM((STACK, COLS), jnp.bfloat16)] * (2 * PAIRS)
         + [pltpu.VMEM((4 * CH, COLS), jnp.bfloat16)] * (2 * PAIRS)
         + [pltpu.VMEM((4 * CH, COLS), jnp.float32)] * PAIRS
@@ -454,8 +448,7 @@
         place,
         first,
         last,
-        jnp.asarray(SELECT_FIRST, jnp.bfloat16),
-        jnp.asarray(SELECT_LAST, jnp.bfloat16),
+        *selects,
         *arrived,
         fields,
     )
@@ -551,6 +544,90 @@
     return lax.rem(lax.div(block, z_blocks), y_cells // SUB) * SUB, lax.rem(block, z_blocks) * SUB
 
 
+def thin_kernel(
+    y_cells, z_cells, sample_block, place, rows_ref, lines_ref, thin, x_buffer, y_buffer, x_sems, y_sems
+):
+    def corner(x_step, y_step):
+        return corner_of(sample_block, place, x_step, y_step, y_cells, z_cells)
+
+    lane = lax.broadcasted_iota(jnp.int32, (SUB, 128), 1)
+    signs = (-1, 1)
+    copies = []
+    for side, sign in enumerate(signs):
+        z_x, z_y = corner(sign, 0)[1], corner(0, sign)[1]
+        x, y = side * (SUB - 1), side * (y_cells - 8)
+        for field in range(F):
+            copies.append(
+                pltpu.make_async_copy(
+                    rows_ref.at[
+                        pl.ds((field * SUB + x) * y_cells, y_cells),
+                        pl.ds(pl.multiple_of(lax.div(z_x, 128) * 128, 128), 128),
+                    ],
+                    x_buffer.at[pl.ds((side * 8 + field) * y_cells, y_cells)],
+                    x_sems.at[side, field],
+                )
+            )
+        copies.append(
+            pltpu.make_async_copy(
+                lines_ref.at[:, pl.ds(y, 8), pl.ds(pl.multiple_of(lax.div(z_y, 128) * 128, 128), 128)],
+                y_buffer.at[side],
+                y_sems.at[side],
+            )
+        )
+    for copy in copies:
+        copy.start()
+    thin[...] = jnp.zeros(thin.shape, thin.dtype)
+    for copy in copies:
+        copy.wait()
+
+    def moved(values, z, lane_start):
+        return pltpu.roll(values, lax.rem(lane_start - lax.rem(z, 128) + 256, 128), 1)
+
+    for side, sign in enumerate(signs):
+        z = corner(0, sign)[1]
+        total = jnp.zeros((SUB, 128), jnp.float32)
+        for field in range(F):
+            part = y_buffer[side, field * SUB : (field + 1) * SUB, side * 7, :]
+            total = jnp.where(lane // SUB == field, moved(part, z, field * SUB), total)
+        thin[column_of(place, 0, sign), :, side * 128 : (side + 1) * 128] = total
+    for side, sign in enumerate(signs):
+        y, z = corner(sign, 0)
+        for half in range(2):
+            total = jnp.zeros((8, 128), jnp.float32)
+            for step in range(8):
+                row = side * 8 * y_cells + y + half * 8 + step
+                part = moved(x_buffer[pl.ds(row, 8, y_cells), :], z, step * SUB)
+                total = jnp.where(lane[:8] // SUB == step, part, total)
+            at = (column_of(place, sign, 0), slice(side * 8, side * 8 + 8), slice(half * 128, half * 128 + 128))
+            thin[at] = total
+
+
+def thin_faces(sample_block, place, brick, columns):
+    fields, x_cells, y_cells, z_cells = brick.shape
+    vmem = pl.BlockSpec(memory_space=pltpu.VMEM)
+    smem = pl.BlockSpec(memory_space=pltpu.SMEM)
+    hbm = pl.BlockSpec(memory_space=pltpu.HBM)
+    return pl.pallas_call(
+        functools.partial(thin_kernel, y_cells, z_cells),
+        out_shape=jax.ShapeDtypeStruct((columns, SUB, 256), jnp.float32),
+        in_specs=[smem, smem, hbm, hbm],
+        out_specs=vmem,
+        scratch_shapes=[
+            pltpu.VMEM((16 * y_cells, 128), jnp.float32),
+            pltpu.VMEM((2, fields * x_cells, 8, 128), jnp.float32),
+            pltpu.SemaphoreType.DMA((2, fields)),
+            pltpu.SemaphoreType.DMA((2,)),
+        ],
+        compiler_params=pltpu.CompilerParams(vmem_limit_bytes=16 * 1024 * 1024),
+        name="thin_faces",
+    )(
+        sample_block,
+        place,
+        brick.reshape(fields * x_cells * y_cells, z_cells),
+        brick.reshape(fields * x_cells, y_cells, z_cells),
+    )
+
+
 def sample_kernel(
     y_cells,
     z_cells,
@@ -561,7 +638,6 @@
     lower,
     upper,
     own_rows,
-    thin,
     x_edges,
     y_edges,
     windows,
@@ -620,20 +696,6 @@
 
     own_rows[0] = y_row(jnp.maximum(y_start - 1, 0), z_start)
     own_rows[1] = y_row(jnp.minimum(y_start + SUB, y_cells - 1), z_start)
-    thin[...] = jnp.zeros(thin.shape, thin.dtype)
-    thin[column_of(place, 0, -1), :, :128] = y_row(0, corner(0, -1)[1])
-    thin[column_of(place, 0, 1), :, 128:] = y_row(y_cells - 1, corner(0, 1)[1])
-    lane = lane[:8]
-    for face, (x, sign) in enumerate(((0, -1), (SUB - 1, 1))):
-        y_there, z_there = corner(sign, 0)
-        for half in range(2):
-            total = jnp.zeros((8, 128), jnp.float32)
-            for step in range(8):
-                row = x * rows_of_x + y_there + half * 8 + step
-                part = piece(row, 8, rows_of_field, z_there, step * SUB)
-                total = jnp.where(lane // SUB == step, part, total)
-            at = (column_of(place, sign, 0), slice(face * 8, face * 8 + 8), slice(half * 128, half * 128 + 128))
-            thin[at] = total
     up_first = lax.rem(place[2], 2) == 0
     for side in range(2):
         y = jnp.where(up_first == (side == 0), y_cells - 1, 0)
@@ -650,7 +712,7 @@
                 x_edges[side, field, :, w * 128 : (w + 1) * 128] = windows[pl.ds(start, rows_of_x), :]
 
 
-def sample_cube(sample_block, place, brick, columns):
+def sample_cube(sample_block, place, brick):
     fields, x_cells, y_cells, z_cells = brick.shape
     vmem = pl.BlockSpec(memory_space=pltpu.VMEM)
     smem = pl.BlockSpec(memory_space=pltpu.SMEM)
@@ -664,17 +726,17 @@
             cube,
             cube,
             jax.ShapeDtypeStruct((2, SUB, 128), jnp.float32),
-            jax.ShapeDtypeStruct((columns, SUB, 256), jnp.float32),
             jax.ShapeDtypeStruct((2, fields, y_cells, z_cells), jnp.float32),
             jax.ShapeDtypeStruct((2, fields, x_cells, z_cells), jnp.float32),
         ),
         in_specs=[smem, smem, hbm],
-        out_specs=(vmem,) * 7,
+        out_specs=(vmem,) * 6,
         scratch_shapes=[
-            pltpu.VMEM((z_cells // 128 * rows + 4 * x_cells * y_cells, 128), jnp.float32),
+            pltpu.VMEM((z_cells // 128 * rows, 128), jnp.float32),
             pltpu.SemaphoreType.DMA((z_cells // 128,)),
         ],
         compiler_params=pltpu.CompilerParams(vmem_limit_bytes=16 * 1024 * 1024),
+        cost_estimate=pl.CostEstimate(flops=0, bytes_accessed=16_000_000, transcendentals=0),
         name="sample_cube",
     )(sample_block, place, brick.reshape(rows, z_cells))
 
@@ -810,7 +872,8 @@
     def across(apart, held):
         return lax.ppermute(held, everyone, swap(apart * y_devices))
 
-    *cube, thin, x_edges, y_edges = sample_cube(sample_block, place, brick, trainers)
+    thin = thin_faces(sample_block, place, brick, trainers)
+    *cube, x_edges, y_edges = sample_cube(sample_block, place, brick)
     thin = lax.all_to_all(thin, ("gx", "gy"), split_axis=0, concat_axis=0, tiled=True)
     payload = cube_change(sample_block, place, closure, cube, thin, y_cells, z_cells)
     landed = to_trainers(payload)
@@ -825,16 +888,18 @@
 
     first_count = CH * TAPS * F
     first = jnp.pad(master[:first_count].reshape(CH, TAPS * F), ((0, 0), (0, 256 - TAPS * F)))
-    last = jnp.pad(master[first_count:].reshape(TAPS * F, CH).T, ((0, 0), (0, 256 - TAPS * F)))
-
-    first, last = lax.optimization_barrier((first, last))
+    last = jnp.pad(master[first_count:].reshape(TAPS * F, CH), ((0, 256 - TAPS * F), (0, 0)))
+
+    first, last, *selects = lax.optimization_barrier(
+        (first, last, jnp.asarray(SELECT_FIRST, jnp.bfloat16), jnp.asarray(SELECT_LAST, jnp.bfloat16))
+    )
 
     def train_here():
         delta_first, delta_last, new_brick = train_cubes(
-            sample_trainer, place, first, last, arrived, brick, y_devices, x_devices
+            sample_trainer, place, first, last, selects, arrived, brick, y_devices, x_devices
         )
         delta = jnp.concatenate(
-            [delta_first[:, : TAPS * F].reshape(-1), delta_last[:, : TAPS * F].T.reshape(-1)]
+            [delta_first[:, : TAPS * F].reshape(-1), delta_last[: TAPS * F].reshape(-1)]
         )
         return delta, new_brick
 

time: 136 us -> 131 us (0.963)
  waiting for transfers between devices: 54.6 us -> 44.6 us
  starting transfers between devices: 26.4 us -> 29.2 us
  Pallas kernels: 48.4 us -> 50.4 us
    ppermute x3, waiting for transfers between devices: 39.9 us -> 35.2 us  [on_device(): final = final + lax.ppermute(total, everyone, pairs)]
    all_to_all x1, waiting for transfers between devices: 7.45 us -> 2.87 us  [on_device(): lax.all_to_all(thin, ('gx', 'gy'), split_axis=0, concat_axis=0, tiled=True)]
    pallas_call x0 -> x1, Pallas kernels: none -> 2.78 us  [thin_faces(): pl.pallas_call(functools.partial(thin_kernel, y_cells, z_cells), out_shap...]
    ppermute x1, starting transfers between devices: 2.69 us -> 4.58 us  [y_neighbours(): lax.ppermute(for_second, everyone, pairs(0, -1))]
    ppermute x1, waiting for transfers between devices: 3.93 us -> 2.09 us  [y_neighbours(): lax.ppermute(for_second, everyone, pairs(0, -1))]
  transfers between devices with their start and end apart: 18 -> 18, of which waited for: 5 -> 5; matrix products, arithmetic and copies ran while one was open for 1% -> 1% of each run, Pallas kernels for 1% -> 5%
where the time goes in v8:
time: 131 us; the launch traced here: 130 us
  Pallas kernels  50.4 us (38%)
  waiting for transfers between devices  44.6 us (34%)
  starting transfers between devices  29.2 us (22%)
  other arithmetic  2.09 us (2%)
  local copies, waits for them, and re-layouts  1.84 us (1%)
  between operations  1.77 us (1%)
    pallas_call x1, Pallas kernels, evolve(): pl.pallas_call(evolve_kernel, out_shape=jax.ShapeDtypeStruct(fields.shape...  39.7 us
    ppermute x3, waiting for transfers between devices, on_device(): final = final + lax.ppermute(total, everyone, pairs)  35.2 us
    all_to_all x1, starting transfers between devices, on_device(): lax.all_to_all(thin, ('gx', 'gy'), split_axis=0, concat_axis=0, tiled=True)  7.42 us
    ppermute x1, starting transfers between devices, y_neighbours(): lax.ppermute(for_second, everyone, pairs(0, -1))  4.58 us
    pallas_call x1, Pallas kernels, sample_cube(): pl.pallas_call(functools.partial(sample_kernel, y_cells, z_cells), out_sh...  4.54 us
    ppermute x3, starting transfers between devices, to_trainers(): lax.ppermute(payload, everyone, [(g * trainers + c, first_trainer + c) fo...  4.05 us
    ppermute x6, starting transfers between devices, from_line(): lax.ppermute(held, everyone, swap(apart))  4.02 us
    all_to_all x1, waiting for transfers between devices, on_device(): lax.all_to_all(thin, ('gx', 'gy'), split_axis=0, concat_axis=0, tiled=True)  2.87 us
  transfers between devices with their start and end apart: 18, of which 5 were waited for; matrix products, arithmetic and copies ran while one was open for 1% of the time, Pallas kernels for 5%

profile of v8, /device:TPU:0, one launch (start us, length us, event | category | flops | bytes accessed | tf_op | source)
XLA Modules:
  0.0 130.0 jit_solution(15180881713470841763)
XLA Ops:
  0.6 0.1 stack.27.place
  0.7 0.7 copy-done.1
  1.4 2.8 %thin_faces.1 = f32[8,16,256]{2,1,0:T(8,128)} custom-call(s32[24]{0:T(128)S(1)} %copy-done.1, s32[6]{0:T(128)S(1)} %stack.27.place, f32[2560,384]{1,0:T(8,128)} %bitcast.22, f32[80,32,384]{2,1,0:T(8,128)} %bitcast.23), custom_call_target="tpu_custom_call" | custom-call | tf_op jit(solution)/shard_map/thin_faces/pallas_call | solution.py:610
  4.2 0.0 copy-start.6
  4.2 0.0 copy-start.9
  4.2 0.0 copy-start.8
  4.2 0.0 copy-start
  4.2 0.0 copy-start.7
  4.2 0.0 copy-start.5
  4.2 7.4 %all-to-all-start = ((f32[8,16,256]{2,1,0:T(8,128)}), f32[8,16,256]{2,1,0:T(8,128)S(1)}, u32[]{:S(2)}, u32[]{:S(2)}) async-start(f32[8,16,256]{2,1,0:T(8,128)} %thin_faces.1), calls=%async_computation | async-start | bytes 262144 | tf_op jit(solution)/shard_map/all_to_all | solution.py:877
  11.7 0.0 copy-start.3
  11.7 0.0 copy-start.4
  11.7 4.5 %sample_cube.1 = (f32[80,256]{1,0:T(8,128)S(1)}, f32[80,256]{1,0:T(8,128)S(1)}, f32[80,256]{1,0:T(8,128)S(1)}, f32[2,16,128]{2,1,0:T(8,128)S(1)}, f32[2,5,32,384...) custom-call(s32[24]{0:T(128)S(1)} %copy-done.2, s32[6]{0:T(128)S(1)} %stack.27.place, f32[2560,384]{1,0:T(8,128)} %bitcast.24), custom_call_target="tpu_custom_call" | custom-call | bytes 16000000 | tf_op jit(solution)/shard_map/sample_cube/pallas_call | solution.py:722
  16.3 2.9 %all-to-all-done.thin = f32[8,16,256]{2,1,0:T(8,128)S(1)} async-done(((f32[8,16,256]{2,1,0:T(8,128)}), f32[8,16,256]{2,1,0:T(8,128)S(1)}, u32[]{:S(2)}, u32[]{:S(2)}) %all-to-all-start) | async-done | bytes 131104 | tf_op jit(solution)/shard_map/all_to_all | solution.py:877
  19.2 1.6 %cube_change.1 = bf16[160,256]{1,0:T(8,128)(2,1)S(1)} custom-call(s32[24]{0:T(128)S(1)} %copy-done.2, s32[6]{0:T(128)S(1)} %stack.27.place, f32[7,64]{1,0:T(8,128)S(1)} %pad_maximum_fusion.2.closure, bf16[256,256]{1,0:T(8,128)(2,1)S(1)} %copy-done, f32[80,256]{1,0:T(8,128)S(1)} %get-tuple-element.78.centre, f32[80,256]{1,0:T(8,128)S(1)} %get-tuple-element.79.lower, ...), custom_call_target="tpu_custom_call" | custom-call | tf_op jit(solution)/shard_map/cube_change/pallas_call | solution.py:793
  20.8 0.7 collective-permute-start.2
  21.5 0.7 collective-permute-start.1
  22.2 2.7 %collective-permute-start = (bf16[160,256]{1,0:T(8,128)(2,1)S(1)}, bf16[160,256]{1,0:T(8,128)(2,1)S(1)}, u32[]{:S(2)}, u32[]{:S(2)}) collective-permute-start(bf16[160,256]{1,0:T(8,128)(2,1)S(1)} %cube_change.1), channel_id=1, source_target_pairs={{0,24},{1,25},{2,26},{3,27},{4,28},{5,29},{6,30},{7,31}} | collective-permute-start | bytes 245768 | tf_op jit(solution)/shard_map/ppermute | solution.py:860
  24.9 0.0 collective-permute-done.1
  24.9 2.0 %collective-permute-done = bf16[160,256]{1,0:T(8,128)(2,1)S(1)} collective-permute-done((bf16[160,256]{1,0:T(8,128)(2,1)S(1)}, bf16[160,256]{1,0:T(8,128)(2,1)S(1)}, u32[]{:S(2)}, u32[]{:S(2)}) %collective-permute-start) | collective-permute-done | bytes 81952 | tf_op jit(solution)/shard_map/ppermute | solution.py:860
  26.9 0.7 collective-permute-start.8
  27.6 0.7 collective-permute-start.7
  28.3 0.7 collective-permute-start.6
  29.0 2.5 %collective-permute-start.3 = (f32[2,5,32,384]{3,2,1,0:T(8,128)S(1)}, f32[2,5,32,384]{3,2,1,0:T(8,128)}, u32[]{:S(2)}, u32[]{:S(2)}) collective-permute-start(f32[2,5,32,384]{3,2,1,0:T(8,128)S(1)} %get-tuple-element.82), channel_id=1, source_target_pairs={{0,4},{1,5},{2,6},{3,7},{4,0},{5,1},{6,2},{7,3},{8,12},{9,13},{10,... | collective-permute-start | bytes 1474568 | tf_op jit(solution)/shard_map/ppermute | solution.py:844
  31.5 0.0 collective-permute-done.8.refs_3_
  31.5 0.0 collective-permute-done.7.refs_2_
  31.5 1.8 %pick_cubes.1 = bf16[6,160,256]{2,1,0:T(8,128)(2,1)S(1)} custom-call(s32[24]{0:T(128)S(1)} %copy-done.7, s32[6]{0:T(128)S(1)} %stack.27.place, bf16[3,160,256]{2,1,0:T(8,128)(2,1)S(1)} %pad_maximum_fusion.1.refs_0_, bf16[3,160,256]{2,1,0:T(8,128)(2,1)S(1)} %collective-permute-done.6.refs_1_, bf16[3,160,256]{2,1,0:T(8,128)(2,1)S(1)} %collective-permute-done.7.refs_2_, ...), custom_call_target="tpu_custom_call" | custom-call | tf_op jit(solution)/shard_map/pick_cubes/pallas_call | solution.py:106
  33.3 1.5 %collective-permute-start.9 = (bf16[6,160,256]{2,1,0:T(8,128)(2,1)S(1)}, bf16[6,160,256]{2,1,0:T(8,128)(2,1)}, u32[]{:S(2)}, u32[]{:S(2)}) collective-permute-start(bf16[6,160,256]{2,1,0:T(8,128)(2,1)S(1)} %pick_cubes.1), channel_id=1, source_target_pairs={{24,28},{25,29},{26,30},{27,31},{28,24},{29,25},{30,26},{31,27}} | collective-permute-start | bytes 1474568 | tf_op jit(solution)/shard_map/ppermute | solution.py:873
  34.8 0.7 slice_bitcast_fusion
  35.4 4.6 %collective-permute-start.5 = (f32[5,16,384]{2,1,0:T(8,128)}, f32[5,16,384]{2,1,0:T(8,128)}, u32[]{:S(2)}, u32[]{:S(2)}) collective-permute-start(f32[5,16,384]{2,1,0:T(8,128)} %get-tuple-element.95), channel_id=1, source_target_pairs={{0,3},{1,2},{2,1},{3,0},{4,7},{5,6},{6,5},{7,4},{8,11},{9,10},{10,... | collective-permute-start | bytes 368648 | tf_op jit(solution)/shard_map/ppermute | solution.py:851
  40.0 1.9 %collective-permute-start.4 = (f32[5,16,384]{2,1,0:T(8,128)S(1)}, f32[5,16,384]{2,1,0:T(8,128)}, u32[]{:S(2)}, u32[]{:S(2)}) collective-permute-start(f32[5,16,384]{2,1,0:T(8,128)S(1)} %get-tuple-element.96), channel_id=1, source_target_pairs={{0,1},{1,0},{2,3},{3,2},{4,5},{5,4},{6,7},{7,6},{8,9},{9,8},{10,11... | collective-permute-start | bytes 368648 | tf_op jit(solution)/shard_map/ppermute | solution.py:850
  42.0 0.1 fusion
  42.0 0.1 reshape.33
  42.1 0.2 slice.39
  42.4 2.1 %collective-permute-done.5 = f32[5,16,384]{2,1,0:T(8,128)} collective-permute-done((f32[5,16,384]{2,1,0:T(8,128)}, f32[5,16,384]{2,1,0:T(8,128)}, u32[]{:S(2)}, u32[]{:S(2)}) %collective-permute-start.5) | collective-permute-done | bytes 122912 | tf_op jit(solution)/shard_map/ppermute | solution.py:851
  44.5 2.5 %collective-permute-done.4 = f32[5,16,384]{2,1,0:T(8,128)} collective-permute-done((f32[5,16,384]{2,1,0:T(8,128)S(1)}, f32[5,16,384]{2,1,0:T(8,128)}, u32[]{:S(2)}, u32[]{:S(2)}) %collective-permute-start.4) | collective-permute-done | bytes 122912 | tf_op jit(solution)/shard_map/ppermute | solution.py:850
  46.9 39.7 %conditional.1 = (f32[17280]{0:T(1024)S(1)}, f32[1,5,16,32,384]{4,3,2,1,0:T(8,128)}) conditional(s32[]{:T(128)} %convert_element_type.7, (f32[7,64]{1,0:T(8,128)S(1)}, s32[6]{0:T(128)S(1)}, f32[5,16,32,384]{3,2,1,0:T(8,128)}, f32[2,5,32,384]{3,2,1,0:T(8,128)}, f32[5,16,384]{2,1,0:T(8,128)}, /*index=5*/f32[5,16,384]{2,1,0:T(8,128)}) %tuple.31, ...), branch_computations={%region_0.1_spmd, %region_1.2_spmd} | conditional | flops 17280 | bytes 345616 | solution.py:910
  46.9 39.7 %evolve_brick.1 = f32[5,16,32,384]{3,2,1,0:T(8,128)} custom-call(f32[7,64]{1,0:T(8,128)S(1)} %get-tuple-element.37.closure, s32[6]{0:T(128)S(1)} %get-tuple-element.38.place, f32[5,16,32,384]{3,2,1,0:T(8,128)} %get-tuple-element.39.fields, f32[2,5,32,384]{3,2,1,0:T(8,128)} %get-tuple-element.40.x_halo, f32[5,16,384]{2,1,0:T(8,128)} %get-tuple-element.41.y_first, ...), custom_call_target="tpu_custom_call" | custom-call | tf_op jit(solution)/shard_map/cond/branch_0_fun/evolve_brick/pallas_call | solution.py:516
  86.7 0.7 collective-permute-start.12
  87.3 0.7 collective-permute-start.11
  88.0 0.7 collective-permute-start.10
  88.7 0.7 collective-permute-start.13
  89.5 0.7 collective-permute-start.16
  90.1 0.7 collective-permute-start.15
  90.8 1.3 collective-permute-start.14
  92.1 35.2 %collective-permute-done.14 = f32[17280]{0:T(1024)S(1)} collective-permute-done((f32[17280]{0:T(1024)S(1)}, f32[17280]{0:T(1024)S(1)}, u32[]{:S(2)}, u32[]{:S(2)}) %collective-permute-start.14) | collective-permute-done | bytes 69152 | tf_op jit(solution)/shard_map/ppermute | solution.py:917
  127.3 0.6 multiply_reduce_fusion
  128.6 1.4 %multiply_subtract_fusion = (f32[540]{0:T(1024)}, f32[540]{0:T(1024)}) fusion(f32[17280]{0:T(1024)S(1)} %copy-done.5, s32[]{:T(128)S(6)} %select_n.13, f32[]{:T(128)S(6)} %sqrt.3, f32[17280]{0:T(1024)S(1)} %get-tuple-element.94, f32[17280]{0:T(1024)} %param.18), kind=kLoop, calls=%fused_computation.8 | loop fusion | flops 2700 | bytes 10808 | tf_op jit(solution)/shard_map/sub | solution.py:926
  (30 shorter events, 0.2 us)
Async XLA Ops:
  0.7 0.7 copy-start.1
  1.4 10.3 %copy-start.2 = (s32[24]{0:T(128)S(1)}, s32[24]{0:T(128)}, u32[]{:S(2)}) copy-start(s32[24]{0:T(128)} %sample_block.5) | copy-start | bytes 292
  4.2 12.1 %copy-start.6 = (f32[64,5]{0,1:T(8,128)S(1)}, f32[64,5]{0,1:T(8,128)}, u32[]{:S(2)}) copy-start(f32[64,5]{0,1:T(8,128)} %param.14) | copy-start | bytes 3844
  4.2 12.1 %copy-start.9 = (f32[64]{0:T(128)S(1)}, f32[64]{0:T(128)}, u32[]{:S(2)}) copy-start(f32[64]{0:T(128)} %param.15) | copy-start | bytes 772
  4.2 12.1 %copy-start.8 = (f32[64]{0:T(128)S(1)}, f32[64]{0:T(128)}, u32[]{:S(2)}) copy-start(f32[64]{0:T(128)} %param.16) | copy-start | bytes 772
  4.2 15.0 %copy-start = (bf16[256,256]{1,0:T(8,128)(2,1)S(1)}, bf16[256,256]{1,0:T(8,128)(2,1)}, u32[]{:S(2)}) copy-start(bf16[256,256]{1,0:T(8,128)(2,1)} %constant.54.clone.order) | copy-start | bytes 393220
  4.2 27.3 %copy-start.7 = (s32[24]{0:T(128)S(1)}, s32[24]{0:T(128)}, u32[]{:S(2)}) copy-start(s32[24]{0:T(128)} %trainer_of.1) | copy-start | bytes 292
  4.2 37.7 %copy-start.5 = (f32[17280]{0:T(1024)S(1)}, f32[17280]{0:T(1024)}, u32[]{:S(2)}) copy-start(f32[17280]{0:T(1024)} %param.17) | copy-start | bytes 207364
  4.2 14.9 %all-to-all-start = ((f32[8,16,256]{2,1,0:T(8,128)}), f32[8,16,256]{2,1,0:T(8,128)S(1)}, u32[]{:S(2)}, u32[]{:S(2)}) async-start(f32[8,16,256]{2,1,0:T(8,128)} %thin_faces.1), calls=%async_computation | async-start | bytes 262144 | tf_op jit(solution)/shard_map/all_to_all | solution.py:877
  11.7 35.2 %copy-start.3 = (bf16[4,256,240]{2,1,0:T(8,128)(2,1)S(1)}, bf16[4,256,240]{2,1,0:T(8,128)(2,1)}, u32[]{:S(2)}) copy-start(bf16[4,256,240]{2,1,0:T(8,128)(2,1)} %constant.56.clone) | copy-start | bytes 1474564
  11.7 35.2 %copy-start.4 = (bf16[4,256,240]{2,1,0:T(8,128)(2,1)S(1)}, bf16[4,256,240]{2,1,0:T(8,128)(2,1)}, u32[]{:S(2)}) copy-start(bf16[4,256,240]{2,1,0:T(8,128)(2,1)} %constant.55.clone) | copy-start | bytes 1474564
  20.8 4.1 %collective-permute-start.2 = (bf16[160,256]{1,0:T(8,128)(2,1)S(1)}, bf16[160,256]{1,0:T(8,128)(2,1)S(1)}, u32[]{:S(2)}, u32[]{:S(2)}) collective-permute-start(bf16[160,256]{1,0:T(8,128)(2,1)S(1)} %cube_change.1), channel_id=1, source_target_pairs={{16,24},{17,25},{18,26},{19,27},{20,28},{21,29},{22,30},{23,31}} | collective-permute-start | bytes 245768 | tf_op jit(solution)/shard_map/ppermute | solution.py:860
  21.5 3.4 %collective-permute-start.1 = (bf16[160,256]{1,0:T(8,128)(2,1)S(1)}, bf16[160,256]{1,0:T(8,128)(2,1)S(1)}, u32[]{:S(2)}, u32[]{:S(2)}) collective-permute-start(bf16[160,256]{1,0:T(8,128)(2,1)S(1)} %cube_change.1), channel_id=1, source_target_pairs={{8,24},{9,25},{10,26},{11,27},{12,28},{13,29},{14,30},{15,31}} | collective-permute-start | bytes 245768 | tf_op jit(solution)/shard_map/ppermute | solution.py:860
  22.2 4.8 %collective-permute-start = (bf16[160,256]{1,0:T(8,128)(2,1)S(1)}, bf16[160,256]{1,0:T(8,128)(2,1)S(1)}, u32[]{:S(2)}, u32[]{:S(2)}) collective-permute-start(bf16[160,256]{1,0:T(8,128)(2,1)S(1)} %cube_change.1), channel_id=1, source_target_pairs={{0,24},{1,25},{2,26},{3,27},{4,28},{5,29},{6,30},{7,31}} | collective-permute-start | bytes 245768 | tf_op jit(solution)/shard_map/ppermute | solution.py:860
  26.9 4.5 %collective-permute-start.8 = (bf16[3,160,256]{2,1,0:T(8,128)(2,1)S(1)}, bf16[3,160,256]{2,1,0:T(8,128)(2,1)S(1)}, u32[]{:S(2)}, u32[]{:S(2)}) collective-permute-start(bf16[3,160,256]{2,1,0:T(8,128)(2,1)S(1)} %pad_maximum_fusion.1.refs_0_), channel_id=1, source_target_pairs={{24,27},{25,26},{26,25},{27,24},{28,31},{29,30},{30,29},{31,28}} | collective-permute-start | bytes 737288 | tf_op jit(solution)/shard_map/ppermute | solution.py:870
  27.6 3.9 %collective-permute-start.7 = (bf16[3,160,256]{2,1,0:T(8,128)(2,1)S(1)}, bf16[3,160,256]{2,1,0:T(8,128)(2,1)S(1)}, u32[]{:S(2)}, u32[]{:S(2)}) collective-permute-start(bf16[3,160,256]{2,1,0:T(8,128)(2,1)S(1)} %pad_maximum_fusion.1.refs_0_), channel_id=1, source_target_pairs={{24,26},{25,27},{26,24},{27,25},{28,30},{29,31},{30,28},{31,29}} | collective-permute-start | bytes 737288 | tf_op jit(solution)/shard_map/ppermute | solution.py:870
  28.3 3.2 %collective-permute-start.6 = (bf16[3,160,256]{2,1,0:T(8,128)(2,1)S(1)}, bf16[3,160,256]{2,1,0:T(8,128)(2,1)S(1)}, u32[]{:S(2)}, u32[]{:S(2)}) collective-permute-start(bf16[3,160,256]{2,1,0:T(8,128)(2,1)S(1)} %pad_maximum_fusion.1.refs_0_), channel_id=1, source_target_pairs={{24,25},{25,24},{26,27},{27,26},{28,29},{29,28},{30,31},{31,30}} | collective-permute-start | bytes 737288 | tf_op jit(solution)/shard_map/ppermute | solution.py:870
  29.0 17.9 %collective-permute-start.3 = (f32[2,5,32,384]{3,2,1,0:T(8,128)S(1)}, f32[2,5,32,384]{3,2,1,0:T(8,128)}, u32[]{:S(2)}, u32[]{:S(2)}) collective-permute-start(f32[2,5,32,384]{3,2,1,0:T(8,128)S(1)} %get-tuple-element.82), channel_id=1, source_target_pairs={{0,4},{1,5},{2,6},{3,7},{4,0},{5,1},{6,2},{7,3},{8,12},{9,13},{10,... | collective-permute-start | bytes 1474568 | tf_op jit(solution)/shard_map/ppermute | solution.py:844
  33.3 13.6 %collective-permute-start.9 = (bf16[6,160,256]{2,1,0:T(8,128)(2,1)S(1)}, bf16[6,160,256]{2,1,0:T(8,128)(2,1)}, u32[]{:S(2)}, u32[]{:S(2)}) collective-permute-start(bf16[6,160,256]{2,1,0:T(8,128)(2,1)S(1)} %pick_cubes.1), channel_id=1, source_target_pairs={{24,28},{25,29},{26,30},{27,31},{28,24},{29,25},{30,26},{31,27}} | collective-permute-start | bytes 1474568 | tf_op jit(solution)/shard_map/ppermute | solution.py:873
  35.4 9.0 %collective-permute-start.5 = (f32[5,16,384]{2,1,0:T(8,128)}, f32[5,16,384]{2,1,0:T(8,128)}, u32[]{:S(2)}, u32[]{:S(2)}) collective-permute-start(f32[5,16,384]{2,1,0:T(8,128)} %get-tuple-element.95), channel_id=1, source_target_pairs={{0,3},{1,2},{2,1},{3,0},{4,7},{5,6},{6,5},{7,4},{8,11},{9,10},{10,... | collective-permute-start | bytes 368648 | tf_op jit(solution)/shard_map/ppermute | solution.py:851
  40.0 6.9 %collective-permute-start.4 = (f32[5,16,384]{2,1,0:T(8,128)S(1)}, f32[5,16,384]{2,1,0:T(8,128)}, u32[]{:S(2)}, u32[]{:S(2)}) collective-permute-start(f32[5,16,384]{2,1,0:T(8,128)S(1)} %get-tuple-element.96), channel_id=1, source_target_pairs={{0,1},{1,0},{2,3},{3,2},{4,5},{5,4},{6,7},{7,6},{8,9},{9,8},{10,11... | collective-permute-start | bytes 368648 | tf_op jit(solution)/shard_map/ppermute | solution.py:850
  86.7 2.0 %collective-permute-start.12 = (f32[17280]{0:T(1024)S(1)}, f32[17280]{0:T(1024)S(1)}, u32[]{:S(2)}, u32[]{:S(2)}) collective-permute-start(f32[17280]{0:T(1024)S(1)} %get-tuple-element.90), channel_id=1, source_target_pairs={{24,27},{25,26},{26,25},{27,24},{28,31},{29,30},{30,29},{31,28}} | collective-permute-start | bytes 207368 | tf_op jit(solution)/shard_map/ppermute | solution.py:870
  87.3 1.4 %collective-permute-start.11 = (f32[17280]{0:T(1024)S(1)}, f32[17280]{0:T(1024)S(1)}, u32[]{:S(2)}, u32[]{:S(2)}) collective-permute-start(f32[17280]{0:T(1024)S(1)} %get-tuple-element.90), channel_id=1, source_target_pairs={{24,26},{25,27},{26,24},{27,25},{28,30},{29,31},{30,28},{31,29}} | collective-permute-start | bytes 207368 | tf_op jit(solution)/shard_map/ppermute | solution.py:870
  88.0 0.7 collective-permute-start.10
  88.7 0.7 collective-permute-start.13
  89.5 2.7 %collective-permute-start.16 = (f32[17280]{0:T(1024)S(1)}, f32[17280]{0:T(1024)S(1)}, u32[]{:S(2)}, u32[]{:S(2)}) collective-permute-start(f32[17280]{0:T(1024)S(1)} %add.48), channel_id=1, source_target_pairs={{24,16},{25,17},{26,18},{27,19},{28,20},{29,21},{30,22},{31,23}} | collective-permute-start | bytes 207368 | tf_op jit(solution)/shard_map/ppermute | solution.py:917
  90.1 2.0 %collective-permute-start.15 = (f32[17280]{0:T(1024)S(1)}, f32[17280]{0:T(1024)S(1)}, u32[]{:S(2)}, u32[]{:S(2)}) collective-permute-start(f32[17280]{0:T(1024)S(1)} %add.48), channel_id=1, source_target_pairs={{24,8},{25,9},{26,10},{27,11},{28,12},{29,13},{30,14},{31,15}} | collective-permute-start | bytes 207368 | tf_op jit(solution)/shard_map/ppermute | solution.py:917
  90.8 36.5 %collective-permute-start.14 = (f32[17280]{0:T(1024)S(1)}, f32[17280]{0:T(1024)S(1)}, u32[]{:S(2)}, u32[]{:S(2)}) collective-permute-start(f32[17280]{0:T(1024)S(1)} %add.48), channel_id=1, source_target_pairs={{24,0},{25,1},{26,2},{27,3},{28,4},{29,5},{30,6},{31,7}} | collective-permute-start | bytes 207368 | tf_op jit(solution)/shard_map/ppermute | solution.py:917

commit v9 on v8

--- a/solution.py
+++ b/solution.py
@@ -79,7 +79,7 @@
     column = lax.rem(owner, trainers)
     y_apart = xor_of(lax.rem(column, y_devices), place[2], y_devices)
     x_apart = xor_of(lax.div(column, y_devices), place[1], x_devices)
-    return lax.div(owner, trainers), y_apart, x_apart
+    return lax.rem(lax.div(owner, trainers) + 1, 3), y_apart, x_apart
 
 
 def pick_kernel(y_devices, x_devices, apart, trainer_of, place, *refs):
@@ -380,7 +380,7 @@
                         stages[turn - pair](pair, quarter)
                 return carry
 
-            lax.fori_loop(0, 4, run, 0)
+            lax.fori_loop(0, 4, run, 0, unroll=2)
 
         def folded(grad, select_ref):
             total = jnp.zeros((3 * CH, 256), jnp.float32)
@@ -466,20 +466,38 @@
     return base_viscosity + viscosity_gain * soft
 
 
-def evolve_kernel(closure, place, fields, x_halo, y_first, y_second, new_fields):
+def viscosity_kernel(closure, fields, viscosity):
+    x_cells, y_cells = fields.shape[1:3]
+    part = y_cells // 2
+
+    def plane(x, carry):
+        for half in range(2):
+            rows = pl.ds(half * part, part)
+            viscosity[x, rows, :] = viscosity_of([fields[f, x, rows, :] for f in range(F)], closure)
+        return carry
+
+    lax.fori_loop(0, x_cells, plane, 0)
+
+
+def brick_viscosity(closure, fields):
+    vmem = pl.BlockSpec(memory_space=pltpu.VMEM)
+    return pl.pallas_call(
+        viscosity_kernel,
+        out_shape=jax.ShapeDtypeStruct(fields.shape[1:], fields.dtype),
+        in_specs=[pl.BlockSpec(memory_space=pltpu.SMEM), vmem],
+        out_specs=vmem,
+        compiler_params=pltpu.CompilerParams(vmem_limit_bytes=16 * 1024 * 1024),
+        name="brick_viscosity",
+    )(closure, fields)
+
+
+def evolve_kernel(place, viscosity, fields, x_halo, y_first, y_second, new_fields):
     up_first = lax.rem(place[2], 2) == 0
     x_cells, y_cells, z_cells = fields.shape[1:]
     row = lax.broadcasted_iota(jnp.int32, (y_cells, z_cells), 0)
     lane = lax.broadcasted_iota(jnp.int32, (y_cells, z_cells), 1)
-    part = y_cells // 2
 
     def plane(x, carry):
-        eddies = []
-        for half in range(2):
-            rows = pl.ds(half * part, part)
-            cells = [fields[f, x, rows, :] for f in range(F)]
-            eddies.append(viscosity_of(cells, closure))
-        viscosity = jnp.concatenate(eddies, axis=0)
         centre = [fields[f, x] for f in range(F)]
         below = jnp.maximum(x - 1, 0)
         above = jnp.minimum(x + 1, x_cells - 1)
@@ -502,7 +520,7 @@
             advection = (
                 centre[0] * (east - west) + centre[1] * (north - south) + centre[2] * (upper - lower)
             )
-            tendency = viscosity * laplacian - 0.5 * advection
+            tendency = viscosity[x] * laplacian - 0.5 * advection
             if f == 2:
                 tendency = tendency + buoyancy * centre[3]
             new_fields[f, x] = value + time_step * tendency
@@ -511,16 +529,16 @@
     lax.fori_loop(0, x_cells, plane, 0)
 
 
-def evolve(closure, place, fields, x_halo, y_first, y_second):
+def evolve(place, viscosity, fields, x_halo, y_first, y_second):
     vmem = pl.BlockSpec(memory_space=pltpu.VMEM)
     return pl.pallas_call(
         evolve_kernel,
         out_shape=jax.ShapeDtypeStruct(fields.shape, fields.dtype),
-        in_specs=[pl.BlockSpec(memory_space=pltpu.SMEM)] * 2 + [vmem] * 4,
+        in_specs=[pl.BlockSpec(memory_space=pltpu.SMEM)] + [vmem] * 5,
         out_specs=vmem,
         compiler_params=pltpu.CompilerParams(vmem_limit_bytes=16 * 1024 * 1024),
         name="evolve_brick",
-    )(closure, place, fields, x_halo, y_first, y_second)
+    )(place, viscosity, fields, x_halo, y_first, y_second)
 
 
 def cell_order():
@@ -855,16 +873,17 @@
         return [(first_trainer + c, first_trainer + (c ^ distance)) for c in range(trainers)]
 
     def to_trainers(payload):
-        return jnp.stack(
-            [
-                lax.ppermute(
-                    payload,
-                    everyone,
-                    [(g * trainers + c, first_trainer + c) for c in range(trainers)],
-                )
-                for g in range(sim_groups)
-            ]
+        hop = lax.ppermute(
+            payload,
+            everyone,
+            [(g * trainers + c, (g + 2) * trainers + c) for g in range(2) for c in range(trainers)],
         )
+        both = lax.ppermute(
+            jnp.stack([payload, hop]),
+            everyone,
+            [(2 * trainers + c, first_trainer + c) for c in range(trainers)],
+        )
+        return jnp.concatenate([both, hop[None]], axis=0)
 
     def from_line(held):
         return [lax.ppermute(held, everyone, swap(apart)) for apart in range(1, y_devices)]
@@ -877,7 +896,13 @@
     thin = lax.all_to_all(thin, ("gx", "gy"), split_axis=0, concat_axis=0, tiled=True)
     payload = cube_change(sample_block, place, closure, cube, thin, y_cells, z_cells)
     landed = to_trainers(payload)
-    x_edges, y_edges, landed = lax.optimization_barrier((x_edges, y_edges, landed))
+    closure, landed = lax.optimization_barrier((closure, landed))
+    viscosity = lax.cond(
+        is_trainer,
+        lambda: jnp.zeros(brick.shape[1:], jnp.float32),
+        lambda: brick_viscosity(closure, brick),
+    )
+    x_edges, y_edges, viscosity = lax.optimization_barrier((x_edges, y_edges, viscosity))
     halo = (x_neighbours(x_edges), *y_neighbours(y_edges[0], y_edges[1]))
     near = [landed, *from_line(landed)]
     far = [
@@ -904,17 +929,31 @@
         return delta, new_brick
 
     def evolve_here():
-        new_brick = evolve(closure, place, brick, *halo)
+        new_brick = evolve(place, viscosity, brick, *halo)
         return jnp.zeros((NPARAM,), jnp.float32), new_brick
 
     delta, new_brick = lax.cond(is_trainer, train_here, evolve_here)
 
-    line = sum(from_line(delta), delta)
-    total = sum((across(apart, line) for apart in range(1, x_devices)), line)
-    final = jnp.where(is_trainer, total, 0.0)
+    held = delta
     for g in range(sim_groups):
-        pairs = [(first_trainer + c, g * trainers + c) for c in range(trainers)]
-        final = final + lax.ppermute(total, everyone, pairs)
+        held = held + lax.ppermute(
+            delta, everyone, [(first_trainer + c, g * trainers + c) for c in range(trainers)]
+        )
+    final = delta
+    for first_apart in range(1, trainers, group_count):
+        meets = [
+            (g * trainers + c, g * trainers + (c ^ (first_apart + g)))
+            for g in range(group_count)
+            for c in range(trainers)
+            if first_apart + g < trainers
+        ]
+        final = final + lax.ppermute(held, everyone, meets)
+    for apart in (1, 2):
+        final = final + lax.ppermute(
+            final,
+            everyone,
+            [(g * trainers + c, (g ^ apart) * trainers + c) for g in range(group_count) for c in range(trainers)],
+        )
 
     share_size = NPARAM // (group_count * trainers)
     share_start = (my_group * trainers + my_column) * share_size

time: 131 us -> 121 us (0.924)
  waiting for transfers between devices: 44.6 us -> 29.6 us
  Pallas kernels: 50.4 us -> 53 us
  local copies, waits for them, and re-layouts: 1.84 us -> 4.18 us
    pallas_call x0 -> x1, Pallas kernels: none -> 33.5 us  [brick_viscosity(): pl.pallas_call(viscosity_kernel, out_shape=jax.ShapeDtypeStruct(fields.sh...]
    pallas_call x1, Pallas kernels: 39.7 us -> 8.78 us  [evolve(): pl.pallas_call(evolve_kernel, out_shape=jax.ShapeDtypeStruct(fields.shape...]
    ppermute x6 -> x9, waiting for transfers between devices: 37.2 us -> 24.2 us  [the longest x3 13.5 us: on_device(): lax.ppermute(delta, everyone, [(first_trainer + c, g * trainers + c) for...]
    ppermute x6 -> x9, starting transfers between devices: 6.67 us -> 10.8 us  [the longest x2 3.99 us: on_device(): final = final + lax.ppermute(held, everyone, meets)]
    ppermute x6 -> x3, starting transfers between devices: 4.02 us -> 2.03 us  [from_line(): lax.ppermute(held, everyone, swap(apart))]
    ppermute x1, waiting for transfers between devices: 2.09 us -> 0.59 us  [y_neighbours(): lax.ppermute(for_second, everyone, pairs(0, -1))]
  transfers between devices with their start and end apart: 18 -> 17, of which waited for: 5 -> 8; matrix products, arithmetic and copies ran while one was open for 1% -> 3% of each run, Pallas kernels for 5% -> 33%
where the time goes in v9:
time: 121 us; the launch traced here: 120 us
  Pallas kernels  53 us (44%)
  starting transfers between devices  29.9 us (25%)
  waiting for transfers between devices  29.6 us (24%)
  local copies, waits for them, and re-layouts  4.18 us (3%)
  other arithmetic  2.13 us (2%)
  between operations  1.68 us (1%)
    pallas_call x1, Pallas kernels, brick_viscosity(): pl.pallas_call(viscosity_kernel, out_shape=jax.ShapeDtypeStruct(fields.sh...  33.5 us
    ppermute x3, waiting for transfers between devices, on_device(): lax.ppermute(delta, everyone, [(first_trainer + c, g * trainers + c) for...  13.5 us
    pallas_call x1, Pallas kernels, evolve(): pl.pallas_call(evolve_kernel, out_shape=jax.ShapeDtypeStruct(fields.shape...  8.78 us
    all_to_all x1, starting transfers between devices, on_device(): lax.all_to_all(thin, ('gx', 'gy'), split_axis=0, concat_axis=0, tiled=True)  7.42 us
    ppermute x2, waiting for transfers between devices, on_device(): lax.ppermute(final, everyone, [(g * trainers + c, (g ^ apart) * trainers...  5.53 us
    pallas_call x1, Pallas kernels, sample_cube(): pl.pallas_call(functools.partial(sample_kernel, y_cells, z_cells), out_sh...  4.53 us
    ppermute x2, starting transfers between devices, on_device(): final = final + lax.ppermute(held, everyone, meets)  3.99 us
    ppermute x1, starting transfers between devices, y_neighbours(): lax.ppermute(for_second, everyone, pairs(0, -1))  3.76 us
  transfers between devices with their start and end apart: 17, of which 8 were waited for; matrix products, arithmetic and copies ran while one was open for 3% of the time, Pallas kernels for 33%

profile of v9, /device:TPU:0, one launch (start us, length us, event | category | flops | bytes accessed | tf_op | source)
XLA Modules:
  0.0 120.5 jit_solution(10251963554142993518)
XLA Ops:
  0.6 0.1 stack.24.place
  0.7 0.7 copy-done.1
  1.4 2.8 %thin_faces.1 = f32[8,16,256]{2,1,0:T(8,128)} custom-call(s32[24]{0:T(128)S(1)} %copy-done.1, s32[6]{0:T(128)S(1)} %stack.24.place, f32[2560,384]{1,0:T(8,128)} %bitcast.22, f32[80,32,384]{2,1,0:T(8,128)} %bitcast.23), custom_call_target="tpu_custom_call" | custom-call | tf_op jit(solution)/shard_map/thin_faces/pallas_call | solution.py:628
  4.2 0.0 copy-start.4
  4.2 0.0 copy-start.7
  4.2 0.0 copy-start.6
  4.2 0.0 copy-start
  4.2 7.4 %all-to-all-start = ((f32[8,16,256]{2,1,0:T(8,128)}), f32[8,16,256]{2,1,0:T(8,128)S(1)}, u32[]{:S(2)}, u32[]{:S(2)}) async-start(f32[8,16,256]{2,1,0:T(8,128)} %thin_faces.1), calls=%async_computation | async-start | bytes 262144 | tf_op jit(solution)/shard_map/all_to_all | solution.py:896
  11.7 4.5 %sample_cube.1 = (f32[80,256]{1,0:T(8,128)S(1)}, f32[80,256]{1,0:T(8,128)S(1)}, f32[80,256]{1,0:T(8,128)S(1)}, f32[2,16,128]{2,1,0:T(8,128)S(1)}, f32[2,5,32,384...) custom-call(s32[24]{0:T(128)S(1)} %copy-done.2, s32[6]{0:T(128)S(1)} %stack.24.place, f32[2560,384]{1,0:T(8,128)} %bitcast.24), custom_call_target="tpu_custom_call" | custom-call | bytes 16000000 | tf_op jit(solution)/shard_map/sample_cube/pallas_call | solution.py:740
  16.2 0.0 copy-start.5
  16.3 2.9 %all-to-all-done.thin = f32[8,16,256]{2,1,0:T(8,128)S(1)} async-done(((f32[8,16,256]{2,1,0:T(8,128)}), f32[8,16,256]{2,1,0:T(8,128)S(1)}, u32[]{:S(2)}, u32[]{:S(2)}) %all-to-all-start) | async-done | bytes 131104 | tf_op jit(solution)/shard_map/all_to_all | solution.py:896
  19.2 1.6 %cube_change.1 = bf16[160,256]{1,0:T(8,128)(2,1)S(1)} custom-call(s32[24]{0:T(128)S(1)} %copy-done.2, s32[6]{0:T(128)S(1)} %stack.24.place, f32[7,64]{1,0:T(8,128)S(1)} %pad_maximum_fusion.3.closure, bf16[256,256]{1,0:T(8,128)(2,1)S(1)} %copy-done, f32[80,256]{1,0:T(8,128)S(1)} %get-tuple-element.89.centre, f32[80,256]{1,0:T(8,128)S(1)} %get-tuple-element.90.lower, ...), custom_call_target="tpu_custom_call" | custom-call | tf_op jit(solution)/shard_map/cube_change/pallas_call | solution.py:811
  20.8 3.4 %collective-permute-start = (bf16[160,256]{1,0:T(8,128)(2,1)S(1)}, bf16[160,256]{1,0:T(8,128)(2,1)S(1)}, u32[]{:S(2)}, u32[]{:S(2)}) collective-permute-start(bf16[160,256]{1,0:T(8,128)(2,1)S(1)} %cube_change.1), channel_id=1, source_target_pairs={{0,16},{1,17},{2,18},{3,19},{4,20},{5,21},{6,22},{7,23},{8,24},{9,... | collective-permute-start | bytes 245768 | tf_op jit(solution)/shard_map/ppermute | solution.py:876
  24.2 2.0 %collective-permute-done = bf16[160,256]{1,0:T(8,128)(2,1)S(1)} collective-permute-done((bf16[160,256]{1,0:T(8,128)(2,1)S(1)}, bf16[160,256]{1,0:T(8,128)(2,1)S(1)}, u32[]{:S(2)}, u32[]{:S(2)}) %collective-permute-start) | collective-permute-done | bytes 81952 | tf_op jit(solution)/shard_map/ppermute | solution.py:876
  26.2 0.7 collective-permute-start.1
  27.0 0.7 collective-permute-start.7
  27.7 0.7 collective-permute-start.6
  28.3 0.7 collective-permute-start.5
  29.0 0.0 copy-start.3
  29.0 33.5 %conditional.2 = (f32[16,32,384]{2,1,0:T(8,128)S(1)}) conditional(s32[]{:T(128)} %convert_element_type.8, (f32[7,64]{1,0:T(8,128)S(1)}, f32[5,16,32,384]{3,2,1,0:T(8,128)}) %tuple.43, () %tuple.29), branch_computations={%region_0.0_spmd, %region_1.0_spmd} | conditional | bytes 786444 | solution.py:900
  29.1 33.5 %brick_viscosity.1 = f32[16,32,384]{2,1,0:T(8,128)S(1)} custom-call(f32[7,64]{1,0:T(8,128)S(1)} %get-tuple-element.44.closure, f32[5,16,32,384]{3,2,1,0:T(8,128)} %get-tuple-element.45.fields), custom_call_target="tpu_custom_call" | custom-call | tf_op jit(solution)/shard_map/cond/branch_0_fun/brick_viscosity/pallas_call | solution.py:484
  62.6 2.5 %collective-permute-start.2 = (f32[2,5,32,384]{3,2,1,0:T(8,128)S(1)}, f32[2,5,32,384]{3,2,1,0:T(8,128)}, u32[]{:S(2)}, u32[]{:S(2)}) collective-permute-start(f32[2,5,32,384]{3,2,1,0:T(8,128)S(1)} %get-tuple-element.95), channel_id=1, source_target_pairs={{0,4},{1,5},{2,6},{3,7},{4,0},{5,1},{6,2},{7,3},{8,12},{9,13},{10,... | collective-permute-start | bytes 1474568 | tf_op jit(solution)/shard_map/ppermute | solution.py:862
  65.1 1.8 %pick_cubes.1 = bf16[6,160,256]{2,1,0:T(8,128)(2,1)S(1)} custom-call(s32[24]{0:T(128)S(1)} %copy-done.5, s32[6]{0:T(128)S(1)} %stack.24.place, bf16[3,160,256]{2,1,0:T(8,128)(2,1)S(1)} %pad_maximum_fusion.1.refs_0_, bf16[3,160,256]{2,1,0:T(8,128)(2,1)S(1)} %collective-permute-done.5.refs_1_, bf16[3,160,256]{2,1,0:T(8,128)(2,1)S(1)} %collective-permute-done.6.refs_2_, ...), custom_call_target="tpu_custom_call" | custom-call | tf_op jit(solution)/shard_map/pick_cubes/pallas_call | solution.py:106
  66.9 1.5 %collective-permute-start.8 = (bf16[6,160,256]{2,1,0:T(8,128)(2,1)S(1)}, bf16[6,160,256]{2,1,0:T(8,128)(2,1)}, u32[]{:S(2)}, u32[]{:S(2)}) collective-permute-start(bf16[6,160,256]{2,1,0:T(8,128)(2,1)S(1)} %pick_cubes.1), channel_id=1, source_target_pairs={{24,28},{25,29},{26,30},{27,31},{28,24},{29,25},{30,26},{31,27}} | collective-permute-start | bytes 1474568 | tf_op jit(solution)/shard_map/ppermute | solution.py:892
  68.4 0.7 slice_bitcast_fusion
  69.1 3.8 %collective-permute-start.4 = (f32[5,16,384]{2,1,0:T(8,128)}, f32[5,16,384]{2,1,0:T(8,128)}, u32[]{:S(2)}, u32[]{:S(2)}) collective-permute-start(f32[5,16,384]{2,1,0:T(8,128)} %get-tuple-element.108), channel_id=1, source_target_pairs={{0,3},{1,2},{2,1},{3,0},{4,7},{5,6},{6,5},{7,4},{8,11},{9,10},{10,... | collective-permute-start | bytes 368648 | tf_op jit(solution)/shard_map/ppermute | solution.py:869
  72.8 1.9 %collective-permute-start.3 = (f32[5,16,384]{2,1,0:T(8,128)}, f32[5,16,384]{2,1,0:T(8,128)}, u32[]{:S(2)}, u32[]{:S(2)}) collective-permute-start(f32[5,16,384]{2,1,0:T(8,128)} %get-tuple-element.109), channel_id=1, source_target_pairs={{0,1},{1,0},{2,3},{3,2},{4,5},{5,4},{6,7},{7,6},{8,9},{9,8},{10,11... | collective-permute-start | bytes 368648 | tf_op jit(solution)/shard_map/ppermute | solution.py:868
  74.8 0.9 fusion
  75.7 0.1 reshape.33
  75.8 0.8 slice.39
  76.6 0.8 pad.8
  77.5 0.6 collective-permute-done.4
  78.0 1.9 %collective-permute-done.3 = f32[5,16,384]{2,1,0:T(8,128)} collective-permute-done((f32[5,16,384]{2,1,0:T(8,128)}, f32[5,16,384]{2,1,0:T(8,128)}, u32[]{:S(2)}, u32[]{:S(2)}) %collective-permute-start.3) | collective-permute-done | bytes 122912 | tf_op jit(solution)/shard_map/ppermute | solution.py:868
  79.9 8.8 %conditional.3 = (f32[17280]{0:T(1024)S(1)}, f32[1,5,16,32,384]{4,3,2,1,0:T(8,128)}) conditional(s32[]{:T(128)} %convert_element_type.8, (s32[6]{0:T(128)S(1)}, f32[16,32,384]{2,1,0:T(8,128)S(1)}, f32[5,16,32,384]{3,2,1,0:T(8,128)}, f32[2,5,32,384]{3,2,1,0:T(8,128)}, f32[5,16,384]{2,1,0:T(8,128)}, /*index=5*/f32[5,16,384]{2,1,0:T(8,128)}) %tuple.44, ...), branch_computations={%region_2.3_spmd, %region_3.4_spmd} | conditional | flops 17280 | bytes 345616 | solution.py:935
  79.9 8.8 %evolve_brick.1 = f32[5,16,32,384]{3,2,1,0:T(8,128)} custom-call(s32[6]{0:T(128)S(1)} %get-tuple-element.46.place, f32[16,32,384]{2,1,0:T(8,128)S(1)} %get-tuple-element.47.viscosity, f32[5,16,32,384]{3,2,1,0:T(8,128)} %get-tuple-element.48.fields, f32[2,5,32,384]{3,2,1,0:T(8,128)} %get-tuple-element.49.x_halo, f32[5,16,384]{2,1,0:T(8,128)} %get-tuple-element.50.y_first, ...), custom_call_target="tpu_custom_call" | custom-call | tf_op jit(solution)/shard_map/cond/branch_0_fun/evolve_brick/pallas_call | solution.py:534
  88.7 0.7 collective-permute-start.11
  89.4 0.7 collective-permute-start.10
  90.1 1.3 %collective-permute-start.9 = (f32[17280]{0:T(1024)S(1)}, f32[17280]{0:T(1024)S(1)}, u32[]{:S(2)}, u32[]{:S(2)}) collective-permute-start(f32[17280]{0:T(1024)S(1)} %get-tuple-element.103), channel_id=1, source_target_pairs={{24,0},{25,1},{26,2},{27,3},{28,4},{29,5},{30,6},{31,7}} | collective-permute-start | bytes 207368 | tf_op jit(solution)/shard_map/ppermute | solution.py:939
  91.4 13.5 %collective-permute-done.9 = f32[17280]{0:T(1024)S(1)} collective-permute-done((f32[17280]{0:T(1024)S(1)}, f32[17280]{0:T(1024)S(1)}, u32[]{:S(2)}, u32[]{:S(2)}) %collective-permute-start.9) | collective-permute-done | bytes 69152 | tf_op jit(solution)/shard_map/ppermute | solution.py:939
  104.9 1.9 %collective-permute-start.13 = (f32[17280]{0:T(1024)S(1)}, f32[17280]{0:T(1024)S(1)}, u32[]{:S(2)}, u32[]{:S(2)}) collective-permute-start(f32[17280]{0:T(1024)S(1)} %add_add_fusion.1), channel_id=1, source_target_pairs={{0,5},{1,4},{2,7},{3,6},{4,1},{5,0},{6,3},{7,2},{8,14},{9,15},{10,... | collective-permute-start | bytes 207368 | tf_op jit(solution)/shard_map/ppermute | solution.py:950
  106.8 2.1 %collective-permute-start.12 = (f32[17280]{0:T(1024)S(1)}, f32[17280]{0:T(1024)S(1)}, u32[]{:S(2)}, u32[]{:S(2)}) collective-permute-start(f32[17280]{0:T(1024)S(1)} %add_add_fusion.1), channel_id=1, source_target_pairs={{0,1},{1,0},{2,3},{3,2},{4,5},{5,4},{6,7},{7,6},{8,10},{9,11},{10,... | collective-permute-start | bytes 207368 | tf_op jit(solution)/shard_map/ppermute | solution.py:950
  108.9 3.1 %collective-permute-done.13 = f32[17280]{0:T(1024)S(1)} collective-permute-done((f32[17280]{0:T(1024)S(1)}, f32[17280]{0:T(1024)S(1)}, u32[]{:S(2)}, u32[]{:S(2)}) %collective-permute-start.13) | collective-permute-done | bytes 69152 | tf_op jit(solution)/shard_map/ppermute | solution.py:950
  112.1 0.1 collective-permute-start.14
  112.2 1.2 %collective-permute-done.14 = f32[17280]{0:T(1024)S(1)} collective-permute-done((f32[17280]{0:T(1024)S(1)}, f32[17280]{0:T(1024)S(1)}, u32[]{:S(2)}, u32[]{:S(2)}) %collective-permute-start.14) | collective-permute-done | bytes 69152 | tf_op jit(solution)/shard_map/ppermute | solution.py:952
  113.4 0.1 collective-permute-start.15
  113.5 4.3 %collective-permute-done.15 = f32[17280]{0:T(1024)S(1)} collective-permute-done((f32[17280]{0:T(1024)S(1)}, f32[17280]{0:T(1024)S(1)}, u32[]{:S(2)}, u32[]{:S(2)}) %collective-permute-start.15) | collective-permute-done | bytes 69152 | tf_op jit(solution)/shard_map/ppermute | solution.py:952
  117.8 0.6 multiply_reduce_fusion
  119.1 1.4 %multiply_subtract_fusion = (f32[540]{0:T(1024)}, f32[540]{0:T(1024)}) fusion(f32[17280]{0:T(1024)} %param.19, s32[]{:T(128)S(6)} %select_n.2, f32[]{:T(128)S(6)} %sqrt.3, f32[17280]{0:T(1024)S(1)} %get-tuple-element.107, f32[17280]{0:T(1024)} %param.20), kind=kLoop, calls=%fused_computation.9 | loop fusion | flops 2700 | bytes 10808 | tf_op jit(solution)/shard_map/sub | solution.py:965
  (28 shorter events, 0.2 us)
Async XLA Ops:
  0.7 0.7 copy-start.1
  1.4 10.3 %copy-start.2 = (s32[24]{0:T(128)S(1)}, s32[24]{0:T(128)}, u32[]{:S(2)}) copy-start(s32[24]{0:T(128)} %sample_block.5) | copy-start | bytes 292
  4.2 12.0 %copy-start.4 = (f32[64,5]{0,1:T(8,128)S(1)}, f32[64,5]{0,1:T(8,128)}, u32[]{:S(2)}) copy-start(f32[64,5]{0,1:T(8,128)} %param.16) | copy-start | bytes 3844
  4.2 12.0 %copy-start.7 = (f32[64]{0:T(128)S(1)}, f32[64]{0:T(128)}, u32[]{:S(2)}) copy-start(f32[64]{0:T(128)} %param.17) | copy-start | bytes 772
  4.2 12.0 %copy-start.6 = (f32[64]{0:T(128)S(1)}, f32[64]{0:T(128)}, u32[]{:S(2)}) copy-start(f32[64]{0:T(128)} %param.18) | copy-start | bytes 772
  4.2 15.0 %copy-start = (bf16[256,256]{1,0:T(8,128)(2,1)S(1)}, bf16[256,256]{1,0:T(8,128)(2,1)}, u32[]{:S(2)}) copy-start(bf16[256,256]{1,0:T(8,128)(2,1)} %constant.56.clone.order) | copy-start | bytes 393220
  4.2 14.9 %all-to-all-start = ((f32[8,16,256]{2,1,0:T(8,128)}), f32[8,16,256]{2,1,0:T(8,128)S(1)}, u32[]{:S(2)}, u32[]{:S(2)}) async-start(f32[8,16,256]{2,1,0:T(8,128)} %thin_faces.1), calls=%async_computation | async-start | bytes 262144 | tf_op jit(solution)/shard_map/all_to_all | solution.py:896
  16.2 48.9 %copy-start.5 = (s32[24]{0:T(128)S(1)}, s32[24]{0:T(128)}, u32[]{:S(2)}) copy-start(s32[24]{0:T(128)} %trainer_of.1) | copy-start | bytes 292
  20.8 5.4 %collective-permute-start = (bf16[160,256]{1,0:T(8,128)(2,1)S(1)}, bf16[160,256]{1,0:T(8,128)(2,1)S(1)}, u32[]{:S(2)}, u32[]{:S(2)}) collective-permute-start(bf16[160,256]{1,0:T(8,128)(2,1)S(1)} %cube_change.1), channel_id=1, source_target_pairs={{0,16},{1,17},{2,18},{3,19},{4,20},{5,21},{6,22},{7,23},{8,24},{9,... | collective-permute-start | bytes 245768 | tf_op jit(solution)/shard_map/ppermute | solution.py:876
  26.2 0.7 collective-permute-start.1
  27.0 38.1 %collective-permute-start.7 = (bf16[3,160,256]{2,1,0:T(8,128)(2,1)S(1)}, bf16[3,160,256]{2,1,0:T(8,128)(2,1)S(1)}, u32[]{:S(2)}, u32[]{:S(2)}) collective-permute-start(bf16[3,160,256]{2,1,0:T(8,128)(2,1)S(1)} %pad_maximum_fusion.1.refs_0_), channel_id=1, source_target_pairs={{24,27},{25,26},{26,25},{27,24},{28,31},{29,30},{30,29},{31,28}} | collective-permute-start | bytes 737288 | tf_op jit(solution)/shard_map/ppermute | solution.py:889
  27.7 37.4 %collective-permute-start.6 = (bf16[3,160,256]{2,1,0:T(8,128)(2,1)S(1)}, bf16[3,160,256]{2,1,0:T(8,128)(2,1)S(1)}, u32[]{:S(2)}, u32[]{:S(2)}) collective-permute-start(bf16[3,160,256]{2,1,0:T(8,128)(2,1)S(1)} %pad_maximum_fusion.1.refs_0_), channel_id=1, source_target_pairs={{24,26},{25,27},{26,24},{27,25},{28,30},{29,31},{30,28},{31,29}} | collective-permute-start | bytes 737288 | tf_op jit(solution)/shard_map/ppermute | solution.py:889
  28.3 36.7 %collective-permute-start.5 = (bf16[3,160,256]{2,1,0:T(8,128)(2,1)S(1)}, bf16[3,160,256]{2,1,0:T(8,128)(2,1)S(1)}, u32[]{:S(2)}, u32[]{:S(2)}) collective-permute-start(bf16[3,160,256]{2,1,0:T(8,128)(2,1)S(1)} %pad_maximum_fusion.1.refs_0_), channel_id=1, source_target_pairs={{24,25},{25,24},{26,27},{27,26},{28,29},{29,28},{30,31},{31,30}} | collective-permute-start | bytes 737288 | tf_op jit(solution)/shard_map/ppermute | solution.py:889
  29.0 50.9 %copy-start.3 = (bf16[4,256,240]{2,1,0:T(8,128)(2,1)S(1)}, bf16[4,256,240]{2,1,0:T(8,128)(2,1)}, u32[]{:S(2)}) copy-start(bf16[4,256,240]{2,1,0:T(8,128)(2,1)} %constant.58.clone) | copy-start | bytes 1474564
  62.6 17.4 %collective-permute-start.2 = (f32[2,5,32,384]{3,2,1,0:T(8,128)S(1)}, f32[2,5,32,384]{3,2,1,0:T(8,128)}, u32[]{:S(2)}, u32[]{:S(2)}) collective-permute-start(f32[2,5,32,384]{3,2,1,0:T(8,128)S(1)} %get-tuple-element.95), channel_id=1, source_target_pairs={{0,4},{1,5},{2,6},{3,7},{4,0},{5,1},{6,2},{7,3},{8,12},{9,13},{10,... | collective-permute-start | bytes 1474568 | tf_op jit(solution)/shard_map/ppermute | solution.py:862
  66.9 13.0 %collective-permute-start.8 = (bf16[6,160,256]{2,1,0:T(8,128)(2,1)S(1)}, bf16[6,160,256]{2,1,0:T(8,128)(2,1)}, u32[]{:S(2)}, u32[]{:S(2)}) collective-permute-start(bf16[6,160,256]{2,1,0:T(8,128)(2,1)S(1)} %pick_cubes.1), channel_id=1, source_target_pairs={{24,28},{25,29},{26,30},{27,31},{28,24},{29,25},{30,26},{31,27}} | collective-permute-start | bytes 1474568 | tf_op jit(solution)/shard_map/ppermute | solution.py:892
  69.1 9.0 %collective-permute-start.4 = (f32[5,16,384]{2,1,0:T(8,128)}, f32[5,16,384]{2,1,0:T(8,128)}, u32[]{:S(2)}, u32[]{:S(2)}) collective-permute-start(f32[5,16,384]{2,1,0:T(8,128)} %get-tuple-element.108), channel_id=1, source_target_pairs={{0,3},{1,2},{2,1},{3,0},{4,7},{5,6},{6,5},{7,4},{8,11},{9,10},{10,... | collective-permute-start | bytes 368648 | tf_op jit(solution)/shard_map/ppermute | solution.py:869
  72.8 7.1 %collective-permute-start.3 = (f32[5,16,384]{2,1,0:T(8,128)}, f32[5,16,384]{2,1,0:T(8,128)}, u32[]{:S(2)}, u32[]{:S(2)}) collective-permute-start(f32[5,16,384]{2,1,0:T(8,128)} %get-tuple-element.109), channel_id=1, source_target_pairs={{0,1},{1,0},{2,3},{3,2},{4,5},{5,4},{6,7},{7,6},{8,9},{9,8},{10,11... | collective-permute-start | bytes 368648 | tf_op jit(solution)/shard_map/ppermute | solution.py:868
  88.7 2.6 %collective-permute-start.11 = (f32[17280]{0:T(1024)S(1)}, f32[17280]{0:T(1024)S(1)}, u32[]{:S(2)}, u32[]{:S(2)}) collective-permute-start(f32[17280]{0:T(1024)S(1)} %get-tuple-element.103), channel_id=1, source_target_pairs={{24,16},{25,17},{26,18},{27,19},{28,20},{29,21},{30,22},{31,23}} | collective-permute-start | bytes 207368 | tf_op jit(solution)/shard_map/ppermute | solution.py:939
  89.4 2.0 %collective-permute-start.10 = (f32[17280]{0:T(1024)S(1)}, f32[17280]{0:T(1024)S(1)}, u32[]{:S(2)}, u32[]{:S(2)}) collective-permute-start(f32[17280]{0:T(1024)S(1)} %get-tuple-element.103), channel_id=1, source_target_pairs={{24,8},{25,9},{26,10},{27,11},{28,12},{29,13},{30,14},{31,15}} | collective-permute-start | bytes 207368 | tf_op jit(solution)/shard_map/ppermute | solution.py:939
  90.1 14.8 %collective-permute-start.9 = (f32[17280]{0:T(1024)S(1)}, f32[17280]{0:T(1024)S(1)}, u32[]{:S(2)}, u32[]{:S(2)}) collective-permute-start(f32[17280]{0:T(1024)S(1)} %get-tuple-element.103), channel_id=1, source_target_pairs={{24,0},{25,1},{26,2},{27,3},{28,4},{29,5},{30,6},{31,7}} | collective-permute-start | bytes 207368 | tf_op jit(solution)/shard_map/ppermute | solution.py:939
  104.9 7.1 %collective-permute-start.13 = (f32[17280]{0:T(1024)S(1)}, f32[17280]{0:T(1024)S(1)}, u32[]{:S(2)}, u32[]{:S(2)}) collective-permute-start(f32[17280]{0:T(1024)S(1)} %add_add_fusion.1), channel_id=1, source_target_pairs={{0,5},{1,4},{2,7},{3,6},{4,1},{5,0},{6,3},{7,2},{8,14},{9,15},{10,... | collective-permute-start | bytes 207368 | tf_op jit(solution)/shard_map/ppermute | solution.py:950
  106.8 5.2 %collective-permute-start.12 = (f32[17280]{0:T(1024)S(1)}, f32[17280]{0:T(1024)S(1)}, u32[]{:S(2)}, u32[]{:S(2)}) collective-permute-start(f32[17280]{0:T(1024)S(1)} %add_add_fusion.1), channel_id=1, source_target_pairs={{0,1},{1,0},{2,3},{3,2},{4,5},{5,4},{6,7},{7,6},{8,10},{9,11},{10,... | collective-permute-start | bytes 207368 | tf_op jit(solution)/shard_map/ppermute | solution.py:950
  112.1 1.3 %collective-permute-start.14 = (f32[17280]{0:T(1024)S(1)}, f32[17280]{0:T(1024)S(1)}, u32[]{:S(2)}, u32[]{:S(2)}) collective-permute-start(f32[17280]{0:T(1024)S(1)} %add_add_fusion), channel_id=1, source_target_pairs={{0,8},{1,9},{2,10},{3,11},{4,12},{5,13},{6,14},{7,15},{8,0},{9,1},... | collective-permute-start | bytes 207368 | tf_op jit(solution)/shard_map/ppermute | solution.py:952
  113.4 4.4 %collective-permute-start.15 = (f32[17280]{0:T(1024)S(1)}, f32[17280]{0:T(1024)S(1)}, u32[]{:S(2)}, u32[]{:S(2)}) collective-permute-start(f32[17280]{0:T(1024)S(1)} %add.50), channel_id=1, source_target_pairs={{0,16},{1,17},{2,18},{3,19},{4,20},{5,21},{6,22},{7,23},{8,24},{9,... | collective-permute-start | bytes 207368 | tf_op jit(solution)/shard_map/ppermute | solution.py:952

commit v10 on v9

--- a/solution.py
+++ b/solution.py
@@ -66,38 +66,37 @@
     return gx * place[4] + gy
 
 
-def xor_of(left, right, size):
-    total = jnp.int32(0)
-    for bit in range(size.bit_length() - 1):
-        one, other = lax.rem(lax.div(left, 1 << bit), 2), lax.rem(lax.div(right, 1 << bit), 2)
-        total = total + jnp.where(one == other, 0, 1 << bit)
-    return total
-
-
 def owner_apart(owner, place, y_devices, x_devices):
-    trainers = x_devices * y_devices
-    column = lax.rem(owner, trainers)
-    y_apart = xor_of(lax.rem(column, y_devices), place[2], y_devices)
-    x_apart = xor_of(lax.div(column, y_devices), place[1], x_devices)
-    return lax.rem(lax.div(owner, trainers) + 1, 3), y_apart, x_apart
+    group, column = divmod(owner, x_devices * y_devices)
+    y_apart = jnp.bitwise_xor(place[2], jnp.int32(column % y_devices))
+    return group, y_apart, jnp.bitwise_xor(place[1], jnp.int32(column // y_devices))
 
 
 def pick_kernel(y_devices, x_devices, apart, trainer_of, place, *refs):
-    near, chosen = refs[:y_devices], refs[y_devices]
-    wanted = xor_of(place[1], apart, x_devices) * y_devices + place[2]
-
-    def visit(owner, count):
+    near, chosen, owners = refs[:y_devices], refs[y_devices], refs[y_devices + 1]
+    wanted = jnp.bitwise_xor(place[1], jnp.int32(apart)) * y_devices + place[2]
+    count = jnp.int32(0)
+    for owner in range(trainer_of.shape[0]):
         group, y_apart, x_apart = owner_apart(owner, place, y_devices, x_devices)
         mine = (trainer_of[owner] == wanted) & (x_apart == 0)
+
+        @pl.when(mine)
+        def _():
+            owners[0, count] = y_apart
+            owners[1, count] = group
+
+        count = count + jnp.where(mine, 1, 0)
+
+    def copy_slot(slot, carry):
         for source in range(y_devices):
 
-            @pl.when(mine & (y_apart == source))
+            @pl.when(owners[0, slot] == source)
             def _():
-                chosen[count] = near[source][group]
-
-        return count + jnp.where(mine, 1, 0)
-
-    lax.fori_loop(0, trainer_of.shape[0], visit, jnp.int32(0))
+                chosen[slot] = near[source][owners[1, slot]]
+
+        return carry
+
+    lax.fori_loop(0, count, copy_slot, 0)
 
 
 def pick_cubes(trainer_of, place, near, y_devices, x_devices, apart):
@@ -108,6 +107,7 @@
         out_shape=jax.ShapeDtypeStruct((TCAP, *near[0].shape[1:]), near[0].dtype),
         in_specs=[smem, smem] + [vmem] * len(near),
         out_specs=vmem,
+        scratch_shapes=[pltpu.SMEM((2, TCAP), jnp.int32)],
         compiler_params=pltpu.CompilerParams(vmem_limit_bytes=16 * 1024 * 1024),
         name="pick_cubes",
     )(trainer_of, place, *near)
@@ -198,24 +198,22 @@
         pltpu.make_async_copy(far_last, select_last, select_sems.at[1]),
     ]
 
-    groups = place[3]
+    column = place[1] * y_devices + place[2]
     for other in range(x_devices):
         picked[other] = 0
-
-    def visit(owner, count):
-        mine = trainer_of[owner] == column_of(place, 0, 0)
+    count = jnp.int32(0)
+    for owner in range(trainer_of.shape[0]):
+        group, y_apart, x_apart = owner_apart(owner, place, y_devices, x_devices)
+        mine = trainer_of[owner] == column
 
         @pl.when(mine)
         def _():
-            group, y_apart, x_apart = owner_apart(owner, place, y_devices, x_devices)
             near = x_apart == 0
             slots[0, count] = jnp.where(near, y_apart, y_devices - 1 + x_apart)
             slots[1, count] = jnp.where(near, group, picked[x_apart])
             picked[x_apart] = picked[x_apart] + 1
 
-        return count + jnp.where(mine, 1, 0)
-
-    count = lax.fori_loop(0, trainer_of.shape[0], visit, jnp.int32(0))
+        count = count + jnp.where(mine, 1, 0)
 
     def fetch(slot, wait):
         for source in range(sources):
@@ -237,7 +235,7 @@
 
         @pl.when(slot >= count)
         def _():
-            cubes[slot] = jnp.zeros((2 * SUB * F, 256), jnp.bfloat16)
+            cubes[slot] = jnp.zeros(cubes.shape[1:], jnp.bfloat16)
 
     masks = patch_masks()
     for ref in (*errors, *inputs):
@@ -246,8 +244,6 @@
     for ref in partial_out:
         ref[:, :128] = jnp.zeros((STACK, 128), jnp.float32)
         ref[:, COLS - 128 :] = jnp.zeros((STACK, 128), jnp.float32)
-    for ref in (*tables, *targets):
-        ref[...] = jnp.zeros(ref.shape, ref.dtype)
     lane = lax.broadcasted_iota(jnp.int32, (8, 128), 1)
     full_weight = 2.0 * (1.0 / (jnp.full((8, 128), count, jnp.int32).astype(jnp.float32) * CELLS))
     weights = [
@@ -261,41 +257,31 @@
     for slot in range(TCAP):
         fetch(slot, True)
 
-    low_lanes = lax.broadcasted_iota(jnp.int32, (SUB * F, 128), 1) < 64
-
-    def spread_rows(pair, kind, put):
-        rows = slice(kind * SUB * F, (kind + 1) * SUB * F)
-        even = cubes[2 * pair, rows, :].astype(jnp.float32)
-        odd = cubes[2 * pair + 1, rows, :].astype(jnp.float32)
-        for half in range(2):
-            left = even[:, half * 128 : (half + 1) * 128]
-            right = odd[:, half * 128 : (half + 1) * 128]
-            put(2 * half, jnp.where(low_lanes, left, pltpu.roll(right, 64, 1)))
-            put(2 * half + 1, jnp.where(low_lanes, pltpu.roll(left, 64, 1), right))
-
+    low_lanes = lax.broadcasted_iota(jnp.int32, (SUB * F * 2, 128), 1) < 64
     for pair in range(PAIRS):
-
-        def put_input(cell, values):
-            tables[pair][pl.ds(cell, SUB * F, 8), :] = values
-
-        def put_target(cell, values):
-            targets[pair][pl.ds(cell, SUB * F, 8), :] = values
-
-        spread_rows(pair, 0, put_input)
-        spread_rows(pair, 1, put_target)
+        for kind, ref in enumerate((tables[pair], targets[pair])):
+            rows = slice(kind * SUB * F * 2, (kind + 1) * SUB * F * 2)
+            even = cubes[2 * pair, rows, :].astype(jnp.float32)
+            odd = cubes[2 * pair + 1, rows, :].astype(jnp.float32)
+            ref[0] = jnp.where(low_lanes, even, pltpu.roll(odd, 64, 1))
+            ref[1] = jnp.where(low_lanes, pltpu.roll(even, 64, 1), odd)
+
+    def patch_cells(ref, quarter, plane, channel):
+        start = pl.multiple_of(channel * 32 + quarter % 2 * 16 + plane // 2 * 8, 8)
+        rows = ref[quarter // 2, pl.ds(start, 8), :]
+        return rows if plane % 2 == 0 else pltpu.roll(rows, 4, 0)
 
     def stack_planes(quarter, carry):
         for pair in range(PAIRS):
             for plane in range(4):
                 x = quarter * 4 + plane
                 channels = [
-                    patch_stack(tables[pair][pl.ds(pl.multiple_of((c * SUB + x) * 8, 8), 8), :], masks)
-                    for c in range(F)
+                    patch_stack(patch_cells(tables[pair], quarter, plane, c), masks) for c in range(F)
                 ]
                 store_planes(inputs[pair], x, channels)
         return carry
 
-    lax.fori_loop(0, 4, stack_planes, 0)
+    lax.fori_loop(0, 4, stack_planes, 0, unroll=2)
 
     for copy in select_copies:
         copy.wait()
@@ -350,8 +336,8 @@
                     predicted = patch_fold(
                         total[16 * c : 16 * c + 8], total[16 * c + 8 : 16 * c + 16], masks
                     )
-                    row = pl.multiple_of((c * SUB + x) * 8, 8)
-                    error = weights[pair] * (predicted - targets[pair][pl.ds(row, 8), :])
+                    wanted = patch_cells(targets[pair], quarter, plane, c)
+                    error = weights[pair] * (predicted - wanted)
                     channels.append(patch_stack(error, masks))
                 store_planes(errors[pair], x, channels)
 
@@ -380,7 +366,7 @@
                         stages[turn - pair](pair, quarter)
                 return carry
 
-            lax.fori_loop(0, 4, run, 0, unroll=2)
+            lax.fori_loop(0, 4, run, 0, unroll=4)
 
         def folded(grad, select_ref):
             total = jnp.zeros((3 * CH, 256), jnp.float32)
@@ -420,7 +406,7 @@
         scratch_shapes=[
             pltpu.SMEM((2, TCAP), jnp.int32),
             pltpu.SMEM((x_devices,), jnp.int32),
-            pltpu.VMEM((TCAP, 2 * SUB * F, 256), jnp.bfloat16),
+            pltpu.VMEM((TCAP, 4 * SUB * F, 128), jnp.bfloat16),
             pltpu.VMEM((4 * CH, STACK), jnp.bfloat16),
             pltpu.VMEM((4 * CH, STACK), jnp.bfloat16),
             pltpu.VMEM((STACK, 4 * CH), jnp.bfloat16),
@@ -435,7 +421,7 @@
             pltpu.SemaphoreType.DMA,
             pltpu.SemaphoreType.DMA((2,)),
         ]
-        + [pltpu.VMEM((SUB * F * 8, 128), jnp.float32)] * (2 * PAIRS)
+        + [pltpu.VMEM((2, SUB * F * 2, 128), jnp.float32)] * (2 * PAIRS)
         + [pltpu.VMEM((STACK, COLS), jnp.bfloat16)] * (2 * PAIRS)
         + [pltpu.VMEM((4 * CH, COLS), jnp.bfloat16)] * (2 * PAIRS)
         + [pltpu.VMEM((4 * CH, COLS), jnp.float32)] * PAIRS
@@ -772,6 +758,7 @@
     own_rows,
     thin,
     payload,
+    table,
 ):
     y_start = corner_of(sample_block, place, 0, 0, y_cells, z_cells)[0]
     row = lax.broadcasted_iota(jnp.int32, (SUB, 256), 0)
@@ -801,8 +788,19 @@
         if f == 2:
             change = change + buoyancy * cells[3]
         changes.append(change)
-    both = jnp.concatenate(cells + changes, axis=0).astype(jnp.bfloat16)
-    payload[...] = dot_rows(both, order[...]).astype(jnp.bfloat16)
+    ordered = dot_rows(jnp.concatenate(cells + changes, axis=0).astype(jnp.bfloat16), order[...])
+    low_lanes = lane[:8, :128] < 64
+    for part in range(2 * F):
+        for cell in range(4):
+            columns = slice(cell // 2 * 128, cell // 2 * 128 + 128)
+            low = ordered[part * SUB : part * SUB + 8, columns]
+            high = ordered[part * SUB + 8 : part * SUB + SUB, columns]
+            if cell % 2 == 0:
+                high = pltpu.roll(high, 64, 1)
+            else:
+                low = pltpu.roll(low, 64, 1)
+            table[pl.ds(part * 32 + cell, 8, 4), :] = jnp.where(low_lanes, low, high)
+    payload[...] = table[...].astype(jnp.bfloat16)
 
 
 def cube_change(sample_block, place, closure, cube, thin, y_cells, z_cells):
@@ -810,9 +808,10 @@
     smem = pl.BlockSpec(memory_space=pltpu.SMEM)
     return pl.pallas_call(
         functools.partial(change_kernel, y_cells, z_cells),
-        out_shape=jax.ShapeDtypeStruct((2 * F * SUB, 256), jnp.bfloat16),
+        out_shape=jax.ShapeDtypeStruct((4 * F * SUB, 128), jnp.bfloat16),
         in_specs=[smem] * 3 + [vmem] * 6,
         out_specs=vmem,
+        scratch_shapes=[pltpu.VMEM((4 * F * SUB, 128), jnp.float32)],
         compiler_params=pltpu.CompilerParams(vmem_limit_bytes=16 * 1024 * 1024),
         name="cube_change",
     )(sample_block, place, closure, jnp.asarray(CELL_ORDER, jnp.bfloat16), *cube, thin)
@@ -873,17 +872,14 @@
         return [(first_trainer + c, first_trainer + (c ^ distance)) for c in range(trainers)]
 
     def to_trainers(payload):
-        hop = lax.ppermute(
-            payload,
-            everyone,
-            [(g * trainers + c, (g + 2) * trainers + c) for g in range(2) for c in range(trainers)],
+        return jnp.stack(
+            [
+                lax.ppermute(
+                    payload, everyone, [(g * trainers + c, first_trainer + c) for c in range(trainers)]
+                )
+                for g in range(sim_groups)
+            ]
         )
-        both = lax.ppermute(
-            jnp.stack([payload, hop]),
-            everyone,
-            [(2 * trainers + c, first_trainer + c) for c in range(trainers)],
-        )
-        return jnp.concatenate([both, hop[None]], axis=0)
 
     def from_line(held):
         return [lax.ppermute(held, everyone, swap(apart)) for apart in range(1, y_devices)]

time: 121 us -> 112 us (0.926)
  waiting for transfers between devices: 29.6 us -> 20.4 us
    ppermute x3, waiting for transfers between devices: 13.5 us -> 4.31 us  [on_device(): lax.ppermute(delta, everyone, [(first_trainer + c, g * trainers + c) for...]
    ppermute x2 -> x3, starting transfers between devices: 4.07 us -> 4.05 us  [to_trainers(): lax.ppermute(payload, everyone, [(g * trainers + c, first_trainer + c) fo...]
  transfers between devices with their start and end apart: 17 -> 18, of which waited for: 8 -> 7; matrix products, arithmetic and copies ran while one was open for 3% -> 3% of each run, Pallas kernels for 33% -> 35%
where the time goes in v10:
time: 112 us; the launch traced here: 111 us
  Pallas kernels  52 us (46%)
  starting transfers between devices  30.7 us (27%)
  waiting for transfers between devices  20.4 us (18%)
  local copies, waits for them, and re-layouts  4.17 us (4%)
  other arithmetic  2.11 us (2%)
  between operations  1.7 us (2%)
    pallas_call x1, Pallas kernels, brick_viscosity(): pl.pallas_call(viscosity_kernel, out_shape=jax.ShapeDtypeStruct(fields.sh...  33.5 us
    pallas_call x1, Pallas kernels, evolve(): pl.pallas_call(evolve_kernel, out_shape=jax.ShapeDtypeStruct(fields.shape...  8.78 us
    all_to_all x1, starting transfers between devices, on_device(): lax.all_to_all(thin, ('gx', 'gy'), split_axis=0, concat_axis=0, tiled=True)  7.42 us
    ppermute x2, waiting for transfers between devices, on_device(): lax.ppermute(final, everyone, [(g * trainers + c, (g ^ apart) * trainers...  5.53 us
    ppermute x1, starting transfers between devices, y_neighbours(): lax.ppermute(for_second, everyone, pairs(0, -1))  4.62 us
    pallas_call x1, Pallas kernels, sample_cube(): pl.pallas_call(functools.partial(sample_kernel, y_cells, z_cells), out_sh...  4.53 us
    ppermute x3, waiting for transfers between devices, on_device(): lax.ppermute(delta, everyone, [(first_trainer + c, g * trainers + c) for...  4.31 us
    ppermute x3, starting transfers between devices, to_trainers(): lax.ppermute(payload, everyone, [(g * trainers + c, first_trainer + c) fo...  4.05 us
  transfers between devices with their start and end apart: 18, of which 7 were waited for; matrix products, arithmetic and copies ran while one was open for 3% of the time, Pallas kernels for 35%

profile of v10, /device:TPU:0, one launch (start us, length us, event | category | flops | bytes accessed | tf_op | source)
XLA Modules:
  0.0 111.3 jit_solution(10277281961909052671)
XLA Ops:
  0.6 0.1 stack.27.place
  0.7 0.7 copy-done.1
  1.4 2.8 %thin_faces.1 = f32[8,16,256]{2,1,0:T(8,128)} custom-call(s32[24]{0:T(128)S(1)} %copy-done.1, s32[6]{0:T(128)S(1)} %stack.27.place, f32[2560,384]{1,0:T(8,128)} %bitcast.22, f32[80,32,384]{2,1,0:T(8,128)} %bitcast.23), custom_call_target="tpu_custom_call" | custom-call | tf_op jit(solution)/shard_map/thin_faces/pallas_call | solution.py:614
  4.2 0.0 copy-start.4
  4.2 0.0 copy-start.7
  4.2 0.0 copy-start.6
  4.2 0.0 copy-start
  4.2 7.4 %all-to-all-start = ((f32[8,16,256]{2,1,0:T(8,128)}), f32[8,16,256]{2,1,0:T(8,128)S(1)}, u32[]{:S(2)}, u32[]{:S(2)}) async-start(f32[8,16,256]{2,1,0:T(8,128)} %thin_faces.1), calls=%async_computation | async-start | bytes 262144 | tf_op jit(solution)/shard_map/all_to_all | solution.py:892
  11.7 4.5 %sample_cube.1 = (f32[80,256]{1,0:T(8,128)S(1)}, f32[80,256]{1,0:T(8,128)S(1)}, f32[80,256]{1,0:T(8,128)S(1)}, f32[2,16,128]{2,1,0:T(8,128)S(1)}, f32[2,5,32,384...) custom-call(s32[24]{0:T(128)S(1)} %copy-done.2, s32[6]{0:T(128)S(1)} %stack.27.place, f32[2560,384]{1,0:T(8,128)} %bitcast.24), custom_call_target="tpu_custom_call" | custom-call | bytes 16000000 | tf_op jit(solution)/shard_map/sample_cube/pallas_call | solution.py:726
  16.2 0.0 copy-start.5
  16.3 2.9 %all-to-all-done.thin = f32[8,16,256]{2,1,0:T(8,128)S(1)} async-done(((f32[8,16,256]{2,1,0:T(8,128)}), f32[8,16,256]{2,1,0:T(8,128)S(1)}, u32[]{:S(2)}, u32[]{:S(2)}) %all-to-all-start) | async-done | bytes 131104 | tf_op jit(solution)/shard_map/all_to_all | solution.py:892
  19.2 1.7 %cube_change.1 = bf16[320,128]{1,0:T(8,128)(2,1)S(1)} custom-call(s32[24]{0:T(128)S(1)} %copy-done.2, s32[6]{0:T(128)S(1)} %stack.27.place, f32[7,64]{1,0:T(8,128)S(1)} %pad_maximum_fusion.2.closure, bf16[256,256]{1,0:T(8,128)(2,1)S(1)} %copy-done, f32[80,256]{1,0:T(8,128)S(1)} %get-tuple-element.89.centre, f32[80,256]{1,0:T(8,128)S(1)} %get-tuple-element.90.lower, ...), custom_call_target="tpu_custom_call" | custom-call | tf_op jit(solution)/shard_map/cube_change/pallas_call | solution.py:809
  20.9 0.7 collective-permute-start.2
  21.6 0.7 collective-permute-start.1
  22.2 2.7 %collective-permute-start = (bf16[320,128]{1,0:T(8,128)(2,1)S(1)}, bf16[320,128]{1,0:T(8,128)(2,1)S(1)}, u32[]{:S(2)}, u32[]{:S(2)}) collective-permute-start(bf16[320,128]{1,0:T(8,128)(2,1)S(1)} %cube_change.1), channel_id=1, source_target_pairs={{0,24},{1,25},{2,26},{3,27},{4,28},{5,29},{6,30},{7,31}} | collective-permute-start | bytes 245768 | tf_op jit(solution)/shard_map/ppermute | solution.py:877
  25.0 2.0 %collective-permute-done = bf16[320,128]{1,0:T(8,128)(2,1)S(1)} collective-permute-done((bf16[320,128]{1,0:T(8,128)(2,1)S(1)}, bf16[320,128]{1,0:T(8,128)(2,1)S(1)}, u32[]{:S(2)}, u32[]{:S(2)}) %collective-permute-start) | collective-permute-done | bytes 81952 | tf_op jit(solution)/shard_map/ppermute | solution.py:877
  27.0 0.7 collective-permute-start.8
  27.7 0.7 collective-permute-start.7
  28.4 0.7 collective-permute-start.6
  29.1 0.0 copy-start.3
  29.1 33.5 %conditional.2 = (f32[16,32,384]{2,1,0:T(8,128)S(1)}) conditional(s32[]{:T(128)} %convert_element_type.8, (f32[7,64]{1,0:T(8,128)S(1)}, f32[5,16,32,384]{3,2,1,0:T(8,128)}) %tuple.43, () %tuple.29), branch_computations={%region_0.0_spmd, %region_1.0_spmd} | conditional | bytes 786444 | solution.py:896
  29.1 33.5 %brick_viscosity.1 = f32[16,32,384]{2,1,0:T(8,128)S(1)} custom-call(f32[7,64]{1,0:T(8,128)S(1)} %get-tuple-element.44.closure, f32[5,16,32,384]{3,2,1,0:T(8,128)} %get-tuple-element.45.fields), custom_call_target="tpu_custom_call" | custom-call | tf_op jit(solution)/shard_map/cond/branch_0_fun/brick_viscosity/pallas_call | solution.py:470
  62.6 2.5 %collective-permute-start.3 = (f32[2,5,32,384]{3,2,1,0:T(8,128)S(1)}, f32[2,5,32,384]{3,2,1,0:T(8,128)}, u32[]{:S(2)}, u32[]{:S(2)}) collective-permute-start(f32[2,5,32,384]{3,2,1,0:T(8,128)S(1)} %get-tuple-element.95), channel_id=1, source_target_pairs={{0,4},{1,5},{2,6},{3,7},{4,0},{5,1},{6,2},{7,3},{8,12},{9,13},{10,... | collective-permute-start | bytes 1474568 | tf_op jit(solution)/shard_map/ppermute | solution.py:861
  65.1 0.7 pick_cubes.1
  65.8 1.5 %collective-permute-start.9 = (bf16[6,320,128]{2,1,0:T(8,128)(2,1)S(1)}, bf16[6,320,128]{2,1,0:T(8,128)(2,1)}, u32[]{:S(2)}, u32[]{:S(2)}) collective-permute-start(bf16[6,320,128]{2,1,0:T(8,128)(2,1)S(1)} %pick_cubes.1), channel_id=1, source_target_pairs={{24,28},{25,29},{26,30},{27,31},{28,24},{29,25},{30,26},{31,27}} | collective-permute-start | bytes 1474568 | tf_op jit(solution)/shard_map/ppermute | solution.py:888
  67.3 0.7 slice_bitcast_fusion
  68.0 4.6 %collective-permute-start.5 = (f32[5,16,384]{2,1,0:T(8,128)}, f32[5,16,384]{2,1,0:T(8,128)}, u32[]{:S(2)}, u32[]{:S(2)}) collective-permute-start(f32[5,16,384]{2,1,0:T(8,128)} %get-tuple-element.108), channel_id=1, source_target_pairs={{0,3},{1,2},{2,1},{3,0},{4,7},{5,6},{6,5},{7,4},{8,11},{9,10},{10,... | collective-permute-start | bytes 368648 | tf_op jit(solution)/shard_map/ppermute | solution.py:868
  72.6 1.9 %collective-permute-start.4 = (f32[5,16,384]{2,1,0:T(8,128)}, f32[5,16,384]{2,1,0:T(8,128)}, u32[]{:S(2)}, u32[]{:S(2)}) collective-permute-start(f32[5,16,384]{2,1,0:T(8,128)} %get-tuple-element.109), channel_id=1, source_target_pairs={{0,1},{1,0},{2,3},{3,2},{4,5},{5,4},{6,7},{7,6},{8,9},{9,8},{10,11... | collective-permute-start | bytes 368648 | tf_op jit(solution)/shard_map/ppermute | solution.py:867
  74.6 0.9 fusion
  75.5 0.1 reshape.33
  75.6 0.8 slice.39
  76.4 0.8 pad.8
  77.3 2.5 %collective-permute-done.4 = f32[5,16,384]{2,1,0:T(8,128)} collective-permute-done((f32[5,16,384]{2,1,0:T(8,128)}, f32[5,16,384]{2,1,0:T(8,128)}, u32[]{:S(2)}, u32[]{:S(2)}) %collective-permute-start.4) | collective-permute-done | bytes 122912 | tf_op jit(solution)/shard_map/ppermute | solution.py:867
  79.7 9.0 %conditional.3 = (f32[17280]{0:T(1024)S(1)}, f32[1,5,16,32,384]{4,3,2,1,0:T(8,128)}) conditional(s32[]{:T(128)} %convert_element_type.8, (s32[6]{0:T(128)S(1)}, f32[16,32,384]{2,1,0:T(8,128)S(1)}, f32[5,16,32,384]{3,2,1,0:T(8,128)}, f32[2,5,32,384]{3,2,1,0:T(8,128)}, f32[5,16,384]{2,1,0:T(8,128)}, /*index=5*/f32[5,16,384]{2,1,0:T(8,128)}) %tuple.44, ...), branch_computations={%region_2.3_spmd, %region_3.4_spmd} | conditional | flops 17280 | bytes 345616 | solution.py:931
  79.8 8.8 %evolve_brick.1 = f32[5,16,32,384]{3,2,1,0:T(8,128)} custom-call(s32[6]{0:T(128)S(1)} %get-tuple-element.46.place, f32[16,32,384]{2,1,0:T(8,128)S(1)} %get-tuple-element.47.viscosity, f32[5,16,32,384]{3,2,1,0:T(8,128)} %get-tuple-element.48.fields, f32[2,5,32,384]{3,2,1,0:T(8,128)} %get-tuple-element.49.x_halo, f32[5,16,384]{2,1,0:T(8,128)} %get-tuple-element.50.y_first, ...), custom_call_target="tpu_custom_call" | custom-call | tf_op jit(solution)/shard_map/cond/branch_0_fun/evolve_brick/pallas_call | solution.py:520
  88.8 0.7 collective-permute-start.12
  89.5 0.7 collective-permute-start.11
  90.1 1.3 %collective-permute-start.10 = (f32[17280]{0:T(1024)S(1)}, f32[17280]{0:T(1024)S(1)}, u32[]{:S(2)}, u32[]{:S(2)}) collective-permute-start(f32[17280]{0:T(1024)S(1)} %get-tuple-element.103), channel_id=1, source_target_pairs={{24,0},{25,1},{26,2},{27,3},{28,4},{29,5},{30,6},{31,7}} | collective-permute-start | bytes 207368 | tf_op jit(solution)/shard_map/ppermute | solution.py:935
  91.5 4.3 %collective-permute-done.10 = f32[17280]{0:T(1024)S(1)} collective-permute-done((f32[17280]{0:T(1024)S(1)}, f32[17280]{0:T(1024)S(1)}, u32[]{:S(2)}, u32[]{:S(2)}) %collective-permute-start.10) | collective-permute-done | bytes 69152 | tf_op jit(solution)/shard_map/ppermute | solution.py:935
  95.8 1.9 %collective-permute-start.14 = (f32[17280]{0:T(1024)S(1)}, f32[17280]{0:T(1024)S(1)}, u32[]{:S(2)}, u32[]{:S(2)}) collective-permute-start(f32[17280]{0:T(1024)S(1)} %add_add_fusion.1), channel_id=1, source_target_pairs={{0,5},{1,4},{2,7},{3,6},{4,1},{5,0},{6,3},{7,2},{8,14},{9,15},{10,... | collective-permute-start | bytes 207368 | tf_op jit(solution)/shard_map/ppermute | solution.py:946
  97.7 2.0 %collective-permute-start.13 = (f32[17280]{0:T(1024)S(1)}, f32[17280]{0:T(1024)S(1)}, u32[]{:S(2)}, u32[]{:S(2)}) collective-permute-start(f32[17280]{0:T(1024)S(1)} %add_add_fusion.1), channel_id=1, source_target_pairs={{0,1},{1,0},{2,3},{3,2},{4,5},{5,4},{6,7},{7,6},{8,10},{9,11},{10,... | collective-permute-start | bytes 207368 | tf_op jit(solution)/shard_map/ppermute | solution.py:946
  99.7 3.2 %collective-permute-done.14 = f32[17280]{0:T(1024)S(1)} collective-permute-done((f32[17280]{0:T(1024)S(1)}, f32[17280]{0:T(1024)S(1)}, u32[]{:S(2)}, u32[]{:S(2)}) %collective-permute-start.14) | collective-permute-done | bytes 69152 | tf_op jit(solution)/shard_map/ppermute | solution.py:946
  102.9 0.1 collective-permute-start.15
  103.0 1.2 %collective-permute-done.15 = f32[17280]{0:T(1024)S(1)} collective-permute-done((f32[17280]{0:T(1024)S(1)}, f32[17280]{0:T(1024)S(1)}, u32[]{:S(2)}, u32[]{:S(2)}) %collective-permute-start.15) | collective-permute-done | bytes 69152 | tf_op jit(solution)/shard_map/ppermute | solution.py:948
  104.2 0.1 collective-permute-start.16
  104.3 4.3 %collective-permute-done.16 = f32[17280]{0:T(1024)S(1)} collective-permute-done((f32[17280]{0:T(1024)S(1)}, f32[17280]{0:T(1024)S(1)}, u32[]{:S(2)}, u32[]{:S(2)}) %collective-permute-start.16) | collective-permute-done | bytes 69152 | tf_op jit(solution)/shard_map/ppermute | solution.py:948
  108.6 0.6 multiply_reduce_fusion
  109.9 1.4 %multiply_subtract_fusion = (f32[540]{0:T(1024)}, f32[540]{0:T(1024)}) fusion(f32[17280]{0:T(1024)} %param.19, s32[]{:T(128)S(6)} %select_n.2, f32[]{:T(128)S(6)} %sqrt.3, f32[17280]{0:T(1024)S(1)} %get-tuple-element.107, f32[17280]{0:T(1024)} %param.20), kind=kLoop, calls=%fused_computation.8 | loop fusion | flops 2700 | bytes 10808 | tf_op jit(solution)/shard_map/sub | solution.py:961
  (29 shorter events, 0.2 us)
Async XLA Ops:
  0.7 0.7 copy-start.1
  1.4 10.3 %copy-start.2 = (s32[24]{0:T(128)S(1)}, s32[24]{0:T(128)}, u32[]{:S(2)}) copy-start(s32[24]{0:T(128)} %sample_block.5) | copy-start | bytes 292
  4.2 12.0 %copy-start.4 = (f32[64,5]{0,1:T(8,128)S(1)}, f32[64,5]{0,1:T(8,128)}, u32[]{:S(2)}) copy-start(f32[64,5]{0,1:T(8,128)} %param.16) | copy-start | bytes 3844
  4.2 12.0 %copy-start.7 = (f32[64]{0:T(128)S(1)}, f32[64]{0:T(128)}, u32[]{:S(2)}) copy-start(f32[64]{0:T(128)} %param.17) | copy-start | bytes 772
  4.2 12.0 %copy-start.6 = (f32[64]{0:T(128)S(1)}, f32[64]{0:T(128)}, u32[]{:S(2)}) copy-start(f32[64]{0:T(128)} %param.18) | copy-start | bytes 772
  4.2 15.0 %copy-start = (bf16[256,256]{1,0:T(8,128)(2,1)S(1)}, bf16[256,256]{1,0:T(8,128)(2,1)}, u32[]{:S(2)}) copy-start(bf16[256,256]{1,0:T(8,128)(2,1)} %constant.56.clone.order) | copy-start | bytes 393220
  4.2 14.9 %all-to-all-start = ((f32[8,16,256]{2,1,0:T(8,128)}), f32[8,16,256]{2,1,0:T(8,128)S(1)}, u32[]{:S(2)}, u32[]{:S(2)}) async-start(f32[8,16,256]{2,1,0:T(8,128)} %thin_faces.1), calls=%async_computation | async-start | bytes 262144 | tf_op jit(solution)/shard_map/all_to_all | solution.py:892
  16.2 48.9 %copy-start.5 = (s32[24]{0:T(128)S(1)}, s32[24]{0:T(128)}, u32[]{:S(2)}) copy-start(s32[24]{0:T(128)} %trainer_of.1) | copy-start | bytes 292
  20.9 4.1 %collective-permute-start.2 = (bf16[320,128]{1,0:T(8,128)(2,1)S(1)}, bf16[320,128]{1,0:T(8,128)(2,1)S(1)}, u32[]{:S(2)}, u32[]{:S(2)}) collective-permute-start(bf16[320,128]{1,0:T(8,128)(2,1)S(1)} %cube_change.1), channel_id=1, source_target_pairs={{16,24},{17,25},{18,26},{19,27},{20,28},{21,29},{22,30},{23,31}} | collective-permute-start | bytes 245768 | tf_op jit(solution)/shard_map/ppermute | solution.py:877
  21.6 3.4 %collective-permute-start.1 = (bf16[320,128]{1,0:T(8,128)(2,1)S(1)}, bf16[320,128]{1,0:T(8,128)(2,1)S(1)}, u32[]{:S(2)}, u32[]{:S(2)}) collective-permute-start(bf16[320,128]{1,0:T(8,128)(2,1)S(1)} %cube_change.1), channel_id=1, source_target_pairs={{8,24},{9,25},{10,26},{11,27},{12,28},{13,29},{14,30},{15,31}} | collective-permute-start | bytes 245768 | tf_op jit(solution)/shard_map/ppermute | solution.py:877
  22.2 4.8 %collective-permute-start = (bf16[320,128]{1,0:T(8,128)(2,1)S(1)}, bf16[320,128]{1,0:T(8,128)(2,1)S(1)}, u32[]{:S(2)}, u32[]{:S(2)}) collective-permute-start(bf16[320,128]{1,0:T(8,128)(2,1)S(1)} %cube_change.1), channel_id=1, source_target_pairs={{0,24},{1,25},{2,26},{3,27},{4,28},{5,29},{6,30},{7,31}} | collective-permute-start | bytes 245768 | tf_op jit(solution)/shard_map/ppermute | solution.py:877
  27.0 38.1 %collective-permute-start.8 = (bf16[3,320,128]{2,1,0:T(8,128)(2,1)S(1)}, bf16[3,320,128]{2,1,0:T(8,128)(2,1)S(1)}, u32[]{:S(2)}, u32[]{:S(2)}) collective-permute-start(bf16[3,320,128]{2,1,0:T(8,128)(2,1)S(1)} %pad_maximum_fusion.1.refs_0_), channel_id=1, source_target_pairs={{24,27},{25,26},{26,25},{27,24},{28,31},{29,30},{30,29},{31,28}} | collective-permute-start | bytes 737288 | tf_op jit(solution)/shard_map/ppermute | solution.py:885
  27.7 37.4 %collective-permute-start.7 = (bf16[3,320,128]{2,1,0:T(8,128)(2,1)S(1)}, bf16[3,320,128]{2,1,0:T(8,128)(2,1)S(1)}, u32[]{:S(2)}, u32[]{:S(2)}) collective-permute-start(bf16[3,320,128]{2,1,0:T(8,128)(2,1)S(1)} %pad_maximum_fusion.1.refs_0_), channel_id=1, source_target_pairs={{24,26},{25,27},{26,24},{27,25},{28,30},{29,31},{30,28},{31,29}} | collective-permute-start | bytes 737288 | tf_op jit(solution)/shard_map/ppermute | solution.py:885
  28.4 36.7 %collective-permute-start.6 = (bf16[3,320,128]{2,1,0:T(8,128)(2,1)S(1)}, bf16[3,320,128]{2,1,0:T(8,128)(2,1)S(1)}, u32[]{:S(2)}, u32[]{:S(2)}) collective-permute-start(bf16[3,320,128]{2,1,0:T(8,128)(2,1)S(1)} %pad_maximum_fusion.1.refs_0_), channel_id=1, source_target_pairs={{24,25},{25,24},{26,27},{27,26},{28,29},{29,28},{30,31},{31,30}} | collective-permute-start | bytes 737288 | tf_op jit(solution)/shard_map/ppermute | solution.py:885
  29.1 50.7 %copy-start.3 = (bf16[4,256,240]{2,1,0:T(8,128)(2,1)S(1)}, bf16[4,256,240]{2,1,0:T(8,128)(2,1)}, u32[]{:S(2)}) copy-start(bf16[4,256,240]{2,1,0:T(8,128)(2,1)} %constant.58.clone) | copy-start | bytes 1474564
  62.6 17.1 %collective-permute-start.3 = (f32[2,5,32,384]{3,2,1,0:T(8,128)S(1)}, f32[2,5,32,384]{3,2,1,0:T(8,128)}, u32[]{:S(2)}, u32[]{:S(2)}) collective-permute-start(f32[2,5,32,384]{3,2,1,0:T(8,128)S(1)} %get-tuple-element.95), channel_id=1, source_target_pairs={{0,4},{1,5},{2,6},{3,7},{4,0},{5,1},{6,2},{7,3},{8,12},{9,13},{10,... | collective-permute-start | bytes 1474568 | tf_op jit(solution)/shard_map/ppermute | solution.py:861
  65.8 13.9 %collective-permute-start.9 = (bf16[6,320,128]{2,1,0:T(8,128)(2,1)S(1)}, bf16[6,320,128]{2,1,0:T(8,128)(2,1)}, u32[]{:S(2)}, u32[]{:S(2)}) collective-permute-start(bf16[6,320,128]{2,1,0:T(8,128)(2,1)S(1)} %pick_cubes.1), channel_id=1, source_target_pairs={{24,28},{25,29},{26,30},{27,31},{28,24},{29,25},{30,26},{31,27}} | collective-permute-start | bytes 1474568 | tf_op jit(solution)/shard_map/ppermute | solution.py:888
  68.0 9.2 %collective-permute-start.5 = (f32[5,16,384]{2,1,0:T(8,128)}, f32[5,16,384]{2,1,0:T(8,128)}, u32[]{:S(2)}, u32[]{:S(2)}) collective-permute-start(f32[5,16,384]{2,1,0:T(8,128)} %get-tuple-element.108), channel_id=1, source_target_pairs={{0,3},{1,2},{2,1},{3,0},{4,7},{5,6},{6,5},{7,4},{8,11},{9,10},{10,... | collective-permute-start | bytes 368648 | tf_op jit(solution)/shard_map/ppermute | solution.py:868
  72.6 7.1 %collective-permute-start.4 = (f32[5,16,384]{2,1,0:T(8,128)}, f32[5,16,384]{2,1,0:T(8,128)}, u32[]{:S(2)}, u32[]{:S(2)}) collective-permute-start(f32[5,16,384]{2,1,0:T(8,128)} %get-tuple-element.109), channel_id=1, source_target_pairs={{0,1},{1,0},{2,3},{3,2},{4,5},{5,4},{6,7},{7,6},{8,9},{9,8},{10,11... | collective-permute-start | bytes 368648 | tf_op jit(solution)/shard_map/ppermute | solution.py:867
  88.8 2.6 %collective-permute-start.12 = (f32[17280]{0:T(1024)S(1)}, f32[17280]{0:T(1024)S(1)}, u32[]{:S(2)}, u32[]{:S(2)}) collective-permute-start(f32[17280]{0:T(1024)S(1)} %get-tuple-element.103), channel_id=1, source_target_pairs={{24,16},{25,17},{26,18},{27,19},{28,20},{29,21},{30,22},{31,23}} | collective-permute-start | bytes 207368 | tf_op jit(solution)/shard_map/ppermute | solution.py:935
  89.5 2.0 %collective-permute-start.11 = (f32[17280]{0:T(1024)S(1)}, f32[17280]{0:T(1024)S(1)}, u32[]{:S(2)}, u32[]{:S(2)}) collective-permute-start(f32[17280]{0:T(1024)S(1)} %get-tuple-element.103), channel_id=1, source_target_pairs={{24,8},{25,9},{26,10},{27,11},{28,12},{29,13},{30,14},{31,15}} | collective-permute-start | bytes 207368 | tf_op jit(solution)/shard_map/ppermute | solution.py:935
  90.1 5.6 %collective-permute-start.10 = (f32[17280]{0:T(1024)S(1)}, f32[17280]{0:T(1024)S(1)}, u32[]{:S(2)}, u32[]{:S(2)}) collective-permute-start(f32[17280]{0:T(1024)S(1)} %get-tuple-element.103), channel_id=1, source_target_pairs={{24,0},{25,1},{26,2},{27,3},{28,4},{29,5},{30,6},{31,7}} | collective-permute-start | bytes 207368 | tf_op jit(solution)/shard_map/ppermute | solution.py:935
  95.8 7.1 %collective-permute-start.14 = (f32[17280]{0:T(1024)S(1)}, f32[17280]{0:T(1024)S(1)}, u32[]{:S(2)}, u32[]{:S(2)}) collective-permute-start(f32[17280]{0:T(1024)S(1)} %add_add_fusion.1), channel_id=1, source_target_pairs={{0,5},{1,4},{2,7},{3,6},{4,1},{5,0},{6,3},{7,2},{8,14},{9,15},{10,... | collective-permute-start | bytes 207368 | tf_op jit(solution)/shard_map/ppermute | solution.py:946
  97.7 5.2 %collective-permute-start.13 = (f32[17280]{0:T(1024)S(1)}, f32[17280]{0:T(1024)S(1)}, u32[]{:S(2)}, u32[]{:S(2)}) collective-permute-start(f32[17280]{0:T(1024)S(1)} %add_add_fusion.1), channel_id=1, source_target_pairs={{0,1},{1,0},{2,3},{3,2},{4,5},{5,4},{6,7},{7,6},{8,10},{9,11},{10,... | collective-permute-start | bytes 207368 | tf_op jit(solution)/shard_map/ppermute | solution.py:946
  102.9 1.3 %collective-permute-start.15 = (f32[17280]{0:T(1024)S(1)}, f32[17280]{0:T(1024)S(1)}, u32[]{:S(2)}, u32[]{:S(2)}) collective-permute-start(f32[17280]{0:T(1024)S(1)} %add_add_fusion), channel_id=1, source_target_pairs={{0,8},{1,9},{2,10},{3,11},{4,12},{5,13},{6,14},{7,15},{8,0},{9,1},... | collective-permute-start | bytes 207368 | tf_op jit(solution)/shard_map/ppermute | solution.py:948
  104.2 4.4 %collective-permute-start.16 = (f32[17280]{0:T(1024)S(1)}, f32[17280]{0:T(1024)S(1)}, u32[]{:S(2)}, u32[]{:S(2)}) collective-permute-start(f32[17280]{0:T(1024)S(1)} %add.50), channel_id=1, source_target_pairs={{0,16},{1,17},{2,18},{3,19},{4,20},{5,21},{6,22},{7,23},{8,24},{9,... | collective-permute-start | bytes 207368 | tf_op jit(solution)/shard_map/ppermute | solution.py:948

commit v11 on v10

--- a/solution.py
+++ b/solution.py
@@ -281,7 +281,7 @@
                 store_planes(inputs[pair], x, channels)
         return carry
 
-    lax.fori_loop(0, 4, stack_planes, 0, unroll=2)
+    lax.fori_loop(0, 4, stack_planes, 0, unroll=4)
 
     for copy in select_copies:
         copy.wait()
@@ -445,9 +445,12 @@
         half = closure[F, h] + closure[0, h] * cells[0]
         for f in range(1, F):
             half = half + closure[f, h] * cells[f]
-        return total + closure[F + 1, h] * (half + half * jnp.tanh(half))
-
-    total = lax.fori_loop(0, HID, unit, jnp.zeros(cells[0].shape, jnp.float32), unroll=4)
+        return total + closure[F + 1, h] * (half * jnp.tanh(half))
+
+    total = closure[F, HID] + closure[0, HID] * cells[0]
+    for f in range(1, F):
+        total = total + closure[f, HID] * cells[f]
+    total = lax.fori_loop(0, HID, unit, total, unroll=8)
     soft = jnp.maximum(total, 0.0) + jnp.log1p(jnp.exp(-jnp.abs(total)))
     return base_viscosity + viscosity_gain * soft
 
@@ -465,19 +468,23 @@
     lax.fori_loop(0, x_cells, plane, 0)
 
 
-def brick_viscosity(closure, fields):
-    vmem = pl.BlockSpec(memory_space=pltpu.VMEM)
+def half_viscosity(closure, fields, side):
+    count, x_cells, y_cells, z_cells = fields.shape
     return pl.pallas_call(
         viscosity_kernel,
-        out_shape=jax.ShapeDtypeStruct(fields.shape[1:], fields.dtype),
-        in_specs=[pl.BlockSpec(memory_space=pltpu.SMEM), vmem],
-        out_specs=vmem,
+        grid=(1,),
+        out_shape=jax.ShapeDtypeStruct((x_cells // 2, y_cells, z_cells), fields.dtype),
+        in_specs=[
+            pl.BlockSpec(memory_space=pltpu.SMEM),
+            pl.BlockSpec((count, x_cells // 2, y_cells, z_cells), lambda i: (0, side, 0, 0)),
+        ],
+        out_specs=pl.BlockSpec((x_cells // 2, y_cells, z_cells), lambda i: (0, 0, 0)),
         compiler_params=pltpu.CompilerParams(vmem_limit_bytes=16 * 1024 * 1024),
-        name="brick_viscosity",
+        name="half_viscosity",
     )(closure, fields)
 
 
-def evolve_kernel(place, viscosity, fields, x_halo, y_first, y_second, new_fields):
+def evolve_kernel(place, low_viscosity, high_viscosity, fields, x_halo, y_first, y_second, new_fields):
     up_first = lax.rem(place[2], 2) == 0
     x_cells, y_cells, z_cells = fields.shape[1:]
     row = lax.broadcasted_iota(jnp.int32, (y_cells, z_cells), 0)
@@ -485,6 +492,9 @@
 
     def plane(x, carry):
         centre = [fields[f, x] for f in range(F)]
+        low_x = jnp.minimum(x, x_cells // 2 - 1)
+        high_x = jnp.maximum(x - x_cells // 2, 0)
+        viscosity = jnp.where(x < x_cells // 2, low_viscosity[low_x], high_viscosity[high_x])
         below = jnp.maximum(x - 1, 0)
         above = jnp.minimum(x + 1, x_cells - 1)
         for f in range(F):
@@ -506,7 +516,7 @@
             advection = (
                 centre[0] * (east - west) + centre[1] * (north - south) + centre[2] * (upper - lower)
             )
-            tendency = viscosity[x] * laplacian - 0.5 * advection
+            tendency = viscosity * laplacian - 0.5 * advection
             if f == 2:
                 tendency = tendency + buoyancy * centre[3]
             new_fields[f, x] = value + time_step * tendency
@@ -515,16 +525,16 @@
     lax.fori_loop(0, x_cells, plane, 0)
 
 
-def evolve(place, viscosity, fields, x_halo, y_first, y_second):
+def evolve(place, viscosities, fields, x_halo, y_first, y_second):
     vmem = pl.BlockSpec(memory_space=pltpu.VMEM)
     return pl.pallas_call(
         evolve_kernel,
         out_shape=jax.ShapeDtypeStruct(fields.shape, fields.dtype),
-        in_specs=[pl.BlockSpec(memory_space=pltpu.SMEM)] + [vmem] * 5,
+        in_specs=[pl.BlockSpec(memory_space=pltpu.SMEM)] + [vmem] * 6,
         out_specs=vmem,
         compiler_params=pltpu.CompilerParams(vmem_limit_bytes=16 * 1024 * 1024),
         name="evolve_brick",
-    )(place, viscosity, fields, x_halo, y_first, y_second)
+    )(place, *viscosities, fields, x_halo, y_first, y_second)
 
 
 def cell_order():
@@ -664,9 +674,8 @@
     def corner(x_step, y_step):
         return corner_of(sample_block, place, x_step, y_step, y_cells, z_cells)
 
-    def piece(row, count, stride, z, lane_start):
-        values = windows[pl.ds(lax.div(z, 128) * window_rows + row, count, stride), :]
-        return pltpu.roll(values, lax.rem(lane_start - lax.rem(z, 128) + 256, 128), 1)
+    def window(row, z):
+        return windows[pl.ds(lax.div(z, 128) * window_rows + row, SUB, rows_of_x), :]
 
     lane = lax.broadcasted_iota(jnp.int32, (SUB, 128), 1)
     y_start, z_start = corner(0, 0)
@@ -680,12 +689,14 @@
             for step in range(8):
                 row = field * rows_of_field + y_start + half * 8 + step
                 first = step * SUB
-                inside = jnp.where(lane // SUB == step, piece(row, SUB, rows_of_x, z_start, first), inside)
-                below = jnp.where(lane == first, piece(row, SUB, rows_of_x, z_below, first), below)
-                last = first + SUB - 1
-                above = jnp.where(lane == last, piece(row, SUB, rows_of_x, z_above, last), above)
-            below = jnp.where(z_start == 0, 0.0, below)
-            above = jnp.where(z_start + SUB == z_cells, 0.0, above)
+                values = jnp.where(lane == 127, window(row, z_below), window(row, z_start))
+                values = jnp.where(lane == 0, window(row, z_above), values)
+                values = pltpu.roll(values, lax.rem(first - lax.rem(z_start, 128) + 256, 128), 1)
+                inside = jnp.where(lane // SUB == step, values, inside)
+                below = jnp.where(lane == (first - 1) % 128, values, below)
+                above = jnp.where(lane == (first + SUB) % 128, values, above)
+            below = jnp.where(z_start == 0, 0.0, pltpu.roll(below, 1, 1))
+            above = jnp.where(z_start + SUB == z_cells, 0.0, pltpu.roll(above, 127, 1))
             at = (slice(field * SUB, (field + 1) * SUB), slice(half * 128, (half + 1) * 128))
             centre[at] = inside
             lower[at] = jnp.where(lane % SUB == 0, below, pltpu.roll(inside, 1, 1))
@@ -694,7 +705,8 @@
     def y_row(y, z):
         total = jnp.zeros((SUB, 128), jnp.float32)
         for field in range(F):
-            part = piece(field * rows_of_field + y, SUB, rows_of_x, z, field * SUB)
+            part = window(field * rows_of_field + y, z)
+            part = pltpu.roll(part, lax.rem(field * SUB - lax.rem(z, 128) + 256, 128), 1)
             total = jnp.where(lane // SUB == field, part, total)
         return total
 
@@ -835,6 +847,8 @@
     closure = jnp.concatenate(
         [0.5 * closure_in.T, 0.5 * closure_bias[None], closure_out[None]], axis=0
     )
+    linear = jnp.sum(closure * closure_out[None], axis=1, keepdims=True)
+    closure = jnp.concatenate([closure, linear], axis=1)
     place = jnp.stack(
         [
             my_group,
@@ -872,14 +886,13 @@
         return [(first_trainer + c, first_trainer + (c ^ distance)) for c in range(trainers)]
 
     def to_trainers(payload):
-        return jnp.stack(
-            [
-                lax.ppermute(
-                    payload, everyone, [(g * trainers + c, first_trainer + c) for c in range(trainers)]
-                )
-                for g in range(sim_groups)
-            ]
-        )
+        landed = [
+            lax.ppermute(
+                payload, everyone, [(g * trainers + c, first_trainer + c) for c in range(trainers)]
+            )
+            for g in reversed(range(sim_groups))
+        ]
+        return jnp.stack(landed[::-1])
 
     def from_line(held):
         return [lax.ppermute(held, everyone, swap(apart)) for apart in range(1, y_devices)]
@@ -889,31 +902,40 @@
 
     thin = thin_faces(sample_block, place, brick, trainers)
     *cube, x_edges, y_edges = sample_cube(sample_block, place, brick)
+    first_count = CH * TAPS * F
+    first = jnp.pad(master[:first_count].reshape(CH, TAPS * F), ((0, 0), (0, 256 - TAPS * F)))
+    last = jnp.pad(master[first_count:].reshape(TAPS * F, CH), ((0, 256 - TAPS * F), (0, 0)))
+
+    *cube, first, last = lax.optimization_barrier((*cube, first, last))
+    selects = lax.optimization_barrier(
+        (jnp.asarray(SELECT_FIRST, jnp.bfloat16), jnp.asarray(SELECT_LAST, jnp.bfloat16))
+    )
+
     thin = lax.all_to_all(thin, ("gx", "gy"), split_axis=0, concat_axis=0, tiled=True)
     payload = cube_change(sample_block, place, closure, cube, thin, y_cells, z_cells)
     landed = to_trainers(payload)
     closure, landed = lax.optimization_barrier((closure, landed))
-    viscosity = lax.cond(
-        is_trainer,
-        lambda: jnp.zeros(brick.shape[1:], jnp.float32),
-        lambda: brick_viscosity(closure, brick),
-    )
-    x_edges, y_edges, viscosity = lax.optimization_barrier((x_edges, y_edges, viscosity))
-    halo = (x_neighbours(x_edges), *y_neighbours(y_edges[0], y_edges[1]))
+
+    def viscosity_part(closure, side):
+        return lax.cond(
+            is_trainer,
+            lambda: jnp.zeros((brick.shape[1] // 2, y_cells, z_cells), jnp.float32),
+            lambda: half_viscosity(closure, brick, side),
+        )
+
+    low_part = viscosity_part(closure, 0)
+    x_edges, y_edges, low_part = lax.optimization_barrier((x_edges, y_edges, low_part))
+    x_halo = x_neighbours(x_edges)
+    y_halo = y_neighbours(y_edges[0], y_edges[1])
+    closure, *y_halo = lax.optimization_barrier((closure, *y_halo))
+    viscosity = (low_part, viscosity_part(closure, 1))
+    halo = (x_halo, *y_halo)
     near = [landed, *from_line(landed)]
     far = [
         across(apart, pick_cubes(sample_trainer, place, near, y_devices, x_devices, apart))
         for apart in range(1, x_devices)
     ]
     arrived = [*near, *far]
-
-    first_count = CH * TAPS * F
-    first = jnp.pad(master[:first_count].reshape(CH, TAPS * F), ((0, 0), (0, 256 - TAPS * F)))
-    last = jnp.pad(master[first_count:].reshape(TAPS * F, CH), ((0, 256 - TAPS * F), (0, 0)))
-
-    first, last, *selects = lax.optimization_barrier(
-        (first, last, jnp.asarray(SELECT_FIRST, jnp.bfloat16), jnp.asarray(SELECT_LAST, jnp.bfloat16))
-    )
 
     def train_here():
         delta_first, delta_last, new_brick = train_cubes(

time: 112 us -> 110 us (0.982)
  waiting for transfers between devices: 20.4 us -> 25.4 us
  Pallas kernels: 52 us -> 48.8 us
  local copies, waits for them, and re-layouts: 4.17 us -> 1.27 us
    pallas_call x1 -> x2, Pallas kernels: 33.5 us -> 30.8 us  [half_viscosity(): pl.pallas_call(viscosity_kernel, grid=(1,), out_shape=jax.ShapeDtypeStruc...]
    ppermute x1, waiting for transfers between devices: 0.01 us -> 2.08 us  [y_neighbours(): lax.ppermute(for_second, everyone, pairs(0, -1))]
    ppermute x3, waiting for transfers between devices: 4.31 us -> 6.26 us  [on_device(): lax.ppermute(delta, everyone, [(first_trainer + c, g * trainers + c) for...]
  transfers between devices with their start and end apart: 18 -> 18, of which waited for: 7 -> 8; matrix products, arithmetic and copies ran while one was open for 3% -> 1% of each run, Pallas kernels for 35% -> 33%
where the time goes in v11:
time: 110 us
  Pallas kernels  48.8 us (44%)
  starting transfers between devices  30.4 us (28%)
  waiting for transfers between devices  25.4 us (23%)
  other arithmetic  2.28 us (2%)
  between operations  1.71 us (2%)
  local copies, waits for them, and re-layouts  1.27 us (1%)
    pallas_call x2, Pallas kernels, half_viscosity(): pl.pallas_call(viscosity_kernel, grid=(1,), out_shape=jax.ShapeDtypeStruc...  30.8 us
    pallas_call x1, Pallas kernels, evolve(): pl.pallas_call(evolve_kernel, out_shape=jax.ShapeDtypeStruct(fields.shape...  8.68 us
    all_to_all x1, starting transfers between devices, on_device(): lax.all_to_all(thin, ('gx', 'gy'), split_axis=0, concat_axis=0, tiled=True)  7.42 us
    ppermute x3, waiting for transfers between devices, on_device(): lax.ppermute(delta, everyone, [(first_trainer + c, g * trainers + c) for...  6.26 us
    ppermute x2, waiting for transfers between devices, on_device(): lax.ppermute(final, everyone, [(g * trainers + c, (g ^ apart) * trainers...  5.53 us
    ppermute x1, starting transfers between devices, y_neighbours(): lax.ppermute(for_second, everyone, pairs(0, -1))  4.89 us
    pallas_call x1, Pallas kernels, sample_cube(): pl.pallas_call(functools.partial(sample_kernel, y_cells, z_cells), out_sh...  4.28 us
    ppermute x2, waiting for transfers between devices, on_device(): final = final + lax.ppermute(held, everyone, meets)  4.25 us
  transfers between devices with their start and end apart: 18, of which 8 were waited for; matrix products, arithmetic and copies ran while one was open for 1% of the time, Pallas kernels for 33%

profile of v11, /device:TPU:0, one launch (start us, length us, event | category | flops | bytes accessed | tf_op | source)
XLA Modules:
  0.0 109.9 jit_solution(11119331050710152949)
XLA Ops:
  0.6 0.1 stack.27.place
  0.7 0.7 copy-done.1
  1.4 2.8 %thin_faces.1 = f32[8,16,256]{2,1,0:T(8,128)} custom-call(s32[24]{0:T(128)S(1)} %copy-done.1, s32[6]{0:T(128)S(1)} %stack.27.place, f32[2560,384]{1,0:T(8,128)} %bitcast.23, f32[80,32,384]{2,1,0:T(8,128)} %bitcast.24), custom_call_target="tpu_custom_call" | custom-call | tf_op jit(solution)/shard_map/thin_faces/pallas_call | solution.py:624
  4.2 0.0 copy-start.4
  4.2 0.0 copy-start
  4.2 7.4 %all-to-all-start = ((f32[8,16,256]{2,1,0:T(8,128)}), f32[8,16,256]{2,1,0:T(8,128)S(1)}, u32[]{:S(2)}, u32[]{:S(2)}) async-start(f32[8,16,256]{2,1,0:T(8,128)} %thin_faces.1), calls=%async_computation | async-start | bytes 262144 | tf_op jit(solution)/shard_map/all_to_all | solution.py:914
  11.7 0.1 fusion.1
  11.8 4.3 %sample_cube.1 = (f32[80,256]{1,0:T(8,128)S(1)}, f32[80,256]{1,0:T(8,128)S(1)}, f32[80,256]{1,0:T(8,128)S(1)}, f32[2,16,128]{2,1,0:T(8,128)S(1)}, f32[2,5,32,384...) custom-call(s32[24]{0:T(128)S(1)} %copy-done.2, s32[6]{0:T(128)S(1)} %stack.27.place, f32[2560,384]{1,0:T(8,128)} %bitcast.25), custom_call_target="tpu_custom_call" | custom-call | bytes 16000000 | tf_op jit(solution)/shard_map/sample_cube/pallas_call | solution.py:738
  16.1 0.1 fusion
  16.2 0.1 copy.15
  16.3 0.1 reshape.34
  16.4 0.2 slice.37
  16.6 0.1 pad_maximum_fusion.2.closure
  16.7 2.5 %all-to-all-done.thin = f32[8,16,256]{2,1,0:T(8,128)S(1)} async-done(((f32[8,16,256]{2,1,0:T(8,128)}), f32[8,16,256]{2,1,0:T(8,128)S(1)}, u32[]{:S(2)}, u32[]{:S(2)}) %all-to-all-start) | async-done | bytes 131104 | tf_op jit(solution)/shard_map/all_to_all | solution.py:914
  19.2 1.6 %cube_change.1 = bf16[320,128]{1,0:T(8,128)(2,1)S(1)} custom-call(s32[24]{0:T(128)S(1)} %copy-done.2, s32[6]{0:T(128)S(1)} %stack.27.place, f32[7,65]{1,0:T(8,128)S(1)} %pad_maximum_fusion.2.closure, bf16[256,256]{1,0:T(8,128)(2,1)S(1)} %copy-done, f32[80,256]{1,0:T(8,128)S(1)} %get-tuple-element.112.centre, f32[80,256]{1,0:T(8,128)S(1)} %get-tuple-element.113.lower, ...), custom_call_target="tpu_custom_call" | custom-call | tf_op jit(solution)/shard_map/cube_change/pallas_call | solution.py:821
  20.8 0.7 collective-permute-start.2
  21.4 0.7 collective-permute-start.1
  22.1 2.7 %collective-permute-start = (bf16[320,128]{1,0:T(8,128)(2,1)S(1)}, bf16[320,128]{1,0:T(8,128)(2,1)S(1)}, u32[]{:S(2)}, u32[]{:S(2)}) collective-permute-start(bf16[320,128]{1,0:T(8,128)(2,1)S(1)} %cube_change.1), channel_id=1, source_target_pairs={{0,24},{1,25},{2,26},{3,27},{4,28},{5,29},{6,30},{7,31}} | collective-permute-start | bytes 245768 | tf_op jit(solution)/shard_map/ppermute | solution.py:890
  24.8 2.0 %collective-permute-done = bf16[320,128]{1,0:T(8,128)(2,1)S(1)} collective-permute-done((bf16[320,128]{1,0:T(8,128)(2,1)S(1)}, bf16[320,128]{1,0:T(8,128)(2,1)S(1)}, u32[]{:S(2)}, u32[]{:S(2)}) %collective-permute-start) | collective-permute-done | bytes 81952 | tf_op jit(solution)/shard_map/ppermute | solution.py:890
  26.9 0.7 collective-permute-start.8
  27.6 0.7 collective-permute-start.7
  28.3 0.7 collective-permute-start.6
  29.0 15.4 %conditional.3 = (f32[8,32,384]{2,1,0:T(8,128)S(1)}) conditional(s32[]{:T(128)} %convert_element_type.6, (f32[7,65]{1,0:T(8,128)S(1)}, f32[5,16,32,384]{3,2,1,0:T(8,128)}) %tuple.57, () %tuple.38), branch_computations={%region_1.2_spmd, %region_2.3_spmd} | conditional | bytes 393228 | solution.py:920
  29.0 15.4 %half_viscosity.2 = f32[8,32,384]{2,1,0:T(8,128)S(1)} custom-call(f32[7,65]{1,0:T(8,128)S(1)} %get-tuple-element.33.closure, f32[5,16,32,384]{3,2,1,0:T(8,128)} %get-tuple-element.54.fields), custom_call_target="tpu_custom_call" | custom-call | tf_op jit(solution)/shard_map/cond/branch_0_fun/half_viscosity/pallas_call | solution.py:473
  44.4 2.5 %collective-permute-start.5 = (f32[2,5,32,384]{3,2,1,0:T(8,128)S(1)}, f32[2,5,32,384]{3,2,1,0:T(8,128)}, u32[]{:S(2)}, u32[]{:S(2)}) collective-permute-start(f32[2,5,32,384]{3,2,1,0:T(8,128)S(1)} %get-tuple-element.120), channel_id=1, source_target_pairs={{0,4},{1,5},{2,6},{3,7},{4,0},{5,1},{6,2},{7,3},{8,12},{9,13},{10,... | collective-permute-start | bytes 1474568 | tf_op jit(solution)/shard_map/ppermute | solution.py:875
  46.9 0.7 pick_cubes.1
  47.6 1.5 %collective-permute-start.9 = (bf16[6,320,128]{2,1,0:T(8,128)(2,1)S(1)}, bf16[6,320,128]{2,1,0:T(8,128)(2,1)}, u32[]{:S(2)}, u32[]{:S(2)}) collective-permute-start(bf16[6,320,128]{2,1,0:T(8,128)(2,1)S(1)} %pick_cubes.1), channel_id=1, source_target_pairs={{24,28},{25,29},{26,30},{27,31},{28,24},{29,25},{30,26},{31,27}} | collective-permute-start | bytes 1474568 | tf_op jit(solution)/shard_map/ppermute | solution.py:901
  49.1 4.9 %collective-permute-start.4 = (f32[5,16,384]{2,1,0:T(8,128)S(1)}, f32[5,16,384]{2,1,0:T(8,128)S(1)}, u32[]{:S(2)}, u32[]{:S(2)}) collective-permute-start(f32[5,16,384]{2,1,0:T(8,128)S(1)} %get-tuple-element.134), channel_id=1, source_target_pairs={{0,3},{1,2},{2,1},{3,0},{4,7},{5,6},{6,5},{7,4},{8,11},{9,10},{10,... | collective-permute-start | bytes 368648 | tf_op jit(solution)/shard_map/ppermute | solution.py:882
  54.0 1.9 %collective-permute-start.3 = (f32[5,16,384]{2,1,0:T(8,128)S(1)}, f32[5,16,384]{2,1,0:T(8,128)S(1)}, u32[]{:S(2)}, u32[]{:S(2)}) collective-permute-start(f32[5,16,384]{2,1,0:T(8,128)S(1)} %get-tuple-element.135), channel_id=1, source_target_pairs={{0,1},{1,0},{2,3},{3,2},{4,5},{5,4},{6,7},{7,6},{8,9},{9,8},{10,11... | collective-permute-start | bytes 368648 | tf_op jit(solution)/shard_map/ppermute | solution.py:881
  55.9 2.1 %collective-permute-done.4 = f32[5,16,384]{2,1,0:T(8,128)S(1)} collective-permute-done((f32[5,16,384]{2,1,0:T(8,128)S(1)}, f32[5,16,384]{2,1,0:T(8,128)S(1)}, u32[]{:S(2)}, u32[]{:S(2)}) %collective-permute-start.4) | collective-permute-done | bytes 122912 | tf_op jit(solution)/shard_map/ppermute | solution.py:882
  58.0 2.8 %collective-permute-done.3 = f32[5,16,384]{2,1,0:T(8,128)S(1)} collective-permute-done((f32[5,16,384]{2,1,0:T(8,128)S(1)}, f32[5,16,384]{2,1,0:T(8,128)S(1)}, u32[]{:S(2)}, u32[]{:S(2)}) %collective-permute-start.3) | collective-permute-done | bytes 122912 | tf_op jit(solution)/shard_map/ppermute | solution.py:881
  60.8 15.4 %conditional.4 = (f32[8,32,384]{2,1,0:T(8,128)S(1)}) conditional(s32[]{:T(128)} %convert_element_type.6, (f32[7,65]{1,0:T(8,128)S(1)}, f32[5,16,32,384]{3,2,1,0:T(8,128)}) %tuple.58, () %tuple.42), branch_computations={%region_3.4_spmd, %region_4.5_spmd} | conditional | bytes 393228 | solution.py:920
  60.8 15.4 %half_viscosity.3 = f32[8,32,384]{2,1,0:T(8,128)S(1)} custom-call(f32[7,65]{1,0:T(8,128)S(1)} %get-tuple-element.55.closure, f32[5,16,32,384]{3,2,1,0:T(8,128)} %get-tuple-element.56.fields), custom_call_target="tpu_custom_call" | custom-call | tf_op jit(solution)/shard_map/cond/branch_0_fun/half_viscosity/pallas_call | solution.py:473
  76.2 8.7 %conditional.5 = (f32[17280]{0:T(1024)S(1)}, f32[1,5,16,32,384]{4,3,2,1,0:T(8,128)}) conditional(s32[]{:T(128)} %convert_element_type.6, (s32[6]{0:T(128)S(1)}, f32[8,32,384]{2,1,0:T(8,128)S(1)}, f32[8,32,384]{2,1,0:T(8,128)S(1)}, f32[5,16,32,384]{3,2,1,0:T(8,128)}, f32[2,5,32,384]{3,2,1,0:T(8,128)}, /*index=5*/f32[5,16,384]{2,1,0:T(8,128)S(1)}, ...), branch_computations={%region_5.6_spmd, %region_6.7_spmd} | conditional | flops 17280 | bytes 345616 | solution.py:953
  76.2 8.7 %evolve_brick.1 = f32[5,16,32,384]{3,2,1,0:T(8,128)} custom-call(s32[6]{0:T(128)S(1)} %get-tuple-element.57.place, f32[8,32,384]{2,1,0:T(8,128)S(1)} %get-tuple-element.58.low_viscosity, f32[8,32,384]{2,1,0:T(8,128)S(1)} %get-tuple-element.59.high_viscosity, f32[5,16,32,384]{3,2,1,0:T(8,128)} %get-tuple-element.60.fields, ...), custom_call_target="tpu_custom_call" | custom-call | tf_op jit(solution)/shard_map/cond/branch_0_fun/evolve_brick/pallas_call | solution.py:530
  84.9 0.7 collective-permute-start.12
  85.6 0.7 collective-permute-start.11
  86.3 1.3 %collective-permute-start.10 = (f32[17280]{0:T(1024)S(1)}, f32[17280]{0:T(1024)S(1)}, u32[]{:S(2)}, u32[]{:S(2)}) collective-permute-start(f32[17280]{0:T(1024)S(1)} %get-tuple-element.129), channel_id=1, source_target_pairs={{24,0},{25,1},{26,2},{27,3},{28,4},{29,5},{30,6},{31,7}} | collective-permute-start | bytes 207368 | tf_op jit(solution)/shard_map/ppermute | solution.py:957
  87.6 6.3 %collective-permute-done.10 = f32[17280]{0:T(1024)S(1)} collective-permute-done((f32[17280]{0:T(1024)S(1)}, f32[17280]{0:T(1024)S(1)}, u32[]{:S(2)}, u32[]{:S(2)}) %collective-permute-start.10) | collective-permute-done | bytes 69152 | tf_op jit(solution)/shard_map/ppermute | solution.py:957
  93.8 1.9 %collective-permute-start.14 = (f32[17280]{0:T(1024)S(1)}, f32[17280]{0:T(1024)S(1)}, u32[]{:S(2)}, u32[]{:S(2)}) collective-permute-start(f32[17280]{0:T(1024)S(1)} %add_add_fusion.1), channel_id=1, source_target_pairs={{0,5},{1,4},{2,7},{3,6},{4,1},{5,0},{6,3},{7,2},{8,14},{9,15},{10,... | collective-permute-start | bytes 207368 | tf_op jit(solution)/shard_map/ppermute | solution.py:968
  95.8 1.4 %collective-permute-start.13 = (f32[17280]{0:T(1024)S(1)}, f32[17280]{0:T(1024)S(1)}, u32[]{:S(2)}, u32[]{:S(2)}) collective-permute-start(f32[17280]{0:T(1024)S(1)} %add_add_fusion.1), channel_id=1, source_target_pairs={{0,1},{1,0},{2,3},{3,2},{4,5},{5,4},{6,7},{7,6},{8,10},{9,11},{10,... | collective-permute-start | bytes 207368 | tf_op jit(solution)/shard_map/ppermute | solution.py:968
  97.2 4.2 %collective-permute-done.14 = f32[17280]{0:T(1024)S(1)} collective-permute-done((f32[17280]{0:T(1024)S(1)}, f32[17280]{0:T(1024)S(1)}, u32[]{:S(2)}, u32[]{:S(2)}) %collective-permute-start.14) | collective-permute-done | bytes 69152 | tf_op jit(solution)/shard_map/ppermute | solution.py:968
  101.5 0.1 collective-permute-start.15
  101.6 1.2 %collective-permute-done.15 = f32[17280]{0:T(1024)S(1)} collective-permute-done((f32[17280]{0:T(1024)S(1)}, f32[17280]{0:T(1024)S(1)}, u32[]{:S(2)}, u32[]{:S(2)}) %collective-permute-start.15) | collective-permute-done | bytes 69152 | tf_op jit(solution)/shard_map/ppermute | solution.py:970
  102.8 0.1 collective-permute-start.16
  102.9 4.3 %collective-permute-done.16 = f32[17280]{0:T(1024)S(1)} collective-permute-done((f32[17280]{0:T(1024)S(1)}, f32[17280]{0:T(1024)S(1)}, u32[]{:S(2)}, u32[]{:S(2)}) %collective-permute-start.16) | collective-permute-done | bytes 69152 | tf_op jit(solution)/shard_map/ppermute | solution.py:970
  107.2 0.6 multiply_reduce_fusion
  108.5 1.4 %multiply_subtract_fusion = (f32[540]{0:T(1024)}, f32[540]{0:T(1024)}) fusion(f32[17280]{0:T(1024)S(1)} %copy-done.3, s32[]{:T(128)S(6)} %select_n.2, f32[]{:T(128)S(6)} %sqrt.3, f32[17280]{0:T(1024)S(1)} %get-tuple-element.133, f32[17280]{0:T(1024)} %param.22), kind=kLoop, calls=%fused_computation.10 | loop fusion | flops 2700 | bytes 10808 | tf_op jit(solution)/shard_map/sub | solution.py:983
  (33 shorter events, 0.2 us)
Async XLA Ops:
  0.7 0.7 copy-start.1
  1.4 10.3 %copy-start.5 = (f32[64,5]{0,1:T(8,128)S(1)}, f32[64,5]{0,1:T(8,128)}, u32[]{:S(2)}) copy-start(f32[64,5]{0,1:T(8,128)} %param.18) | copy-start | bytes 3844
  1.4 10.3 %copy-start.3 = (f32[17280]{0:T(1024)S(1)}, f32[17280]{0:T(1024)}, u32[]{:S(2)}) copy-start(f32[17280]{0:T(1024)} %param.21) | copy-start | bytes 207364
  1.4 10.4 %copy-start.7 = (f32[64]{0:T(128)S(1)}, f32[64]{0:T(128)}, u32[]{:S(2)}) copy-start(f32[64]{0:T(128)} %param.19) | copy-start | bytes 772
  1.4 10.4 %copy-start.2 = (s32[24]{0:T(128)S(1)}, s32[24]{0:T(128)}, u32[]{:S(2)}) copy-start(s32[24]{0:T(128)} %sample_block.5) | copy-start | bytes 292
  4.2 11.9 %copy-start.4 = (f32[64]{0:T(128)S(1)}, f32[64]{0:T(128)}, u32[]{:S(2)}) copy-start(f32[64]{0:T(128)} %param.20) | copy-start | bytes 772
  4.2 15.0 %copy-start = (bf16[256,256]{1,0:T(8,128)(2,1)S(1)}, bf16[256,256]{1,0:T(8,128)(2,1)}, u32[]{:S(2)}) copy-start(bf16[256,256]{1,0:T(8,128)(2,1)} %constant.60.clone.order) | copy-start | bytes 393220
  4.2 14.9 %all-to-all-start = ((f32[8,16,256]{2,1,0:T(8,128)}), f32[8,16,256]{2,1,0:T(8,128)S(1)}, u32[]{:S(2)}, u32[]{:S(2)}) async-start(f32[8,16,256]{2,1,0:T(8,128)} %thin_faces.1), calls=%async_computation | async-start | bytes 262144 | tf_op jit(solution)/shard_map/all_to_all | solution.py:914
  16.1 30.8 %copy-start.6 = (s32[24]{0:T(128)S(1)}, s32[24]{0:T(128)}, u32[]{:S(2)}) copy-start(s32[24]{0:T(128)} %trainer_of.1) | copy-start | bytes 292
  20.8 4.1 %collective-permute-start.2 = (bf16[320,128]{1,0:T(8,128)(2,1)S(1)}, bf16[320,128]{1,0:T(8,128)(2,1)S(1)}, u32[]{:S(2)}, u32[]{:S(2)}) collective-permute-start(bf16[320,128]{1,0:T(8,128)(2,1)S(1)} %cube_change.1), channel_id=1, source_target_pairs={{16,24},{17,25},{18,26},{19,27},{20,28},{21,29},{22,30},{23,31}} | collective-permute-start | bytes 245768 | tf_op jit(solution)/shard_map/ppermute | solution.py:890
  21.4 3.4 %collective-permute-start.1 = (bf16[320,128]{1,0:T(8,128)(2,1)S(1)}, bf16[320,128]{1,0:T(8,128)(2,1)S(1)}, u32[]{:S(2)}, u32[]{:S(2)}) collective-permute-start(bf16[320,128]{1,0:T(8,128)(2,1)S(1)} %cube_change.1), channel_id=1, source_target_pairs={{8,24},{9,25},{10,26},{11,27},{12,28},{13,29},{14,30},{15,31}} | collective-permute-start | bytes 245768 | tf_op jit(solution)/shard_map/ppermute | solution.py:890
  22.1 4.8 %collective-permute-start = (bf16[320,128]{1,0:T(8,128)(2,1)S(1)}, bf16[320,128]{1,0:T(8,128)(2,1)S(1)}, u32[]{:S(2)}, u32[]{:S(2)}) collective-permute-start(bf16[320,128]{1,0:T(8,128)(2,1)S(1)} %cube_change.1), channel_id=1, source_target_pairs={{0,24},{1,25},{2,26},{3,27},{4,28},{5,29},{6,30},{7,31}} | collective-permute-start | bytes 245768 | tf_op jit(solution)/shard_map/ppermute | solution.py:890
  26.9 19.9 %collective-permute-start.8 = (bf16[3,320,128]{2,1,0:T(8,128)(2,1)S(1)}, bf16[3,320,128]{2,1,0:T(8,128)(2,1)S(1)}, u32[]{:S(2)}, u32[]{:S(2)}) collective-permute-start(bf16[3,320,128]{2,1,0:T(8,128)(2,1)S(1)} %pad_maximum_fusion.1.refs_0_), channel_id=1, source_target_pairs={{24,27},{25,26},{26,25},{27,24},{28,31},{29,30},{30,29},{31,28}} | collective-permute-start | bytes 737288 | tf_op jit(solution)/shard_map/ppermute | solution.py:898
  27.6 19.3 %collective-permute-start.7 = (bf16[3,320,128]{2,1,0:T(8,128)(2,1)S(1)}, bf16[3,320,128]{2,1,0:T(8,128)(2,1)S(1)}, u32[]{:S(2)}, u32[]{:S(2)}) collective-permute-start(bf16[3,320,128]{2,1,0:T(8,128)(2,1)S(1)} %pad_maximum_fusion.1.refs_0_), channel_id=1, source_target_pairs={{24,26},{25,27},{26,24},{27,25},{28,30},{29,31},{30,28},{31,29}} | collective-permute-start | bytes 737288 | tf_op jit(solution)/shard_map/ppermute | solution.py:898
  28.3 18.6 %collective-permute-start.6 = (bf16[3,320,128]{2,1,0:T(8,128)(2,1)S(1)}, bf16[3,320,128]{2,1,0:T(8,128)(2,1)S(1)}, u32[]{:S(2)}, u32[]{:S(2)}) collective-permute-start(bf16[3,320,128]{2,1,0:T(8,128)(2,1)S(1)} %pad_maximum_fusion.1.refs_0_), channel_id=1, source_target_pairs={{24,25},{25,24},{26,27},{27,26},{28,29},{29,28},{30,31},{31,30}} | collective-permute-start | bytes 737288 | tf_op jit(solution)/shard_map/ppermute | solution.py:898
  44.4 31.8 %collective-permute-start.5 = (f32[2,5,32,384]{3,2,1,0:T(8,128)S(1)}, f32[2,5,32,384]{3,2,1,0:T(8,128)}, u32[]{:S(2)}, u32[]{:S(2)}) collective-permute-start(f32[2,5,32,384]{3,2,1,0:T(8,128)S(1)} %get-tuple-element.120), channel_id=1, source_target_pairs={{0,4},{1,5},{2,6},{3,7},{4,0},{5,1},{6,2},{7,3},{8,12},{9,13},{10,... | collective-permute-start | bytes 1474568 | tf_op jit(solution)/shard_map/ppermute | solution.py:875
  47.6 28.6 %collective-permute-start.9 = (bf16[6,320,128]{2,1,0:T(8,128)(2,1)S(1)}, bf16[6,320,128]{2,1,0:T(8,128)(2,1)}, u32[]{:S(2)}, u32[]{:S(2)}) collective-permute-start(bf16[6,320,128]{2,1,0:T(8,128)(2,1)S(1)} %pick_cubes.1), channel_id=1, source_target_pairs={{24,28},{25,29},{26,30},{27,31},{28,24},{29,25},{30,26},{31,27}} | collective-permute-start | bytes 1474568 | tf_op jit(solution)/shard_map/ppermute | solution.py:901
  49.1 8.9 %collective-permute-start.4 = (f32[5,16,384]{2,1,0:T(8,128)S(1)}, f32[5,16,384]{2,1,0:T(8,128)S(1)}, u32[]{:S(2)}, u32[]{:S(2)}) collective-permute-start(f32[5,16,384]{2,1,0:T(8,128)S(1)} %get-tuple-element.134), channel_id=1, source_target_pairs={{0,3},{1,2},{2,1},{3,0},{4,7},{5,6},{6,5},{7,4},{8,11},{9,10},{10,... | collective-permute-start | bytes 368648 | tf_op jit(solution)/shard_map/ppermute | solution.py:882
  54.0 6.8 %collective-permute-start.3 = (f32[5,16,384]{2,1,0:T(8,128)S(1)}, f32[5,16,384]{2,1,0:T(8,128)S(1)}, u32[]{:S(2)}, u32[]{:S(2)}) collective-permute-start(f32[5,16,384]{2,1,0:T(8,128)S(1)} %get-tuple-element.135), channel_id=1, source_target_pairs={{0,1},{1,0},{2,3},{3,2},{4,5},{5,4},{6,7},{7,6},{8,9},{9,8},{10,11... | collective-permute-start | bytes 368648 | tf_op jit(solution)/shard_map/ppermute | solution.py:881
  84.9 2.6 %collective-permute-start.12 = (f32[17280]{0:T(1024)S(1)}, f32[17280]{0:T(1024)S(1)}, u32[]{:S(2)}, u32[]{:S(2)}) collective-permute-start(f32[17280]{0:T(1024)S(1)} %get-tuple-element.129), channel_id=1, source_target_pairs={{24,16},{25,17},{26,18},{27,19},{28,20},{29,21},{30,22},{31,23}} | collective-permute-start | bytes 207368 | tf_op jit(solution)/shard_map/ppermute | solution.py:957
  85.6 2.0 %collective-permute-start.11 = (f32[17280]{0:T(1024)S(1)}, f32[17280]{0:T(1024)S(1)}, u32[]{:S(2)}, u32[]{:S(2)}) collective-permute-start(f32[17280]{0:T(1024)S(1)} %get-tuple-element.129), channel_id=1, source_target_pairs={{24,8},{25,9},{26,10},{27,11},{28,12},{29,13},{30,14},{31,15}} | collective-permute-start | bytes 207368 | tf_op jit(solution)/shard_map/ppermute | solution.py:957
  86.3 7.6 %collective-permute-start.10 = (f32[17280]{0:T(1024)S(1)}, f32[17280]{0:T(1024)S(1)}, u32[]{:S(2)}, u32[]{:S(2)}) collective-permute-start(f32[17280]{0:T(1024)S(1)} %get-tuple-element.129), channel_id=1, source_target_pairs={{24,0},{25,1},{26,2},{27,3},{28,4},{29,5},{30,6},{31,7}} | collective-permute-start | bytes 207368 | tf_op jit(solution)/shard_map/ppermute | solution.py:957
  93.8 7.6 %collective-permute-start.14 = (f32[17280]{0:T(1024)S(1)}, f32[17280]{0:T(1024)S(1)}, u32[]{:S(2)}, u32[]{:S(2)}) collective-permute-start(f32[17280]{0:T(1024)S(1)} %add_add_fusion.1), channel_id=1, source_target_pairs={{0,5},{1,4},{2,7},{3,6},{4,1},{5,0},{6,3},{7,2},{8,14},{9,15},{10,... | collective-permute-start | bytes 207368 | tf_op jit(solution)/shard_map/ppermute | solution.py:968
  95.8 5.7 %collective-permute-start.13 = (f32[17280]{0:T(1024)S(1)}, f32[17280]{0:T(1024)S(1)}, u32[]{:S(2)}, u32[]{:S(2)}) collective-permute-start(f32[17280]{0:T(1024)S(1)} %add_add_fusion.1), channel_id=1, source_target_pairs={{0,1},{1,0},{2,3},{3,2},{4,5},{5,4},{6,7},{7,6},{8,10},{9,11},{10,... | collective-permute-start | bytes 207368 | tf_op jit(solution)/shard_map/ppermute | solution.py:968
  101.5 1.3 %collective-permute-start.15 = (f32[17280]{0:T(1024)S(1)}, f32[17280]{0:T(1024)S(1)}, u32[]{:S(2)}, u32[]{:S(2)}) collective-permute-start(f32[17280]{0:T(1024)S(1)} %add_add_fusion), channel_id=1, source_target_pairs={{0,8},{1,9},{2,10},{3,11},{4,12},{5,13},{6,14},{7,15},{8,0},{9,1},... | collective-permute-start | bytes 207368 | tf_op jit(solution)/shard_map/ppermute | solution.py:970
  102.8 4.4 %collective-permute-start.16 = (f32[17280]{0:T(1024)S(1)}, f32[17280]{0:T(1024)S(1)}, u32[]{:S(2)}, u32[]{:S(2)}) collective-permute-start(f32[17280]{0:T(1024)S(1)} %add.50), channel_id=1, source_target_pairs={{0,16},{1,17},{2,18},{3,19},{4,20},{5,21},{6,22},{7,23},{8,24},{9,... | collective-permute-start | bytes 207368 | tf_op jit(solution)/shard_map/ppermute | solution.py:970

commit v12 on v11

--- a/solution.py
+++ b/solution.py
@@ -281,7 +281,7 @@
                 store_planes(inputs[pair], x, channels)
         return carry
 
-    lax.fori_loop(0, 4, stack_planes, 0, unroll=4)
+    lax.fori_loop(0, 4, stack_planes, 0, unroll=2)
 
     for copy in select_copies:
         copy.wait()
@@ -455,36 +455,65 @@
     return base_viscosity + viscosity_gain * soft
 
 
-def viscosity_kernel(closure, fields, viscosity):
-    x_cells, y_cells = fields.shape[1:3]
-    part = y_cells // 2
-
-    def plane(x, carry):
-        for half in range(2):
-            rows = pl.ds(half * part, part)
-            viscosity[x, rows, :] = viscosity_of([fields[f, x, rows, :] for f in range(F)], closure)
+def viscosity_kernel(closure, fields, viscosity, weights, out_column):
+    x_cells, y_cells, z_cells = fields.shape[1:]
+    plain = closure[...]
+    high = plain.astype(jnp.bfloat16).astype(jnp.float32)
+    low = plain - high
+    blank = jnp.zeros((8, 128), jnp.float32)
+    for j in range(8):
+        turned = [pltpu.roll(part, j, 0) if j else part for part in (high, high, low)]
+        stacked = jnp.concatenate([*turned, blank], axis=0)
+        weights[j] = stacked.T[: HID + 8].astype(jnp.bfloat16)
+    out_column[...] = jnp.broadcast_to(plain.T[:HID, F + 1 : F + 2], (HID, 128))
+    sublane = lax.broadcasted_iota(jnp.int32, (8, z_cells), 0)
+    wide = z_cells // 128
+    tiles = y_cells // 8
+
+    def tile(index, carry):
+        x, rows = index // tiles, pl.ds(pl.multiple_of(index % tiles * 8, 8), 8)
+        turned = [fields[f, x, rows, :] for f in range(F)]
+        turned = [pltpu.roll(turned[f], f, 0) if f else turned[f] for f in range(F)]
+        sums = jnp.zeros((8, z_cells), jnp.float32)
+        for j in range(8):
+            cells = jnp.where(sublane == (j + F) % 8, 1.0, 0.0)
+            for f in range(F):
+                cells = jnp.where(sublane == (j + f) % 8, turned[f], cells)
+            top = cells.astype(jnp.bfloat16).astype(jnp.float32)
+            stacked = jnp.concatenate([top, cells - top, top, jnp.zeros_like(top)], axis=0)
+            half = dot_rows(weights[j], stacked.astype(jnp.bfloat16))
+            total = half[HID:]
+            for group in range(HID // 8):
+                part = half[group * 8 : group * 8 + 8]
+                column = jnp.concatenate([out_column[group * 8 : group * 8 + 8, :]] * wide, axis=1)
+                total = total + column * (part * jnp.tanh(part))
+            for step in (4, 2, 1):
+                total = total + pltpu.roll(total, step, 0)
+            sums = jnp.where(sublane == j, total, sums)
+        soft = jnp.maximum(sums, 0.0) + jnp.log1p(jnp.exp(-jnp.abs(sums)))
+        viscosity[x, rows, :] = base_viscosity + viscosity_gain * soft
         return carry
 
-    lax.fori_loop(0, x_cells, plane, 0)
-
-
-def half_viscosity(closure, fields, side):
-    count, x_cells, y_cells, z_cells = fields.shape
+    lax.fori_loop(0, x_cells * tiles, tile, 0)
+
+
+def brick_viscosity(closure, fields):
+    vmem = pl.BlockSpec(memory_space=pltpu.VMEM)
     return pl.pallas_call(
         viscosity_kernel,
-        grid=(1,),
-        out_shape=jax.ShapeDtypeStruct((x_cells // 2, y_cells, z_cells), fields.dtype),
-        in_specs=[
-            pl.BlockSpec(memory_space=pltpu.SMEM),
-            pl.BlockSpec((count, x_cells // 2, y_cells, z_cells), lambda i: (0, side, 0, 0)),
+        out_shape=jax.ShapeDtypeStruct(fields.shape[1:], fields.dtype),
+        in_specs=[vmem, vmem],
+        out_specs=vmem,
+        scratch_shapes=[
+            pltpu.VMEM((8, HID + 8, 32), jnp.bfloat16),
+            pltpu.VMEM((HID, 128), jnp.float32),
         ],
-        out_specs=pl.BlockSpec((x_cells // 2, y_cells, z_cells), lambda i: (0, 0, 0)),
         compiler_params=pltpu.CompilerParams(vmem_limit_bytes=16 * 1024 * 1024),
-        name="half_viscosity",
+        name="brick_viscosity",
     )(closure, fields)
 
 
-def evolve_kernel(place, low_viscosity, high_viscosity, fields, x_halo, y_first, y_second, new_fields):
+def evolve_kernel(place, viscosity, fields, x_halo, y_first, y_second, new_fields):
     up_first = lax.rem(place[2], 2) == 0
     x_cells, y_cells, z_cells = fields.shape[1:]
     row = lax.broadcasted_iota(jnp.int32, (y_cells, z_cells), 0)
@@ -492,9 +521,6 @@
 
     def plane(x, carry):
         centre = [fields[f, x] for f in range(F)]
-        low_x = jnp.minimum(x, x_cells // 2 - 1)
-        high_x = jnp.maximum(x - x_cells // 2, 0)
-        viscosity = jnp.where(x < x_cells // 2, low_viscosity[low_x], high_viscosity[high_x])
         below = jnp.maximum(x - 1, 0)
         above = jnp.minimum(x + 1, x_cells - 1)
         for f in range(F):
@@ -516,7 +542,7 @@
             advection = (
                 centre[0] * (east - west) + centre[1] * (north - south) + centre[2] * (upper - lower)
             )
-            tendency = viscosity * laplacian - 0.5 * advection
+            tendency = viscosity[x] * laplacian - 0.5 * advection
             if f == 2:
                 tendency = tendency + buoyancy * centre[3]
             new_fields[f, x] = value + time_step * tendency
@@ -525,16 +551,16 @@
     lax.fori_loop(0, x_cells, plane, 0)
 
 
-def evolve(place, viscosities, fields, x_halo, y_first, y_second):
+def evolve(place, viscosity, fields, x_halo, y_first, y_second):
     vmem = pl.BlockSpec(memory_space=pltpu.VMEM)
     return pl.pallas_call(
         evolve_kernel,
         out_shape=jax.ShapeDtypeStruct(fields.shape, fields.dtype),
-        in_specs=[pl.BlockSpec(memory_space=pltpu.SMEM)] + [vmem] * 6,
+        in_specs=[pl.BlockSpec(memory_space=pltpu.SMEM)] + [vmem] * 5,
         out_specs=vmem,
         compiler_params=pltpu.CompilerParams(vmem_limit_bytes=16 * 1024 * 1024),
         name="evolve_brick",
-    )(place, *viscosities, fields, x_halo, y_first, y_second)
+    )(place, viscosity, fields, x_halo, y_first, y_second)
 
 
 def cell_order():
@@ -848,7 +874,7 @@
         [0.5 * closure_in.T, 0.5 * closure_bias[None], closure_out[None]], axis=0
     )
     linear = jnp.sum(closure * closure_out[None], axis=1, keepdims=True)
-    closure = jnp.concatenate([closure, linear], axis=1)
+    closure = jnp.pad(jnp.concatenate([closure, linear], axis=1), ((0, 1), (0, 127 - HID)))
     place = jnp.stack(
         [
             my_group,
@@ -916,20 +942,15 @@
     landed = to_trainers(payload)
     closure, landed = lax.optimization_barrier((closure, landed))
 
-    def viscosity_part(closure, side):
-        return lax.cond(
-            is_trainer,
-            lambda: jnp.zeros((brick.shape[1] // 2, y_cells, z_cells), jnp.float32),
-            lambda: half_viscosity(closure, brick, side),
-        )
-
-    low_part = viscosity_part(closure, 0)
-    x_edges, y_edges, low_part = lax.optimization_barrier((x_edges, y_edges, low_part))
-    x_halo = x_neighbours(x_edges)
+    viscosity = lax.cond(
+        is_trainer,
+        lambda: jnp.zeros(brick.shape[1:], jnp.float32),
+        lambda: brick_viscosity(closure, brick),
+    )
+    y_edges, viscosity = lax.optimization_barrier((y_edges, viscosity))
     y_halo = y_neighbours(y_edges[0], y_edges[1])
-    closure, *y_halo = lax.optimization_barrier((closure, *y_halo))
-    viscosity = (low_part, viscosity_part(closure, 1))
-    halo = (x_halo, *y_halo)
+    x_edges, *y_halo = lax.optimization_barrier((x_edges, *y_halo))
+    halo = (x_neighbours(x_edges), *y_halo)
     near = [landed, *from_line(landed)]
     far = [
         across(apart, pick_cubes(sample_trainer, place, near, y_devices, x_devices, apart))

time: 110 us -> 110 us (level)
  Pallas kernels: 48.8 us -> 42.9 us
  waiting for transfers between devices: 25.4 us -> 30.7 us
    ppermute x1, waiting for transfers between devices: 0.01 us -> 8.53 us  [x_neighbours(): return lax.ppermute(edges, everyone, pairs(1, 0))]
    pallas_call x2 -> x1, Pallas kernels: 30.8 us -> 24.9 us  [brick_viscosity(): pl.pallas_call(viscosity_kernel, out_shape=jax.ShapeDtypeStruct(fields.sh...]
    ppermute x3, waiting for transfers between devices: 6.26 us -> 4.31 us  [on_device(): lax.ppermute(delta, everyone, [(first_trainer + c, g * trainers + c) for...]
    ppermute x2, waiting for transfers between devices: 4.25 us -> 2.94 us  [on_device(): final = final + lax.ppermute(held, everyone, meets)]
    ppermute x2, starting transfers between devices: 3.35 us -> 4.6 us  [on_device(): final = final + lax.ppermute(held, everyone, meets)]
  transfers between devices with their start and end apart: 18 -> 18, of which waited for: 8 -> 10; matrix products, arithmetic and copies ran while one was open for 1% -> 1% of each run, Pallas kernels for 33% -> 27%
where the time goes in v12:
time: 110 us
  Pallas kernels  42.9 us (39%)
  starting transfers between devices  30.9 us (28%)
  waiting for transfers between devices  30.7 us (28%)
  other arithmetic  2.28 us (2%)
  between operations  1.7 us (2%)
  local copies, waits for them, and re-layouts  1.27 us (1%)
    pallas_call x1, Pallas kernels, brick_viscosity(): pl.pallas_call(viscosity_kernel, out_shape=jax.ShapeDtypeStruct(fields.sh...  24.9 us
    pallas_call x1, Pallas kernels, evolve(): pl.pallas_call(evolve_kernel, out_shape=jax.ShapeDtypeStruct(fields.shape...  8.59 us
    ppermute x1, waiting for transfers between devices, x_neighbours(): return lax.ppermute(edges, everyone, pairs(1, 0))  8.53 us
    all_to_all x1, starting transfers between devices, on_device(): lax.all_to_all(thin, ('gx', 'gy'), split_axis=0, concat_axis=0, tiled=True)  7.42 us
    ppermute x2, waiting for transfers between devices, on_device(): lax.ppermute(final, everyone, [(g * trainers + c, (g ^ apart) * trainers...  5.53 us
    ppermute x2, starting transfers between devices, on_device(): final = final + lax.ppermute(held, everyone, meets)  4.6 us
    ppermute x3, waiting for transfers between devices, on_device(): lax.ppermute(delta, everyone, [(first_trainer + c, g * trainers + c) for...  4.31 us
    pallas_call x1, Pallas kernels, sample_cube(): pl.pallas_call(functools.partial(sample_kernel, y_cells, z_cells), out_sh...  4.28 us
  transfers between devices with their start and end apart: 18, of which 10 were waited for; matrix products, arithmetic and copies ran while one was open for 1% of the time, Pallas kernels for 27%

profile of v12, /device:TPU:0, one launch (start us, length us, event | category | flops | bytes accessed | tf_op | source)
XLA Modules:
  0.0 109.7 jit_solution(1806556573302535725)
XLA Ops:
  0.6 0.1 stack.27.place
  0.7 0.7 copy-done.1
  1.4 2.8 %thin_faces.1 = f32[8,16,256]{2,1,0:T(8,128)} custom-call(s32[24]{0:T(128)S(1)} %copy-done.1, s32[6]{0:T(128)S(1)} %stack.27.place, f32[2560,384]{1,0:T(8,128)} %bitcast.23, f32[80,32,384]{2,1,0:T(8,128)} %bitcast.24), custom_call_target="tpu_custom_call" | custom-call | tf_op jit(solution)/shard_map/thin_faces/pallas_call | solution.py:650
  4.2 0.0 copy-start.5
  4.2 0.0 copy-start
  4.2 7.4 %all-to-all-start = ((f32[8,16,256]{2,1,0:T(8,128)}), f32[8,16,256]{2,1,0:T(8,128)S(1)}, u32[]{:S(2)}, u32[]{:S(2)}) async-start(f32[8,16,256]{2,1,0:T(8,128)} %thin_faces.1), calls=%async_computation | async-start | bytes 262144 | tf_op jit(solution)/shard_map/all_to_all | solution.py:940
  11.7 0.1 fusion.1
  11.8 4.3 %sample_cube.1 = (f32[80,256]{1,0:T(8,128)S(1)}, f32[80,256]{1,0:T(8,128)S(1)}, f32[80,256]{1,0:T(8,128)S(1)}, f32[2,16,128]{2,1,0:T(8,128)S(1)}, f32[2,5,32,384...) custom-call(s32[24]{0:T(128)S(1)} %copy-done.2, s32[6]{0:T(128)S(1)} %stack.27.place, f32[2560,384]{1,0:T(8,128)} %bitcast.25), custom_call_target="tpu_custom_call" | custom-call | bytes 16000000 | tf_op jit(solution)/shard_map/sample_cube/pallas_call | solution.py:764
  16.1 0.1 fusion
  16.2 0.1 copy.15
  16.3 0.1 reshape.34
  16.4 0.2 slice.37
  16.6 0.1 select_maximum_fusion.closure
  16.7 2.5 %all-to-all-done.thin = f32[8,16,256]{2,1,0:T(8,128)S(1)} async-done(((f32[8,16,256]{2,1,0:T(8,128)}), f32[8,16,256]{2,1,0:T(8,128)S(1)}, u32[]{:S(2)}, u32[]{:S(2)}) %all-to-all-start) | async-done | bytes 131104 | tf_op jit(solution)/shard_map/all_to_all | solution.py:940
  19.2 1.6 %cube_change.1 = bf16[320,128]{1,0:T(8,128)(2,1)S(1)} custom-call(s32[24]{0:T(128)S(1)} %copy-done.2, s32[6]{0:T(128)S(1)} %stack.27.place, f32[8,128]{1,0:T(8,128)S(1)} %select_maximum_fusion.closure, bf16[256,256]{1,0:T(8,128)(2,1)S(1)} %copy-done, f32[80,256]{1,0:T(8,128)S(1)} %get-tuple-element.98.centre, f32[80,256]{1,0:T(8,128)S(1)} %get-tuple-element.99.lower, ...), custom_call_target="tpu_custom_call" | custom-call | tf_op jit(solution)/shard_map/cube_change/pallas_call | solution.py:847
  20.8 0.7 collective-permute-start.2
  21.4 0.7 collective-permute-start.1
  22.1 2.7 %collective-permute-start = (bf16[320,128]{1,0:T(8,128)(2,1)S(1)}, bf16[320,128]{1,0:T(8,128)(2,1)S(1)}, u32[]{:S(2)}, u32[]{:S(2)}) collective-permute-start(bf16[320,128]{1,0:T(8,128)(2,1)S(1)} %cube_change.1), channel_id=1, source_target_pairs={{0,24},{1,25},{2,26},{3,27},{4,28},{5,29},{6,30},{7,31}} | collective-permute-start | bytes 245768 | tf_op jit(solution)/shard_map/ppermute | solution.py:916
  24.8 2.0 %collective-permute-done = bf16[320,128]{1,0:T(8,128)(2,1)S(1)} collective-permute-done((bf16[320,128]{1,0:T(8,128)(2,1)S(1)}, bf16[320,128]{1,0:T(8,128)(2,1)S(1)}, u32[]{:S(2)}, u32[]{:S(2)}) %collective-permute-start) | collective-permute-done | bytes 81952 | tf_op jit(solution)/shard_map/ppermute | solution.py:916
  26.9 0.8 collective-permute-start.8
  27.7 0.7 collective-permute-start.7
  28.4 0.7 collective-permute-start.6
  29.1 24.9 %conditional.2 = (f32[16,32,384]{2,1,0:T(8,128)S(1)}) conditional(s32[]{:T(128)} %convert_element_type.10, (f32[8,128]{1,0:T(8,128)S(1)}, f32[5,16,32,384]{3,2,1,0:T(8,128)}) %tuple.47, () %tuple.32), branch_computations={%region_1.2_spmd, %region_2.3_spmd} | conditional | bytes 786444 | solution.py:945
  29.1 24.9 %brick_viscosity.1 = f32[16,32,384]{2,1,0:T(8,128)S(1)} custom-call(f32[8,128]{1,0:T(8,128)S(1)} %get-tuple-element.44.closure, f32[5,16,32,384]{3,2,1,0:T(8,128)} %get-tuple-element.45.fields), custom_call_target="tpu_custom_call" | custom-call | tf_op jit(solution)/shard_map/cond/branch_0_fun/brick_viscosity/pallas_call | solution.py:502
  54.1 3.9 %collective-permute-start.4 = (f32[5,16,384]{2,1,0:T(8,128)S(1)}, f32[5,16,384]{2,1,0:T(8,128)S(1)}, u32[]{:S(2)}, u32[]{:S(2)}) collective-permute-start(f32[5,16,384]{2,1,0:T(8,128)S(1)} %get-tuple-element.120), channel_id=1, source_target_pairs={{0,3},{1,2},{2,1},{3,0},{4,7},{5,6},{6,5},{7,4},{8,11},{9,10},{10,... | collective-permute-start | bytes 368648 | tf_op jit(solution)/shard_map/ppermute | solution.py:908
  58.0 1.9 %collective-permute-start.3 = (f32[5,16,384]{2,1,0:T(8,128)S(1)}, f32[5,16,384]{2,1,0:T(8,128)S(1)}, u32[]{:S(2)}, u32[]{:S(2)}) collective-permute-start(f32[5,16,384]{2,1,0:T(8,128)S(1)} %get-tuple-element.121), channel_id=1, source_target_pairs={{0,1},{1,0},{2,3},{3,2},{4,5},{5,4},{6,7},{7,6},{8,9},{9,8},{10,11... | collective-permute-start | bytes 368648 | tf_op jit(solution)/shard_map/ppermute | solution.py:907
  59.9 3.1 %collective-permute-done.4 = f32[5,16,384]{2,1,0:T(8,128)S(1)} collective-permute-done((f32[5,16,384]{2,1,0:T(8,128)S(1)}, f32[5,16,384]{2,1,0:T(8,128)S(1)}, u32[]{:S(2)}, u32[]{:S(2)}) %collective-permute-start.4) | collective-permute-done | bytes 122912 | tf_op jit(solution)/shard_map/ppermute | solution.py:908
  63.0 1.7 %collective-permute-done.3 = f32[5,16,384]{2,1,0:T(8,128)S(1)} collective-permute-done((f32[5,16,384]{2,1,0:T(8,128)S(1)}, f32[5,16,384]{2,1,0:T(8,128)S(1)}, u32[]{:S(2)}, u32[]{:S(2)}) %collective-permute-start.3) | collective-permute-done | bytes 122912 | tf_op jit(solution)/shard_map/ppermute | solution.py:907
  64.7 3.4 %collective-permute-start.5 = (f32[2,5,32,384]{3,2,1,0:T(8,128)S(1)}, f32[2,5,32,384]{3,2,1,0:T(8,128)S(1)}, u32[]{:S(2)}, u32[]{:S(2)}) collective-permute-start(f32[2,5,32,384]{3,2,1,0:T(8,128)S(1)} %get-tuple-element.106), channel_id=1, source_target_pairs={{0,4},{1,5},{2,6},{3,7},{4,0},{5,1},{6,2},{7,3},{8,12},{9,13},{10,... | collective-permute-start | bytes 1474568 | tf_op jit(solution)/shard_map/ppermute | solution.py:901
  68.2 0.7 pick_cubes.1
  68.9 0.7 collective-permute-start.9
  69.6 8.5 %collective-permute-done.5 = f32[2,5,32,384]{3,2,1,0:T(8,128)S(1)} collective-permute-done((f32[2,5,32,384]{3,2,1,0:T(8,128)S(1)}, f32[2,5,32,384]{3,2,1,0:T(8,128)S(1)}, u32[]{:S(2)}, u32[]{:S(2)}) %collective-permute-start.5) | collective-permute-done | bytes 491552 | tf_op jit(solution)/shard_map/ppermute | solution.py:901
  78.1 8.6 %conditional.3 = (f32[17280]{0:T(1024)S(1)}, f32[1,5,16,32,384]{4,3,2,1,0:T(8,128)}) conditional(s32[]{:T(128)} %convert_element_type.10, (s32[6]{0:T(128)S(1)}, f32[16,32,384]{2,1,0:T(8,128)S(1)}, f32[5,16,32,384]{3,2,1,0:T(8,128)}, f32[2,5,32,384]{3,2,1,0:T(8,128)S(1)}, f32[5,16,384]{2,1,0:T(8,128)S(1)}, ...), branch_computations={%region_3.4_spmd, %region_4.5_spmd} | conditional | flops 17280 | bytes 345616 | solution.py:974
  78.1 8.6 %evolve_brick.1 = f32[5,16,32,384]{3,2,1,0:T(8,128)} custom-call(s32[6]{0:T(128)S(1)} %get-tuple-element.46.place, f32[16,32,384]{2,1,0:T(8,128)S(1)} %get-tuple-element.47.viscosity, f32[5,16,32,384]{3,2,1,0:T(8,128)} %get-tuple-element.48.fields, f32[2,5,32,384]{3,2,1,0:T(8,128)S(1)} %get-tuple-element.49.x_halo, ...), custom_call_target="tpu_custom_call" | custom-call | tf_op jit(solution)/shard_map/cond/branch_0_fun/evolve_brick/pallas_call | solution.py:556
  86.7 0.7 collective-permute-start.12
  87.4 0.7 collective-permute-start.11
  88.0 1.3 %collective-permute-start.10 = (f32[17280]{0:T(1024)S(1)}, f32[17280]{0:T(1024)S(1)}, u32[]{:S(2)}, u32[]{:S(2)}) collective-permute-start(f32[17280]{0:T(1024)S(1)} %get-tuple-element.115), channel_id=1, source_target_pairs={{24,0},{25,1},{26,2},{27,3},{28,4},{29,5},{30,6},{31,7}} | collective-permute-start | bytes 207368 | tf_op jit(solution)/shard_map/ppermute | solution.py:978
  89.4 4.3 %collective-permute-done.10 = f32[17280]{0:T(1024)S(1)} collective-permute-done((f32[17280]{0:T(1024)S(1)}, f32[17280]{0:T(1024)S(1)}, u32[]{:S(2)}, u32[]{:S(2)}) %collective-permute-start.10) | collective-permute-done | bytes 69152 | tf_op jit(solution)/shard_map/ppermute | solution.py:978
  93.7 2.3 %collective-permute-start.14 = (f32[17280]{0:T(1024)S(1)}, f32[17280]{0:T(1024)S(1)}, u32[]{:S(2)}, u32[]{:S(2)}) collective-permute-start(f32[17280]{0:T(1024)S(1)} %add_add_fusion.1), channel_id=1, source_target_pairs={{0,5},{1,4},{2,7},{3,6},{4,1},{5,0},{6,3},{7,2},{8,14},{9,15},{10,... | collective-permute-start | bytes 207368 | tf_op jit(solution)/shard_map/ppermute | solution.py:989
  96.1 2.3 %collective-permute-start.13 = (f32[17280]{0:T(1024)S(1)}, f32[17280]{0:T(1024)S(1)}, u32[]{:S(2)}, u32[]{:S(2)}) collective-permute-start(f32[17280]{0:T(1024)S(1)} %add_add_fusion.1), channel_id=1, source_target_pairs={{0,1},{1,0},{2,3},{3,2},{4,5},{5,4},{6,7},{7,6},{8,10},{9,11},{10,... | collective-permute-start | bytes 207368 | tf_op jit(solution)/shard_map/ppermute | solution.py:989
  98.3 2.5 %collective-permute-done.14 = f32[17280]{0:T(1024)S(1)} collective-permute-done((f32[17280]{0:T(1024)S(1)}, f32[17280]{0:T(1024)S(1)}, u32[]{:S(2)}, u32[]{:S(2)}) %collective-permute-start.14) | collective-permute-done | bytes 69152 | tf_op jit(solution)/shard_map/ppermute | solution.py:989
  100.8 0.4 collective-permute-done.13
  101.3 0.1 collective-permute-start.15
  101.3 1.2 %collective-permute-done.15 = f32[17280]{0:T(1024)S(1)} collective-permute-done((f32[17280]{0:T(1024)S(1)}, f32[17280]{0:T(1024)S(1)}, u32[]{:S(2)}, u32[]{:S(2)}) %collective-permute-start.15) | collective-permute-done | bytes 69152 | tf_op jit(solution)/shard_map/ppermute | solution.py:991
  102.6 0.1 collective-permute-start.16
  102.7 4.3 %collective-permute-done.16 = f32[17280]{0:T(1024)S(1)} collective-permute-done((f32[17280]{0:T(1024)S(1)}, f32[17280]{0:T(1024)S(1)}, u32[]{:S(2)}, u32[]{:S(2)}) %collective-permute-start.16) | collective-permute-done | bytes 69152 | tf_op jit(solution)/shard_map/ppermute | solution.py:991
  107.0 0.6 multiply_reduce_fusion
  108.3 1.4 %multiply_subtract_fusion = (f32[540]{0:T(1024)}, f32[540]{0:T(1024)}) fusion(f32[17280]{0:T(1024)S(1)} %copy-done.4, s32[]{:T(128)S(6)} %select_n.2, f32[]{:T(128)S(6)} %sqrt.3, f32[17280]{0:T(1024)S(1)} %get-tuple-element.119, f32[17280]{0:T(1024)} %param.20), kind=kLoop, calls=%fused_computation.14 | loop fusion | flops 2700 | bytes 10808 | tf_op jit(solution)/shard_map/sub | solution.py:1004
  (33 shorter events, 0.2 us)
Async XLA Ops:
  0.7 0.7 copy-start.1
  1.4 10.3 %copy-start.6 = (f32[64,5]{0,1:T(8,128)S(1)}, f32[64,5]{0,1:T(8,128)}, u32[]{:S(2)}) copy-start(f32[64,5]{0,1:T(8,128)} %param.16) | copy-start | bytes 3844
  1.4 10.3 %copy-start.4 = (f32[17280]{0:T(1024)S(1)}, f32[17280]{0:T(1024)}, u32[]{:S(2)}) copy-start(f32[17280]{0:T(1024)} %param.19) | copy-start | bytes 207364
  1.4 10.4 %copy-start.8 = (f32[64]{0:T(128)S(1)}, f32[64]{0:T(128)}, u32[]{:S(2)}) copy-start(f32[64]{0:T(128)} %param.17) | copy-start | bytes 772
  1.4 10.4 %copy-start.2 = (s32[24]{0:T(128)S(1)}, s32[24]{0:T(128)}, u32[]{:S(2)}) copy-start(s32[24]{0:T(128)} %sample_block.5) | copy-start | bytes 292
  4.2 11.9 %copy-start.5 = (f32[64]{0:T(128)S(1)}, f32[64]{0:T(128)}, u32[]{:S(2)}) copy-start(f32[64]{0:T(128)} %param.18) | copy-start | bytes 772
  4.2 15.0 %copy-start = (bf16[256,256]{1,0:T(8,128)(2,1)S(1)}, bf16[256,256]{1,0:T(8,128)(2,1)}, u32[]{:S(2)}) copy-start(bf16[256,256]{1,0:T(8,128)(2,1)} %constant.58.clone.order) | copy-start | bytes 393220
  4.2 14.9 %all-to-all-start = ((f32[8,16,256]{2,1,0:T(8,128)}), f32[8,16,256]{2,1,0:T(8,128)S(1)}, u32[]{:S(2)}, u32[]{:S(2)}) async-start(f32[8,16,256]{2,1,0:T(8,128)} %thin_faces.1), calls=%async_computation | async-start | bytes 262144 | tf_op jit(solution)/shard_map/all_to_all | solution.py:940
  16.1 52.1 %copy-start.7 = (s32[24]{0:T(128)S(1)}, s32[24]{0:T(128)}, u32[]{:S(2)}) copy-start(s32[24]{0:T(128)} %trainer_of.1) | copy-start | bytes 292
  20.8 4.1 %collective-permute-start.2 = (bf16[320,128]{1,0:T(8,128)(2,1)S(1)}, bf16[320,128]{1,0:T(8,128)(2,1)S(1)}, u32[]{:S(2)}, u32[]{:S(2)}) collective-permute-start(bf16[320,128]{1,0:T(8,128)(2,1)S(1)} %cube_change.1), channel_id=1, source_target_pairs={{16,24},{17,25},{18,26},{19,27},{20,28},{21,29},{22,30},{23,31}} | collective-permute-start | bytes 245768 | tf_op jit(solution)/shard_map/ppermute | solution.py:916
  21.4 3.4 %collective-permute-start.1 = (bf16[320,128]{1,0:T(8,128)(2,1)S(1)}, bf16[320,128]{1,0:T(8,128)(2,1)S(1)}, u32[]{:S(2)}, u32[]{:S(2)}) collective-permute-start(bf16[320,128]{1,0:T(8,128)(2,1)S(1)} %cube_change.1), channel_id=1, source_target_pairs={{8,24},{9,25},{10,26},{11,27},{12,28},{13,29},{14,30},{15,31}} | collective-permute-start | bytes 245768 | tf_op jit(solution)/shard_map/ppermute | solution.py:916
  22.1 4.8 %collective-permute-start = (bf16[320,128]{1,0:T(8,128)(2,1)S(1)}, bf16[320,128]{1,0:T(8,128)(2,1)S(1)}, u32[]{:S(2)}, u32[]{:S(2)}) collective-permute-start(bf16[320,128]{1,0:T(8,128)(2,1)S(1)} %cube_change.1), channel_id=1, source_target_pairs={{0,24},{1,25},{2,26},{3,27},{4,28},{5,29},{6,30},{7,31}} | collective-permute-start | bytes 245768 | tf_op jit(solution)/shard_map/ppermute | solution.py:916
  26.9 51.2 %copy-start.3 = (bf16[4,256,240]{2,1,0:T(8,128)(2,1)S(1)}, bf16[4,256,240]{2,1,0:T(8,128)(2,1)}, u32[]{:S(2)}) copy-start(bf16[4,256,240]{2,1,0:T(8,128)(2,1)} %constant.57.clone) | copy-start | bytes 1474564
  26.9 41.2 %collective-permute-start.8 = (bf16[3,320,128]{2,1,0:T(8,128)(2,1)S(1)}, bf16[3,320,128]{2,1,0:T(8,128)(2,1)S(1)}, u32[]{:S(2)}, u32[]{:S(2)}) collective-permute-start(bf16[3,320,128]{2,1,0:T(8,128)(2,1)S(1)} %pad_maximum_fusion.1.refs_0_), channel_id=1, source_target_pairs={{24,27},{25,26},{26,25},{27,24},{28,31},{29,30},{30,29},{31,28}} | collective-permute-start | bytes 737288 | tf_op jit(solution)/shard_map/ppermute | solution.py:924
  27.7 40.4 %collective-permute-start.7 = (bf16[3,320,128]{2,1,0:T(8,128)(2,1)S(1)}, bf16[3,320,128]{2,1,0:T(8,128)(2,1)S(1)}, u32[]{:S(2)}, u32[]{:S(2)}) collective-permute-start(bf16[3,320,128]{2,1,0:T(8,128)(2,1)S(1)} %pad_maximum_fusion.1.refs_0_), channel_id=1, source_target_pairs={{24,26},{25,27},{26,24},{27,25},{28,30},{29,31},{30,28},{31,29}} | collective-permute-start | bytes 737288 | tf_op jit(solution)/shard_map/ppermute | solution.py:924
  28.4 39.7 %collective-permute-start.6 = (bf16[3,320,128]{2,1,0:T(8,128)(2,1)S(1)}, bf16[3,320,128]{2,1,0:T(8,128)(2,1)S(1)}, u32[]{:S(2)}, u32[]{:S(2)}) collective-permute-start(bf16[3,320,128]{2,1,0:T(8,128)(2,1)S(1)} %pad_maximum_fusion.1.refs_0_), channel_id=1, source_target_pairs={{24,25},{25,24},{26,27},{27,26},{28,29},{29,28},{30,31},{31,30}} | collective-permute-start | bytes 737288 | tf_op jit(solution)/shard_map/ppermute | solution.py:924
  54.1 9.0 %collective-permute-start.4 = (f32[5,16,384]{2,1,0:T(8,128)S(1)}, f32[5,16,384]{2,1,0:T(8,128)S(1)}, u32[]{:S(2)}, u32[]{:S(2)}) collective-permute-start(f32[5,16,384]{2,1,0:T(8,128)S(1)} %get-tuple-element.120), channel_id=1, source_target_pairs={{0,3},{1,2},{2,1},{3,0},{4,7},{5,6},{6,5},{7,4},{8,11},{9,10},{10,... | collective-permute-start | bytes 368648 | tf_op jit(solution)/shard_map/ppermute | solution.py:908
  58.0 6.8 %collective-permute-start.3 = (f32[5,16,384]{2,1,0:T(8,128)S(1)}, f32[5,16,384]{2,1,0:T(8,128)S(1)}, u32[]{:S(2)}, u32[]{:S(2)}) collective-permute-start(f32[5,16,384]{2,1,0:T(8,128)S(1)} %get-tuple-element.121), channel_id=1, source_target_pairs={{0,1},{1,0},{2,3},{3,2},{4,5},{5,4},{6,7},{7,6},{8,9},{9,8},{10,11... | collective-permute-start | bytes 368648 | tf_op jit(solution)/shard_map/ppermute | solution.py:907
  64.7 13.3 %collective-permute-start.5 = (f32[2,5,32,384]{3,2,1,0:T(8,128)S(1)}, f32[2,5,32,384]{3,2,1,0:T(8,128)S(1)}, u32[]{:S(2)}, u32[]{:S(2)}) collective-permute-start(f32[2,5,32,384]{3,2,1,0:T(8,128)S(1)} %get-tuple-element.106), channel_id=1, source_target_pairs={{0,4},{1,5},{2,6},{3,7},{4,0},{5,1},{6,2},{7,3},{8,12},{9,13},{10,... | collective-permute-start | bytes 1474568 | tf_op jit(solution)/shard_map/ppermute | solution.py:901
  68.9 9.2 %collective-permute-start.9 = (bf16[6,320,128]{2,1,0:T(8,128)(2,1)S(1)}, bf16[6,320,128]{2,1,0:T(8,128)(2,1)S(1)}, u32[]{:S(2)}, u32[]{:S(2)}) collective-permute-start(bf16[6,320,128]{2,1,0:T(8,128)(2,1)S(1)} %pick_cubes.1), channel_id=1, source_target_pairs={{24,28},{25,29},{26,30},{27,31},{28,24},{29,25},{30,26},{31,27}} | collective-permute-start | bytes 1474568 | tf_op jit(solution)/shard_map/ppermute | solution.py:927
  86.7 2.6 %collective-permute-start.12 = (f32[17280]{0:T(1024)S(1)}, f32[17280]{0:T(1024)S(1)}, u32[]{:S(2)}, u32[]{:S(2)}) collective-permute-start(f32[17280]{0:T(1024)S(1)} %get-tuple-element.115), channel_id=1, source_target_pairs={{24,16},{25,17},{26,18},{27,19},{28,20},{29,21},{30,22},{31,23}} | collective-permute-start | bytes 207368 | tf_op jit(solution)/shard_map/ppermute | solution.py:978
  87.4 2.0 %collective-permute-start.11 = (f32[17280]{0:T(1024)S(1)}, f32[17280]{0:T(1024)S(1)}, u32[]{:S(2)}, u32[]{:S(2)}) collective-permute-start(f32[17280]{0:T(1024)S(1)} %get-tuple-element.115), channel_id=1, source_target_pairs={{24,8},{25,9},{26,10},{27,11},{28,12},{29,13},{30,14},{31,15}} | collective-permute-start | bytes 207368 | tf_op jit(solution)/shard_map/ppermute | solution.py:978
  88.0 5.6 %collective-permute-start.10 = (f32[17280]{0:T(1024)S(1)}, f32[17280]{0:T(1024)S(1)}, u32[]{:S(2)}, u32[]{:S(2)}) collective-permute-start(f32[17280]{0:T(1024)S(1)} %get-tuple-element.115), channel_id=1, source_target_pairs={{24,0},{25,1},{26,2},{27,3},{28,4},{29,5},{30,6},{31,7}} | collective-permute-start | bytes 207368 | tf_op jit(solution)/shard_map/ppermute | solution.py:978
  93.7 7.1 %collective-permute-start.14 = (f32[17280]{0:T(1024)S(1)}, f32[17280]{0:T(1024)S(1)}, u32[]{:S(2)}, u32[]{:S(2)}) collective-permute-start(f32[17280]{0:T(1024)S(1)} %add_add_fusion.1), channel_id=1, source_target_pairs={{0,5},{1,4},{2,7},{3,6},{4,1},{5,0},{6,3},{7,2},{8,14},{9,15},{10,... | collective-permute-start | bytes 207368 | tf_op jit(solution)/shard_map/ppermute | solution.py:989
  96.1 5.2 %collective-permute-start.13 = (f32[17280]{0:T(1024)S(1)}, f32[17280]{0:T(1024)S(1)}, u32[]{:S(2)}, u32[]{:S(2)}) collective-permute-start(f32[17280]{0:T(1024)S(1)} %add_add_fusion.1), channel_id=1, source_target_pairs={{0,1},{1,0},{2,3},{3,2},{4,5},{5,4},{6,7},{7,6},{8,10},{9,11},{10,... | collective-permute-start | bytes 207368 | tf_op jit(solution)/shard_map/ppermute | solution.py:989
  101.3 1.3 %collective-permute-start.15 = (f32[17280]{0:T(1024)S(1)}, f32[17280]{0:T(1024)S(1)}, u32[]{:S(2)}, u32[]{:S(2)}) collective-permute-start(f32[17280]{0:T(1024)S(1)} %add_add_fusion), channel_id=1, source_target_pairs={{0,8},{1,9},{2,10},{3,11},{4,12},{5,13},{6,14},{7,15},{8,0},{9,1},... | collective-permute-start | bytes 207368 | tf_op jit(solution)/shard_map/ppermute | solution.py:991
  102.6 4.4 %collective-permute-start.16 = (f32[17280]{0:T(1024)S(1)}, f32[17280]{0:T(1024)S(1)}, u32[]{:S(2)}, u32[]{:S(2)}) collective-permute-start(f32[17280]{0:T(1024)S(1)} %add.52), channel_id=1, source_target_pairs={{0,16},{1,17},{2,18},{3,19},{4,20},{5,21},{6,22},{7,23},{8,24},{9,... | collective-permute-start | bytes 207368 | tf_op jit(solution)/shard_map/ppermute | solution.py:991

commit v13 on v12

--- a/solution.py
+++ b/solution.py
@@ -455,8 +455,15 @@
     return base_viscosity + viscosity_gain * soft
 
 
-def viscosity_kernel(closure, fields, viscosity, weights, out_column):
+def viscosity_kernel(closure, place, fields, viscosity, x_edges, y_edges, weights, out_column):
     x_cells, y_cells, z_cells = fields.shape[1:]
+    up_first = lax.rem(place[2], 2) == 0
+    for f in range(F):
+        x_edges[0, f] = fields[f, 0]
+        x_edges[1, f] = fields[f, x_cells - 1]
+        low, high = fields[f, :, 0, :], fields[f, :, y_cells - 1, :]
+        y_edges[0, f] = jnp.where(up_first, high, low)
+        y_edges[1, f] = jnp.where(up_first, low, high)
     plain = closure[...]
     high = plain.astype(jnp.bfloat16).astype(jnp.float32)
     low = plain - high
@@ -497,20 +504,25 @@
     lax.fori_loop(0, x_cells * tiles, tile, 0)
 
 
-def brick_viscosity(closure, fields):
+def brick_viscosity(closure, place, fields):
+    count, x_cells, y_cells, z_cells = fields.shape
     vmem = pl.BlockSpec(memory_space=pltpu.VMEM)
     return pl.pallas_call(
         viscosity_kernel,
-        out_shape=jax.ShapeDtypeStruct(fields.shape[1:], fields.dtype),
-        in_specs=[vmem, vmem],
-        out_specs=vmem,
+        out_shape=(
+            jax.ShapeDtypeStruct(fields.shape[1:], fields.dtype),
+            jax.ShapeDtypeStruct((2, count, y_cells, z_cells), fields.dtype),
+            jax.ShapeDtypeStruct((2, count, x_cells, z_cells), fields.dtype),
+        ),
+        in_specs=[vmem, pl.BlockSpec(memory_space=pltpu.SMEM), vmem],
+        out_specs=(vmem,) * 3,
         scratch_shapes=[
             pltpu.VMEM((8, HID + 8, 32), jnp.bfloat16),
             pltpu.VMEM((HID, 128), jnp.float32),
         ],
         compiler_params=pltpu.CompilerParams(vmem_limit_bytes=16 * 1024 * 1024),
         name="brick_viscosity",
-    )(closure, fields)
+    )(closure, place, fields)
 
 
 def evolve_kernel(place, viscosity, fields, x_halo, y_first, y_second, new_fields):
@@ -678,35 +690,39 @@
     lower,
     upper,
     own_rows,
-    x_edges,
-    y_edges,
     windows,
     sems,
 ):
     rows_of_x = y_cells
     rows_of_field = SUB * y_cells
     window_rows = F * rows_of_field
+
+    def corner(x_step, y_step):
+        return corner_of(sample_block, place, x_step, y_step, y_cells, z_cells)
+
+    y_start, z_start = corner(0, 0)
+    z_below = jnp.maximum(z_start - 1, 0)
+    z_above = jnp.minimum(z_start + SUB, z_cells - 1)
+    first_window = lax.div(z_below, 128)
+    second_window = jnp.minimum(first_window + 1, z_cells // 128 - 1)
     copies = [
         pltpu.make_async_copy(
-            brick.at[:, pl.ds(w * 128, 128)], windows.at[pl.ds(w * window_rows, window_rows)], sems.at[w]
+            brick.at[:, pl.ds(pl.multiple_of(at * 128, 128), 128)],
+            windows.at[pl.ds(slot * window_rows, window_rows)],
+            sems.at[slot],
         )
-        for w in range(z_cells // 128)
+        for slot, at in enumerate((first_window, second_window))
     ]
     for copy in copies:
         copy.start()
     for copy in copies:
         copy.wait()
 
-    def corner(x_step, y_step):
-        return corner_of(sample_block, place, x_step, y_step, y_cells, z_cells)
-
     def window(row, z):
-        return windows[pl.ds(lax.div(z, 128) * window_rows + row, SUB, rows_of_x), :]
+        slot = lax.div(z, 128) - first_window
+        return windows[pl.ds(slot * window_rows + row, SUB, rows_of_x), :]
 
     lane = lax.broadcasted_iota(jnp.int32, (SUB, 128), 1)
-    y_start, z_start = corner(0, 0)
-    z_below = jnp.maximum(z_start - 1, 0)
-    z_above = jnp.minimum(z_start + SUB, z_cells - 1)
     for field in range(F):
         for half in range(2):
             inside = jnp.zeros((SUB, 128), jnp.float32)
@@ -738,21 +754,6 @@
 
     own_rows[0] = y_row(jnp.maximum(y_start - 1, 0), z_start)
     own_rows[1] = y_row(jnp.minimum(y_start + SUB, y_cells - 1), z_start)
-    up_first = lax.rem(place[2], 2) == 0
-    for side in range(2):
-        y = jnp.where(up_first == (side == 0), y_cells - 1, 0)
-        for field in range(F):
-            for w in range(z_cells // 128):
-                start = w * window_rows + field * rows_of_field + y
-                y_edges[side, field, :, w * 128 : (w + 1) * 128] = windows[
-                    pl.ds(start, SUB, rows_of_x), :
-                ]
-    for side, x in enumerate((0, SUB - 1)):
-        for field in range(F):
-            for w in range(z_cells // 128):
-                start = w * window_rows + field * rows_of_field + x * rows_of_x
-                x_edges[side, field, :, w * 128 : (w + 1) * 128] = windows[pl.ds(start, rows_of_x), :]
-
 
 def sample_cube(sample_block, place, brick):
     fields, x_cells, y_cells, z_cells = brick.shape
@@ -768,14 +769,12 @@
             cube,
             cube,
             jax.ShapeDtypeStruct((2, SUB, 128), jnp.float32),
-            jax.ShapeDtypeStruct((2, fields, y_cells, z_cells), jnp.float32),
-            jax.ShapeDtypeStruct((2, fields, x_cells, z_cells), jnp.float32),
         ),
         in_specs=[smem, smem, hbm],
-        out_specs=(vmem,) * 6,
+        out_specs=(vmem,) * 4,
         scratch_shapes=[
-            pltpu.VMEM((z_cells // 128 * rows, 128), jnp.float32),
-            pltpu.SemaphoreType.DMA((z_cells // 128,)),
+            pltpu.VMEM((2 * rows, 128), jnp.float32),
+            pltpu.SemaphoreType.DMA((2,)),
         ],
         compiler_params=pltpu.CompilerParams(vmem_limit_bytes=16 * 1024 * 1024),
         cost_estimate=pl.CostEstimate(flops=0, bytes_accessed=16_000_000, transcendentals=0),
@@ -927,7 +926,7 @@
         return lax.ppermute(held, everyone, swap(apart * y_devices))
 
     thin = thin_faces(sample_block, place, brick, trainers)
-    *cube, x_edges, y_edges = sample_cube(sample_block, place, brick)
+    cube = sample_cube(sample_block, place, brick)
     first_count = CH * TAPS * F
     first = jnp.pad(master[:first_count].reshape(CH, TAPS * F), ((0, 0), (0, 256 - TAPS * F)))
     last = jnp.pad(master[first_count:].reshape(TAPS * F, CH), ((0, 256 - TAPS * F), (0, 0)))
@@ -942,15 +941,17 @@
     landed = to_trainers(payload)
     closure, landed = lax.optimization_barrier((closure, landed))
 
-    viscosity = lax.cond(
+    fields_count, x_cells = brick.shape[:2]
+    viscosity, x_edges, y_edges = lax.cond(
         is_trainer,
-        lambda: jnp.zeros(brick.shape[1:], jnp.float32),
-        lambda: brick_viscosity(closure, brick),
+        lambda: (
+            jnp.zeros((x_cells, y_cells, z_cells), jnp.float32),
+            jnp.zeros((2, fields_count, y_cells, z_cells), jnp.float32),
+            jnp.zeros((2, fields_count, x_cells, z_cells), jnp.float32),
+        ),
+        lambda: brick_viscosity(closure, place, brick),
     )
-    y_edges, viscosity = lax.optimization_barrier((y_edges, viscosity))
-    y_halo = y_neighbours(y_edges[0], y_edges[1])
-    x_edges, *y_halo = lax.optimization_barrier((x_edges, *y_halo))
-    halo = (x_neighbours(x_edges), *y_halo)
+    halo = (x_neighbours(x_edges), *y_neighbours(y_edges[0], y_edges[1]))
     near = [landed, *from_line(landed)]
     far = [
         across(apart, pick_cubes(sample_trainer, place, near, y_devices, x_devices, apart))

time: 110 us -> 104 us (0.945)
  waiting for transfers between devices: 30.7 us -> 25.9 us
  starting transfers between devices: 30.9 us -> 29.6 us
    ppermute x1, waiting for transfers between devices: 8.53 us -> 0.01 us  [x_neighbours(): return lax.ppermute(edges, everyone, pairs(1, 0))]
    ppermute x3, waiting for transfers between devices: 4.31 us -> 6.77 us  [on_device(): lax.ppermute(delta, everyone, [(first_trainer + c, g * trainers + c) for...]
  transfers between devices with their start and end apart: 18 -> 18, of which waited for: 10 -> 8; matrix products, arithmetic and copies ran while one was open for 1% -> 1% of each run, Pallas kernels for 27% -> 29%
where the time goes in v13:
time: 104 us; the launch traced here: 103 us
  Pallas kernels  42.6 us (41%)
  starting transfers between devices  29.6 us (28%)
  waiting for transfers between devices  25.9 us (25%)
  other arithmetic  2.28 us (2%)
  between operations  1.71 us (2%)
  local copies, waits for them, and re-layouts  1.28 us (1%)
    pallas_call x1, Pallas kernels, brick_viscosity(): pl.pallas_call(viscosity_kernel, out_shape=(jax.ShapeDtypeStruct(fields.s...  25.2 us
    pallas_call x1, Pallas kernels, evolve(): pl.pallas_call(evolve_kernel, out_shape=jax.ShapeDtypeStruct(fields.shape...  8.75 us
    all_to_all x1, starting transfers between devices, on_device(): lax.all_to_all(thin, ('gx', 'gy'), split_axis=0, concat_axis=0, tiled=True)  7.42 us
    ppermute x3, waiting for transfers between devices, on_device(): lax.ppermute(delta, everyone, [(first_trainer + c, g * trainers + c) for...  6.77 us
    ppermute x2, waiting for transfers between devices, on_device(): lax.ppermute(final, everyone, [(g * trainers + c, (g ^ apart) * trainers...  5.53 us
    ppermute x1, starting transfers between devices, y_neighbours(): lax.ppermute(for_second, everyone, pairs(0, -1))  4.37 us
    ppermute x3, starting transfers between devices, to_trainers(): lax.ppermute(payload, everyone, [(g * trainers + c, first_trainer + c) fo...  4.05 us
    ppermute x2, starting transfers between devices, on_device(): final = final + lax.ppermute(held, everyone, meets)  3.71 us
  transfers between devices with their start and end apart: 18, of which 8 were waited for; matrix products, arithmetic and copies ran while one was open for 1% of the time, Pallas kernels for 29%

profile of v13, /device:TPU:0, one launch (start us, length us, event | category | flops | bytes accessed | tf_op | source)
XLA Modules:
  0.0 103.4 jit_solution(6255906139259551518)
XLA Ops:
  0.6 0.1 stack.27.place
  0.7 0.7 copy-done.1
  1.4 2.8 %thin_faces.1 = f32[8,16,256]{2,1,0:T(8,128)} custom-call(s32[24]{0:T(128)S(1)} %copy-done.1, s32[6]{0:T(128)S(1)} %stack.27.place, f32[2560,384]{1,0:T(8,128)} %bitcast.23, f32[80,32,384]{2,1,0:T(8,128)} %bitcast.24), custom_call_target="tpu_custom_call" | custom-call | tf_op jit(solution)/shard_map/thin_faces/pallas_call | solution.py:662
  4.2 0.0 copy-start.6
  4.2 0.0 copy-start
  4.2 7.4 %all-to-all-start = ((f32[8,16,256]{2,1,0:T(8,128)}), f32[8,16,256]{2,1,0:T(8,128)S(1)}, u32[]{:S(2)}, u32[]{:S(2)}) async-start(f32[8,16,256]{2,1,0:T(8,128)} %thin_faces.1), calls=%async_computation | async-start | bytes 262144 | tf_op jit(solution)/shard_map/all_to_all | solution.py:939
  11.7 0.1 fusion.1
  11.8 3.6 %sample_cube.1 = (f32[80,256]{1,0:T(8,128)S(1)}, f32[80,256]{1,0:T(8,128)S(1)}, f32[80,256]{1,0:T(8,128)S(1)}, f32[2,16,128]{2,1,0:T(8,128)S(1)}) custom-call(s32[24]{0:T(128)S(1)} %copy-done.2, s32[6]{0:T(128)S(1)} %stack.27.place, f32[2560,384]{1,0:T(8,128)} %bitcast.25), custom_call_target="tpu_custom_call" | custom-call | bytes 16000000 | tf_op jit(solution)/shard_map/sample_cube/pallas_call | solution.py:765
  15.4 0.0 copy-start.8
  15.4 0.1 fusion
  15.6 0.1 copy.15
  15.6 0.1 reshape.34
  15.7 0.2 slice.37
  16.0 0.1 select_maximum_fusion.closure
  16.0 3.1 %all-to-all-done.thin = f32[8,16,256]{2,1,0:T(8,128)S(1)} async-done(((f32[8,16,256]{2,1,0:T(8,128)}), f32[8,16,256]{2,1,0:T(8,128)S(1)}, u32[]{:S(2)}, u32[]{:S(2)}) %all-to-all-start) | async-done | bytes 131104 | tf_op jit(solution)/shard_map/all_to_all | solution.py:939
  19.2 1.6 %cube_change.1 = bf16[320,128]{1,0:T(8,128)(2,1)S(1)} custom-call(s32[24]{0:T(128)S(1)} %copy-done.2, s32[6]{0:T(128)S(1)} %stack.27.place, f32[8,128]{1,0:T(8,128)S(1)} %select_maximum_fusion.closure, bf16[256,256]{1,0:T(8,128)(2,1)S(1)} %copy-done, f32[80,256]{1,0:T(8,128)S(1)} %get-tuple-element.93.centre, f32[80,256]{1,0:T(8,128)S(1)} %get-tuple-element.94.lower, ...), custom_call_target="tpu_custom_call" | custom-call | tf_op jit(solution)/shard_map/cube_change/pallas_call | solution.py:846
  20.8 0.7 collective-permute-start.2
  21.4 0.7 collective-permute-start.1
  22.1 2.7 %collective-permute-start = (bf16[320,128]{1,0:T(8,128)(2,1)S(1)}, bf16[320,128]{1,0:T(8,128)(2,1)S(1)}, u32[]{:S(2)}, u32[]{:S(2)}) collective-permute-start(bf16[320,128]{1,0:T(8,128)(2,1)S(1)} %cube_change.1), channel_id=1, source_target_pairs={{0,24},{1,25},{2,26},{3,27},{4,28},{5,29},{6,30},{7,31}} | collective-permute-start | bytes 245768 | tf_op jit(solution)/shard_map/ppermute | solution.py:915
  24.8 0.0 collective-permute-done.2
  24.8 2.0 %collective-permute-done = bf16[320,128]{1,0:T(8,128)(2,1)S(1)} collective-permute-done((bf16[320,128]{1,0:T(8,128)(2,1)S(1)}, bf16[320,128]{1,0:T(8,128)(2,1)S(1)}, u32[]{:S(2)}, u32[]{:S(2)}) %collective-permute-start) | collective-permute-done | bytes 81952 | tf_op jit(solution)/shard_map/ppermute | solution.py:915
  26.9 0.8 collective-permute-start.8
  27.7 0.7 collective-permute-start.7
  28.4 0.7 collective-permute-start.6
  29.1 25.2 %conditional.2 = ((f32[16,32,384]{2,1,0:T(8,128)S(1)}, f32[2,5,32,384]{3,2,1,0:T(8,128)}, f32[2,5,16,384]{3,2,1,0:T(8,128)S(1)})) conditional(s32[]{:T(128)} %convert_element_type.10, (f32[8,128]{1,0:T(8,128)S(1)}, s32[6]{0:T(128)S(1)}, f32[5,16,32,384]{3,2,1,0:T(8,128)}) %tuple.46, () %tuple.31), branch_computations={%region_1.2_spmd, %region_2.3_spmd} | conditional | bytes 1523756 | solution.py:945
  29.1 25.2 %brick_viscosity.1 = (f32[16,32,384]{2,1,0:T(8,128)S(1)}, f32[2,5,32,384]{3,2,1,0:T(8,128)}, f32[2,5,16,384]{3,2,1,0:T(8,128)S(1)}) custom-call(f32[8,128]{1,0:T(8,128)S(1)} %get-tuple-element.43.closure, s32[6]{0:T(128)S(1)} %get-tuple-element.44.place, f32[5,16,32,384]{3,2,1,0:T(8,128)} %get-tuple-element.45.fields), custom_call_target="tpu_custom_call" | custom-call | tf_op jit(solution)/shard_map/cond/branch_0_fun/brick_viscosity/pallas_call | solution.py:510
  54.3 2.5 %collective-permute-start.3 = (f32[2,5,32,384]{3,2,1,0:T(8,128)}, f32[2,5,32,384]{3,2,1,0:T(8,128)S(1)}, u32[]{:S(2)}, u32[]{:S(2)}) collective-permute-start(f32[2,5,32,384]{3,2,1,0:T(8,128)} %get-tuple-element.99), channel_id=1, source_target_pairs={{0,4},{1,5},{2,6},{3,7},{4,0},{5,1},{6,2},{7,3},{8,12},{9,13},{10,... | collective-permute-start | bytes 1474568 | tf_op jit(solution)/shard_map/ppermute | solution.py:900
  56.8 0.7 pick_cubes.1
  57.5 0.7 collective-permute-start.9
  58.2 4.4 %collective-permute-start.5 = (f32[5,16,384]{2,1,0:T(8,128)S(1)}, f32[5,16,384]{2,1,0:T(8,128)S(1)}, u32[]{:S(2)}, u32[]{:S(2)}) collective-permute-start(f32[5,16,384]{2,1,0:T(8,128)S(1)} %get-tuple-element.112), channel_id=1, source_target_pairs={{0,3},{1,2},{2,1},{3,0},{4,7},{5,6},{6,5},{7,4},{8,11},{9,10},{10,... | collective-permute-start | bytes 368648 | tf_op jit(solution)/shard_map/ppermute | solution.py:907
  62.6 1.9 %collective-permute-start.4 = (f32[5,16,384]{2,1,0:T(8,128)S(1)}, f32[5,16,384]{2,1,0:T(8,128)S(1)}, u32[]{:S(2)}, u32[]{:S(2)}) collective-permute-start(f32[5,16,384]{2,1,0:T(8,128)S(1)} %get-tuple-element.113), channel_id=1, source_target_pairs={{0,1},{1,0},{2,3},{3,2},{4,5},{5,4},{6,7},{7,6},{8,9},{9,8},{10,11... | collective-permute-start | bytes 368648 | tf_op jit(solution)/shard_map/ppermute | solution.py:906
  64.5 2.6 %collective-permute-done.5 = f32[5,16,384]{2,1,0:T(8,128)S(1)} collective-permute-done((f32[5,16,384]{2,1,0:T(8,128)S(1)}, f32[5,16,384]{2,1,0:T(8,128)S(1)}, u32[]{:S(2)}, u32[]{:S(2)}) %collective-permute-start.5) | collective-permute-done | bytes 122912 | tf_op jit(solution)/shard_map/ppermute | solution.py:907
  67.1 2.2 %collective-permute-done.4 = f32[5,16,384]{2,1,0:T(8,128)S(1)} collective-permute-done((f32[5,16,384]{2,1,0:T(8,128)S(1)}, f32[5,16,384]{2,1,0:T(8,128)S(1)}, u32[]{:S(2)}, u32[]{:S(2)}) %collective-permute-start.4) | collective-permute-done | bytes 122912 | tf_op jit(solution)/shard_map/ppermute | solution.py:906
  69.4 8.8 %conditional.3 = (f32[17280]{0:T(1024)S(1)}, f32[1,5,16,32,384]{4,3,2,1,0:T(8,128)}) conditional(s32[]{:T(128)} %convert_element_type.10, (s32[6]{0:T(128)S(1)}, f32[16,32,384]{2,1,0:T(8,128)S(1)}, f32[5,16,32,384]{3,2,1,0:T(8,128)}, f32[2,5,32,384]{3,2,1,0:T(8,128)S(1)}, f32[5,16,384]{2,1,0:T(8,128)S(1)}, ...), branch_computations={%region_3.4_spmd, %region_4.5_spmd} | conditional | flops 17280 | bytes 345616 | solution.py:975
  69.4 8.8 %evolve_brick.1 = f32[5,16,32,384]{3,2,1,0:T(8,128)} custom-call(s32[6]{0:T(128)S(1)} %get-tuple-element.46.place, f32[16,32,384]{2,1,0:T(8,128)S(1)} %get-tuple-element.47.viscosity, f32[5,16,32,384]{3,2,1,0:T(8,128)} %get-tuple-element.48.fields, f32[2,5,32,384]{3,2,1,0:T(8,128)S(1)} %get-tuple-element.49.x_halo, ...), custom_call_target="tpu_custom_call" | custom-call | tf_op jit(solution)/shard_map/cond/branch_0_fun/evolve_brick/pallas_call | solution.py:568
  78.2 0.7 collective-permute-start.12
  78.8 0.7 collective-permute-start.11
  79.5 1.3 %collective-permute-start.10 = (f32[17280]{0:T(1024)S(1)}, f32[17280]{0:T(1024)S(1)}, u32[]{:S(2)}, u32[]{:S(2)}) collective-permute-start(f32[17280]{0:T(1024)S(1)} %get-tuple-element.107), channel_id=1, source_target_pairs={{24,0},{25,1},{26,2},{27,3},{28,4},{29,5},{30,6},{31,7}} | collective-permute-start | bytes 207368 | tf_op jit(solution)/shard_map/ppermute | solution.py:979
  80.8 6.8 %collective-permute-done.10 = f32[17280]{0:T(1024)S(1)} collective-permute-done((f32[17280]{0:T(1024)S(1)}, f32[17280]{0:T(1024)S(1)}, u32[]{:S(2)}, u32[]{:S(2)}) %collective-permute-start.10) | collective-permute-done | bytes 69152 | tf_op jit(solution)/shard_map/ppermute | solution.py:979
  87.6 1.9 %collective-permute-start.14 = (f32[17280]{0:T(1024)S(1)}, f32[17280]{0:T(1024)S(1)}, u32[]{:S(2)}, u32[]{:S(2)}) collective-permute-start(f32[17280]{0:T(1024)S(1)} %add_add_fusion.1), channel_id=1, source_target_pairs={{0,5},{1,4},{2,7},{3,6},{4,1},{5,0},{6,3},{7,2},{8,14},{9,15},{10,... | collective-permute-start | bytes 207368 | tf_op jit(solution)/shard_map/ppermute | solution.py:990
  89.5 1.8 %collective-permute-start.13 = (f32[17280]{0:T(1024)S(1)}, f32[17280]{0:T(1024)S(1)}, u32[]{:S(2)}, u32[]{:S(2)}) collective-permute-start(f32[17280]{0:T(1024)S(1)} %add_add_fusion.1), channel_id=1, source_target_pairs={{0,1},{1,0},{2,3},{3,2},{4,5},{5,4},{6,7},{7,6},{8,10},{9,11},{10,... | collective-permute-start | bytes 207368 | tf_op jit(solution)/shard_map/ppermute | solution.py:990
  91.3 3.6 %collective-permute-done.14 = f32[17280]{0:T(1024)S(1)} collective-permute-done((f32[17280]{0:T(1024)S(1)}, f32[17280]{0:T(1024)S(1)}, u32[]{:S(2)}, u32[]{:S(2)}) %collective-permute-start.14) | collective-permute-done | bytes 69152 | tf_op jit(solution)/shard_map/ppermute | solution.py:990
  95.0 0.1 collective-permute-start.15
  95.0 1.2 %collective-permute-done.15 = f32[17280]{0:T(1024)S(1)} collective-permute-done((f32[17280]{0:T(1024)S(1)}, f32[17280]{0:T(1024)S(1)}, u32[]{:S(2)}, u32[]{:S(2)}) %collective-permute-start.15) | collective-permute-done | bytes 69152 | tf_op jit(solution)/shard_map/ppermute | solution.py:992
  96.3 0.1 collective-permute-start.16
  96.4 4.3 %collective-permute-done.16 = f32[17280]{0:T(1024)S(1)} collective-permute-done((f32[17280]{0:T(1024)S(1)}, f32[17280]{0:T(1024)S(1)}, u32[]{:S(2)}, u32[]{:S(2)}) %collective-permute-start.16) | collective-permute-done | bytes 69152 | tf_op jit(solution)/shard_map/ppermute | solution.py:992
  100.7 0.6 multiply_reduce_fusion
  102.0 1.4 %multiply_subtract_fusion = (f32[540]{0:T(1024)}, f32[540]{0:T(1024)}) fusion(f32[17280]{0:T(1024)S(1)} %copy-done.5, s32[]{:T(128)S(6)} %select_n.2, f32[]{:T(128)S(6)} %sqrt.3, f32[17280]{0:T(1024)S(1)} %get-tuple-element.111, f32[17280]{0:T(1024)} %param.20), kind=kLoop, calls=%fused_computation.14 | loop fusion | flops 2700 | bytes 10808 | tf_op jit(solution)/shard_map/sub | solution.py:1005
  (35 shorter events, 0.2 us)
Async XLA Ops:
  0.7 0.7 copy-start.1
  1.4 10.3 %copy-start.7 = (f32[64,5]{0,1:T(8,128)S(1)}, f32[64,5]{0,1:T(8,128)}, u32[]{:S(2)}) copy-start(f32[64,5]{0,1:T(8,128)} %param.16) | copy-start | bytes 3844
  1.4 10.3 %copy-start.5 = (f32[17280]{0:T(1024)S(1)}, f32[17280]{0:T(1024)}, u32[]{:S(2)}) copy-start(f32[17280]{0:T(1024)} %param.19) | copy-start | bytes 207364
  1.4 10.4 %copy-start.9 = (f32[64]{0:T(128)S(1)}, f32[64]{0:T(128)}, u32[]{:S(2)}) copy-start(f32[64]{0:T(128)} %param.17) | copy-start | bytes 772
  1.4 10.4 %copy-start.2 = (s32[24]{0:T(128)S(1)}, s32[24]{0:T(128)}, u32[]{:S(2)}) copy-start(s32[24]{0:T(128)} %sample_block.5) | copy-start | bytes 292
  4.2 11.2 %copy-start.6 = (f32[64]{0:T(128)S(1)}, f32[64]{0:T(128)}, u32[]{:S(2)}) copy-start(f32[64]{0:T(128)} %param.18) | copy-start | bytes 772
  4.2 15.0 %copy-start = (bf16[256,256]{1,0:T(8,128)(2,1)S(1)}, bf16[256,256]{1,0:T(8,128)(2,1)}, u32[]{:S(2)}) copy-start(bf16[256,256]{1,0:T(8,128)(2,1)} %constant.60.clone.order) | copy-start | bytes 393220
  4.2 14.9 %all-to-all-start = ((f32[8,16,256]{2,1,0:T(8,128)}), f32[8,16,256]{2,1,0:T(8,128)S(1)}, u32[]{:S(2)}, u32[]{:S(2)}) async-start(f32[8,16,256]{2,1,0:T(8,128)} %thin_faces.1), calls=%async_computation | async-start | bytes 262144 | tf_op jit(solution)/shard_map/all_to_all | solution.py:939
  15.4 41.4 %copy-start.8 = (s32[24]{0:T(128)S(1)}, s32[24]{0:T(128)}, u32[]{:S(2)}) copy-start(s32[24]{0:T(128)} %trainer_of.1) | copy-start | bytes 292
  20.8 4.1 %collective-permute-start.2 = (bf16[320,128]{1,0:T(8,128)(2,1)S(1)}, bf16[320,128]{1,0:T(8,128)(2,1)S(1)}, u32[]{:S(2)}, u32[]{:S(2)}) collective-permute-start(bf16[320,128]{1,0:T(8,128)(2,1)S(1)} %cube_change.1), channel_id=1, source_target_pairs={{16,24},{17,25},{18,26},{19,27},{20,28},{21,29},{22,30},{23,31}} | collective-permute-start | bytes 245768 | tf_op jit(solution)/shard_map/ppermute | solution.py:915
  21.4 3.4 %collective-permute-start.1 = (bf16[320,128]{1,0:T(8,128)(2,1)S(1)}, bf16[320,128]{1,0:T(8,128)(2,1)S(1)}, u32[]{:S(2)}, u32[]{:S(2)}) collective-permute-start(bf16[320,128]{1,0:T(8,128)(2,1)S(1)} %cube_change.1), channel_id=1, source_target_pairs={{8,24},{9,25},{10,26},{11,27},{12,28},{13,29},{14,30},{15,31}} | collective-permute-start | bytes 245768 | tf_op jit(solution)/shard_map/ppermute | solution.py:915
  22.1 4.8 %collective-permute-start = (bf16[320,128]{1,0:T(8,128)(2,1)S(1)}, bf16[320,128]{1,0:T(8,128)(2,1)S(1)}, u32[]{:S(2)}, u32[]{:S(2)}) collective-permute-start(bf16[320,128]{1,0:T(8,128)(2,1)S(1)} %cube_change.1), channel_id=1, source_target_pairs={{0,24},{1,25},{2,26},{3,27},{4,28},{5,29},{6,30},{7,31}} | collective-permute-start | bytes 245768 | tf_op jit(solution)/shard_map/ppermute | solution.py:915
  26.9 42.5 %copy-start.3 = (bf16[4,256,240]{2,1,0:T(8,128)(2,1)S(1)}, bf16[4,256,240]{2,1,0:T(8,128)(2,1)}, u32[]{:S(2)}) copy-start(bf16[4,256,240]{2,1,0:T(8,128)(2,1)} %constant.59.clone) | copy-start | bytes 1474564
  26.9 42.5 %copy-start.4 = (bf16[4,256,240]{2,1,0:T(8,128)(2,1)S(1)}, bf16[4,256,240]{2,1,0:T(8,128)(2,1)}, u32[]{:S(2)}) copy-start(bf16[4,256,240]{2,1,0:T(8,128)(2,1)} %constant.58.clone) | copy-start | bytes 1474564
  26.9 29.9 %collective-permute-start.8 = (bf16[3,320,128]{2,1,0:T(8,128)(2,1)S(1)}, bf16[3,320,128]{2,1,0:T(8,128)(2,1)S(1)}, u32[]{:S(2)}, u32[]{:S(2)}) collective-permute-start(bf16[3,320,128]{2,1,0:T(8,128)(2,1)S(1)} %pad_maximum_fusion.1.refs_0_), channel_id=1, source_target_pairs={{24,27},{25,26},{26,25},{27,24},{28,31},{29,30},{30,29},{31,28}} | collective-permute-start | bytes 737288 | tf_op jit(solution)/shard_map/ppermute | solution.py:923
  27.7 29.1 %collective-permute-start.7 = (bf16[3,320,128]{2,1,0:T(8,128)(2,1)S(1)}, bf16[3,320,128]{2,1,0:T(8,128)(2,1)S(1)}, u32[]{:S(2)}, u32[]{:S(2)}) collective-permute-start(bf16[3,320,128]{2,1,0:T(8,128)(2,1)S(1)} %pad_maximum_fusion.1.refs_0_), channel_id=1, source_target_pairs={{24,26},{25,27},{26,24},{27,25},{28,30},{29,31},{30,28},{31,29}} | collective-permute-start | bytes 737288 | tf_op jit(solution)/shard_map/ppermute | solution.py:923
  28.4 28.4 %collective-permute-start.6 = (bf16[3,320,128]{2,1,0:T(8,128)(2,1)S(1)}, bf16[3,320,128]{2,1,0:T(8,128)(2,1)S(1)}, u32[]{:S(2)}, u32[]{:S(2)}) collective-permute-start(bf16[3,320,128]{2,1,0:T(8,128)(2,1)S(1)} %pad_maximum_fusion.1.refs_0_), channel_id=1, source_target_pairs={{24,25},{25,24},{26,27},{27,26},{28,29},{29,28},{30,31},{31,30}} | collective-permute-start | bytes 737288 | tf_op jit(solution)/shard_map/ppermute | solution.py:923
  54.3 15.1 %collective-permute-start.3 = (f32[2,5,32,384]{3,2,1,0:T(8,128)}, f32[2,5,32,384]{3,2,1,0:T(8,128)S(1)}, u32[]{:S(2)}, u32[]{:S(2)}) collective-permute-start(f32[2,5,32,384]{3,2,1,0:T(8,128)} %get-tuple-element.99), channel_id=1, source_target_pairs={{0,4},{1,5},{2,6},{3,7},{4,0},{5,1},{6,2},{7,3},{8,12},{9,13},{10,... | collective-permute-start | bytes 1474568 | tf_op jit(solution)/shard_map/ppermute | solution.py:900
  57.5 11.9 %collective-permute-start.9 = (bf16[6,320,128]{2,1,0:T(8,128)(2,1)S(1)}, bf16[6,320,128]{2,1,0:T(8,128)(2,1)S(1)}, u32[]{:S(2)}, u32[]{:S(2)}) collective-permute-start(bf16[6,320,128]{2,1,0:T(8,128)(2,1)S(1)} %pick_cubes.1), channel_id=1, source_target_pairs={{24,28},{25,29},{26,30},{27,31},{28,24},{29,25},{30,26},{31,27}} | collective-permute-start | bytes 1474568 | tf_op jit(solution)/shard_map/ppermute | solution.py:926
  58.2 8.9 %collective-permute-start.5 = (f32[5,16,384]{2,1,0:T(8,128)S(1)}, f32[5,16,384]{2,1,0:T(8,128)S(1)}, u32[]{:S(2)}, u32[]{:S(2)}) collective-permute-start(f32[5,16,384]{2,1,0:T(8,128)S(1)} %get-tuple-element.112), channel_id=1, source_target_pairs={{0,3},{1,2},{2,1},{3,0},{4,7},{5,6},{6,5},{7,4},{8,11},{9,10},{10,... | collective-permute-start | bytes 368648 | tf_op jit(solution)/shard_map/ppermute | solution.py:907
  62.6 6.8 %collective-permute-start.4 = (f32[5,16,384]{2,1,0:T(8,128)S(1)}, f32[5,16,384]{2,1,0:T(8,128)S(1)}, u32[]{:S(2)}, u32[]{:S(2)}) collective-permute-start(f32[5,16,384]{2,1,0:T(8,128)S(1)} %get-tuple-element.113), channel_id=1, source_target_pairs={{0,1},{1,0},{2,3},{3,2},{4,5},{5,4},{6,7},{7,6},{8,9},{9,8},{10,11... | collective-permute-start | bytes 368648 | tf_op jit(solution)/shard_map/ppermute | solution.py:906
  78.2 2.6 %collective-permute-start.12 = (f32[17280]{0:T(1024)S(1)}, f32[17280]{0:T(1024)S(1)}, u32[]{:S(2)}, u32[]{:S(2)}) collective-permute-start(f32[17280]{0:T(1024)S(1)} %get-tuple-element.107), channel_id=1, source_target_pairs={{24,16},{25,17},{26,18},{27,19},{28,20},{29,21},{30,22},{31,23}} | collective-permute-start | bytes 207368 | tf_op jit(solution)/shard_map/ppermute | solution.py:979
  78.8 2.0 %collective-permute-start.11 = (f32[17280]{0:T(1024)S(1)}, f32[17280]{0:T(1024)S(1)}, u32[]{:S(2)}, u32[]{:S(2)}) collective-permute-start(f32[17280]{0:T(1024)S(1)} %get-tuple-element.107), channel_id=1, source_target_pairs={{24,8},{25,9},{26,10},{27,11},{28,12},{29,13},{30,14},{31,15}} | collective-permute-start | bytes 207368 | tf_op jit(solution)/shard_map/ppermute | solution.py:979
  79.5 8.1 %collective-permute-start.10 = (f32[17280]{0:T(1024)S(1)}, f32[17280]{0:T(1024)S(1)}, u32[]{:S(2)}, u32[]{:S(2)}) collective-permute-start(f32[17280]{0:T(1024)S(1)} %get-tuple-element.107), channel_id=1, source_target_pairs={{24,0},{25,1},{26,2},{27,3},{28,4},{29,5},{30,6},{31,7}} | collective-permute-start | bytes 207368 | tf_op jit(solution)/shard_map/ppermute | solution.py:979
  87.6 7.3 %collective-permute-start.14 = (f32[17280]{0:T(1024)S(1)}, f32[17280]{0:T(1024)S(1)}, u32[]{:S(2)}, u32[]{:S(2)}) collective-permute-start(f32[17280]{0:T(1024)S(1)} %add_add_fusion.1), channel_id=1, source_target_pairs={{0,5},{1,4},{2,7},{3,6},{4,1},{5,0},{6,3},{7,2},{8,14},{9,15},{10,... | collective-permute-start | bytes 207368 | tf_op jit(solution)/shard_map/ppermute | solution.py:990
  89.5 5.4 %collective-permute-start.13 = (f32[17280]{0:T(1024)S(1)}, f32[17280]{0:T(1024)S(1)}, u32[]{:S(2)}, u32[]{:S(2)}) collective-permute-start(f32[17280]{0:T(1024)S(1)} %add_add_fusion.1), channel_id=1, source_target_pairs={{0,1},{1,0},{2,3},{3,2},{4,5},{5,4},{6,7},{7,6},{8,10},{9,11},{10,... | collective-permute-start | bytes 207368 | tf_op jit(solution)/shard_map/ppermute | solution.py:990
  95.0 1.3 %collective-permute-start.15 = (f32[17280]{0:T(1024)S(1)}, f32[17280]{0:T(1024)S(1)}, u32[]{:S(2)}, u32[]{:S(2)}) collective-permute-start(f32[17280]{0:T(1024)S(1)} %add_add_fusion), channel_id=1, source_target_pairs={{0,8},{1,9},{2,10},{3,11},{4,12},{5,13},{6,14},{7,15},{8,0},{9,1},... | collective-permute-start | bytes 207368 | tf_op jit(solution)/shard_map/ppermute | solution.py:992
  96.3 4.4 %collective-permute-start.16 = (f32[17280]{0:T(1024)S(1)}, f32[17280]{0:T(1024)S(1)}, u32[]{:S(2)}, u32[]{:S(2)}) collective-permute-start(f32[17280]{0:T(1024)S(1)} %add.52), channel_id=1, source_target_pairs={{0,16},{1,17},{2,18},{3,19},{4,20},{5,21},{6,22},{7,23},{8,24},{9,... | collective-permute-start | bytes 207368 | tf_op jit(solution)/shard_map/ppermute | solution.py:992

commit v14 on v13

--- a/solution.py
+++ b/solution.py
@@ -66,18 +66,20 @@
     return gx * place[4] + gy
 
 
-def owner_apart(owner, place, y_devices, x_devices):
+def owner_apart(owner, groups, place, y_devices, x_devices):
     group, column = divmod(owner, x_devices * y_devices)
+    entry = groups - 1 - group
     y_apart = jnp.bitwise_xor(place[2], jnp.int32(column % y_devices))
-    return group, y_apart, jnp.bitwise_xor(place[1], jnp.int32(column // y_devices))
+    return entry, y_apart, jnp.bitwise_xor(place[1], jnp.int32(column // y_devices))
 
 
 def pick_kernel(y_devices, x_devices, apart, trainer_of, place, *refs):
     near, chosen, owners = refs[:y_devices], refs[y_devices], refs[y_devices + 1]
     wanted = jnp.bitwise_xor(place[1], jnp.int32(apart)) * y_devices + place[2]
     count = jnp.int32(0)
+    groups = trainer_of.shape[0] // (x_devices * y_devices)
     for owner in range(trainer_of.shape[0]):
-        group, y_apart, x_apart = owner_apart(owner, place, y_devices, x_devices)
+        group, y_apart, x_apart = owner_apart(owner, groups, place, y_devices, x_devices)
         mine = (trainer_of[owner] == wanted) & (x_apart == 0)
 
         @pl.when(mine)
@@ -202,8 +204,9 @@
     for other in range(x_devices):
         picked[other] = 0
     count = jnp.int32(0)
+    groups = trainer_of.shape[0] // (x_devices * y_devices)
     for owner in range(trainer_of.shape[0]):
-        group, y_apart, x_apart = owner_apart(owner, place, y_devices, x_devices)
+        group, y_apart, x_apart = owner_apart(owner, groups, place, y_devices, x_devices)
         mine = trainer_of[owner] == column
 
         @pl.when(mine)
@@ -455,6 +458,12 @@
     return base_viscosity + viscosity_gain * soft
 
 
+def logistic(half):
+    below = 1.0 + jnp.exp2((-2.0 / np.log(2.0)) * half)
+    inverse = pl.reciprocal(below, approx=True)
+    return inverse * (2.0 - below * inverse)
+
+
 def viscosity_kernel(closure, place, fields, viscosity, x_edges, y_edges, weights, out_column):
     x_cells, y_cells, z_cells = fields.shape[1:]
     up_first = lax.rem(place[2], 2) == 0
@@ -471,8 +480,8 @@
     for j in range(8):
         turned = [pltpu.roll(part, j, 0) if j else part for part in (high, high, low)]
         stacked = jnp.concatenate([*turned, blank], axis=0)
-        weights[j] = stacked.T[: HID + 8].astype(jnp.bfloat16)
-    out_column[...] = jnp.broadcast_to(plain.T[:HID, F + 1 : F + 2], (HID, 128))
+        weights[j] = stacked.T[:HID].astype(jnp.bfloat16)
+    out_column[...] = jnp.broadcast_to(2.0 * plain.T[:HID, F + 1 : F + 2], (HID, 128))
     sublane = lax.broadcasted_iota(jnp.int32, (8, z_cells), 0)
     wide = z_cells // 128
     tiles = y_cells // 8
@@ -489,11 +498,11 @@
             top = cells.astype(jnp.bfloat16).astype(jnp.float32)
             stacked = jnp.concatenate([top, cells - top, top, jnp.zeros_like(top)], axis=0)
             half = dot_rows(weights[j], stacked.astype(jnp.bfloat16))
-            total = half[HID:]
+            total = jnp.zeros((8, z_cells), jnp.float32)
             for group in range(HID // 8):
                 part = half[group * 8 : group * 8 + 8]
                 column = jnp.concatenate([out_column[group * 8 : group * 8 + 8, :]] * wide, axis=1)
-                total = total + column * (part * jnp.tanh(part))
+                total = total + column * (part * logistic(part))
             for step in (4, 2, 1):
                 total = total + pltpu.roll(total, step, 0)
             sums = jnp.where(sublane == j, total, sums)
@@ -517,7 +526,7 @@
         in_specs=[vmem, pl.BlockSpec(memory_space=pltpu.SMEM), vmem],
         out_specs=(vmem,) * 3,
         scratch_shapes=[
-            pltpu.VMEM((8, HID + 8, 32), jnp.bfloat16),
+            pltpu.VMEM((8, HID, 32), jnp.bfloat16),
             pltpu.VMEM((HID, 128), jnp.float32),
         ],
         compiler_params=pltpu.CompilerParams(vmem_limit_bytes=16 * 1024 * 1024),
@@ -560,7 +569,7 @@
             new_fields[f, x] = value + time_step * tendency
         return carry
 
-    lax.fori_loop(0, x_cells, plane, 0)
+    lax.fori_loop(0, x_cells, plane, 0, unroll=2)
 
 
 def evolve(place, viscosity, fields, x_halo, y_first, y_second):
@@ -917,7 +926,7 @@
             )
             for g in reversed(range(sim_groups))
         ]
-        return jnp.stack(landed[::-1])
+        return jnp.stack(landed)
 
     def from_line(held):
         return [lax.ppermute(held, everyone, swap(apart)) for apart in range(1, y_devices)]
@@ -975,7 +984,7 @@
     delta, new_brick = lax.cond(is_trainer, train_here, evolve_here)
 
     held = delta
-    for g in range(sim_groups):
+    for g in reversed(range(sim_groups)):
         held = held + lax.ppermute(
             delta, everyone, [(first_trainer + c, g * trainers + c) for c in range(trainers)]
         )

time: 104 us -> 112 us (1.077)
  Pallas kernels: 42.6 us -> 53.1 us
  waiting for transfers between devices: 25.9 us -> 20.4 us
  starting transfers between devices: 29.6 us -> 32.8 us
    pallas_call x1, Pallas kernels: 25.2 us -> 35.7 us  [brick_viscosity(): pl.pallas_call(viscosity_kernel, out_shape=(jax.ShapeDtypeStruct(fields.s...]
    ppermute x3, waiting for transfers between devices: 6.77 us -> 2.99 us  [on_device(): lax.ppermute(delta, everyone, [(first_trainer + c, g * trainers + c) for...]
    ppermute x2, starting transfers between devices: 0.14 us -> 3.74 us  [on_device(): lax.ppermute(final, everyone, [(g * trainers + c, (g ^ apart) * trainers...]
    ppermute x2, waiting for transfers between devices: 5.53 us -> 3.41 us  [on_device(): lax.ppermute(final, everyone, [(g * trainers + c, (g ^ apart) * trainers...]
    ppermute x3, starting transfers between devices: 4.05 us -> 2.8 us  [to_trainers(): lax.ppermute(payload, everyone, [(g * trainers + c, first_trainer + c) fo...]
    ppermute x3, waiting for transfers between devices: 2.02 us -> 0.78 us  [to_trainers(): lax.ppermute(payload, everyone, [(g * trainers + c, first_trainer + c) fo...]
    ppermute x1, waiting for transfers between devices: 2.61 us -> 3.73 us  [y_neighbours(): lax.ppermute(for_second, everyone, pairs(0, -1))]
  transfers between devices with their start and end apart: 18 -> 18, of which waited for: 8 -> 9; matrix products, arithmetic and copies ran while one was open for 1% -> 1% of each run, Pallas kernels for 29% -> 36%
where the time goes in v14:
time: 112 us
  Pallas kernels  53.1 us (47%)
  starting transfers between devices  32.8 us (29%)
  waiting for transfers between devices  20.4 us (18%)
  other arithmetic  2.29 us (2%)
  between operations  1.66 us (1%)
  local copies, waits for them, and re-layouts  1.28 us (1%)
    pallas_call x1, Pallas kernels, brick_viscosity(): pl.pallas_call(viscosity_kernel, out_shape=(jax.ShapeDtypeStruct(fields.s...  35.7 us
    pallas_call x1, Pallas kernels, evolve(): pl.pallas_call(evolve_kernel, out_shape=jax.ShapeDtypeStruct(fields.shape...  8.6 us
    all_to_all x1, starting transfers between devices, on_device(): lax.all_to_all(thin, ('gx', 'gy'), split_axis=0, concat_axis=0, tiled=True)  7.42 us
    ppermute x2, starting transfers between devices, on_device(): final = final + lax.ppermute(held, everyone, meets)  4.76 us
    ppermute x1, starting transfers between devices, y_neighbours(): lax.ppermute(for_second, everyone, pairs(0, -1))  4.19 us
    ppermute x2, waiting for transfers between devices, on_device(): final = final + lax.ppermute(held, everyone, meets)  4.05 us
    ppermute x2, starting transfers between devices, on_device(): lax.ppermute(final, everyone, [(g * trainers + c, (g ^ apart) * trainers...  3.74 us
    ppermute x1, waiting for transfers between devices, y_neighbours(): lax.ppermute(for_second, everyone, pairs(0, -1))  3.73 us
  transfers between devices with their start and end apart: 18, of which 9 were waited for; matrix products, arithmetic and copies ran while one was open for 1% of the time, Pallas kernels for 36%

profile of v14, /device:TPU:0, one launch (start us, length us, event | category | flops | bytes accessed | tf_op | source)
XLA Modules:
  0.0 111.5 jit_solution(276339704839080765)
XLA Ops:
  0.6 0.1 stack.27.place
  0.7 0.7 copy-done.1
  1.4 2.8 %thin_faces.1 = f32[8,16,256]{2,1,0:T(8,128)} custom-call(s32[24]{0:T(128)S(1)} %copy-done.1, s32[6]{0:T(128)S(1)} %stack.27.place, f32[2560,384]{1,0:T(8,128)} %bitcast.23, f32[80,32,384]{2,1,0:T(8,128)} %bitcast.24), custom_call_target="tpu_custom_call" | custom-call | tf_op jit(solution)/shard_map/thin_faces/pallas_call | solution.py:671
  4.2 0.0 copy-start.6
  4.2 0.0 copy-start
  4.2 7.4 %all-to-all-start = ((f32[8,16,256]{2,1,0:T(8,128)}), f32[8,16,256]{2,1,0:T(8,128)S(1)}, u32[]{:S(2)}, u32[]{:S(2)}) async-start(f32[8,16,256]{2,1,0:T(8,128)} %thin_faces.1), calls=%async_computation | async-start | bytes 262144 | tf_op jit(solution)/shard_map/all_to_all | solution.py:948
  11.7 0.1 fusion.1
  11.8 3.6 %sample_cube.1 = (f32[80,256]{1,0:T(8,128)S(1)}, f32[80,256]{1,0:T(8,128)S(1)}, f32[80,256]{1,0:T(8,128)S(1)}, f32[2,16,128]{2,1,0:T(8,128)S(1)}) custom-call(s32[24]{0:T(128)S(1)} %copy-done.2, s32[6]{0:T(128)S(1)} %stack.27.place, f32[2560,384]{1,0:T(8,128)} %bitcast.25), custom_call_target="tpu_custom_call" | custom-call | bytes 16000000 | tf_op jit(solution)/shard_map/sample_cube/pallas_call | solution.py:774
  15.4 0.0 copy-start.8
  15.4 0.1 fusion
  15.6 0.1 copy.15
  15.6 0.1 reshape.34
  15.7 0.2 slice.37
  16.0 0.1 select_maximum_fusion.closure
  16.0 3.1 %all-to-all-done.thin = f32[8,16,256]{2,1,0:T(8,128)S(1)} async-done(((f32[8,16,256]{2,1,0:T(8,128)}), f32[8,16,256]{2,1,0:T(8,128)S(1)}, u32[]{:S(2)}, u32[]{:S(2)}) %all-to-all-start) | async-done | bytes 131104 | tf_op jit(solution)/shard_map/all_to_all | solution.py:948
  19.2 1.6 %cube_change.1 = bf16[320,128]{1,0:T(8,128)(2,1)S(1)} custom-call(s32[24]{0:T(128)S(1)} %copy-done.2, s32[6]{0:T(128)S(1)} %stack.27.place, f32[8,128]{1,0:T(8,128)S(1)} %select_maximum_fusion.closure, bf16[256,256]{1,0:T(8,128)(2,1)S(1)} %copy-done, f32[80,256]{1,0:T(8,128)S(1)} %get-tuple-element.93.centre, f32[80,256]{1,0:T(8,128)S(1)} %get-tuple-element.94.lower, ...), custom_call_target="tpu_custom_call" | custom-call | tf_op jit(solution)/shard_map/cube_change/pallas_call | solution.py:855
  20.8 1.5 %collective-permute-start.2 = (bf16[320,128]{1,0:T(8,128)(2,1)S(1)}, bf16[320,128]{1,0:T(8,128)(2,1)S(1)}, u32[]{:S(2)}, u32[]{:S(2)}) collective-permute-start(bf16[320,128]{1,0:T(8,128)(2,1)S(1)} %cube_change.1), channel_id=1, source_target_pairs={{0,24},{1,25},{2,26},{3,27},{4,28},{5,29},{6,30},{7,31}} | collective-permute-start | bytes 245768 | tf_op jit(solution)/shard_map/ppermute | solution.py:924
  22.2 0.7 collective-permute-start.1
  22.9 0.7 collective-permute-start
  23.6 0.8 collective-permute-done.2
  24.4 0.8 collective-permute-start.8
  25.2 0.7 collective-permute-start.7
  25.9 0.7 collective-permute-start.6
  26.6 35.7 %conditional.2 = ((f32[16,32,384]{2,1,0:T(8,128)S(1)}, f32[2,5,32,384]{3,2,1,0:T(8,128)}, f32[2,5,16,384]{3,2,1,0:T(8,128)S(1)})) conditional(s32[]{:T(128)} %convert_element_type.10, (f32[8,128]{1,0:T(8,128)S(1)}, s32[6]{0:T(128)S(1)}, f32[5,16,32,384]{3,2,1,0:T(8,128)}) %tuple.46, () %tuple.31), branch_computations={%region_1.2_spmd, %region_2.3_spmd} | conditional | bytes 1523756 | solution.py:954
  26.6 35.7 %brick_viscosity.1 = (f32[16,32,384]{2,1,0:T(8,128)S(1)}, f32[2,5,32,384]{3,2,1,0:T(8,128)}, f32[2,5,16,384]{3,2,1,0:T(8,128)S(1)}) custom-call(f32[8,128]{1,0:T(8,128)S(1)} %get-tuple-element.43.closure, s32[6]{0:T(128)S(1)} %get-tuple-element.44.place, f32[5,16,32,384]{3,2,1,0:T(8,128)} %get-tuple-element.45.fields), custom_call_target="tpu_custom_call" | custom-call | tf_op jit(solution)/shard_map/cond/branch_0_fun/brick_viscosity/pallas_call | solution.py:519
  62.3 2.5 %collective-permute-start.3 = (f32[2,5,32,384]{3,2,1,0:T(8,128)}, f32[2,5,32,384]{3,2,1,0:T(8,128)S(1)}, u32[]{:S(2)}, u32[]{:S(2)}) collective-permute-start(f32[2,5,32,384]{3,2,1,0:T(8,128)} %get-tuple-element.99), channel_id=1, source_target_pairs={{0,4},{1,5},{2,6},{3,7},{4,0},{5,1},{6,2},{7,3},{8,12},{9,13},{10,... | collective-permute-start | bytes 1474568 | tf_op jit(solution)/shard_map/ppermute | solution.py:909
  64.8 0.8 pick_cubes.1
  65.7 0.7 collective-permute-start.9
  66.4 4.2 %collective-permute-start.5 = (f32[5,16,384]{2,1,0:T(8,128)S(1)}, f32[5,16,384]{2,1,0:T(8,128)S(1)}, u32[]{:S(2)}, u32[]{:S(2)}) collective-permute-start(f32[5,16,384]{2,1,0:T(8,128)S(1)} %get-tuple-element.112), channel_id=1, source_target_pairs={{0,3},{1,2},{2,1},{3,0},{4,7},{5,6},{6,5},{7,4},{8,11},{9,10},{10,... | collective-permute-start | bytes 368648 | tf_op jit(solution)/shard_map/ppermute | solution.py:916
  70.6 1.9 %collective-permute-start.4 = (f32[5,16,384]{2,1,0:T(8,128)S(1)}, f32[5,16,384]{2,1,0:T(8,128)S(1)}, u32[]{:S(2)}, u32[]{:S(2)}) collective-permute-start(f32[5,16,384]{2,1,0:T(8,128)S(1)} %get-tuple-element.113), channel_id=1, source_target_pairs={{0,1},{1,0},{2,3},{3,2},{4,5},{5,4},{6,7},{7,6},{8,9},{9,8},{10,11... | collective-permute-start | bytes 368648 | tf_op jit(solution)/shard_map/ppermute | solution.py:915
  72.5 3.7 %collective-permute-done.5 = f32[5,16,384]{2,1,0:T(8,128)S(1)} collective-permute-done((f32[5,16,384]{2,1,0:T(8,128)S(1)}, f32[5,16,384]{2,1,0:T(8,128)S(1)}, u32[]{:S(2)}, u32[]{:S(2)}) %collective-permute-start.5) | collective-permute-done | bytes 122912 | tf_op jit(solution)/shard_map/ppermute | solution.py:916
  76.2 2.3 %collective-permute-done.4 = f32[5,16,384]{2,1,0:T(8,128)S(1)} collective-permute-done((f32[5,16,384]{2,1,0:T(8,128)S(1)}, f32[5,16,384]{2,1,0:T(8,128)S(1)}, u32[]{:S(2)}, u32[]{:S(2)}) %collective-permute-start.4) | collective-permute-done | bytes 122912 | tf_op jit(solution)/shard_map/ppermute | solution.py:915
  78.6 8.6 %conditional.3 = (f32[17280]{0:T(1024)S(1)}, f32[1,5,16,32,384]{4,3,2,1,0:T(8,128)}) conditional(s32[]{:T(128)} %convert_element_type.10, (s32[6]{0:T(128)S(1)}, f32[16,32,384]{2,1,0:T(8,128)S(1)}, f32[5,16,32,384]{3,2,1,0:T(8,128)}, f32[2,5,32,384]{3,2,1,0:T(8,128)S(1)}, f32[5,16,384]{2,1,0:T(8,128)S(1)}, ...), branch_computations={%region_3.4_spmd, %region_4.5_spmd} | conditional | flops 17280 | bytes 345616 | solution.py:984
  78.6 8.6 %evolve_brick.1 = f32[5,16,32,384]{3,2,1,0:T(8,128)} custom-call(s32[6]{0:T(128)S(1)} %get-tuple-element.46.place, f32[16,32,384]{2,1,0:T(8,128)S(1)} %get-tuple-element.47.viscosity, f32[5,16,32,384]{3,2,1,0:T(8,128)} %get-tuple-element.48.fields, f32[2,5,32,384]{3,2,1,0:T(8,128)S(1)} %get-tuple-element.49.x_halo, ...), custom_call_target="tpu_custom_call" | custom-call | tf_op jit(solution)/shard_map/cond/branch_0_fun/evolve_brick/pallas_call | solution.py:577
  87.2 1.3 %collective-permute-start.12 = (f32[17280]{0:T(1024)S(1)}, f32[17280]{0:T(1024)S(1)}, u32[]{:S(2)}, u32[]{:S(2)}) collective-permute-start(f32[17280]{0:T(1024)S(1)} %get-tuple-element.107), channel_id=1, source_target_pairs={{24,0},{25,1},{26,2},{27,3},{28,4},{29,5},{30,6},{31,7}} | collective-permute-start | bytes 207368 | tf_op jit(solution)/shard_map/ppermute | solution.py:988
  88.5 0.7 collective-permute-start.11
  89.2 0.7 collective-permute-start.10
  89.8 3.0 %collective-permute-done.12 = f32[17280]{0:T(1024)S(1)} collective-permute-done((f32[17280]{0:T(1024)S(1)}, f32[17280]{0:T(1024)S(1)}, u32[]{:S(2)}, u32[]{:S(2)}) %collective-permute-start.12) | collective-permute-done | bytes 69152 | tf_op jit(solution)/shard_map/ppermute | solution.py:988
  92.9 2.3 %collective-permute-start.14 = (f32[17280]{0:T(1024)S(1)}, f32[17280]{0:T(1024)S(1)}, u32[]{:S(2)}, u32[]{:S(2)}) collective-permute-start(f32[17280]{0:T(1024)S(1)} %add_add_fusion.1), channel_id=1, source_target_pairs={{0,5},{1,4},{2,7},{3,6},{4,1},{5,0},{6,3},{7,2},{8,14},{9,15},{10,... | collective-permute-start | bytes 207368 | tf_op jit(solution)/shard_map/ppermute | solution.py:999
  95.1 2.5 %collective-permute-start.13 = (f32[17280]{0:T(1024)S(1)}, f32[17280]{0:T(1024)S(1)}, u32[]{:S(2)}, u32[]{:S(2)}) collective-permute-start(f32[17280]{0:T(1024)S(1)} %add_add_fusion.1), channel_id=1, source_target_pairs={{0,1},{1,0},{2,3},{3,2},{4,5},{5,4},{6,7},{7,6},{8,10},{9,11},{10,... | collective-permute-start | bytes 207368 | tf_op jit(solution)/shard_map/ppermute | solution.py:999
  97.6 2.3 %collective-permute-done.14 = f32[17280]{0:T(1024)S(1)} collective-permute-done((f32[17280]{0:T(1024)S(1)}, f32[17280]{0:T(1024)S(1)}, u32[]{:S(2)}, u32[]{:S(2)}) %collective-permute-start.14) | collective-permute-done | bytes 69152 | tf_op jit(solution)/shard_map/ppermute | solution.py:999
  100.0 1.7 %collective-permute-done.13 = f32[17280]{0:T(1024)S(1)} collective-permute-done((f32[17280]{0:T(1024)S(1)}, f32[17280]{0:T(1024)S(1)}, u32[]{:S(2)}, u32[]{:S(2)}) %collective-permute-start.13) | collective-permute-done | bytes 69152 | tf_op jit(solution)/shard_map/ppermute | solution.py:999
  101.7 0.8 collective-permute-start.15
  102.5 0.9 collective-permute-done.15
  103.4 2.9 %collective-permute-start.16 = (f32[17280]{0:T(1024)S(1)}, f32[17280]{0:T(1024)S(1)}, u32[]{:S(2)}, u32[]{:S(2)}) collective-permute-start(f32[17280]{0:T(1024)S(1)} %add.52), channel_id=1, source_target_pairs={{0,16},{1,17},{2,18},{3,19},{4,20},{5,21},{6,22},{7,23},{8,24},{9,... | collective-permute-start | bytes 207368 | tf_op jit(solution)/shard_map/ppermute | solution.py:1001
  106.3 2.5 %collective-permute-done.16 = f32[17280]{0:T(1024)S(1)} collective-permute-done((f32[17280]{0:T(1024)S(1)}, f32[17280]{0:T(1024)S(1)}, u32[]{:S(2)}, u32[]{:S(2)}) %collective-permute-start.16) | collective-permute-done | bytes 69152 | tf_op jit(solution)/shard_map/ppermute | solution.py:1001
  108.8 0.6 multiply_reduce_fusion
  110.2 1.4 %multiply_subtract_fusion = (f32[540]{0:T(1024)}, f32[540]{0:T(1024)}) fusion(f32[17280]{0:T(1024)S(1)} %copy-done.5, s32[]{:T(128)S(6)} %select_n.2, f32[]{:T(128)S(6)} %sqrt.3, f32[17280]{0:T(1024)S(1)} %get-tuple-element.111, f32[17280]{0:T(1024)} %param.20), kind=kLoop, calls=%fused_computation.14 | loop fusion | flops 2700 | bytes 10808 | tf_op jit(solution)/shard_map/sub | solution.py:1014
  (35 shorter events, 0.2 us)
Async XLA Ops:
  0.7 0.7 copy-start.1
  1.4 10.3 %copy-start.7 = (f32[64,5]{0,1:T(8,128)S(1)}, f32[64,5]{0,1:T(8,128)}, u32[]{:S(2)}) copy-start(f32[64,5]{0,1:T(8,128)} %param.16) | copy-start | bytes 3844
  1.4 10.3 %copy-start.5 = (f32[17280]{0:T(1024)S(1)}, f32[17280]{0:T(1024)}, u32[]{:S(2)}) copy-start(f32[17280]{0:T(1024)} %param.19) | copy-start | bytes 207364
  1.4 10.4 %copy-start.9 = (f32[64]{0:T(128)S(1)}, f32[64]{0:T(128)}, u32[]{:S(2)}) copy-start(f32[64]{0:T(128)} %param.17) | copy-start | bytes 772
  1.4 10.4 %copy-start.2 = (s32[24]{0:T(128)S(1)}, s32[24]{0:T(128)}, u32[]{:S(2)}) copy-start(s32[24]{0:T(128)} %sample_block.5) | copy-start | bytes 292
  4.2 11.2 %copy-start.6 = (f32[64]{0:T(128)S(1)}, f32[64]{0:T(128)}, u32[]{:S(2)}) copy-start(f32[64]{0:T(128)} %param.18) | copy-start | bytes 772
  4.2 15.0 %copy-start = (bf16[256,256]{1,0:T(8,128)(2,1)S(1)}, bf16[256,256]{1,0:T(8,128)(2,1)}, u32[]{:S(2)}) copy-start(bf16[256,256]{1,0:T(8,128)(2,1)} %constant.60.clone.order) | copy-start | bytes 393220
  4.2 14.9 %all-to-all-start = ((f32[8,16,256]{2,1,0:T(8,128)}), f32[8,16,256]{2,1,0:T(8,128)S(1)}, u32[]{:S(2)}, u32[]{:S(2)}) async-start(f32[8,16,256]{2,1,0:T(8,128)} %thin_faces.1), calls=%async_computation | async-start | bytes 262144 | tf_op jit(solution)/shard_map/all_to_all | solution.py:948
  15.4 49.4 %copy-start.8 = (s32[24]{0:T(128)S(1)}, s32[24]{0:T(128)}, u32[]{:S(2)}) copy-start(s32[24]{0:T(128)} %trainer_of.1) | copy-start | bytes 292
  20.8 3.6 %collective-permute-start.2 = (bf16[320,128]{1,0:T(8,128)(2,1)S(1)}, bf16[320,128]{1,0:T(8,128)(2,1)S(1)}, u32[]{:S(2)}, u32[]{:S(2)}) collective-permute-start(bf16[320,128]{1,0:T(8,128)(2,1)S(1)} %cube_change.1), channel_id=1, source_target_pairs={{0,24},{1,25},{2,26},{3,27},{4,28},{5,29},{6,30},{7,31}} | collective-permute-start | bytes 245768 | tf_op jit(solution)/shard_map/ppermute | solution.py:924
  22.2 2.1 %collective-permute-start.1 = (bf16[320,128]{1,0:T(8,128)(2,1)S(1)}, bf16[320,128]{1,0:T(8,128)(2,1)S(1)}, u32[]{:S(2)}, u32[]{:S(2)}) collective-permute-start(bf16[320,128]{1,0:T(8,128)(2,1)S(1)} %cube_change.1), channel_id=1, source_target_pairs={{8,24},{9,25},{10,26},{11,27},{12,28},{13,29},{14,30},{15,31}} | collective-permute-start | bytes 245768 | tf_op jit(solution)/shard_map/ppermute | solution.py:924
  22.9 1.5 %collective-permute-start = (bf16[320,128]{1,0:T(8,128)(2,1)S(1)}, bf16[320,128]{1,0:T(8,128)(2,1)S(1)}, u32[]{:S(2)}, u32[]{:S(2)}) collective-permute-start(bf16[320,128]{1,0:T(8,128)(2,1)S(1)} %cube_change.1), channel_id=1, source_target_pairs={{16,24},{17,25},{18,26},{19,27},{20,28},{21,29},{22,30},{23,31}} | collective-permute-start | bytes 245768 | tf_op jit(solution)/shard_map/ppermute | solution.py:924
  24.4 54.2 %copy-start.3 = (bf16[4,256,240]{2,1,0:T(8,128)(2,1)S(1)}, bf16[4,256,240]{2,1,0:T(8,128)(2,1)}, u32[]{:S(2)}) copy-start(bf16[4,256,240]{2,1,0:T(8,128)(2,1)} %constant.59.clone) | copy-start | bytes 1474564
  24.4 54.2 %copy-start.4 = (bf16[4,256,240]{2,1,0:T(8,128)(2,1)S(1)}, bf16[4,256,240]{2,1,0:T(8,128)(2,1)}, u32[]{:S(2)}) copy-start(bf16[4,256,240]{2,1,0:T(8,128)(2,1)} %constant.58.clone) | copy-start | bytes 1474564
  24.4 40.4 %collective-permute-start.8 = (bf16[3,320,128]{2,1,0:T(8,128)(2,1)S(1)}, bf16[3,320,128]{2,1,0:T(8,128)(2,1)S(1)}, u32[]{:S(2)}, u32[]{:S(2)}) collective-permute-start(bf16[3,320,128]{2,1,0:T(8,128)(2,1)S(1)} %pad_maximum_fusion.1.refs_0_), channel_id=1, source_target_pairs={{24,27},{25,26},{26,25},{27,24},{28,31},{29,30},{30,29},{31,28}} | collective-permute-start | bytes 737288 | tf_op jit(solution)/shard_map/ppermute | solution.py:932
  25.2 39.6 %collective-permute-start.7 = (bf16[3,320,128]{2,1,0:T(8,128)(2,1)S(1)}, bf16[3,320,128]{2,1,0:T(8,128)(2,1)S(1)}, u32[]{:S(2)}, u32[]{:S(2)}) collective-permute-start(bf16[3,320,128]{2,1,0:T(8,128)(2,1)S(1)} %pad_maximum_fusion.1.refs_0_), channel_id=1, source_target_pairs={{24,26},{25,27},{26,24},{27,25},{28,30},{29,31},{30,28},{31,29}} | collective-permute-start | bytes 737288 | tf_op jit(solution)/shard_map/ppermute | solution.py:932
  25.9 38.9 %collective-permute-start.6 = (bf16[3,320,128]{2,1,0:T(8,128)(2,1)S(1)}, bf16[3,320,128]{2,1,0:T(8,128)(2,1)S(1)}, u32[]{:S(2)}, u32[]{:S(2)}) collective-permute-start(bf16[3,320,128]{2,1,0:T(8,128)(2,1)S(1)} %pad_maximum_fusion.1.refs_0_), channel_id=1, source_target_pairs={{24,25},{25,24},{26,27},{27,26},{28,29},{29,28},{30,31},{31,30}} | collective-permute-start | bytes 737288 | tf_op jit(solution)/shard_map/ppermute | solution.py:932
  62.3 16.2 %collective-permute-start.3 = (f32[2,5,32,384]{3,2,1,0:T(8,128)}, f32[2,5,32,384]{3,2,1,0:T(8,128)S(1)}, u32[]{:S(2)}, u32[]{:S(2)}) collective-permute-start(f32[2,5,32,384]{3,2,1,0:T(8,128)} %get-tuple-element.99), channel_id=1, source_target_pairs={{0,4},{1,5},{2,6},{3,7},{4,0},{5,1},{6,2},{7,3},{8,12},{9,13},{10,... | collective-permute-start | bytes 1474568 | tf_op jit(solution)/shard_map/ppermute | solution.py:909
  65.7 12.9 %collective-permute-start.9 = (bf16[6,320,128]{2,1,0:T(8,128)(2,1)S(1)}, bf16[6,320,128]{2,1,0:T(8,128)(2,1)S(1)}, u32[]{:S(2)}, u32[]{:S(2)}) collective-permute-start(bf16[6,320,128]{2,1,0:T(8,128)(2,1)S(1)} %pick_cubes.1), channel_id=1, source_target_pairs={{24,28},{25,29},{26,30},{27,31},{28,24},{29,25},{30,26},{31,27}} | collective-permute-start | bytes 1474568 | tf_op jit(solution)/shard_map/ppermute | solution.py:935
  66.4 9.9 %collective-permute-start.5 = (f32[5,16,384]{2,1,0:T(8,128)S(1)}, f32[5,16,384]{2,1,0:T(8,128)S(1)}, u32[]{:S(2)}, u32[]{:S(2)}) collective-permute-start(f32[5,16,384]{2,1,0:T(8,128)S(1)} %get-tuple-element.112), channel_id=1, source_target_pairs={{0,3},{1,2},{2,1},{3,0},{4,7},{5,6},{6,5},{7,4},{8,11},{9,10},{10,... | collective-permute-start | bytes 368648 | tf_op jit(solution)/shard_map/ppermute | solution.py:916
  70.6 8.0 %collective-permute-start.4 = (f32[5,16,384]{2,1,0:T(8,128)S(1)}, f32[5,16,384]{2,1,0:T(8,128)S(1)}, u32[]{:S(2)}, u32[]{:S(2)}) collective-permute-start(f32[5,16,384]{2,1,0:T(8,128)S(1)} %get-tuple-element.113), channel_id=1, source_target_pairs={{0,1},{1,0},{2,3},{3,2},{4,5},{5,4},{6,7},{7,6},{8,9},{9,8},{10,11... | collective-permute-start | bytes 368648 | tf_op jit(solution)/shard_map/ppermute | solution.py:915
  87.2 5.6 %collective-permute-start.12 = (f32[17280]{0:T(1024)S(1)}, f32[17280]{0:T(1024)S(1)}, u32[]{:S(2)}, u32[]{:S(2)}) collective-permute-start(f32[17280]{0:T(1024)S(1)} %get-tuple-element.107), channel_id=1, source_target_pairs={{24,0},{25,1},{26,2},{27,3},{28,4},{29,5},{30,6},{31,7}} | collective-permute-start | bytes 207368 | tf_op jit(solution)/shard_map/ppermute | solution.py:988
  88.5 4.3 %collective-permute-start.11 = (f32[17280]{0:T(1024)S(1)}, f32[17280]{0:T(1024)S(1)}, u32[]{:S(2)}, u32[]{:S(2)}) collective-permute-start(f32[17280]{0:T(1024)S(1)} %get-tuple-element.107), channel_id=1, source_target_pairs={{24,8},{25,9},{26,10},{27,11},{28,12},{29,13},{30,14},{31,15}} | collective-permute-start | bytes 207368 | tf_op jit(solution)/shard_map/ppermute | solution.py:988
  89.2 3.7 %collective-permute-start.10 = (f32[17280]{0:T(1024)S(1)}, f32[17280]{0:T(1024)S(1)}, u32[]{:S(2)}, u32[]{:S(2)}) collective-permute-start(f32[17280]{0:T(1024)S(1)} %get-tuple-element.107), channel_id=1, source_target_pairs={{24,16},{25,17},{26,18},{27,19},{28,20},{29,21},{30,22},{31,23}} | collective-permute-start | bytes 207368 | tf_op jit(solution)/shard_map/ppermute | solution.py:988
  92.9 7.1 %collective-permute-start.14 = (f32[17280]{0:T(1024)S(1)}, f32[17280]{0:T(1024)S(1)}, u32[]{:S(2)}, u32[]{:S(2)}) collective-permute-start(f32[17280]{0:T(1024)S(1)} %add_add_fusion.1), channel_id=1, source_target_pairs={{0,5},{1,4},{2,7},{3,6},{4,1},{5,0},{6,3},{7,2},{8,14},{9,15},{10,... | collective-permute-start | bytes 207368 | tf_op jit(solution)/shard_map/ppermute | solution.py:999
  95.1 6.5 %collective-permute-start.13 = (f32[17280]{0:T(1024)S(1)}, f32[17280]{0:T(1024)S(1)}, u32[]{:S(2)}, u32[]{:S(2)}) collective-permute-start(f32[17280]{0:T(1024)S(1)} %add_add_fusion.1), channel_id=1, source_target_pairs={{0,1},{1,0},{2,3},{3,2},{4,5},{5,4},{6,7},{7,6},{8,10},{9,11},{10,... | collective-permute-start | bytes 207368 | tf_op jit(solution)/shard_map/ppermute | solution.py:999
  101.7 1.8 %collective-permute-start.15 = (f32[17280]{0:T(1024)S(1)}, f32[17280]{0:T(1024)S(1)}, u32[]{:S(2)}, u32[]{:S(2)}) collective-permute-start(f32[17280]{0:T(1024)S(1)} %add_add_fusion), channel_id=1, source_target_pairs={{0,8},{1,9},{2,10},{3,11},{4,12},{5,13},{6,14},{7,15},{8,0},{9,1},... | collective-permute-start | bytes 207368 | tf_op jit(solution)/shard_map/ppermute | solution.py:1001
  103.4 5.4 %collective-permute-start.16 = (f32[17280]{0:T(1024)S(1)}, f32[17280]{0:T(1024)S(1)}, u32[]{:S(2)}, u32[]{:S(2)}) collective-permute-start(f32[17280]{0:T(1024)S(1)} %add.52), channel_id=1, source_target_pairs={{0,16},{1,17},{2,18},{3,19},{4,20},{5,21},{6,22},{7,23},{8,24},{9,... | collective-permute-start | bytes 207368 | tf_op jit(solution)/shard_map/ppermute | solution.py:1001

commit v15 on v14

--- a/solution.py
+++ b/solution.py
@@ -458,37 +458,39 @@
     return base_viscosity + viscosity_gain * soft
 
 
-def logistic(half):
-    below = 1.0 + jnp.exp2((-2.0 / np.log(2.0)) * half)
-    inverse = pl.reciprocal(below, approx=True)
-    return inverse * (2.0 - below * inverse)
-
-
 def viscosity_kernel(closure, place, fields, viscosity, x_edges, y_edges, weights, out_column):
-    x_cells, y_cells, z_cells = fields.shape[1:]
+    y_cells, z_cells = fields.shape[2:]
+    x, x_cells = pl.program_id(0), pl.num_programs(0)
     up_first = lax.rem(place[2], 2) == 0
     for f in range(F):
-        x_edges[0, f] = fields[f, 0]
-        x_edges[1, f] = fields[f, x_cells - 1]
-        low, high = fields[f, :, 0, :], fields[f, :, y_cells - 1, :]
-        y_edges[0, f] = jnp.where(up_first, high, low)
-        y_edges[1, f] = jnp.where(up_first, low, high)
-    plain = closure[...]
-    high = plain.astype(jnp.bfloat16).astype(jnp.float32)
-    low = plain - high
-    blank = jnp.zeros((8, 128), jnp.float32)
-    for j in range(8):
-        turned = [pltpu.roll(part, j, 0) if j else part for part in (high, high, low)]
-        stacked = jnp.concatenate([*turned, blank], axis=0)
-        weights[j] = stacked.T[:HID].astype(jnp.bfloat16)
-    out_column[...] = jnp.broadcast_to(2.0 * plain.T[:HID, F + 1 : F + 2], (HID, 128))
+        low, high = fields[f, 0, 0:1, :], fields[f, 0, y_cells - 1 : y_cells, :]
+        y_edges[0, f, pl.ds(x, 1), :] = jnp.where(up_first, high, low)
+        y_edges[1, f, pl.ds(x, 1), :] = jnp.where(up_first, low, high)
+
+    @pl.when(x == x_cells - 1)
+    def _():
+        x_edges[1] = fields[:, 0]
+
+    @pl.when(x == 0)
+    def _():
+        x_edges[0] = fields[:, 0]
+        plain = closure[...]
+        high = plain.astype(jnp.bfloat16).astype(jnp.float32)
+        low = plain - high
+        blank = jnp.zeros((8, 128), jnp.float32)
+        for j in range(8):
+            turned = [pltpu.roll(part, j, 0) if j else part for part in (high, high, low)]
+            stacked = jnp.concatenate([*turned, blank], axis=0)
+            weights[j] = stacked.T[: HID + 8].astype(jnp.bfloat16)
+        out_column[...] = jnp.broadcast_to(plain.T[:HID, F + 1 : F + 2], (HID, 128))
+
     sublane = lax.broadcasted_iota(jnp.int32, (8, z_cells), 0)
     wide = z_cells // 128
     tiles = y_cells // 8
 
     def tile(index, carry):
-        x, rows = index // tiles, pl.ds(pl.multiple_of(index % tiles * 8, 8), 8)
-        turned = [fields[f, x, rows, :] for f in range(F)]
+        rows = pl.ds(pl.multiple_of(index * 8, 8), 8)
+        turned = [fields[f, 0, rows, :] for f in range(F)]
         turned = [pltpu.roll(turned[f], f, 0) if f else turned[f] for f in range(F)]
         sums = jnp.zeros((8, z_cells), jnp.float32)
         for j in range(8):
@@ -498,24 +500,23 @@
             top = cells.astype(jnp.bfloat16).astype(jnp.float32)
             stacked = jnp.concatenate([top, cells - top, top, jnp.zeros_like(top)], axis=0)
             half = dot_rows(weights[j], stacked.astype(jnp.bfloat16))
-            total = jnp.zeros((8, z_cells), jnp.float32)
+            total = half[HID:]
             for group in range(HID // 8):
                 part = half[group * 8 : group * 8 + 8]
                 column = jnp.concatenate([out_column[group * 8 : group * 8 + 8, :]] * wide, axis=1)
-                total = total + column * (part * logistic(part))
+                total = total + column * (part * jnp.tanh(part))
             for step in (4, 2, 1):
                 total = total + pltpu.roll(total, step, 0)
             sums = jnp.where(sublane == j, total, sums)
         soft = jnp.maximum(sums, 0.0) + jnp.log1p(jnp.exp(-jnp.abs(sums)))
-        viscosity[x, rows, :] = base_viscosity + viscosity_gain * soft
+        viscosity[0, rows, :] = base_viscosity + viscosity_gain * soft
         return carry
 
-    lax.fori_loop(0, x_cells * tiles, tile, 0)
+    lax.fori_loop(0, tiles, tile, 0)
 
 
 def brick_viscosity(closure, place, fields):
     count, x_cells, y_cells, z_cells = fields.shape
-    vmem = pl.BlockSpec(memory_space=pltpu.VMEM)
     return pl.pallas_call(
         viscosity_kernel,
         out_shape=(
@@ -523,10 +524,19 @@
             jax.ShapeDtypeStruct((2, count, y_cells, z_cells), fields.dtype),
             jax.ShapeDtypeStruct((2, count, x_cells, z_cells), fields.dtype),
         ),
-        in_specs=[vmem, pl.BlockSpec(memory_space=pltpu.SMEM), vmem],
-        out_specs=(vmem,) * 3,
+        grid=(x_cells,),
+        in_specs=[
+            pl.BlockSpec((8, 128), lambda x: (0, 0)),
+            pl.BlockSpec(memory_space=pltpu.SMEM),
+            pl.BlockSpec((count, 1, y_cells, z_cells), lambda x: (0, x, 0, 0)),
+        ],
+        out_specs=(
+            pl.BlockSpec((1, y_cells, z_cells), lambda x: (x, 0, 0)),
+            pl.BlockSpec((2, count, y_cells, z_cells), lambda x: (0, 0, 0, 0)),
+            pl.BlockSpec((2, count, x_cells, z_cells), lambda x: (0, 0, 0, 0)),
+        ),
         scratch_shapes=[
-            pltpu.VMEM((8, HID, 32), jnp.bfloat16),
+            pltpu.VMEM((8, HID + 8, 32), jnp.bfloat16),
             pltpu.VMEM((HID, 128), jnp.float32),
         ],
         compiler_params=pltpu.CompilerParams(vmem_limit_bytes=16 * 1024 * 1024),
@@ -540,45 +550,51 @@
     row = lax.broadcasted_iota(jnp.int32, (y_cells, z_cells), 0)
     lane = lax.broadcasted_iota(jnp.int32, (y_cells, z_cells), 1)
 
-    def plane(x, carry):
-        centre = [fields[f, x] for f in range(F)]
-        below = jnp.maximum(x - 1, 0)
-        above = jnp.minimum(x + 1, x_cells - 1)
-        for f in range(F):
-            value = centre[f]
-            west = jnp.where(x == 0, x_halo[1, f], fields[f, below])
-            east = jnp.where(x == x_cells - 1, x_halo[0, f], fields[f, above])
-            first, second = y_first[f, pl.ds(x, 1), :], y_second[f, pl.ds(x, 1), :]
-            south = jnp.where(
-                row == 0, jnp.where(up_first, second, first), pltpu.roll(value, 1, 0)
-            )
-            north = jnp.where(
-                row == y_cells - 1,
-                jnp.where(up_first, first, second),
-                pltpu.roll(value, y_cells - 1, 0),
-            )
-            lower = jnp.where(lane == 0, 0.0, pltpu.roll(value, 1, 1))
-            upper = jnp.where(lane == z_cells - 1, 0.0, pltpu.roll(value, z_cells - 1, 1))
-            laplacian = east + west + north + south + upper + lower - 6.0 * value
-            advection = (
-                centre[0] * (east - west) + centre[1] * (north - south) + centre[2] * (upper - lower)
-            )
-            tendency = viscosity[x] * laplacian - 0.5 * advection
-            if f == 2:
-                tendency = tendency + buoyancy * centre[3]
-            new_fields[f, x] = value + time_step * tendency
-        return carry
-
-    lax.fori_loop(0, x_cells, plane, 0, unroll=2)
+    x = pl.program_id(0)
+    centre = [fields[f, x] for f in range(F)]
+    below = jnp.maximum(x - 1, 0)
+    above = jnp.minimum(x + 1, x_cells - 1)
+    for f in range(F):
+        value = centre[f]
+        west = jnp.where(x == 0, x_halo[1, f], fields[f, below])
+        east = jnp.where(x == x_cells - 1, x_halo[0, f], fields[f, above])
+        first, second = y_first[f, pl.ds(x, 1), :], y_second[f, pl.ds(x, 1), :]
+        south = jnp.where(
+            row == 0, jnp.where(up_first, second, first), pltpu.roll(value, 1, 0)
+        )
+        north = jnp.where(
+            row == y_cells - 1,
+            jnp.where(up_first, first, second),
+            pltpu.roll(value, y_cells - 1, 0),
+        )
+        lower = jnp.where(lane == 0, 0.0, pltpu.roll(value, 1, 1))
+        upper = jnp.where(lane == z_cells - 1, 0.0, pltpu.roll(value, z_cells - 1, 1))
+        laplacian = east + west + north + south + upper + lower - 6.0 * value
+        advection = (
+            centre[0] * (east - west) + centre[1] * (north - south) + centre[2] * (upper - lower)
+        )
+        tendency = viscosity[0] * laplacian - 0.5 * advection
+        if f == 2:
+            tendency = tendency + buoyancy * centre[3]
+        new_fields[f, 0] = value + time_step * tendency
 
 
 def evolve(place, viscosity, fields, x_halo, y_first, y_second):
-    vmem = pl.BlockSpec(memory_space=pltpu.VMEM)
+    count, x_cells, y_cells, z_cells = fields.shape
+
+    def whole(shape):
+        return pl.BlockSpec(shape, lambda x: (0,) * len(shape), pipeline_mode=pl.Buffered(1))
+
     return pl.pallas_call(
         evolve_kernel,
         out_shape=jax.ShapeDtypeStruct(fields.shape, fields.dtype),
-        in_specs=[pl.BlockSpec(memory_space=pltpu.SMEM)] + [vmem] * 5,
-        out_specs=vmem,
+        grid=(x_cells,),
+        in_specs=[
+            pl.BlockSpec(memory_space=pltpu.SMEM),
+            pl.BlockSpec((1, y_cells, z_cells), lambda x: (x, 0, 0)),
+            *[whole(array.shape) for array in (fields, x_halo, y_first, y_second)],
+        ],
+        out_specs=pl.BlockSpec((count, 1, y_cells, z_cells), lambda x: (0, x, 0, 0)),
         compiler_params=pltpu.CompilerParams(vmem_limit_bytes=16 * 1024 * 1024),
         name="evolve_brick",
     )(place, viscosity, fields, x_halo, y_first, y_second)

time: 112 us -> 104 us (0.929)
  Pallas kernels: 53.1 us -> 44.2 us
    pallas_call x1, Pallas kernels: 35.7 us -> 25 us  [brick_viscosity(): pl.pallas_call(viscosity_kernel, out_shape=(jax.ShapeDtypeStruct(fields.s...]
    pallas_call x1, Pallas kernels: 8.6 us -> 10.4 us  [evolve(): pl.pallas_call(evolve_kernel, out_shape=jax.ShapeDtypeStruct(fields.shape...]
  transfers between devices with their start and end apart: 18 -> 18, of which waited for: 9 -> 9; matrix products, arithmetic and copies ran while one was open for 1% -> 1% of each run, Pallas kernels for 36% -> 29%
where the time goes in v15:
time: 104 us; the launch traced here: 103 us
  Pallas kernels  44.2 us (42%)
  starting transfers between devices  33.2 us (32%)
  waiting for transfers between devices  20.2 us (19%)
  other arithmetic  2.29 us (2%)
  between operations  1.67 us (2%)
  local copies, waits for them, and re-layouts  1.28 us (1%)
    pallas_call x1, Pallas kernels, brick_viscosity(): pl.pallas_call(viscosity_kernel, out_shape=(jax.ShapeDtypeStruct(fields.s...  25 us
    pallas_call x1, Pallas kernels, evolve(): pl.pallas_call(evolve_kernel, out_shape=jax.ShapeDtypeStruct(fields.shape...  10.4 us
    all_to_all x1, starting transfers between devices, on_device(): lax.all_to_all(thin, ('gx', 'gy'), split_axis=0, concat_axis=0, tiled=True)  7.42 us
    ppermute x2, starting transfers between devices, on_device(): final = final + lax.ppermute(held, everyone, meets)  4.8 us
    ppermute x1, starting transfers between devices, y_neighbours(): lax.ppermute(for_second, everyone, pairs(0, -1))  4.44 us
    ppermute x2, waiting for transfers between devices, on_device(): final = final + lax.ppermute(held, everyone, meets)  4.15 us
    ppermute x2, starting transfers between devices, on_device(): lax.ppermute(final, everyone, [(g * trainers + c, (g ^ apart) * trainers...  3.84 us
    pallas_call x1, Pallas kernels, sample_cube(): pl.pallas_call(functools.partial(sample_kernel, y_cells, z_cells), out_sh...  3.63 us
  transfers between devices with their start and end apart: 18, of which 9 were waited for; matrix products, arithmetic and copies ran while one was open for 1% of the time, Pallas kernels for 29%

profile of v15, /device:TPU:0, one launch (start us, length us, event | category | flops | bytes accessed | tf_op | source)
XLA Modules:
  0.0 103.0 jit_solution(22957743629252793)
XLA Ops:
  0.6 0.1 stack.27.place
  0.7 0.7 copy-done.1
  1.4 2.8 %thin_faces.1 = f32[8,16,256]{2,1,0:T(8,128)} custom-call(s32[24]{0:T(128)S(1)} %copy-done.1, s32[6]{0:T(128)S(1)} %stack.27.place, f32[2560,384]{1,0:T(8,128)} %bitcast.23, f32[80,32,384]{2,1,0:T(8,128)} %bitcast.24), custom_call_target="tpu_custom_call" | custom-call | tf_op jit(solution)/shard_map/thin_faces/pallas_call | solution.py:687
  4.2 0.0 copy-start.6
  4.2 0.0 copy-start
  4.2 7.4 %all-to-all-start = ((f32[8,16,256]{2,1,0:T(8,128)}), f32[8,16,256]{2,1,0:T(8,128)S(1)}, u32[]{:S(2)}, u32[]{:S(2)}) async-start(f32[8,16,256]{2,1,0:T(8,128)} %thin_faces.1), calls=%async_computation | async-start | bytes 262144 | tf_op jit(solution)/shard_map/all_to_all | solution.py:964
  11.7 0.1 fusion.1
  11.8 3.6 %sample_cube.1 = (f32[80,256]{1,0:T(8,128)S(1)}, f32[80,256]{1,0:T(8,128)S(1)}, f32[80,256]{1,0:T(8,128)S(1)}, f32[2,16,128]{2,1,0:T(8,128)S(1)}) custom-call(s32[24]{0:T(128)S(1)} %copy-done.2, s32[6]{0:T(128)S(1)} %stack.27.place, f32[2560,384]{1,0:T(8,128)} %bitcast.25), custom_call_target="tpu_custom_call" | custom-call | bytes 16000000 | tf_op jit(solution)/shard_map/sample_cube/pallas_call | solution.py:790
  15.4 0.0 copy-start.8
  15.4 0.1 fusion
  15.6 0.1 copy.15
  15.6 0.1 reshape.34
  15.7 0.2 slice.37
  16.0 0.1 select_maximum_fusion.closure
  16.0 3.1 %all-to-all-done.thin = f32[8,16,256]{2,1,0:T(8,128)S(1)} async-done(((f32[8,16,256]{2,1,0:T(8,128)}), f32[8,16,256]{2,1,0:T(8,128)S(1)}, u32[]{:S(2)}, u32[]{:S(2)}) %all-to-all-start) | async-done | bytes 131104 | tf_op jit(solution)/shard_map/all_to_all | solution.py:964
  19.2 1.6 %cube_change.1 = bf16[320,128]{1,0:T(8,128)(2,1)S(1)} custom-call(s32[24]{0:T(128)S(1)} %copy-done.2, s32[6]{0:T(128)S(1)} %stack.27.place, f32[8,128]{1,0:T(8,128)S(1)} %select_maximum_fusion.closure, bf16[256,256]{1,0:T(8,128)(2,1)S(1)} %copy-done, f32[80,256]{1,0:T(8,128)S(1)} %get-tuple-element.93.centre, f32[80,256]{1,0:T(8,128)S(1)} %get-tuple-element.94.lower, ...), custom_call_target="tpu_custom_call" | custom-call | tf_op jit(solution)/shard_map/cube_change/pallas_call | solution.py:871
  20.8 1.5 %collective-permute-start.2 = (bf16[320,128]{1,0:T(8,128)(2,1)S(1)}, bf16[320,128]{1,0:T(8,128)(2,1)S(1)}, u32[]{:S(2)}, u32[]{:S(2)}) collective-permute-start(bf16[320,128]{1,0:T(8,128)(2,1)S(1)} %cube_change.1), channel_id=1, source_target_pairs={{0,24},{1,25},{2,26},{3,27},{4,28},{5,29},{6,30},{7,31}} | collective-permute-start | bytes 245768 | tf_op jit(solution)/shard_map/ppermute | solution.py:940
  22.2 0.7 collective-permute-start.1
  22.9 0.7 collective-permute-start
  23.6 0.8 collective-permute-done.2
  24.4 0.8 collective-permute-start.8
  25.2 0.7 collective-permute-start.7
  25.9 0.7 collective-permute-start.6
  26.6 25.0 %conditional.2 = ((f32[16,32,384]{2,1,0:T(8,128)S(1)}, f32[2,5,32,384]{3,2,1,0:T(8,128)}, f32[2,5,16,384]{3,2,1,0:T(8,128)S(1)})) conditional(s32[]{:T(128)} %convert_element_type.10, (f32[8,128]{1,0:T(8,128)S(1)}, s32[6]{0:T(128)S(1)}, f32[5,16,32,384]{3,2,1,0:T(8,128)}) %tuple.46, () %tuple.31), branch_computations={%region_1.2_spmd, %region_2.3_spmd} | conditional | bytes 1523756 | solution.py:970
  26.6 25.0 %brick_viscosity.1 = (f32[16,32,384]{2,1,0:T(8,128)S(1)}, f32[2,5,32,384]{3,2,1,0:T(8,128)}, f32[2,5,16,384]{3,2,1,0:T(8,128)S(1)}) custom-call(f32[8,128]{1,0:T(8,128)S(1)} %get-tuple-element.43.closure, s32[6]{0:T(128)S(1)} %get-tuple-element.44.place, f32[5,16,32,384]{3,2,1,0:T(8,128)} %get-tuple-element.45.fields), custom_call_target="tpu_custom_call" | custom-call | tf_op jit(solution)/shard_map/cond/branch_0_fun/brick_viscosity/pallas_call | solution.py:520
  51.6 2.5 %collective-permute-start.3 = (f32[2,5,32,384]{3,2,1,0:T(8,128)}, f32[2,5,32,384]{3,2,1,0:T(8,128)S(1)}, u32[]{:S(2)}, u32[]{:S(2)}) collective-permute-start(f32[2,5,32,384]{3,2,1,0:T(8,128)} %get-tuple-element.99), channel_id=1, source_target_pairs={{0,4},{1,5},{2,6},{3,7},{4,0},{5,1},{6,2},{7,3},{8,12},{9,13},{10,... | collective-permute-start | bytes 1474568 | tf_op jit(solution)/shard_map/ppermute | solution.py:925
  54.1 0.7 pick_cubes.1
  54.9 0.7 collective-permute-start.9
  55.6 4.4 %collective-permute-start.5 = (f32[5,16,384]{2,1,0:T(8,128)S(1)}, f32[5,16,384]{2,1,0:T(8,128)S(1)}, u32[]{:S(2)}, u32[]{:S(2)}) collective-permute-start(f32[5,16,384]{2,1,0:T(8,128)S(1)} %get-tuple-element.112), channel_id=1, source_target_pairs={{0,3},{1,2},{2,1},{3,0},{4,7},{5,6},{6,5},{7,4},{8,11},{9,10},{10,... | collective-permute-start | bytes 368648 | tf_op jit(solution)/shard_map/ppermute | solution.py:932
  60.0 1.9 %collective-permute-start.4 = (f32[5,16,384]{2,1,0:T(8,128)S(1)}, f32[5,16,384]{2,1,0:T(8,128)S(1)}, u32[]{:S(2)}, u32[]{:S(2)}) collective-permute-start(f32[5,16,384]{2,1,0:T(8,128)S(1)} %get-tuple-element.113), channel_id=1, source_target_pairs={{0,1},{1,0},{2,3},{3,2},{4,5},{5,4},{6,7},{7,6},{8,9},{9,8},{10,11... | collective-permute-start | bytes 368648 | tf_op jit(solution)/shard_map/ppermute | solution.py:931
  62.0 3.5 %collective-permute-done.5 = f32[5,16,384]{2,1,0:T(8,128)S(1)} collective-permute-done((f32[5,16,384]{2,1,0:T(8,128)S(1)}, f32[5,16,384]{2,1,0:T(8,128)S(1)}, u32[]{:S(2)}, u32[]{:S(2)}) %collective-permute-start.5) | collective-permute-done | bytes 122912 | tf_op jit(solution)/shard_map/ppermute | solution.py:932
  65.4 2.3 %collective-permute-done.4 = f32[5,16,384]{2,1,0:T(8,128)S(1)} collective-permute-done((f32[5,16,384]{2,1,0:T(8,128)S(1)}, f32[5,16,384]{2,1,0:T(8,128)S(1)}, u32[]{:S(2)}, u32[]{:S(2)}) %collective-permute-start.4) | collective-permute-done | bytes 122912 | tf_op jit(solution)/shard_map/ppermute | solution.py:931
  67.8 10.6 %conditional.3 = (f32[17280]{0:T(1024)S(1)}, f32[1,5,16,32,384]{4,3,2,1,0:T(8,128)}) conditional(s32[]{:T(128)} %convert_element_type.10, (s32[6]{0:T(128)S(1)}, f32[16,32,384]{2,1,0:T(8,128)S(1)}, f32[5,16,32,384]{3,2,1,0:T(8,128)}, f32[2,5,32,384]{3,2,1,0:T(8,128)S(1)}, f32[5,16,384]{2,1,0:T(8,128)S(1)}, ...), branch_computations={%region_3.4_spmd, %region_4.5_spmd} | conditional | flops 17280 | bytes 345616 | solution.py:1000
  67.8 10.4 %evolve_brick.1 = f32[5,16,32,384]{3,2,1,0:T(8,128)} custom-call(s32[6]{0:T(128)S(1)} %get-tuple-element.46.place, f32[16,32,384]{2,1,0:T(8,128)S(1)} %get-tuple-element.47.viscosity, f32[5,16,32,384]{3,2,1,0:T(8,128)} %get-tuple-element.48.fields, f32[2,5,32,384]{3,2,1,0:T(8,128)S(1)} %get-tuple-element.49.x_halo, ...), custom_call_target="tpu_custom_call" | custom-call | tf_op jit(solution)/shard_map/cond/branch_0_fun/evolve_brick/pallas_call | solution.py:588
  78.4 1.3 %collective-permute-start.12 = (f32[17280]{0:T(1024)S(1)}, f32[17280]{0:T(1024)S(1)}, u32[]{:S(2)}, u32[]{:S(2)}) collective-permute-start(f32[17280]{0:T(1024)S(1)} %get-tuple-element.107), channel_id=1, source_target_pairs={{24,0},{25,1},{26,2},{27,3},{28,4},{29,5},{30,6},{31,7}} | collective-permute-start | bytes 207368 | tf_op jit(solution)/shard_map/ppermute | solution.py:1004
  79.7 0.7 collective-permute-start.11
  80.3 0.7 collective-permute-start.10
  81.0 3.0 %collective-permute-done.12 = f32[17280]{0:T(1024)S(1)} collective-permute-done((f32[17280]{0:T(1024)S(1)}, f32[17280]{0:T(1024)S(1)}, u32[]{:S(2)}, u32[]{:S(2)}) %collective-permute-start.12) | collective-permute-done | bytes 69152 | tf_op jit(solution)/shard_map/ppermute | solution.py:1004
  84.0 2.5 %collective-permute-start.14 = (f32[17280]{0:T(1024)S(1)}, f32[17280]{0:T(1024)S(1)}, u32[]{:S(2)}, u32[]{:S(2)}) collective-permute-start(f32[17280]{0:T(1024)S(1)} %add_add_fusion.1), channel_id=1, source_target_pairs={{0,5},{1,4},{2,7},{3,6},{4,1},{5,0},{6,3},{7,2},{8,14},{9,15},{10,... | collective-permute-start | bytes 207368 | tf_op jit(solution)/shard_map/ppermute | solution.py:1015
  86.6 2.3 %collective-permute-start.13 = (f32[17280]{0:T(1024)S(1)}, f32[17280]{0:T(1024)S(1)}, u32[]{:S(2)}, u32[]{:S(2)}) collective-permute-start(f32[17280]{0:T(1024)S(1)} %add_add_fusion.1), channel_id=1, source_target_pairs={{0,1},{1,0},{2,3},{3,2},{4,5},{5,4},{6,7},{7,6},{8,10},{9,11},{10,... | collective-permute-start | bytes 207368 | tf_op jit(solution)/shard_map/ppermute | solution.py:1015
  88.8 2.3 %collective-permute-done.14 = f32[17280]{0:T(1024)S(1)} collective-permute-done((f32[17280]{0:T(1024)S(1)}, f32[17280]{0:T(1024)S(1)}, u32[]{:S(2)}, u32[]{:S(2)}) %collective-permute-start.14) | collective-permute-done | bytes 69152 | tf_op jit(solution)/shard_map/ppermute | solution.py:1015
  91.1 1.9 %collective-permute-done.13 = f32[17280]{0:T(1024)S(1)} collective-permute-done((f32[17280]{0:T(1024)S(1)}, f32[17280]{0:T(1024)S(1)}, u32[]{:S(2)}, u32[]{:S(2)}) %collective-permute-start.13) | collective-permute-done | bytes 69152 | tf_op jit(solution)/shard_map/ppermute | solution.py:1015
  93.0 0.8 collective-permute-start.15
  93.8 0.9 collective-permute-done.15
  94.8 3.0 %collective-permute-start.16 = (f32[17280]{0:T(1024)S(1)}, f32[17280]{0:T(1024)S(1)}, u32[]{:S(2)}, u32[]{:S(2)}) collective-permute-start(f32[17280]{0:T(1024)S(1)} %add.52), channel_id=1, source_target_pairs={{0,16},{1,17},{2,18},{3,19},{4,20},{5,21},{6,22},{7,23},{8,24},{9,... | collective-permute-start | bytes 207368 | tf_op jit(solution)/shard_map/ppermute | solution.py:1017
  97.8 2.5 %collective-permute-done.16 = f32[17280]{0:T(1024)S(1)} collective-permute-done((f32[17280]{0:T(1024)S(1)}, f32[17280]{0:T(1024)S(1)}, u32[]{:S(2)}, u32[]{:S(2)}) %collective-permute-start.16) | collective-permute-done | bytes 69152 | tf_op jit(solution)/shard_map/ppermute | solution.py:1017
  100.3 0.6 multiply_reduce_fusion
  101.6 1.4 %multiply_subtract_fusion = (f32[540]{0:T(1024)}, f32[540]{0:T(1024)}) fusion(f32[17280]{0:T(1024)S(1)} %copy-done.5, s32[]{:T(128)S(6)} %select_n.2, f32[]{:T(128)S(6)} %sqrt.3, f32[17280]{0:T(1024)S(1)} %get-tuple-element.111, f32[17280]{0:T(1024)} %param.20), kind=kLoop, calls=%fused_computation.14 | loop fusion | flops 2700 | bytes 10808 | tf_op jit(solution)/shard_map/sub | solution.py:1030
  (35 shorter events, 0.2 us)
Async XLA Ops:
  0.7 0.7 copy-start.1
  1.4 10.3 %copy-start.7 = (f32[64,5]{0,1:T(8,128)S(1)}, f32[64,5]{0,1:T(8,128)}, u32[]{:S(2)}) copy-start(f32[64,5]{0,1:T(8,128)} %param.16) | copy-start | bytes 3844
  1.4 10.3 %copy-start.5 = (f32[17280]{0:T(1024)S(1)}, f32[17280]{0:T(1024)}, u32[]{:S(2)}) copy-start(f32[17280]{0:T(1024)} %param.19) | copy-start | bytes 207364
  1.4 10.4 %copy-start.9 = (f32[64]{0:T(128)S(1)}, f32[64]{0:T(128)}, u32[]{:S(2)}) copy-start(f32[64]{0:T(128)} %param.17) | copy-start | bytes 772
  1.4 10.4 %copy-start.2 = (s32[24]{0:T(128)S(1)}, s32[24]{0:T(128)}, u32[]{:S(2)}) copy-start(s32[24]{0:T(128)} %sample_block.5) | copy-start | bytes 292
  4.2 11.2 %copy-start.6 = (f32[64]{0:T(128)S(1)}, f32[64]{0:T(128)}, u32[]{:S(2)}) copy-start(f32[64]{0:T(128)} %param.18) | copy-start | bytes 772
  4.2 15.0 %copy-start = (bf16[256,256]{1,0:T(8,128)(2,1)S(1)}, bf16[256,256]{1,0:T(8,128)(2,1)}, u32[]{:S(2)}) copy-start(bf16[256,256]{1,0:T(8,128)(2,1)} %constant.60.clone.order) | copy-start | bytes 393220
  4.2 14.9 %all-to-all-start = ((f32[8,16,256]{2,1,0:T(8,128)}), f32[8,16,256]{2,1,0:T(8,128)S(1)}, u32[]{:S(2)}, u32[]{:S(2)}) async-start(f32[8,16,256]{2,1,0:T(8,128)} %thin_faces.1), calls=%async_computation | async-start | bytes 262144 | tf_op jit(solution)/shard_map/all_to_all | solution.py:964
  15.4 38.7 %copy-start.8 = (s32[24]{0:T(128)S(1)}, s32[24]{0:T(128)}, u32[]{:S(2)}) copy-start(s32[24]{0:T(128)} %trainer_of.1) | copy-start | bytes 292
  20.8 3.6 %collective-permute-start.2 = (bf16[320,128]{1,0:T(8,128)(2,1)S(1)}, bf16[320,128]{1,0:T(8,128)(2,1)S(1)}, u32[]{:S(2)}, u32[]{:S(2)}) collective-permute-start(bf16[320,128]{1,0:T(8,128)(2,1)S(1)} %cube_change.1), channel_id=1, source_target_pairs={{0,24},{1,25},{2,26},{3,27},{4,28},{5,29},{6,30},{7,31}} | collective-permute-start | bytes 245768 | tf_op jit(solution)/shard_map/ppermute | solution.py:940
  22.2 2.1 %collective-permute-start.1 = (bf16[320,128]{1,0:T(8,128)(2,1)S(1)}, bf16[320,128]{1,0:T(8,128)(2,1)S(1)}, u32[]{:S(2)}, u32[]{:S(2)}) collective-permute-start(bf16[320,128]{1,0:T(8,128)(2,1)S(1)} %cube_change.1), channel_id=1, source_target_pairs={{8,24},{9,25},{10,26},{11,27},{12,28},{13,29},{14,30},{15,31}} | collective-permute-start | bytes 245768 | tf_op jit(solution)/shard_map/ppermute | solution.py:940
  22.9 1.5 %collective-permute-start = (bf16[320,128]{1,0:T(8,128)(2,1)S(1)}, bf16[320,128]{1,0:T(8,128)(2,1)S(1)}, u32[]{:S(2)}, u32[]{:S(2)}) collective-permute-start(bf16[320,128]{1,0:T(8,128)(2,1)S(1)} %cube_change.1), channel_id=1, source_target_pairs={{16,24},{17,25},{18,26},{19,27},{20,28},{21,29},{22,30},{23,31}} | collective-permute-start | bytes 245768 | tf_op jit(solution)/shard_map/ppermute | solution.py:940
  24.4 43.4 %copy-start.3 = (bf16[4,256,240]{2,1,0:T(8,128)(2,1)S(1)}, bf16[4,256,240]{2,1,0:T(8,128)(2,1)}, u32[]{:S(2)}) copy-start(bf16[4,256,240]{2,1,0:T(8,128)(2,1)} %constant.59.clone) | copy-start | bytes 1474564
  24.4 43.4 %copy-start.4 = (bf16[4,256,240]{2,1,0:T(8,128)(2,1)S(1)}, bf16[4,256,240]{2,1,0:T(8,128)(2,1)}, u32[]{:S(2)}) copy-start(bf16[4,256,240]{2,1,0:T(8,128)(2,1)} %constant.58.clone) | copy-start | bytes 1474564
  24.4 29.7 %collective-permute-start.8 = (bf16[3,320,128]{2,1,0:T(8,128)(2,1)S(1)}, bf16[3,320,128]{2,1,0:T(8,128)(2,1)S(1)}, u32[]{:S(2)}, u32[]{:S(2)}) collective-permute-start(bf16[3,320,128]{2,1,0:T(8,128)(2,1)S(1)} %pad_maximum_fusion.1.refs_0_), channel_id=1, source_target_pairs={{24,27},{25,26},{26,25},{27,24},{28,31},{29,30},{30,29},{31,28}} | collective-permute-start | bytes 737288 | tf_op jit(solution)/shard_map/ppermute | solution.py:948
  25.2 28.9 %collective-permute-start.7 = (bf16[3,320,128]{2,1,0:T(8,128)(2,1)S(1)}, bf16[3,320,128]{2,1,0:T(8,128)(2,1)S(1)}, u32[]{:S(2)}, u32[]{:S(2)}) collective-permute-start(bf16[3,320,128]{2,1,0:T(8,128)(2,1)S(1)} %pad_maximum_fusion.1.refs_0_), channel_id=1, source_target_pairs={{24,26},{25,27},{26,24},{27,25},{28,30},{29,31},{30,28},{31,29}} | collective-permute-start | bytes 737288 | tf_op jit(solution)/shard_map/ppermute | solution.py:948
  25.9 28.2 %collective-permute-start.6 = (bf16[3,320,128]{2,1,0:T(8,128)(2,1)S(1)}, bf16[3,320,128]{2,1,0:T(8,128)(2,1)S(1)}, u32[]{:S(2)}, u32[]{:S(2)}) collective-permute-start(bf16[3,320,128]{2,1,0:T(8,128)(2,1)S(1)} %pad_maximum_fusion.1.refs_0_), channel_id=1, source_target_pairs={{24,25},{25,24},{26,27},{27,26},{28,29},{29,28},{30,31},{31,30}} | collective-permute-start | bytes 737288 | tf_op jit(solution)/shard_map/ppermute | solution.py:948
  51.6 16.2 %collective-permute-start.3 = (f32[2,5,32,384]{3,2,1,0:T(8,128)}, f32[2,5,32,384]{3,2,1,0:T(8,128)S(1)}, u32[]{:S(2)}, u32[]{:S(2)}) collective-permute-start(f32[2,5,32,384]{3,2,1,0:T(8,128)} %get-tuple-element.99), channel_id=1, source_target_pairs={{0,4},{1,5},{2,6},{3,7},{4,0},{5,1},{6,2},{7,3},{8,12},{9,13},{10,... | collective-permute-start | bytes 1474568 | tf_op jit(solution)/shard_map/ppermute | solution.py:925
  54.9 12.9 %collective-permute-start.9 = (bf16[6,320,128]{2,1,0:T(8,128)(2,1)S(1)}, bf16[6,320,128]{2,1,0:T(8,128)(2,1)S(1)}, u32[]{:S(2)}, u32[]{:S(2)}) collective-permute-start(bf16[6,320,128]{2,1,0:T(8,128)(2,1)S(1)} %pick_cubes.1), channel_id=1, source_target_pairs={{24,28},{25,29},{26,30},{27,31},{28,24},{29,25},{30,26},{31,27}} | collective-permute-start | bytes 1474568 | tf_op jit(solution)/shard_map/ppermute | solution.py:951
  55.6 9.9 %collective-permute-start.5 = (f32[5,16,384]{2,1,0:T(8,128)S(1)}, f32[5,16,384]{2,1,0:T(8,128)S(1)}, u32[]{:S(2)}, u32[]{:S(2)}) collective-permute-start(f32[5,16,384]{2,1,0:T(8,128)S(1)} %get-tuple-element.112), channel_id=1, source_target_pairs={{0,3},{1,2},{2,1},{3,0},{4,7},{5,6},{6,5},{7,4},{8,11},{9,10},{10,... | collective-permute-start | bytes 368648 | tf_op jit(solution)/shard_map/ppermute | solution.py:932
  60.0 7.7 %collective-permute-start.4 = (f32[5,16,384]{2,1,0:T(8,128)S(1)}, f32[5,16,384]{2,1,0:T(8,128)S(1)}, u32[]{:S(2)}, u32[]{:S(2)}) collective-permute-start(f32[5,16,384]{2,1,0:T(8,128)S(1)} %get-tuple-element.113), channel_id=1, source_target_pairs={{0,1},{1,0},{2,3},{3,2},{4,5},{5,4},{6,7},{7,6},{8,9},{9,8},{10,11... | collective-permute-start | bytes 368648 | tf_op jit(solution)/shard_map/ppermute | solution.py:931
  78.4 5.6 %collective-permute-start.12 = (f32[17280]{0:T(1024)S(1)}, f32[17280]{0:T(1024)S(1)}, u32[]{:S(2)}, u32[]{:S(2)}) collective-permute-start(f32[17280]{0:T(1024)S(1)} %get-tuple-element.107), channel_id=1, source_target_pairs={{24,0},{25,1},{26,2},{27,3},{28,4},{29,5},{30,6},{31,7}} | collective-permute-start | bytes 207368 | tf_op jit(solution)/shard_map/ppermute | solution.py:1004
  79.7 4.3 %collective-permute-start.11 = (f32[17280]{0:T(1024)S(1)}, f32[17280]{0:T(1024)S(1)}, u32[]{:S(2)}, u32[]{:S(2)}) collective-permute-start(f32[17280]{0:T(1024)S(1)} %get-tuple-element.107), channel_id=1, source_target_pairs={{24,8},{25,9},{26,10},{27,11},{28,12},{29,13},{30,14},{31,15}} | collective-permute-start | bytes 207368 | tf_op jit(solution)/shard_map/ppermute | solution.py:1004
  80.3 3.7 %collective-permute-start.10 = (f32[17280]{0:T(1024)S(1)}, f32[17280]{0:T(1024)S(1)}, u32[]{:S(2)}, u32[]{:S(2)}) collective-permute-start(f32[17280]{0:T(1024)S(1)} %get-tuple-element.107), channel_id=1, source_target_pairs={{24,16},{25,17},{26,18},{27,19},{28,20},{29,21},{30,22},{31,23}} | collective-permute-start | bytes 207368 | tf_op jit(solution)/shard_map/ppermute | solution.py:1004
  84.0 7.1 %collective-permute-start.14 = (f32[17280]{0:T(1024)S(1)}, f32[17280]{0:T(1024)S(1)}, u32[]{:S(2)}, u32[]{:S(2)}) collective-permute-start(f32[17280]{0:T(1024)S(1)} %add_add_fusion.1), channel_id=1, source_target_pairs={{0,5},{1,4},{2,7},{3,6},{4,1},{5,0},{6,3},{7,2},{8,14},{9,15},{10,... | collective-permute-start | bytes 207368 | tf_op jit(solution)/shard_map/ppermute | solution.py:1015
  86.6 6.4 %collective-permute-start.13 = (f32[17280]{0:T(1024)S(1)}, f32[17280]{0:T(1024)S(1)}, u32[]{:S(2)}, u32[]{:S(2)}) collective-permute-start(f32[17280]{0:T(1024)S(1)} %add_add_fusion.1), channel_id=1, source_target_pairs={{0,1},{1,0},{2,3},{3,2},{4,5},{5,4},{6,7},{7,6},{8,10},{9,11},{10,... | collective-permute-start | bytes 207368 | tf_op jit(solution)/shard_map/ppermute | solution.py:1015
  93.0 1.8 %collective-permute-start.15 = (f32[17280]{0:T(1024)S(1)}, f32[17280]{0:T(1024)S(1)}, u32[]{:S(2)}, u32[]{:S(2)}) collective-permute-start(f32[17280]{0:T(1024)S(1)} %add_add_fusion), channel_id=1, source_target_pairs={{0,8},{1,9},{2,10},{3,11},{4,12},{5,13},{6,14},{7,15},{8,0},{9,1},... | collective-permute-start | bytes 207368 | tf_op jit(solution)/shard_map/ppermute | solution.py:1017
  94.8 5.5 %collective-permute-start.16 = (f32[17280]{0:T(1024)S(1)}, f32[17280]{0:T(1024)S(1)}, u32[]{:S(2)}, u32[]{:S(2)}) collective-permute-start(f32[17280]{0:T(1024)S(1)} %add.52), channel_id=1, source_target_pairs={{0,16},{1,17},{2,18},{3,19},{4,20},{5,21},{6,22},{7,23},{8,24},{9,... | collective-permute-start | bytes 207368 | tf_op jit(solution)/shard_map/ppermute | solution.py:1017

commit v16 on v15

--- a/solution.py
+++ b/solution.py
@@ -40,24 +40,29 @@
 
 
 def selections():
-    first = np.zeros((4, 256, STACK), np.float32)
-    last = np.zeros((4, 256, STACK), np.float32)
+    found = np.zeros((4, 256, STACK), np.float32)
     for cell in range(4):
         py, pz = cell // 2, cell % 2
         for kx in range(3):
             for channel in range(F):
                 for row in range(16):
                     ypos, zpos = patch_position(row)
-                    column = kx * PATCH + channel * 16 + row
                     dy, dz = ypos - py, zpos - pz
                     if abs(dy) <= 1 and abs(dz) <= 1:
                         tap = 9 * kx + 3 * (dy + 1) + dz + 1
-                        first[cell, tap * F + channel, column] = 1.0
-                        last[cell, channel * TAPS + 26 - tap, column] = 1.0
-    return first, last
-
-
-SELECT_FIRST, SELECT_LAST = selections()
+                        found[cell, tap * F + channel, kx * PATCH + channel * 16 + row] = 1.0
+    return found
+
+
+def last_order():
+    order = np.zeros((256, 256), np.float32)
+    for channel in range(F):
+        for tap in range(TAPS):
+            order[channel * TAPS + tap, (TAPS - 1 - tap) * F + channel] = 1.0
+    return order
+
+
+SELECT, LAST_ORDER = selections(), last_order()
 
 
 def column_of(place, x_step, y_step):
@@ -121,6 +126,14 @@
 
 def dot_lanes(left, right):
     return lax.dot_general(left, right, (((1,), (1,)), ((), ())), preferred_element_type=jnp.float32)
+
+
+def exact_parts(values):
+    parts = []
+    for _ in range(3):
+        parts.append(values.astype(jnp.bfloat16))
+        values = values - parts[-1].astype(jnp.float32)
+    return jnp.concatenate(parts, axis=0)
 
 
 def patch_masks():
@@ -166,7 +179,7 @@
 
 def train_kernel(y_devices, x_devices, *refs):
     sources = y_devices + x_devices - 1
-    (trainer_of, place, first_ref, last_ref, far_first, far_last) = refs[:6]
+    (trainer_of, place, first_ref, last_ref, far_select, far_order) = refs[:6]
     arrived = refs[6 : 6 + sources]
     fields_ref = refs[6 + sources]
     delta_first, delta_last, new_fields_ref = refs[7 + sources : 10 + sources]
@@ -179,11 +192,10 @@
         big_last_t,
         grad_first,
         grad_last,
-        now_first,
-        now_last,
+        now,
         brick,
-        select_first,
-        select_last,
+        select,
+        order,
         slot_sems,
         field_sem,
         select_sems,
@@ -196,8 +208,8 @@
     field_in = pltpu.make_async_copy(fields_ref, brick, field_sem)
     field_out = pltpu.make_async_copy(brick, new_fields_ref, field_sem)
     select_copies = [
-        pltpu.make_async_copy(far_first, select_first, select_sems.at[0]),
-        pltpu.make_async_copy(far_last, select_last, select_sems.at[1]),
+        pltpu.make_async_copy(far_select, select, select_sems.at[0]),
+        pltpu.make_async_copy(far_order, order, select_sems.at[1]),
     ]
 
     column = place[1] * y_devices + place[2]
@@ -252,11 +264,6 @@
     weights = [
         jnp.where(lane // 64 + 2 * pair < count, full_weight, 0.0) for pair in range(PAIRS)
     ]
-    start_first = first_ref[...].astype(jnp.bfloat16).astype(jnp.float32)
-    start_last = last_ref[...].T.astype(jnp.bfloat16).astype(jnp.float32)
-    now_first[...] = start_first
-    now_last[...] = start_last
-
     for slot in range(TCAP):
         fetch(slot, True)
 
@@ -288,18 +295,21 @@
 
     for copy in select_copies:
         copy.wait()
+    start_first = first_ref[...].astype(jnp.bfloat16).astype(jnp.float32)
+    start_last = dot_rows(last_ref[...].T.astype(jnp.bfloat16), order[...])
+    now[:CH] = start_first
+    now[CH:] = start_last
     field_in.wait()
     field_out.start()
 
     def train_step(step, step_carry):
-        first_now = now_first[...].astype(jnp.bfloat16)
-        last_now = now_last[...].astype(jnp.bfloat16)
+        rounded = now[...].astype(jnp.bfloat16)
         for cell in range(4):
             rows = slice(cell * CH, (cell + 1) * CH)
-            big_first[rows, :] = (0.5 * dot_rows(first_now, select_first[cell])).astype(jnp.bfloat16)
-            spread_last = dot_rows(last_now, select_last[cell])
-            big_last[rows, :] = (0.5 * spread_last).astype(jnp.bfloat16)
-            big_last_t[:, rows] = spread_last.T.astype(jnp.bfloat16)
+            spread = dot_rows(rounded, select[cell])
+            big_first[rows, :] = (0.5 * spread[:CH]).astype(jnp.bfloat16)
+            big_last[rows, :] = (0.5 * spread[CH:]).astype(jnp.bfloat16)
+            big_last_t[:, rows] = spread[CH:].T.astype(jnp.bfloat16)
         grad_first[...] = jnp.zeros(grad_first.shape, jnp.float32)
         grad_last[...] = jnp.zeros(grad_last.shape, jnp.float32)
 
@@ -371,24 +381,19 @@
 
             lax.fori_loop(0, 4, run, 0, unroll=4)
 
-        def folded(grad, select_ref):
-            total = jnp.zeros((3 * CH, 256), jnp.float32)
-            for cell in range(4):
-                rest = grad[cell * CH : (cell + 1) * CH, :]
-                parts = []
-                for _ in range(3):
-                    parts.append(rest.astype(jnp.bfloat16))
-                    rest = rest - parts[-1].astype(jnp.float32)
-                total = total + dot_lanes(jnp.concatenate(parts, axis=0), select_ref[cell])
-            return total[:CH] + total[CH : 2 * CH] + total[2 * CH :]
-
-        now_first[...] = now_first[...] - inner_rate * folded(grad_first, select_first)
-        now_last[...] = now_last[...] - inner_rate * folded(grad_last, select_last)
+        total = jnp.zeros((6 * CH, 256), jnp.float32)
+        for cell in range(4):
+            rows = slice(cell * CH, (cell + 1) * CH)
+            parts = exact_parts(jnp.concatenate([grad_first[rows, :], grad_last[rows, :]], axis=0))
+            total = total + dot_lanes(parts, select[cell])
+        both = 2 * CH
+        now[...] = now[...] - inner_rate * (total[:both] + total[both : 2 * both] + total[2 * both :])
         return step_carry
 
     lax.fori_loop(0, INNER, train_step, 0)
-    delta_first[...] = start_first - now_first[...]
-    delta_last[...] = (start_last - now_last[...]).T
+    delta_first[...] = start_first - now[:CH]
+    ordered = dot_lanes(exact_parts(start_last - now[CH:]), order[...])
+    delta_last[...] = (ordered[:CH] + ordered[CH : 2 * CH] + ordered[2 * CH :]).T
     field_out.wait()
 
 
@@ -415,11 +420,10 @@
             pltpu.VMEM((STACK, 4 * CH), jnp.bfloat16),
             pltpu.VMEM((4 * CH, STACK), jnp.float32),
             pltpu.VMEM((4 * CH, STACK), jnp.float32),
-            pltpu.VMEM((CH, 256), jnp.float32),
-            pltpu.VMEM((CH, 256), jnp.float32),
+            pltpu.VMEM((2 * CH, 256), jnp.float32),
             pltpu.VMEM(fields.shape, fields.dtype),
             pltpu.VMEM((4, 256, STACK), jnp.bfloat16),
-            pltpu.VMEM((4, 256, STACK), jnp.bfloat16),
+            pltpu.VMEM((256, 256), jnp.bfloat16),
             pltpu.SemaphoreType.DMA((TCAP,)),
             pltpu.SemaphoreType.DMA,
             pltpu.SemaphoreType.DMA((2,)),
@@ -550,51 +554,45 @@
     row = lax.broadcasted_iota(jnp.int32, (y_cells, z_cells), 0)
     lane = lax.broadcasted_iota(jnp.int32, (y_cells, z_cells), 1)
 
-    x = pl.program_id(0)
-    centre = [fields[f, x] for f in range(F)]
-    below = jnp.maximum(x - 1, 0)
-    above = jnp.minimum(x + 1, x_cells - 1)
-    for f in range(F):
-        value = centre[f]
-        west = jnp.where(x == 0, x_halo[1, f], fields[f, below])
-        east = jnp.where(x == x_cells - 1, x_halo[0, f], fields[f, above])
-        first, second = y_first[f, pl.ds(x, 1), :], y_second[f, pl.ds(x, 1), :]
-        south = jnp.where(
-            row == 0, jnp.where(up_first, second, first), pltpu.roll(value, 1, 0)
-        )
-        north = jnp.where(
-            row == y_cells - 1,
-            jnp.where(up_first, first, second),
-            pltpu.roll(value, y_cells - 1, 0),
-        )
-        lower = jnp.where(lane == 0, 0.0, pltpu.roll(value, 1, 1))
-        upper = jnp.where(lane == z_cells - 1, 0.0, pltpu.roll(value, z_cells - 1, 1))
-        laplacian = east + west + north + south + upper + lower - 6.0 * value
-        advection = (
-            centre[0] * (east - west) + centre[1] * (north - south) + centre[2] * (upper - lower)
-        )
-        tendency = viscosity[0] * laplacian - 0.5 * advection
-        if f == 2:
-            tendency = tendency + buoyancy * centre[3]
-        new_fields[f, 0] = value + time_step * tendency
+    def plane(x, carry):
+        centre = [fields[f, x] for f in range(F)]
+        below = jnp.maximum(x - 1, 0)
+        above = jnp.minimum(x + 1, x_cells - 1)
+        for f in range(F):
+            value = centre[f]
+            west = jnp.where(x == 0, x_halo[1, f], fields[f, below])
+            east = jnp.where(x == x_cells - 1, x_halo[0, f], fields[f, above])
+            first, second = y_first[f, pl.ds(x, 1), :], y_second[f, pl.ds(x, 1), :]
+            south = jnp.where(
+                row == 0, jnp.where(up_first, second, first), pltpu.roll(value, 1, 0)
+            )
+            north = jnp.where(
+                row == y_cells - 1,
+                jnp.where(up_first, first, second),
+                pltpu.roll(value, y_cells - 1, 0),
+            )
+            lower = jnp.where(lane == 0, 0.0, pltpu.roll(value, 1, 1))
+            upper = jnp.where(lane == z_cells - 1, 0.0, pltpu.roll(value, z_cells - 1, 1))
+            laplacian = east + west + north + south + upper + lower - 6.0 * value
+            advection = (
+                centre[0] * (east - west) + centre[1] * (north - south) + centre[2] * (upper - lower)
+            )
+            tendency = viscosity[x] * laplacian - 0.5 * advection
+            if f == 2:
+                tendency = tendency + buoyancy * centre[3]
+            new_fields[f, x] = value + time_step * tendency
+        return carry
+
+    lax.fori_loop(0, x_cells, plane, 0)
 
 
 def evolve(place, viscosity, fields, x_halo, y_first, y_second):
-    count, x_cells, y_cells, z_cells = fields.shape
-
-    def whole(shape):
-        return pl.BlockSpec(shape, lambda x: (0,) * len(shape), pipeline_mode=pl.Buffered(1))
-
+    vmem = pl.BlockSpec(memory_space=pltpu.VMEM)
     return pl.pallas_call(
         evolve_kernel,
         out_shape=jax.ShapeDtypeStruct(fields.shape, fields.dtype),
-        grid=(x_cells,),
-        in_specs=[
-            pl.BlockSpec(memory_space=pltpu.SMEM),
-            pl.BlockSpec((1, y_cells, z_cells), lambda x: (x, 0, 0)),
-            *[whole(array.shape) for array in (fields, x_halo, y_first, y_second)],
-        ],
-        out_specs=pl.BlockSpec((count, 1, y_cells, z_cells), lambda x: (0, x, 0, 0)),
+        in_specs=[pl.BlockSpec(memory_space=pltpu.SMEM)] + [vmem] * 5,
+        out_specs=vmem,
         compiler_params=pltpu.CompilerParams(vmem_limit_bytes=16 * 1024 * 1024),
         name="evolve_brick",
     )(place, viscosity, fields, x_halo, y_first, y_second)
@@ -958,7 +956,7 @@
 
     *cube, first, last = lax.optimization_barrier((*cube, first, last))
     selects = lax.optimization_barrier(
-        (jnp.asarray(SELECT_FIRST, jnp.bfloat16), jnp.asarray(SELECT_LAST, jnp.bfloat16))
+        (jnp.asarray(SELECT, jnp.bfloat16), jnp.asarray(LAST_ORDER, jnp.bfloat16))
     )
 
     thin = lax.all_to_all(thin, ("gx", "gy"), split_axis=0, concat_axis=0, tiled=True)
@@ -975,6 +973,13 @@
             jnp.zeros((2, fields_count, x_cells, z_cells), jnp.float32),
         ),
         lambda: brick_viscosity(closure, place, brick),
+    )
+    share_size = NPARAM // (group_count * trainers)
+    share_start = (my_group * trainers + my_column) * share_size
+    momentum_share = lax.dynamic_slice_in_dim(momentum, share_start, share_size)
+    master_share = lax.dynamic_slice_in_dim(master, share_start, share_size)
+    viscosity, momentum_share, master_share = lax.optimization_barrier(
+        (viscosity, momentum_share, master_share)
     )
     halo = (x_neighbours(x_edges), *y_neighbours(y_edges[0], y_edges[1]))
     near = [landed, *from_line(landed)]
@@ -1020,10 +1025,6 @@
             [(g * trainers + c, (g ^ apart) * trainers + c) for g in range(group_count) for c in range(trainers)],
         )
 
-    share_size = NPARAM // (group_count * trainers)
-    share_start = (my_group * trainers + my_column) * share_size
-    momentum_share = lax.dynamic_slice_in_dim(momentum, share_start, share_size)
-    master_share = lax.dynamic_slice_in_dim(master, share_start, share_size)
     inverse = 1.0 / jnp.sqrt(jnp.sum(final * final) / NPARAM + norm_epsilon)
     delta_share = lax.dynamic_slice_in_dim(final, share_start, share_size)
     new_momentum = momentum_decay * momentum_share + delta_share * inverse

time: 104 us -> 105 us (level)
  local copies, waits for them, and re-layouts: 1.28 us -> 4.48 us
  Pallas kernels: 44.2 us -> 42.7 us
    squeeze x1, local copies, waits for them, and re-layouts: 0.02 us -> 1.68 us  [on_device(): halo = (x_neighbours(x_edges), *y_neighbours(y_edges[0], y_edges[1]))]
    pallas_call x1, Pallas kernels: 10.4 us -> 8.96 us  [evolve(): pl.pallas_call(evolve_kernel, out_shape=jax.ShapeDtypeStruct(fields.shape...]
  transfers between devices with their start and end apart: 18 -> 18, of which waited for: 9 -> 9; matrix products, arithmetic and copies ran while one was open for 1% -> 3% of each run, Pallas kernels for 29% -> 28%
where the time goes in v16:
time: 105 us; the launch traced here: 104 us
  Pallas kernels  42.7 us (41%)
  starting transfers between devices  33.8 us (32%)
  waiting for transfers between devices  19.9 us (19%)
  local copies, waits for them, and re-layouts  4.48 us (4%)
  between operations  1.65 us (2%)
  other arithmetic  1.58 us (2%)
    pallas_call x1, Pallas kernels, brick_viscosity(): pl.pallas_call(viscosity_kernel, out_shape=(jax.ShapeDtypeStruct(fields.s...  25 us
    pallas_call x1, Pallas kernels, evolve(): pl.pallas_call(evolve_kernel, out_shape=jax.ShapeDtypeStruct(fields.shape...  8.96 us
    all_to_all x1, starting transfers between devices, on_device(): lax.all_to_all(thin, ('gx', 'gy'), split_axis=0, concat_axis=0, tiled=True)  7.42 us
    ppermute x2, starting transfers between devices, on_device(): final = final + lax.ppermute(held, everyone, meets)  4.85 us
    ppermute x1, starting transfers between devices, y_neighbours(): lax.ppermute(for_second, everyone, pairs(0, -1))  4.31 us
    ppermute x2, waiting for transfers between devices, on_device(): final = final + lax.ppermute(held, everyone, meets)  4.22 us
    ppermute x2, starting transfers between devices, on_device(): lax.ppermute(final, everyone, [(g * trainers + c, (g ^ apart) * trainers...  3.85 us
    pallas_call x1, Pallas kernels, sample_cube(): pl.pallas_call(functools.partial(sample_kernel, y_cells, z_cells), out_sh...  3.63 us
  transfers between devices with their start and end apart: 18, of which 9 were waited for; matrix products, arithmetic and copies ran while one was open for 3% of the time, Pallas kernels for 28%

profile of v16, /device:TPU:0, one launch (start us, length us, event | category | flops | bytes accessed | tf_op | source)
XLA Modules:
  0.0 104.2 jit_solution(15215133349340424879)
XLA Ops:
  0.6 0.1 stack.27.place
  0.7 0.7 copy-done.1
  1.4 2.8 %thin_faces.1 = f32[8,16,256]{2,1,0:T(8,128)} custom-call(s32[24]{0:T(128)S(1)} %copy-done.1, s32[6]{0:T(128)S(1)} %stack.27.place, f32[2560,384]{1,0:T(8,128)} %bitcast.23, f32[80,32,384]{2,1,0:T(8,128)} %bitcast.24), custom_call_target="tpu_custom_call" | custom-call | tf_op jit(solution)/shard_map/thin_faces/pallas_call | solution.py:685
  4.2 7.4 %all-to-all-start = ((f32[8,16,256]{2,1,0:T(8,128)}), f32[8,16,256]{2,1,0:T(8,128)S(1)}, u32[]{:S(2)}, u32[]{:S(2)}) async-start(f32[8,16,256]{2,1,0:T(8,128)} %thin_faces.1), calls=%async_computation | async-start | bytes 262144 | tf_op jit(solution)/shard_map/all_to_all | solution.py:962
  11.7 0.1 fusion.1
  11.8 3.6 %sample_cube.1 = (f32[80,256]{1,0:T(8,128)S(1)}, f32[80,256]{1,0:T(8,128)S(1)}, f32[80,256]{1,0:T(8,128)S(1)}, f32[2,16,128]{2,1,0:T(8,128)S(1)}) custom-call(s32[24]{0:T(128)S(1)} %copy-done.2, s32[6]{0:T(128)S(1)} %stack.27.place, f32[2560,384]{1,0:T(8,128)} %bitcast.25), custom_call_target="tpu_custom_call" | custom-call | bytes 16000000 | tf_op jit(solution)/shard_map/sample_cube/pallas_call | solution.py:788
  15.4 0.1 fusion
  15.6 0.1 copy.15
  15.7 0.2 slice.37
  16.0 0.1 select_maximum_fusion.closure
  16.0 3.1 %all-to-all-done.thin = f32[8,16,256]{2,1,0:T(8,128)S(1)} async-done(((f32[8,16,256]{2,1,0:T(8,128)}), f32[8,16,256]{2,1,0:T(8,128)S(1)}, u32[]{:S(2)}, u32[]{:S(2)}) %all-to-all-start) | async-done | bytes 131104 | tf_op jit(solution)/shard_map/all_to_all | solution.py:962
  19.2 1.6 %cube_change.1 = bf16[320,128]{1,0:T(8,128)(2,1)S(1)} custom-call(s32[24]{0:T(128)S(1)} %copy-done.2, s32[6]{0:T(128)S(1)} %stack.27.place, f32[8,128]{1,0:T(8,128)S(1)} %select_maximum_fusion.closure, bf16[256,256]{1,0:T(8,128)(2,1)S(1)} %copy-done, f32[80,256]{1,0:T(8,128)S(1)} %get-tuple-element.96.centre, f32[80,256]{1,0:T(8,128)S(1)} %get-tuple-element.97.lower, ...), custom_call_target="tpu_custom_call" | custom-call | tf_op jit(solution)/shard_map/cube_change/pallas_call | solution.py:869
  20.8 1.5 %collective-permute-start.2 = (bf16[320,128]{1,0:T(8,128)(2,1)S(1)}, bf16[320,128]{1,0:T(8,128)(2,1)S(1)}, u32[]{:S(2)}, u32[]{:S(2)}) collective-permute-start(bf16[320,128]{1,0:T(8,128)(2,1)S(1)} %cube_change.1), channel_id=1, source_target_pairs={{0,24},{1,25},{2,26},{3,27},{4,28},{5,29},{6,30},{7,31}} | collective-permute-start | bytes 245768 | tf_op jit(solution)/shard_map/ppermute | solution.py:938
  22.2 0.7 collective-permute-start.1
  22.9 0.7 collective-permute-start
  23.6 0.8 collective-permute-done.2
  24.4 0.8 collective-permute-start.8
  25.2 0.7 collective-permute-start.7
  25.9 0.7 collective-permute-start.6
  26.6 25.0 %conditional.2 = ((f32[16,32,384]{2,1,0:T(8,128)S(1)}, f32[2,5,32,384]{3,2,1,0:T(8,128)}, f32[2,5,16,384]{3,2,1,0:T(8,128)S(1)})) conditional(s32[]{:T(128)} %convert_element_type.10, (f32[8,128]{1,0:T(8,128)S(1)}, s32[6]{0:T(128)S(1)}, f32[5,16,32,384]{3,2,1,0:T(8,128)}) %tuple.48, () %tuple.32), branch_computations={%region_1.2_spmd, %region_2.3_spmd} | conditional | bytes 1523756 | solution.py:968
  26.6 25.0 %brick_viscosity.1 = (f32[16,32,384]{2,1,0:T(8,128)S(1)}, f32[2,5,32,384]{3,2,1,0:T(8,128)}, f32[2,5,16,384]{3,2,1,0:T(8,128)S(1)}) custom-call(f32[8,128]{1,0:T(8,128)S(1)} %get-tuple-element.43.closure, s32[6]{0:T(128)S(1)} %get-tuple-element.44.place, f32[5,16,32,384]{3,2,1,0:T(8,128)} %get-tuple-element.45.fields), custom_call_target="tpu_custom_call" | custom-call | tf_op jit(solution)/shard_map/cond/branch_0_fun/brick_viscosity/pallas_call | solution.py:524
  51.6 0.7 copy-done.4
  52.3 2.5 %collective-permute-start.3 = (f32[2,5,32,384]{3,2,1,0:T(8,128)}, f32[2,5,32,384]{3,2,1,0:T(8,128)S(1)}, u32[]{:S(2)}, u32[]{:S(2)}) collective-permute-start(f32[2,5,32,384]{3,2,1,0:T(8,128)} %get-tuple-element.103), channel_id=1, source_target_pairs={{0,4},{1,5},{2,6},{3,7},{4,0},{5,1},{6,2},{7,3},{8,12},{9,13},{10,... | collective-permute-start | bytes 1474568 | tf_op jit(solution)/shard_map/ppermute | solution.py:923
  54.8 0.7 pick_cubes.1
  55.6 1.4 %collective-permute-start.9 = (bf16[6,320,128]{2,1,0:T(8,128)(2,1)S(1)}, bf16[6,320,128]{2,1,0:T(8,128)(2,1)}, u32[]{:S(2)}, u32[]{:S(2)}) collective-permute-start(bf16[6,320,128]{2,1,0:T(8,128)(2,1)S(1)} %pick_cubes.1), channel_id=1, source_target_pairs={{24,28},{25,29},{26,30},{27,31},{28,24},{29,25},{30,26},{31,27}} | collective-permute-start | bytes 1474568 | tf_op jit(solution)/shard_map/ppermute | solution.py:949
  57.0 1.7 %slice_bitcast_fusion = (f32[5,16,384]{2,1,0:T(8,128)}, f32[5,16,384]{2,1,0:T(8,128)}) fusion(f32[2,5,16,384]{3,2,1,0:T(8,128)} %copy-done.4), kind=kLoop, calls=%fused_computation.2 | loop fusion | bytes 491520 | tf_op jit(solution)/shard_map/squeeze | solution.py:984
  58.7 4.3 %collective-permute-start.5 = (f32[5,16,384]{2,1,0:T(8,128)}, f32[5,16,384]{2,1,0:T(8,128)}, u32[]{:S(2)}, u32[]{:S(2)}) collective-permute-start(f32[5,16,384]{2,1,0:T(8,128)} %get-tuple-element.118), channel_id=1, source_target_pairs={{0,3},{1,2},{2,1},{3,0},{4,7},{5,6},{6,5},{7,4},{8,11},{9,10},{10,... | collective-permute-start | bytes 368648 | tf_op jit(solution)/shard_map/ppermute | solution.py:930
  63.0 1.9 %collective-permute-start.4 = (f32[5,16,384]{2,1,0:T(8,128)}, f32[5,16,384]{2,1,0:T(8,128)}, u32[]{:S(2)}, u32[]{:S(2)}) collective-permute-start(f32[5,16,384]{2,1,0:T(8,128)} %get-tuple-element.119), channel_id=1, source_target_pairs={{0,1},{1,0},{2,3},{3,2},{4,5},{5,4},{6,7},{7,6},{8,9},{9,8},{10,11... | collective-permute-start | bytes 368648 | tf_op jit(solution)/shard_map/ppermute | solution.py:929
  64.9 0.1 dynamic_slice.10
  65.0 0.8 dynamic_slice.9
  65.8 3.0 %collective-permute-done.5 = f32[5,16,384]{2,1,0:T(8,128)} collective-permute-done((f32[5,16,384]{2,1,0:T(8,128)}, f32[5,16,384]{2,1,0:T(8,128)}, u32[]{:S(2)}, u32[]{:S(2)}) %collective-permute-start.5) | collective-permute-done | bytes 122912 | tf_op jit(solution)/shard_map/ppermute | solution.py:930
  68.8 2.3 %collective-permute-done.4 = f32[5,16,384]{2,1,0:T(8,128)} collective-permute-done((f32[5,16,384]{2,1,0:T(8,128)}, f32[5,16,384]{2,1,0:T(8,128)}, u32[]{:S(2)}, u32[]{:S(2)}) %collective-permute-start.4) | collective-permute-done | bytes 122912 | tf_op jit(solution)/shard_map/ppermute | solution.py:929
  71.2 9.0 %conditional.3 = (f32[17280]{0:T(1024)S(1)}, f32[1,5,16,32,384]{4,3,2,1,0:T(8,128)}) conditional(s32[]{:T(128)} %convert_element_type.10, (s32[6]{0:T(128)S(1)}, f32[16,32,384]{2,1,0:T(8,128)S(1)}, f32[5,16,32,384]{3,2,1,0:T(8,128)}, f32[2,5,32,384]{3,2,1,0:T(8,128)S(1)}, f32[5,16,384]{2,1,0:T(8,128)}, /*index=5*/f32[5,16,384]{2,1,0:T(8,128)}) %tuple.49, ...), branch_computations={%region_3.4_spmd, %region_4.5_spmd} | conditional | flops 17280 | bytes 345616 | solution.py:1005
  71.2 9.0 %evolve_brick.1 = f32[5,16,32,384]{3,2,1,0:T(8,128)} custom-call(s32[6]{0:T(128)S(1)} %get-tuple-element.46.place, f32[16,32,384]{2,1,0:T(8,128)S(1)} %get-tuple-element.47.viscosity, f32[5,16,32,384]{3,2,1,0:T(8,128)} %get-tuple-element.48.fields, f32[2,5,32,384]{3,2,1,0:T(8,128)S(1)} %get-tuple-element.49.x_halo, f32[5,16,384]{2,1,0:T(8,128)} %get-tuple-element.50.y_first, ...), custom_call_target="tpu_custom_call" | custom-call | tf_op jit(solution)/shard_map/cond/branch_0_fun/evolve_brick/pallas_call | solution.py:591
  80.2 1.3 %collective-permute-start.12 = (f32[17280]{0:T(1024)S(1)}, f32[17280]{0:T(1024)S(1)}, u32[]{:S(2)}, u32[]{:S(2)}) collective-permute-start(f32[17280]{0:T(1024)S(1)} %get-tuple-element.113), channel_id=1, source_target_pairs={{24,0},{25,1},{26,2},{27,3},{28,4},{29,5},{30,6},{31,7}} | collective-permute-start | bytes 207368 | tf_op jit(solution)/shard_map/ppermute | solution.py:1009
  81.5 0.7 collective-permute-start.11
  82.1 0.7 collective-permute-start.10
  82.8 3.0 %collective-permute-done.12 = f32[17280]{0:T(1024)S(1)} collective-permute-done((f32[17280]{0:T(1024)S(1)}, f32[17280]{0:T(1024)S(1)}, u32[]{:S(2)}, u32[]{:S(2)}) %collective-permute-start.12) | collective-permute-done | bytes 69152 | tf_op jit(solution)/shard_map/ppermute | solution.py:1009
  85.8 2.7 %collective-permute-start.14 = (f32[17280]{0:T(1024)S(1)}, f32[17280]{0:T(1024)S(1)}, u32[]{:S(2)}, u32[]{:S(2)}) collective-permute-start(f32[17280]{0:T(1024)S(1)} %add_add_fusion.1), channel_id=1, source_target_pairs={{0,5},{1,4},{2,7},{3,6},{4,1},{5,0},{6,3},{7,2},{8,14},{9,15},{10,... | collective-permute-start | bytes 207368 | tf_op jit(solution)/shard_map/ppermute | solution.py:1020
  88.5 2.2 %collective-permute-start.13 = (f32[17280]{0:T(1024)S(1)}, f32[17280]{0:T(1024)S(1)}, u32[]{:S(2)}, u32[]{:S(2)}) collective-permute-start(f32[17280]{0:T(1024)S(1)} %add_add_fusion.1), channel_id=1, source_target_pairs={{0,1},{1,0},{2,3},{3,2},{4,5},{5,4},{6,7},{7,6},{8,10},{9,11},{10,... | collective-permute-start | bytes 207368 | tf_op jit(solution)/shard_map/ppermute | solution.py:1020
  90.7 2.2 %collective-permute-done.14 = f32[17280]{0:T(1024)S(1)} collective-permute-done((f32[17280]{0:T(1024)S(1)}, f32[17280]{0:T(1024)S(1)}, u32[]{:S(2)}, u32[]{:S(2)}) %collective-permute-start.14) | collective-permute-done | bytes 69152 | tf_op jit(solution)/shard_map/ppermute | solution.py:1020
  92.9 2.0 %collective-permute-done.13 = f32[17280]{0:T(1024)S(1)} collective-permute-done((f32[17280]{0:T(1024)S(1)}, f32[17280]{0:T(1024)S(1)}, u32[]{:S(2)}, u32[]{:S(2)}) %collective-permute-start.13) | collective-permute-done | bytes 69152 | tf_op jit(solution)/shard_map/ppermute | solution.py:1020
  94.9 0.8 collective-permute-start.15
  95.7 0.9 collective-permute-done.15
  96.6 3.1 %collective-permute-start.16 = (f32[17280]{0:T(1024)S(1)}, f32[17280]{0:T(1024)S(1)}, u32[]{:S(2)}, u32[]{:S(2)}) collective-permute-start(f32[17280]{0:T(1024)S(1)} %add.52), channel_id=1, source_target_pairs={{0,16},{1,17},{2,18},{3,19},{4,20},{5,21},{6,22},{7,23},{8,24},{9,... | collective-permute-start | bytes 207368 | tf_op jit(solution)/shard_map/ppermute | solution.py:1022
  99.7 2.5 %collective-permute-done.16 = f32[17280]{0:T(1024)S(1)} collective-permute-done((f32[17280]{0:T(1024)S(1)}, f32[17280]{0:T(1024)S(1)}, u32[]{:S(2)}, u32[]{:S(2)}) %collective-permute-start.16) | collective-permute-done | bytes 69152 | tf_op jit(solution)/shard_map/ppermute | solution.py:1022
  102.2 0.6 multiply_reduce_fusion
  103.5 0.7 multiply_subtract_fusion
  (37 shorter events, 0.2 us)
Async XLA Ops:
  0.7 0.7 copy-start.1
  1.4 10.3 %copy-start.7 = (f32[64,5]{0,1:T(8,128)S(1)}, f32[64,5]{0,1:T(8,128)}, u32[]{:S(2)}) copy-start(f32[64,5]{0,1:T(8,128)} %param.16) | copy-start | bytes 3844
  1.4 10.3 %copy-start.5 = (f32[17280]{0:T(1024)S(1)}, f32[17280]{0:T(1024)}, u32[]{:S(2)}) copy-start(f32[17280]{0:T(1024)} %param.19) | copy-start | bytes 207364
  1.4 10.4 %copy-start.9 = (f32[64]{0:T(128)S(1)}, f32[64]{0:T(128)}, u32[]{:S(2)}) copy-start(f32[64]{0:T(128)} %param.17) | copy-start | bytes 772
  1.4 10.4 %copy-start.2 = (s32[24]{0:T(128)S(1)}, s32[24]{0:T(128)}, u32[]{:S(2)}) copy-start(s32[24]{0:T(128)} %sample_block.5) | copy-start | bytes 292
  4.2 11.2 %copy-start.6 = (f32[64]{0:T(128)S(1)}, f32[64]{0:T(128)}, u32[]{:S(2)}) copy-start(f32[64]{0:T(128)} %param.18) | copy-start | bytes 772
  4.2 15.0 %copy-start = (bf16[256,256]{1,0:T(8,128)(2,1)S(1)}, bf16[256,256]{1,0:T(8,128)(2,1)}, u32[]{:S(2)}) copy-start(bf16[256,256]{1,0:T(8,128)(2,1)} %constant.60.clone.order) | copy-start | bytes 393220
  4.2 14.9 %all-to-all-start = ((f32[8,16,256]{2,1,0:T(8,128)}), f32[8,16,256]{2,1,0:T(8,128)S(1)}, u32[]{:S(2)}, u32[]{:S(2)}) async-start(f32[8,16,256]{2,1,0:T(8,128)} %thin_faces.1), calls=%async_computation | async-start | bytes 262144 | tf_op jit(solution)/shard_map/all_to_all | solution.py:962
  15.4 39.4 %copy-start.8 = (s32[24]{0:T(128)S(1)}, s32[24]{0:T(128)}, u32[]{:S(2)}) copy-start(s32[24]{0:T(128)} %trainer_of.1) | copy-start | bytes 292
  20.8 3.6 %collective-permute-start.2 = (bf16[320,128]{1,0:T(8,128)(2,1)S(1)}, bf16[320,128]{1,0:T(8,128)(2,1)S(1)}, u32[]{:S(2)}, u32[]{:S(2)}) collective-permute-start(bf16[320,128]{1,0:T(8,128)(2,1)S(1)} %cube_change.1), channel_id=1, source_target_pairs={{0,24},{1,25},{2,26},{3,27},{4,28},{5,29},{6,30},{7,31}} | collective-permute-start | bytes 245768 | tf_op jit(solution)/shard_map/ppermute | solution.py:938
  22.2 2.1 %collective-permute-start.1 = (bf16[320,128]{1,0:T(8,128)(2,1)S(1)}, bf16[320,128]{1,0:T(8,128)(2,1)S(1)}, u32[]{:S(2)}, u32[]{:S(2)}) collective-permute-start(bf16[320,128]{1,0:T(8,128)(2,1)S(1)} %cube_change.1), channel_id=1, source_target_pairs={{8,24},{9,25},{10,26},{11,27},{12,28},{13,29},{14,30},{15,31}} | collective-permute-start | bytes 245768 | tf_op jit(solution)/shard_map/ppermute | solution.py:938
  22.9 1.5 %collective-permute-start = (bf16[320,128]{1,0:T(8,128)(2,1)S(1)}, bf16[320,128]{1,0:T(8,128)(2,1)S(1)}, u32[]{:S(2)}, u32[]{:S(2)}) collective-permute-start(bf16[320,128]{1,0:T(8,128)(2,1)S(1)} %cube_change.1), channel_id=1, source_target_pairs={{16,24},{17,25},{18,26},{19,27},{20,28},{21,29},{22,30},{23,31}} | collective-permute-start | bytes 245768 | tf_op jit(solution)/shard_map/ppermute | solution.py:938
  24.4 46.8 %copy-start.3 = (bf16[4,256,240]{2,1,0:T(8,128)(2,1)S(1)}, bf16[4,256,240]{2,1,0:T(8,128)(2,1)}, u32[]{:S(2)}) copy-start(bf16[4,256,240]{2,1,0:T(8,128)(2,1)} %constant.58.clone) | copy-start | bytes 1474564
  24.4 30.4 %collective-permute-start.8 = (bf16[3,320,128]{2,1,0:T(8,128)(2,1)S(1)}, bf16[3,320,128]{2,1,0:T(8,128)(2,1)S(1)}, u32[]{:S(2)}, u32[]{:S(2)}) collective-permute-start(bf16[3,320,128]{2,1,0:T(8,128)(2,1)S(1)} %pad_maximum_fusion.1.refs_0_), channel_id=1, source_target_pairs={{24,27},{25,26},{26,25},{27,24},{28,31},{29,30},{30,29},{31,28}} | collective-permute-start | bytes 737288 | tf_op jit(solution)/shard_map/ppermute | solution.py:946
  25.2 29.6 %collective-permute-start.7 = (bf16[3,320,128]{2,1,0:T(8,128)(2,1)S(1)}, bf16[3,320,128]{2,1,0:T(8,128)(2,1)S(1)}, u32[]{:S(2)}, u32[]{:S(2)}) collective-permute-start(bf16[3,320,128]{2,1,0:T(8,128)(2,1)S(1)} %pad_maximum_fusion.1.refs_0_), channel_id=1, source_target_pairs={{24,26},{25,27},{26,24},{27,25},{28,30},{29,31},{30,28},{31,29}} | collective-permute-start | bytes 737288 | tf_op jit(solution)/shard_map/ppermute | solution.py:946
  25.9 28.9 %collective-permute-start.6 = (bf16[3,320,128]{2,1,0:T(8,128)(2,1)S(1)}, bf16[3,320,128]{2,1,0:T(8,128)(2,1)S(1)}, u32[]{:S(2)}, u32[]{:S(2)}) collective-permute-start(bf16[3,320,128]{2,1,0:T(8,128)(2,1)S(1)} %pad_maximum_fusion.1.refs_0_), channel_id=1, source_target_pairs={{24,25},{25,24},{26,27},{27,26},{28,29},{29,28},{30,31},{31,30}} | collective-permute-start | bytes 737288 | tf_op jit(solution)/shard_map/ppermute | solution.py:946
  51.6 0.7 copy-start.4
  52.3 18.9 %collective-permute-start.3 = (f32[2,5,32,384]{3,2,1,0:T(8,128)}, f32[2,5,32,384]{3,2,1,0:T(8,128)S(1)}, u32[]{:S(2)}, u32[]{:S(2)}) collective-permute-start(f32[2,5,32,384]{3,2,1,0:T(8,128)} %get-tuple-element.103), channel_id=1, source_target_pairs={{0,4},{1,5},{2,6},{3,7},{4,0},{5,1},{6,2},{7,3},{8,12},{9,13},{10,... | collective-permute-start | bytes 1474568 | tf_op jit(solution)/shard_map/ppermute | solution.py:923
  55.6 15.6 %collective-permute-start.9 = (bf16[6,320,128]{2,1,0:T(8,128)(2,1)S(1)}, bf16[6,320,128]{2,1,0:T(8,128)(2,1)}, u32[]{:S(2)}, u32[]{:S(2)}) collective-permute-start(bf16[6,320,128]{2,1,0:T(8,128)(2,1)S(1)} %pick_cubes.1), channel_id=1, source_target_pairs={{24,28},{25,29},{26,30},{27,31},{28,24},{29,25},{30,26},{31,27}} | collective-permute-start | bytes 1474568 | tf_op jit(solution)/shard_map/ppermute | solution.py:949
  58.7 10.2 %collective-permute-start.5 = (f32[5,16,384]{2,1,0:T(8,128)}, f32[5,16,384]{2,1,0:T(8,128)}, u32[]{:S(2)}, u32[]{:S(2)}) collective-permute-start(f32[5,16,384]{2,1,0:T(8,128)} %get-tuple-element.118), channel_id=1, source_target_pairs={{0,3},{1,2},{2,1},{3,0},{4,7},{5,6},{6,5},{7,4},{8,11},{9,10},{10,... | collective-permute-start | bytes 368648 | tf_op jit(solution)/shard_map/ppermute | solution.py:930
  63.0 8.2 %collective-permute-start.4 = (f32[5,16,384]{2,1,0:T(8,128)}, f32[5,16,384]{2,1,0:T(8,128)}, u32[]{:S(2)}, u32[]{:S(2)}) collective-permute-start(f32[5,16,384]{2,1,0:T(8,128)} %get-tuple-element.119), channel_id=1, source_target_pairs={{0,1},{1,0},{2,3},{3,2},{4,5},{5,4},{6,7},{7,6},{8,9},{9,8},{10,11... | collective-permute-start | bytes 368648 | tf_op jit(solution)/shard_map/ppermute | solution.py:929
  80.2 5.6 %collective-permute-start.12 = (f32[17280]{0:T(1024)S(1)}, f32[17280]{0:T(1024)S(1)}, u32[]{:S(2)}, u32[]{:S(2)}) collective-permute-start(f32[17280]{0:T(1024)S(1)} %get-tuple-element.113), channel_id=1, source_target_pairs={{24,0},{25,1},{26,2},{27,3},{28,4},{29,5},{30,6},{31,7}} | collective-permute-start | bytes 207368 | tf_op jit(solution)/shard_map/ppermute | solution.py:1009
  81.5 4.3 %collective-permute-start.11 = (f32[17280]{0:T(1024)S(1)}, f32[17280]{0:T(1024)S(1)}, u32[]{:S(2)}, u32[]{:S(2)}) collective-permute-start(f32[17280]{0:T(1024)S(1)} %get-tuple-element.113), channel_id=1, source_target_pairs={{24,8},{25,9},{26,10},{27,11},{28,12},{29,13},{30,14},{31,15}} | collective-permute-start | bytes 207368 | tf_op jit(solution)/shard_map/ppermute | solution.py:1009
  82.1 3.7 %collective-permute-start.10 = (f32[17280]{0:T(1024)S(1)}, f32[17280]{0:T(1024)S(1)}, u32[]{:S(2)}, u32[]{:S(2)}) collective-permute-start(f32[17280]{0:T(1024)S(1)} %get-tuple-element.113), channel_id=1, source_target_pairs={{24,16},{25,17},{26,18},{27,19},{28,20},{29,21},{30,22},{31,23}} | collective-permute-start | bytes 207368 | tf_op jit(solution)/shard_map/ppermute | solution.py:1009
  85.8 7.1 %collective-permute-start.14 = (f32[17280]{0:T(1024)S(1)}, f32[17280]{0:T(1024)S(1)}, u32[]{:S(2)}, u32[]{:S(2)}) collective-permute-start(f32[17280]{0:T(1024)S(1)} %add_add_fusion.1), channel_id=1, source_target_pairs={{0,5},{1,4},{2,7},{3,6},{4,1},{5,0},{6,3},{7,2},{8,14},{9,15},{10,... | collective-permute-start | bytes 207368 | tf_op jit(solution)/shard_map/ppermute | solution.py:1020
  88.5 6.4 %collective-permute-start.13 = (f32[17280]{0:T(1024)S(1)}, f32[17280]{0:T(1024)S(1)}, u32[]{:S(2)}, u32[]{:S(2)}) collective-permute-start(f32[17280]{0:T(1024)S(1)} %add_add_fusion.1), channel_id=1, source_target_pairs={{0,1},{1,0},{2,3},{3,2},{4,5},{5,4},{6,7},{7,6},{8,10},{9,11},{10,... | collective-permute-start | bytes 207368 | tf_op jit(solution)/shard_map/ppermute | solution.py:1020
  94.9 1.7 %collective-permute-start.15 = (f32[17280]{0:T(1024)S(1)}, f32[17280]{0:T(1024)S(1)}, u32[]{:S(2)}, u32[]{:S(2)}) collective-permute-start(f32[17280]{0:T(1024)S(1)} %add_add_fusion), channel_id=1, source_target_pairs={{0,8},{1,9},{2,10},{3,11},{4,12},{5,13},{6,14},{7,15},{8,0},{9,1},... | collective-permute-start | bytes 207368 | tf_op jit(solution)/shard_map/ppermute | solution.py:1022
  96.6 5.6 %collective-permute-start.16 = (f32[17280]{0:T(1024)S(1)}, f32[17280]{0:T(1024)S(1)}, u32[]{:S(2)}, u32[]{:S(2)}) collective-permute-start(f32[17280]{0:T(1024)S(1)} %add.52), channel_id=1, source_target_pairs={{0,16},{1,17},{2,18},{3,19},{4,20},{5,21},{6,22},{7,23},{8,24},{9,... | collective-permute-start | bytes 207368 | tf_op jit(solution)/shard_map/ppermute | solution.py:1022

commit v17 on v16

--- a/solution.py
+++ b/solution.py
@@ -462,14 +462,16 @@
     return base_viscosity + viscosity_gain * soft
 
 
-def viscosity_kernel(closure, place, fields, viscosity, x_edges, y_edges, weights, out_column):
+def viscosity_kernel(
+    closure, place, fields, viscosity, x_edges, y_first, y_second, weights, out_column, masks, ones
+):
     y_cells, z_cells = fields.shape[2:]
     x, x_cells = pl.program_id(0), pl.num_programs(0)
     up_first = lax.rem(place[2], 2) == 0
     for f in range(F):
         low, high = fields[f, 0, 0:1, :], fields[f, 0, y_cells - 1 : y_cells, :]
-        y_edges[0, f, pl.ds(x, 1), :] = jnp.where(up_first, high, low)
-        y_edges[1, f, pl.ds(x, 1), :] = jnp.where(up_first, low, high)
+        y_first[f, pl.ds(x, 1), :] = jnp.where(up_first, high, low)
+        y_second[f, pl.ds(x, 1), :] = jnp.where(up_first, low, high)
 
     @pl.when(x == x_cells - 1)
     def _():
@@ -481,29 +483,31 @@
         plain = closure[...]
         high = plain.astype(jnp.bfloat16).astype(jnp.float32)
         low = plain - high
-        blank = jnp.zeros((8, 128), jnp.float32)
+        row = lax.broadcasted_iota(jnp.int32, (16, z_cells), 0)
         for j in range(8):
-            turned = [pltpu.roll(part, j, 0) if j else part for part in (high, high, low)]
-            stacked = jnp.concatenate([*turned, blank], axis=0)
-            weights[j] = stacked.T[: HID + 8].astype(jnp.bfloat16)
+            turned = [pltpu.roll(part, j, 0) if j else part for part in (high, high, low, low)]
+            weights[j] = jnp.concatenate(turned, axis=0).T[: HID + 8].astype(jnp.bfloat16)
+            masks[j] = jnp.where(row % 8 == j, 1.0, 0.0).astype(jnp.bfloat16)
+            ones[j] = jnp.where(row == (j + F) % 8, 1.0, 0.0).astype(jnp.bfloat16)
         out_column[...] = jnp.broadcast_to(plain.T[:HID, F + 1 : F + 2], (HID, 128))
 
     sublane = lax.broadcasted_iota(jnp.int32, (8, z_cells), 0)
     wide = z_cells // 128
-    tiles = y_cells // 8
 
     def tile(index, carry):
         rows = pl.ds(pl.multiple_of(index * 8, 8), 8)
-        turned = [fields[f, 0, rows, :] for f in range(F)]
-        turned = [pltpu.roll(turned[f], f, 0) if f else turned[f] for f in range(F)]
+        turned = []
+        for f in range(F):
+            value = fields[f, 0, rows, :]
+            value = pltpu.roll(value, f, 0) if f else value
+            top = value.astype(jnp.bfloat16).astype(jnp.float32)
+            turned.append(jnp.concatenate([top, value - top], axis=0).astype(jnp.bfloat16))
         sums = jnp.zeros((8, z_cells), jnp.float32)
         for j in range(8):
-            cells = jnp.where(sublane == (j + F) % 8, 1.0, 0.0)
+            cells = ones[j]
             for f in range(F):
-                cells = jnp.where(sublane == (j + f) % 8, turned[f], cells)
-            top = cells.astype(jnp.bfloat16).astype(jnp.float32)
-            stacked = jnp.concatenate([top, cells - top, top, jnp.zeros_like(top)], axis=0)
-            half = dot_rows(weights[j], stacked.astype(jnp.bfloat16))
+                cells = cells + turned[f] * masks[(j + f) % 8]
+            half = dot_rows(weights[j], jnp.concatenate([cells, cells], axis=0))
             total = half[HID:]
             for group in range(HID // 8):
                 part = half[group * 8 : group * 8 + 8]
@@ -516,17 +520,20 @@
         viscosity[0, rows, :] = base_viscosity + viscosity_gain * soft
         return carry
 
-    lax.fori_loop(0, tiles, tile, 0)
+    lax.fori_loop(0, y_cells // 8, tile, 0)
 
 
 def brick_viscosity(closure, place, fields):
     count, x_cells, y_cells, z_cells = fields.shape
+    line = jax.ShapeDtypeStruct((count, x_cells, z_cells), fields.dtype)
+    line_spec = pl.BlockSpec(line.shape, lambda x: (0, 0, 0))
     return pl.pallas_call(
         viscosity_kernel,
         out_shape=(
             jax.ShapeDtypeStruct(fields.shape[1:], fields.dtype),
             jax.ShapeDtypeStruct((2, count, y_cells, z_cells), fields.dtype),
-            jax.ShapeDtypeStruct((2, count, x_cells, z_cells), fields.dtype),
+            line,
+            line,
         ),
         grid=(x_cells,),
         in_specs=[
@@ -537,11 +544,14 @@
         out_specs=(
             pl.BlockSpec((1, y_cells, z_cells), lambda x: (x, 0, 0)),
             pl.BlockSpec((2, count, y_cells, z_cells), lambda x: (0, 0, 0, 0)),
-            pl.BlockSpec((2, count, x_cells, z_cells), lambda x: (0, 0, 0, 0)),
+            line_spec,
+            line_spec,
         ),
         scratch_shapes=[
             pltpu.VMEM((8, HID + 8, 32), jnp.bfloat16),
             pltpu.VMEM((HID, 128), jnp.float32),
+            pltpu.VMEM((8, 16, z_cells), jnp.bfloat16),
+            pltpu.VMEM((8, 16, z_cells), jnp.bfloat16),
         ],
         compiler_params=pltpu.CompilerParams(vmem_limit_bytes=16 * 1024 * 1024),
         name="brick_viscosity",
@@ -965,12 +975,13 @@
     closure, landed = lax.optimization_barrier((closure, landed))
 
     fields_count, x_cells = brick.shape[:2]
-    viscosity, x_edges, y_edges = lax.cond(
+    viscosity, x_edges, *y_edges = lax.cond(
         is_trainer,
         lambda: (
             jnp.zeros((x_cells, y_cells, z_cells), jnp.float32),
             jnp.zeros((2, fields_count, y_cells, z_cells), jnp.float32),
-            jnp.zeros((2, fields_count, x_cells, z_cells), jnp.float32),
+            jnp.zeros((fields_count, x_cells, z_cells), jnp.float32),
+            jnp.zeros((fields_count, x_cells, z_cells), jnp.float32),
         ),
         lambda: brick_viscosity(closure, place, brick),
     )
@@ -981,7 +992,7 @@
     viscosity, momentum_share, master_share = lax.optimization_barrier(
         (viscosity, momentum_share, master_share)
     )
-    halo = (x_neighbours(x_edges), *y_neighbours(y_edges[0], y_edges[1]))
+    halo = (x_neighbours(x_edges), *y_neighbours(*y_edges))
     near = [landed, *from_line(landed)]
     far = [
         across(apart, pick_cubes(sample_trainer, place, near, y_devices, x_devices, apart))

time: 105 us -> 104 us (level)
  local copies, waits for them, and re-layouts: 4.48 us -> 2.82 us
  Pallas kernels: 42.7 us -> 43.8 us
    ppermute x1, waiting for transfers between devices: 2.33 us -> 0.32 us  [y_neighbours(): lax.ppermute(for_first, everyone, pairs(0, 1))]
    squeeze x1 -> x0, local copies, waits for them, and re-layouts: 1.68 us -> none  [on_device(): halo = (x_neighbours(x_edges), *y_neighbours(y_edges[0], y_edges[1]))]
    ppermute x1, waiting for transfers between devices: 3.04 us -> 4.16 us  [y_neighbours(): lax.ppermute(for_second, everyone, pairs(0, -1))]
    pallas_call x1, Pallas kernels: 25 us -> 26.1 us  [brick_viscosity(): pl.pallas_call(viscosity_kernel, out_shape=(jax.ShapeDtypeStruct(fields.s...]
  transfers between devices with their start and end apart: 18 -> 18, of which waited for: 9 -> 9; matrix products, arithmetic and copies ran while one was open for 3% -> 1% of each run, Pallas kernels for 28% -> 29%
where the time goes in v17:
time: 104 us; the launch traced here: 103 us
  Pallas kernels  43.8 us (42%)
  starting transfers between devices  34 us (33%)
  waiting for transfers between devices  19.6 us (19%)
  local copies, waits for them, and re-layouts  2.82 us (3%)
  between operations  1.66 us (2%)
  other arithmetic  1.58 us (2%)
    pallas_call x1, Pallas kernels, brick_viscosity(): pl.pallas_call(viscosity_kernel, out_shape=(jax.ShapeDtypeStruct(fields.s...  26.1 us
    pallas_call x1, Pallas kernels, evolve(): pl.pallas_call(evolve_kernel, out_shape=jax.ShapeDtypeStruct(fields.shape...  8.96 us
    all_to_all x1, starting transfers between devices, on_device(): lax.all_to_all(thin, ('gx', 'gy'), split_axis=0, concat_axis=0, tiled=True)  7.42 us
    ppermute x2, starting transfers between devices, on_device(): final = final + lax.ppermute(held, everyone, meets)  4.97 us
    ppermute x2, waiting for transfers between devices, on_device(): final = final + lax.ppermute(held, everyone, meets)  4.3 us
    ppermute x1, starting transfers between devices, y_neighbours(): lax.ppermute(for_second, everyone, pairs(0, -1))  4.22 us
    ppermute x1, waiting for transfers between devices, y_neighbours(): lax.ppermute(for_second, everyone, pairs(0, -1))  4.16 us
    ppermute x2, waiting for transfers between devices, on_device(): lax.ppermute(final, everyone, [(g * trainers + c, (g ^ apart) * trainers...  3.94 us
  transfers between devices with their start and end apart: 18, of which 9 were waited for; matrix products, arithmetic and copies ran while one was open for 1% of the time, Pallas kernels for 29%

profile of v17, /device:TPU:0, one launch (start us, length us, event | category | flops | bytes accessed | tf_op | source)
XLA Modules:
  0.0 103.4 jit_solution(7233766973161939263)
XLA Ops:
  0.6 0.1 stack.27.place
  0.7 0.7 copy-done.1
  1.4 2.8 %thin_faces.1 = f32[8,16,256]{2,1,0:T(8,128)} custom-call(s32[24]{0:T(128)S(1)} %copy-done.1, s32[6]{0:T(128)S(1)} %stack.27.place, f32[2560,384]{1,0:T(8,128)} %bitcast.19, f32[80,32,384]{2,1,0:T(8,128)} %bitcast.20), custom_call_target="tpu_custom_call" | custom-call | tf_op jit(solution)/shard_map/thin_faces/pallas_call | solution.py:695
  4.2 7.4 %all-to-all-start = ((f32[8,16,256]{2,1,0:T(8,128)}), f32[8,16,256]{2,1,0:T(8,128)S(1)}, u32[]{:S(2)}, u32[]{:S(2)}) async-start(f32[8,16,256]{2,1,0:T(8,128)} %thin_faces.1), calls=%async_computation | async-start | bytes 262144 | tf_op jit(solution)/shard_map/all_to_all | solution.py:972
  11.7 0.1 fusion.1
  11.8 3.6 %sample_cube.1 = (f32[80,256]{1,0:T(8,128)S(1)}, f32[80,256]{1,0:T(8,128)S(1)}, f32[80,256]{1,0:T(8,128)S(1)}, f32[2,16,128]{2,1,0:T(8,128)S(1)}) custom-call(s32[24]{0:T(128)S(1)} %copy-done.2, s32[6]{0:T(128)S(1)} %stack.27.place, f32[2560,384]{1,0:T(8,128)} %bitcast.21), custom_call_target="tpu_custom_call" | custom-call | bytes 16000000 | tf_op jit(solution)/shard_map/sample_cube/pallas_call | solution.py:798
  15.4 0.1 fusion
  15.6 0.1 copy.15
  15.6 0.1 reshape.34
  15.7 0.2 slice.31
  16.0 0.1 select_maximum_fusion.closure
  16.0 3.1 %all-to-all-done.thin = f32[8,16,256]{2,1,0:T(8,128)S(1)} async-done(((f32[8,16,256]{2,1,0:T(8,128)}), f32[8,16,256]{2,1,0:T(8,128)S(1)}, u32[]{:S(2)}, u32[]{:S(2)}) %all-to-all-start) | async-done | bytes 131104 | tf_op jit(solution)/shard_map/all_to_all | solution.py:972
  19.2 1.6 %cube_change.1 = bf16[320,128]{1,0:T(8,128)(2,1)S(1)} custom-call(s32[24]{0:T(128)S(1)} %copy-done.2, s32[6]{0:T(128)S(1)} %stack.27.place, f32[8,128]{1,0:T(8,128)S(1)} %select_maximum_fusion.closure, bf16[256,256]{1,0:T(8,128)(2,1)S(1)} %copy-done, f32[80,256]{1,0:T(8,128)S(1)} %get-tuple-element.97.centre, f32[80,256]{1,0:T(8,128)S(1)} %get-tuple-element.98.lower, ...), custom_call_target="tpu_custom_call" | custom-call | tf_op jit(solution)/shard_map/cube_change/pallas_call | solution.py:879
  20.8 1.5 %collective-permute-start.2 = (bf16[320,128]{1,0:T(8,128)(2,1)S(1)}, bf16[320,128]{1,0:T(8,128)(2,1)S(1)}, u32[]{:S(2)}, u32[]{:S(2)}) collective-permute-start(bf16[320,128]{1,0:T(8,128)(2,1)S(1)} %cube_change.1), channel_id=1, source_target_pairs={{0,24},{1,25},{2,26},{3,27},{4,28},{5,29},{6,30},{7,31}} | collective-permute-start | bytes 245768 | tf_op jit(solution)/shard_map/ppermute | solution.py:948
  22.2 0.7 collective-permute-start.1
  22.9 0.7 collective-permute-start
  23.6 0.8 collective-permute-done.2
  24.4 0.7 collective-permute-start.8
  25.1 0.7 collective-permute-start.7
  25.8 0.7 collective-permute-start.6
  26.4 26.1 %conditional.2 = ((f32[16,32,384]{2,1,0:T(8,128)S(1)}, f32[2,5,32,384]{3,2,1,0:T(8,128)}, f32[5,16,384]{2,1,0:T(8,128)S(1)}, f32[5,16,384]{2,1,0:T(8,128)S(1)})) conditional(s32[]{:T(128)} %convert_element_type.10, (f32[8,128]{1,0:T(8,128)S(1)}, s32[6]{0:T(128)S(1)}, f32[5,16,32,384]{3,2,1,0:T(8,128)}) %tuple.47, () %tuple.32), branch_computations={%region_1.2_spmd, %region_2.3_spmd} | conditional | bytes 1523768 | solution.py:978
  26.5 26.1 %brick_viscosity.1 = (f32[16,32,384]{2,1,0:T(8,128)S(1)}, f32[2,5,32,384]{3,2,1,0:T(8,128)}, f32[5,16,384]{2,1,0:T(8,128)S(1)}, f32[5,16,384]{2,1,0:T(8,128)S(1)}) custom-call(f32[8,128]{1,0:T(8,128)S(1)} %get-tuple-element.43.closure, s32[6]{0:T(128)S(1)} %get-tuple-element.44.place, f32[5,16,32,384]{3,2,1,0:T(8,128)} %get-tuple-element.45.fields), custom_call_target="tpu_custom_call" | custom-call | tf_op jit(solution)/shard_map/cond/branch_0_fun/brick_viscosity/pallas_call | solution.py:530
  52.5 0.6 copy-done.8
  53.2 2.5 %collective-permute-start.3 = (f32[2,5,32,384]{3,2,1,0:T(8,128)}, f32[2,5,32,384]{3,2,1,0:T(8,128)S(1)}, u32[]{:S(2)}, u32[]{:S(2)}) collective-permute-start(f32[2,5,32,384]{3,2,1,0:T(8,128)} %get-tuple-element.104), channel_id=1, source_target_pairs={{0,4},{1,5},{2,6},{3,7},{4,0},{5,1},{6,2},{7,3},{8,12},{9,13},{10,... | collective-permute-start | bytes 1474568 | tf_op jit(solution)/shard_map/ppermute | solution.py:933
  55.7 0.7 pick_cubes.1
  56.5 1.4 %collective-permute-start.9 = (bf16[6,320,128]{2,1,0:T(8,128)(2,1)S(1)}, bf16[6,320,128]{2,1,0:T(8,128)(2,1)}, u32[]{:S(2)}, u32[]{:S(2)}) collective-permute-start(bf16[6,320,128]{2,1,0:T(8,128)(2,1)S(1)} %pick_cubes.1), channel_id=1, source_target_pairs={{24,28},{25,29},{26,30},{27,31},{28,24},{29,25},{30,26},{31,27}} | collective-permute-start | bytes 1474568 | tf_op jit(solution)/shard_map/ppermute | solution.py:959
  57.9 2.5 %collective-permute-start.4 = (f32[5,16,384]{2,1,0:T(8,128)}, f32[5,16,384]{2,1,0:T(8,128)}, u32[]{:S(2)}, u32[]{:S(2)}) collective-permute-start(f32[5,16,384]{2,1,0:T(8,128)} %copy-done.8), channel_id=1, source_target_pairs={{0,1},{1,0},{2,3},{3,2},{4,5},{5,4},{6,7},{7,6},{8,9},{9,8},{10,11... | collective-permute-start | bytes 368648 | tf_op jit(solution)/shard_map/ppermute | solution.py:939
  60.5 4.2 %collective-permute-start.5 = (f32[5,16,384]{2,1,0:T(8,128)}, f32[5,16,384]{2,1,0:T(8,128)}, u32[]{:S(2)}, u32[]{:S(2)}) collective-permute-start(f32[5,16,384]{2,1,0:T(8,128)} %copy-done.9), channel_id=1, source_target_pairs={{0,3},{1,2},{2,1},{3,0},{4,7},{5,6},{6,5},{7,4},{8,11},{9,10},{10,... | collective-permute-start | bytes 368648 | tf_op jit(solution)/shard_map/ppermute | solution.py:940
  64.7 0.1 dynamic_slice.10
  64.8 0.8 dynamic_slice.9
  65.6 0.3 collective-permute-done.4
  65.9 4.2 %collective-permute-done.5 = f32[5,16,384]{2,1,0:T(8,128)} collective-permute-done((f32[5,16,384]{2,1,0:T(8,128)}, f32[5,16,384]{2,1,0:T(8,128)}, u32[]{:S(2)}, u32[]{:S(2)}) %collective-permute-start.5) | collective-permute-done | bytes 122912 | tf_op jit(solution)/shard_map/ppermute | solution.py:940
  70.1 9.0 %conditional.3 = (f32[17280]{0:T(1024)S(1)}, f32[1,5,16,32,384]{4,3,2,1,0:T(8,128)}) conditional(s32[]{:T(128)} %convert_element_type.10, (s32[6]{0:T(128)S(1)}, f32[16,32,384]{2,1,0:T(8,128)S(1)}, f32[5,16,32,384]{3,2,1,0:T(8,128)}, f32[2,5,32,384]{3,2,1,0:T(8,128)S(1)}, f32[5,16,384]{2,1,0:T(8,128)}, /*index=5*/f32[5,16,384]{2,1,0:T(8,128)}) %tuple.48, ...), branch_computations={%region_3.4_spmd, %region_4.5_spmd} | conditional | flops 17280 | bytes 345616 | solution.py:1016
  70.1 9.0 %evolve_brick.1 = f32[5,16,32,384]{3,2,1,0:T(8,128)} custom-call(s32[6]{0:T(128)S(1)} %get-tuple-element.46.place, f32[16,32,384]{2,1,0:T(8,128)S(1)} %get-tuple-element.47.viscosity, f32[5,16,32,384]{3,2,1,0:T(8,128)} %get-tuple-element.48.fields, f32[2,5,32,384]{3,2,1,0:T(8,128)S(1)} %get-tuple-element.49.x_halo, f32[5,16,384]{2,1,0:T(8,128)} %get-tuple-element.50.y_first, ...), custom_call_target="tpu_custom_call" | custom-call | tf_op jit(solution)/shard_map/cond/branch_0_fun/evolve_brick/pallas_call | solution.py:601
  79.0 1.3 %collective-permute-start.12 = (f32[17280]{0:T(1024)S(1)}, f32[17280]{0:T(1024)S(1)}, u32[]{:S(2)}, u32[]{:S(2)}) collective-permute-start(f32[17280]{0:T(1024)S(1)} %get-tuple-element.115), channel_id=1, source_target_pairs={{24,0},{25,1},{26,2},{27,3},{28,4},{29,5},{30,6},{31,7}} | collective-permute-start | bytes 207368 | tf_op jit(solution)/shard_map/ppermute | solution.py:1020
  80.3 0.7 collective-permute-start.11
  81.0 0.7 collective-permute-start.10
  81.7 3.0 %collective-permute-done.12 = f32[17280]{0:T(1024)S(1)} collective-permute-done((f32[17280]{0:T(1024)S(1)}, f32[17280]{0:T(1024)S(1)}, u32[]{:S(2)}, u32[]{:S(2)}) %collective-permute-start.12) | collective-permute-done | bytes 69152 | tf_op jit(solution)/shard_map/ppermute | solution.py:1020
  84.7 4.9 %collective-permute-start.14 = (f32[17280]{0:T(1024)S(1)}, f32[17280]{0:T(1024)S(1)}, u32[]{:S(2)}, u32[]{:S(2)}) collective-permute-start(f32[17280]{0:T(1024)S(1)} %add_add_fusion.1), channel_id=1, source_target_pairs={{0,5},{1,4},{2,7},{3,6},{4,1},{5,0},{6,3},{7,2},{8,14},{9,15},{10,... | collective-permute-start | bytes 207368 | tf_op jit(solution)/shard_map/ppermute | solution.py:1031
  89.6 0.1 collective-permute-start.13
  89.7 2.2 %collective-permute-done.14 = f32[17280]{0:T(1024)S(1)} collective-permute-done((f32[17280]{0:T(1024)S(1)}, f32[17280]{0:T(1024)S(1)}, u32[]{:S(2)}, u32[]{:S(2)}) %collective-permute-start.14) | collective-permute-done | bytes 69152 | tf_op jit(solution)/shard_map/ppermute | solution.py:1031
  91.9 2.1 %collective-permute-done.13 = f32[17280]{0:T(1024)S(1)} collective-permute-done((f32[17280]{0:T(1024)S(1)}, f32[17280]{0:T(1024)S(1)}, u32[]{:S(2)}, u32[]{:S(2)}) %collective-permute-start.13) | collective-permute-done | bytes 69152 | tf_op jit(solution)/shard_map/ppermute | solution.py:1031
  94.0 2.0 %collective-permute-start.15 = (f32[17280]{0:T(1024)S(1)}, f32[17280]{0:T(1024)S(1)}, u32[]{:S(2)}, u32[]{:S(2)}) collective-permute-start(f32[17280]{0:T(1024)S(1)} %add_add_fusion), channel_id=1, source_target_pairs={{0,8},{1,9},{2,10},{3,11},{4,12},{5,13},{6,14},{7,15},{8,0},{9,1},... | collective-permute-start | bytes 207368 | tf_op jit(solution)/shard_map/ppermute | solution.py:1033
  96.0 0.9 collective-permute-done.15
  96.9 1.5 %collective-permute-start.16 = (f32[17280]{0:T(1024)S(1)}, f32[17280]{0:T(1024)S(1)}, u32[]{:S(2)}, u32[]{:S(2)}) collective-permute-start(f32[17280]{0:T(1024)S(1)} %add.52), channel_id=1, source_target_pairs={{0,16},{1,17},{2,18},{3,19},{4,20},{5,21},{6,22},{7,23},{8,24},{9,... | collective-permute-start | bytes 207368 | tf_op jit(solution)/shard_map/ppermute | solution.py:1033
  98.4 3.0 %collective-permute-done.16 = f32[17280]{0:T(1024)S(1)} collective-permute-done((f32[17280]{0:T(1024)S(1)}, f32[17280]{0:T(1024)S(1)}, u32[]{:S(2)}, u32[]{:S(2)}) %collective-permute-start.16) | collective-permute-done | bytes 69152 | tf_op jit(solution)/shard_map/ppermute | solution.py:1033
  101.4 0.6 multiply_reduce_fusion
  102.7 0.7 multiply_subtract_fusion
  (38 shorter events, 0.2 us)
Async XLA Ops:
  0.7 0.7 copy-start.1
  1.4 10.3 %copy-start.6 = (f32[64,5]{0,1:T(8,128)S(1)}, f32[64,5]{0,1:T(8,128)}, u32[]{:S(2)}) copy-start(f32[64,5]{0,1:T(8,128)} %param.16) | copy-start | bytes 3844
  1.4 10.3 %copy-start.4 = (f32[17280]{0:T(1024)S(1)}, f32[17280]{0:T(1024)}, u32[]{:S(2)}) copy-start(f32[17280]{0:T(1024)} %param.19) | copy-start | bytes 207364
  1.4 10.4 %copy-start.10 = (f32[64]{0:T(128)S(1)}, f32[64]{0:T(128)}, u32[]{:S(2)}) copy-start(f32[64]{0:T(128)} %param.17) | copy-start | bytes 772
  1.4 10.4 %copy-start.2 = (s32[24]{0:T(128)S(1)}, s32[24]{0:T(128)}, u32[]{:S(2)}) copy-start(s32[24]{0:T(128)} %sample_block.5) | copy-start | bytes 292
  4.2 11.2 %copy-start.5 = (f32[64]{0:T(128)S(1)}, f32[64]{0:T(128)}, u32[]{:S(2)}) copy-start(f32[64]{0:T(128)} %param.18) | copy-start | bytes 772
  4.2 15.0 %copy-start = (bf16[256,256]{1,0:T(8,128)(2,1)S(1)}, bf16[256,256]{1,0:T(8,128)(2,1)}, u32[]{:S(2)}) copy-start(bf16[256,256]{1,0:T(8,128)(2,1)} %constant.60.clone.order) | copy-start | bytes 393220
  4.2 14.9 %all-to-all-start = ((f32[8,16,256]{2,1,0:T(8,128)}), f32[8,16,256]{2,1,0:T(8,128)S(1)}, u32[]{:S(2)}, u32[]{:S(2)}) async-start(f32[8,16,256]{2,1,0:T(8,128)} %thin_faces.1), calls=%async_computation | async-start | bytes 262144 | tf_op jit(solution)/shard_map/all_to_all | solution.py:972
  15.4 40.3 %copy-start.7 = (s32[24]{0:T(128)S(1)}, s32[24]{0:T(128)}, u32[]{:S(2)}) copy-start(s32[24]{0:T(128)} %trainer_of.1) | copy-start | bytes 292
  16.0 54.0 %copy-start.3 = (bf16[4,256,240]{2,1,0:T(8,128)(2,1)S(1)}, bf16[4,256,240]{2,1,0:T(8,128)(2,1)}, u32[]{:S(2)}) copy-start(bf16[4,256,240]{2,1,0:T(8,128)(2,1)} %constant.58.clone) | copy-start | bytes 1474564
  20.8 3.6 %collective-permute-start.2 = (bf16[320,128]{1,0:T(8,128)(2,1)S(1)}, bf16[320,128]{1,0:T(8,128)(2,1)S(1)}, u32[]{:S(2)}, u32[]{:S(2)}) collective-permute-start(bf16[320,128]{1,0:T(8,128)(2,1)S(1)} %cube_change.1), channel_id=1, source_target_pairs={{0,24},{1,25},{2,26},{3,27},{4,28},{5,29},{6,30},{7,31}} | collective-permute-start | bytes 245768 | tf_op jit(solution)/shard_map/ppermute | solution.py:948
  22.2 2.1 %collective-permute-start.1 = (bf16[320,128]{1,0:T(8,128)(2,1)S(1)}, bf16[320,128]{1,0:T(8,128)(2,1)S(1)}, u32[]{:S(2)}, u32[]{:S(2)}) collective-permute-start(bf16[320,128]{1,0:T(8,128)(2,1)S(1)} %cube_change.1), channel_id=1, source_target_pairs={{8,24},{9,25},{10,26},{11,27},{12,28},{13,29},{14,30},{15,31}} | collective-permute-start | bytes 245768 | tf_op jit(solution)/shard_map/ppermute | solution.py:948
  22.9 1.5 %collective-permute-start = (bf16[320,128]{1,0:T(8,128)(2,1)S(1)}, bf16[320,128]{1,0:T(8,128)(2,1)S(1)}, u32[]{:S(2)}, u32[]{:S(2)}) collective-permute-start(bf16[320,128]{1,0:T(8,128)(2,1)S(1)} %cube_change.1), channel_id=1, source_target_pairs={{16,24},{17,25},{18,26},{19,27},{20,28},{21,29},{22,30},{23,31}} | collective-permute-start | bytes 245768 | tf_op jit(solution)/shard_map/ppermute | solution.py:948
  24.4 31.3 %collective-permute-start.8 = (bf16[3,320,128]{2,1,0:T(8,128)(2,1)S(1)}, bf16[3,320,128]{2,1,0:T(8,128)(2,1)S(1)}, u32[]{:S(2)}, u32[]{:S(2)}) collective-permute-start(bf16[3,320,128]{2,1,0:T(8,128)(2,1)S(1)} %pad_maximum_fusion.1.refs_0_), channel_id=1, source_target_pairs={{24,27},{25,26},{26,25},{27,24},{28,31},{29,30},{30,29},{31,28}} | collective-permute-start | bytes 737288 | tf_op jit(solution)/shard_map/ppermute | solution.py:956
  25.1 30.6 %collective-permute-start.7 = (bf16[3,320,128]{2,1,0:T(8,128)(2,1)S(1)}, bf16[3,320,128]{2,1,0:T(8,128)(2,1)S(1)}, u32[]{:S(2)}, u32[]{:S(2)}) collective-permute-start(bf16[3,320,128]{2,1,0:T(8,128)(2,1)S(1)} %pad_maximum_fusion.1.refs_0_), channel_id=1, source_target_pairs={{24,26},{25,27},{26,24},{27,25},{28,30},{29,31},{30,28},{31,29}} | collective-permute-start | bytes 737288 | tf_op jit(solution)/shard_map/ppermute | solution.py:956
  25.8 30.0 %collective-permute-start.6 = (bf16[3,320,128]{2,1,0:T(8,128)(2,1)S(1)}, bf16[3,320,128]{2,1,0:T(8,128)(2,1)S(1)}, u32[]{:S(2)}, u32[]{:S(2)}) collective-permute-start(bf16[3,320,128]{2,1,0:T(8,128)(2,1)S(1)} %pad_maximum_fusion.1.refs_0_), channel_id=1, source_target_pairs={{24,25},{25,24},{26,27},{27,26},{28,29},{29,28},{30,31},{31,30}} | collective-permute-start | bytes 737288 | tf_op jit(solution)/shard_map/ppermute | solution.py:956
  52.5 0.6 copy-start.8
  52.5 0.7 copy-start.9
  53.2 16.8 %collective-permute-start.3 = (f32[2,5,32,384]{3,2,1,0:T(8,128)}, f32[2,5,32,384]{3,2,1,0:T(8,128)S(1)}, u32[]{:S(2)}, u32[]{:S(2)}) collective-permute-start(f32[2,5,32,384]{3,2,1,0:T(8,128)} %get-tuple-element.104), channel_id=1, source_target_pairs={{0,4},{1,5},{2,6},{3,7},{4,0},{5,1},{6,2},{7,3},{8,12},{9,13},{10,... | collective-permute-start | bytes 1474568 | tf_op jit(solution)/shard_map/ppermute | solution.py:933
  56.5 13.6 %collective-permute-start.9 = (bf16[6,320,128]{2,1,0:T(8,128)(2,1)S(1)}, bf16[6,320,128]{2,1,0:T(8,128)(2,1)}, u32[]{:S(2)}, u32[]{:S(2)}) collective-permute-start(bf16[6,320,128]{2,1,0:T(8,128)(2,1)S(1)} %pick_cubes.1), channel_id=1, source_target_pairs={{24,28},{25,29},{26,30},{27,31},{28,24},{29,25},{30,26},{31,27}} | collective-permute-start | bytes 1474568 | tf_op jit(solution)/shard_map/ppermute | solution.py:959
  57.9 7.9 %collective-permute-start.4 = (f32[5,16,384]{2,1,0:T(8,128)}, f32[5,16,384]{2,1,0:T(8,128)}, u32[]{:S(2)}, u32[]{:S(2)}) collective-permute-start(f32[5,16,384]{2,1,0:T(8,128)} %copy-done.8), channel_id=1, source_target_pairs={{0,1},{1,0},{2,3},{3,2},{4,5},{5,4},{6,7},{7,6},{8,9},{9,8},{10,11... | collective-permute-start | bytes 368648 | tf_op jit(solution)/shard_map/ppermute | solution.py:939
  60.5 9.6 %collective-permute-start.5 = (f32[5,16,384]{2,1,0:T(8,128)}, f32[5,16,384]{2,1,0:T(8,128)}, u32[]{:S(2)}, u32[]{:S(2)}) collective-permute-start(f32[5,16,384]{2,1,0:T(8,128)} %copy-done.9), channel_id=1, source_target_pairs={{0,3},{1,2},{2,1},{3,0},{4,7},{5,6},{6,5},{7,4},{8,11},{9,10},{10,... | collective-permute-start | bytes 368648 | tf_op jit(solution)/shard_map/ppermute | solution.py:940
  79.0 5.6 %collective-permute-start.12 = (f32[17280]{0:T(1024)S(1)}, f32[17280]{0:T(1024)S(1)}, u32[]{:S(2)}, u32[]{:S(2)}) collective-permute-start(f32[17280]{0:T(1024)S(1)} %get-tuple-element.115), channel_id=1, source_target_pairs={{24,0},{25,1},{26,2},{27,3},{28,4},{29,5},{30,6},{31,7}} | collective-permute-start | bytes 207368 | tf_op jit(solution)/shard_map/ppermute | solution.py:1020
  80.3 4.3 %collective-permute-start.11 = (f32[17280]{0:T(1024)S(1)}, f32[17280]{0:T(1024)S(1)}, u32[]{:S(2)}, u32[]{:S(2)}) collective-permute-start(f32[17280]{0:T(1024)S(1)} %get-tuple-element.115), channel_id=1, source_target_pairs={{24,8},{25,9},{26,10},{27,11},{28,12},{29,13},{30,14},{31,15}} | collective-permute-start | bytes 207368 | tf_op jit(solution)/shard_map/ppermute | solution.py:1020
  81.0 3.7 %collective-permute-start.10 = (f32[17280]{0:T(1024)S(1)}, f32[17280]{0:T(1024)S(1)}, u32[]{:S(2)}, u32[]{:S(2)}) collective-permute-start(f32[17280]{0:T(1024)S(1)} %get-tuple-element.115), channel_id=1, source_target_pairs={{24,16},{25,17},{26,18},{27,19},{28,20},{29,21},{30,22},{31,23}} | collective-permute-start | bytes 207368 | tf_op jit(solution)/shard_map/ppermute | solution.py:1020
  84.7 7.2 %collective-permute-start.14 = (f32[17280]{0:T(1024)S(1)}, f32[17280]{0:T(1024)S(1)}, u32[]{:S(2)}, u32[]{:S(2)}) collective-permute-start(f32[17280]{0:T(1024)S(1)} %add_add_fusion.1), channel_id=1, source_target_pairs={{0,5},{1,4},{2,7},{3,6},{4,1},{5,0},{6,3},{7,2},{8,14},{9,15},{10,... | collective-permute-start | bytes 207368 | tf_op jit(solution)/shard_map/ppermute | solution.py:1031
  89.6 4.4 %collective-permute-start.13 = (f32[17280]{0:T(1024)S(1)}, f32[17280]{0:T(1024)S(1)}, u32[]{:S(2)}, u32[]{:S(2)}) collective-permute-start(f32[17280]{0:T(1024)S(1)} %add_add_fusion.1), channel_id=1, source_target_pairs={{0,1},{1,0},{2,3},{3,2},{4,5},{5,4},{6,7},{7,6},{8,10},{9,11},{10,... | collective-permute-start | bytes 207368 | tf_op jit(solution)/shard_map/ppermute | solution.py:1031
  94.0 2.9 %collective-permute-start.15 = (f32[17280]{0:T(1024)S(1)}, f32[17280]{0:T(1024)S(1)}, u32[]{:S(2)}, u32[]{:S(2)}) collective-permute-start(f32[17280]{0:T(1024)S(1)} %add_add_fusion), channel_id=1, source_target_pairs={{0,8},{1,9},{2,10},{3,11},{4,12},{5,13},{6,14},{7,15},{8,0},{9,1},... | collective-permute-start | bytes 207368 | tf_op jit(solution)/shard_map/ppermute | solution.py:1033
  96.9 4.5 %collective-permute-start.16 = (f32[17280]{0:T(1024)S(1)}, f32[17280]{0:T(1024)S(1)}, u32[]{:S(2)}, u32[]{:S(2)}) collective-permute-start(f32[17280]{0:T(1024)S(1)} %add.52), channel_id=1, source_target_pairs={{0,16},{1,17},{2,18},{3,19},{4,20},{5,21},{6,22},{7,23},{8,24},{9,... | collective-permute-start | bytes 207368 | tf_op jit(solution)/shard_map/ppermute | solution.py:1033

commit v18 on v16

--- a/solution.py
+++ b/solution.py
@@ -462,14 +462,16 @@
     return base_viscosity + viscosity_gain * soft
 
 
-def viscosity_kernel(closure, place, fields, viscosity, x_edges, y_edges, weights, out_column):
+def viscosity_kernel(
+    closure, place, fields, viscosity, x_edges, y_first, y_second, weights, out_column
+):
     y_cells, z_cells = fields.shape[2:]
     x, x_cells = pl.program_id(0), pl.num_programs(0)
     up_first = lax.rem(place[2], 2) == 0
     for f in range(F):
         low, high = fields[f, 0, 0:1, :], fields[f, 0, y_cells - 1 : y_cells, :]
-        y_edges[0, f, pl.ds(x, 1), :] = jnp.where(up_first, high, low)
-        y_edges[1, f, pl.ds(x, 1), :] = jnp.where(up_first, low, high)
+        y_first[f, pl.ds(x, 1), :] = jnp.where(up_first, high, low)
+        y_second[f, pl.ds(x, 1), :] = jnp.where(up_first, low, high)
 
     @pl.when(x == x_cells - 1)
     def _():
@@ -490,7 +492,6 @@
 
     sublane = lax.broadcasted_iota(jnp.int32, (8, z_cells), 0)
     wide = z_cells // 128
-    tiles = y_cells // 8
 
     def tile(index, carry):
         rows = pl.ds(pl.multiple_of(index * 8, 8), 8)
@@ -516,17 +517,20 @@
         viscosity[0, rows, :] = base_viscosity + viscosity_gain * soft
         return carry
 
-    lax.fori_loop(0, tiles, tile, 0)
+    lax.fori_loop(0, y_cells // 8, tile, 0)
 
 
 def brick_viscosity(closure, place, fields):
     count, x_cells, y_cells, z_cells = fields.shape
+    line = jax.ShapeDtypeStruct((count, x_cells, z_cells), fields.dtype)
+    line_spec = pl.BlockSpec(line.shape, lambda x: (0, 0, 0))
     return pl.pallas_call(
         viscosity_kernel,
         out_shape=(
             jax.ShapeDtypeStruct(fields.shape[1:], fields.dtype),
             jax.ShapeDtypeStruct((2, count, y_cells, z_cells), fields.dtype),
-            jax.ShapeDtypeStruct((2, count, x_cells, z_cells), fields.dtype),
+            line,
+            line,
         ),
         grid=(x_cells,),
         in_specs=[
@@ -537,7 +541,8 @@
         out_specs=(
             pl.BlockSpec((1, y_cells, z_cells), lambda x: (x, 0, 0)),
             pl.BlockSpec((2, count, y_cells, z_cells), lambda x: (0, 0, 0, 0)),
-            pl.BlockSpec((2, count, x_cells, z_cells), lambda x: (0, 0, 0, 0)),
+            line_spec,
+            line_spec,
         ),
         scratch_shapes=[
             pltpu.VMEM((8, HID + 8, 32), jnp.bfloat16),
@@ -964,24 +969,30 @@
     landed = to_trainers(payload)
     closure, landed = lax.optimization_barrier((closure, landed))
 
+    share_size = NPARAM // (group_count * trainers)
+    share_start = (my_group * trainers + my_column) * share_size
+
+    def shares():
+        return tuple(
+            lax.dynamic_slice_in_dim(array, share_start, share_size) for array in (momentum, master)
+        )
+
     fields_count, x_cells = brick.shape[:2]
-    viscosity, x_edges, y_edges = lax.cond(
+    viscosity, x_edges, *y_edges, early_shares = lax.cond(
         is_trainer,
         lambda: (
             jnp.zeros((x_cells, y_cells, z_cells), jnp.float32),
             jnp.zeros((2, fields_count, y_cells, z_cells), jnp.float32),
-            jnp.zeros((2, fields_count, x_cells, z_cells), jnp.float32),
+            jnp.zeros((fields_count, x_cells, z_cells), jnp.float32),
+            jnp.zeros((fields_count, x_cells, z_cells), jnp.float32),
+            shares(),
         ),
-        lambda: brick_viscosity(closure, place, brick),
+        lambda: (
+            *brick_viscosity(closure, place, brick),
+            (jnp.zeros((share_size,), jnp.float32),) * 2,
+        ),
     )
-    share_size = NPARAM // (group_count * trainers)
-    share_start = (my_group * trainers + my_column) * share_size
-    momentum_share = lax.dynamic_slice_in_dim(momentum, share_start, share_size)
-    master_share = lax.dynamic_slice_in_dim(master, share_start, share_size)
-    viscosity, momentum_share, master_share = lax.optimization_barrier(
-        (viscosity, momentum_share, master_share)
-    )
-    halo = (x_neighbours(x_edges), *y_neighbours(y_edges[0], y_edges[1]))
+    halo = (x_neighbours(x_edges), *y_neighbours(*y_edges))
     near = [landed, *from_line(landed)]
     far = [
         across(apart, pick_cubes(sample_trainer, place, near, y_devices, x_devices, apart))
@@ -996,13 +1007,13 @@
         delta = jnp.concatenate(
             [delta_first[:, : TAPS * F].reshape(-1), delta_last[: TAPS * F].reshape(-1)]
         )
-        return delta, new_brick
+        return delta, new_brick, early_shares
 
     def evolve_here():
         new_brick = evolve(place, viscosity, brick, *halo)
-        return jnp.zeros((NPARAM,), jnp.float32), new_brick
-
-    delta, new_brick = lax.cond(is_trainer, train_here, evolve_here)
+        return jnp.zeros((NPARAM,), jnp.float32), new_brick, shares()
+
+    delta, new_brick, (momentum_share, master_share) = lax.cond(is_trainer, train_here, evolve_here)
 
     held = delta
     for g in reversed(range(sim_groups)):

time: 105 us -> 106 us (level)
  waiting for transfers between devices: 19.9 us -> 25.2 us
  local copies, waits for them, and re-layouts: 4.48 us -> 2.12 us
  starting transfers between devices: 33.8 us -> 32.4 us
    ppermute x2, starting transfers between devices: 3.85 us -> 0.14 us  [on_device(): lax.ppermute(final, everyone, [(g * trainers + c, (g ^ apart) * trainers...]
    ppermute x3, waiting for transfers between devices: 2.99 us -> 5.45 us  [on_device(): lax.ppermute(delta, everyone, [(first_trainer + c, g * trainers + c) for...]
    ppermute x2, waiting for transfers between devices: 3.41 us -> 5.54 us  [on_device(): lax.ppermute(final, everyone, [(g * trainers + c, (g ^ apart) * trainers...]
    ppermute x1, waiting for transfers between devices: 2.33 us -> 0.44 us  [y_neighbours(): lax.ppermute(for_first, everyone, pairs(0, 1))]
    squeeze x1 -> x0, local copies, waits for them, and re-layouts: 1.68 us -> none  [on_device(): halo = (x_neighbours(x_edges), *y_neighbours(y_edges[0], y_edges[1]))]
    ppermute x3, starting transfers between devices: 2.8 us -> 4.05 us  [to_trainers(): lax.ppermute(payload, everyone, [(g * trainers + c, first_trainer + c) fo...]
    ppermute x2, starting transfers between devices: 4.85 us -> 6.1 us  [on_device(): final = final + lax.ppermute(held, everyone, meets)]
    ppermute x3, waiting for transfers between devices: 0.78 us -> 2.02 us  [to_trainers(): lax.ppermute(payload, everyone, [(g * trainers + c, first_trainer + c) fo...]
  transfers between devices with their start and end apart: 18 -> 18, of which waited for: 9 -> 8; matrix products, arithmetic and copies ran while one was open for 3% -> 1% of each run, Pallas kernels for 28% -> 28%
where the time goes in v18:
time: 106 us; the launch traced here: 105 us
  Pallas kernels  42.3 us (40%)
  starting transfers between devices  32.4 us (31%)
  waiting for transfers between devices  25.2 us (24%)
  local copies, waits for them, and re-layouts  2.12 us (2%)
  between operations  1.71 us (2%)
  other arithmetic  1.58 us (1%)
    pallas_call x1, Pallas kernels, brick_viscosity(): pl.pallas_call(viscosity_kernel, out_shape=(jax.ShapeDtypeStruct(fields.s...  24.9 us
    pallas_call x1, Pallas kernels, evolve(): pl.pallas_call(evolve_kernel, out_shape=jax.ShapeDtypeStruct(fields.shape...  8.61 us
    all_to_all x1, starting transfers between devices, on_device(): lax.all_to_all(thin, ('gx', 'gy'), split_axis=0, concat_axis=0, tiled=True)  7.42 us
    ppermute x2, starting transfers between devices, on_device(): final = final + lax.ppermute(held, everyone, meets)  6.1 us
    ppermute x2, waiting for transfers between devices, on_device(): lax.ppermute(final, everyone, [(g * trainers + c, (g ^ apart) * trainers...  5.54 us
    ppermute x3, waiting for transfers between devices, on_device(): lax.ppermute(delta, everyone, [(first_trainer + c, g * trainers + c) for...  5.45 us
    ppermute x2, waiting for transfers between devices, on_device(): final = final + lax.ppermute(held, everyone, meets)  4.56 us
    ppermute x1, starting transfers between devices, y_neighbours(): lax.ppermute(for_second, everyone, pairs(0, -1))  4.31 us
  transfers between devices with their start and end apart: 18, of which 8 were waited for; matrix products, arithmetic and copies ran while one was open for 1% of the time, Pallas kernels for 28%

profile of v18, /device:TPU:0, one launch (start us, length us, event | category | flops | bytes accessed | tf_op | source)
XLA Modules:
  0.0 105.2 jit_solution(1058124684131141595)
XLA Ops:
  0.6 0.1 stack.27.place
  0.7 0.7 copy-done.1
  1.4 2.8 %thin_faces.1 = f32[8,16,256]{2,1,0:T(8,128)} custom-call(s32[24]{0:T(128)S(1)} %copy-done.1, s32[6]{0:T(128)S(1)} %stack.27.place, f32[2560,384]{1,0:T(8,128)} %bitcast.19, f32[80,32,384]{2,1,0:T(8,128)} %bitcast.20), custom_call_target="tpu_custom_call" | custom-call | tf_op jit(solution)/shard_map/thin_faces/pallas_call | solution.py:690
  4.2 0.0 copy-start.6
  4.2 0.0 copy-start
  4.2 7.4 %all-to-all-start = ((f32[8,16,256]{2,1,0:T(8,128)}), f32[8,16,256]{2,1,0:T(8,128)S(1)}, u32[]{:S(2)}, u32[]{:S(2)}) async-start(f32[8,16,256]{2,1,0:T(8,128)} %thin_faces.1), calls=%async_computation | async-start | bytes 262144 | tf_op jit(solution)/shard_map/all_to_all | solution.py:967
  11.6 0.1 fusion.1
  11.8 3.7 %sample_cube.1 = (f32[80,256]{1,0:T(8,128)S(1)}, f32[80,256]{1,0:T(8,128)S(1)}, f32[80,256]{1,0:T(8,128)S(1)}, f32[2,16,128]{2,1,0:T(8,128)S(1)}) custom-call(s32[24]{0:T(128)S(1)} %copy-done.2, s32[6]{0:T(128)S(1)} %stack.27.place, f32[2560,384]{1,0:T(8,128)} %bitcast.21), custom_call_target="tpu_custom_call" | custom-call | bytes 16000000 | tf_op jit(solution)/shard_map/sample_cube/pallas_call | solution.py:793
  15.5 0.1 reshape.34
  15.6 0.2 slice.31
  15.9 0.1 fusion
  16.0 0.1 copy.15
  16.1 0.1 select_maximum_fusion.closure
  16.2 3.0 %all-to-all-done.thin = f32[8,16,256]{2,1,0:T(8,128)S(1)} async-done(((f32[8,16,256]{2,1,0:T(8,128)}), f32[8,16,256]{2,1,0:T(8,128)S(1)}, u32[]{:S(2)}, u32[]{:S(2)}) %all-to-all-start) | async-done | bytes 131104 | tf_op jit(solution)/shard_map/all_to_all | solution.py:967
  19.2 1.6 %cube_change.1 = bf16[320,128]{1,0:T(8,128)(2,1)S(1)} custom-call(s32[24]{0:T(128)S(1)} %copy-done.2, s32[6]{0:T(128)S(1)} %stack.27.place, f32[8,128]{1,0:T(8,128)S(1)} %select_maximum_fusion.closure, bf16[256,256]{1,0:T(8,128)(2,1)S(1)} %copy-done, f32[80,256]{1,0:T(8,128)S(1)} %get-tuple-element.126.centre, f32[80,256]{1,0:T(8,128)S(1)} %get-tuple-element.127.lower, ...), custom_call_target="tpu_custom_call" | custom-call | tf_op jit(solution)/shard_map/cube_change/pallas_call | solution.py:874
  20.8 0.7 collective-permute-start
  21.4 0.7 collective-permute-start.1
  22.1 2.7 %collective-permute-start.2 = (bf16[320,128]{1,0:T(8,128)(2,1)S(1)}, bf16[320,128]{1,0:T(8,128)(2,1)S(1)}, u32[]{:S(2)}, u32[]{:S(2)}) collective-permute-start(bf16[320,128]{1,0:T(8,128)(2,1)S(1)} %cube_change.1), channel_id=1, source_target_pairs={{0,24},{1,25},{2,26},{3,27},{4,28},{5,29},{6,30},{7,31}} | collective-permute-start | bytes 245768 | tf_op jit(solution)/shard_map/ppermute | solution.py:943
  24.8 2.0 %collective-permute-done.2 = bf16[320,128]{1,0:T(8,128)(2,1)S(1)} collective-permute-done((bf16[320,128]{1,0:T(8,128)(2,1)S(1)}, bf16[320,128]{1,0:T(8,128)(2,1)S(1)}, u32[]{:S(2)}, u32[]{:S(2)}) %collective-permute-start.2) | collective-permute-done | bytes 81952 | tf_op jit(solution)/shard_map/ppermute | solution.py:943
  26.9 0.7 collective-permute-start.6
  27.6 0.7 collective-permute-start.7
  28.3 0.7 collective-permute-start.8
  29.0 24.9 %conditional.2 = (f32[16,32,384]{2,1,0:T(8,128)S(1)}, f32[2,5,32,384]{3,2,1,0:T(8,128)S(1)}, f32[5,16,384]{2,1,0:T(8,128)}, f32[5,16,384]{2,1,0:T(8,128)S(1)}, f32[540]{0:T(1024)S(1)}, /*index=5*/f32[540]{0:T(1024)S(1)}) conditional(s32[]{:T(128)} %convert_element_type.10, (f32[8,128]{1,0:T(8,128)S(1)}, s32[6]{0:T(128)S(1)}, ...), branch_computations={%region_1.2_spmd, %region_2.3_spmd} | conditional | flops 3 | bytes 1532458 | solution.py:981
  29.0 24.9 %brick_viscosity.1 = (f32[16,32,384]{2,1,0:T(8,128)S(1)}, f32[2,5,32,384]{3,2,1,0:T(8,128)S(1)}, f32[5,16,384]{2,1,0:T(8,128)}, f32[5,16,384]{2,1,0:T(8,128)S(1)}) custom-call(f32[8,128]{1,0:T(8,128)S(1)} %get-tuple-element.59.closure, s32[6]{0:T(128)S(1)} %get-tuple-element.60.place, f32[5,16,32,384]{3,2,1,0:T(8,128)} %get-tuple-element.61.fields), custom_call_target="tpu_custom_call" | custom-call | tf_op jit(solution)/shard_map/cond/branch_0_fun/brick_viscosity/pallas_call | solution.py:527
  53.9 2.5 %collective-permute-start.3 = (f32[2,5,32,384]{3,2,1,0:T(8,128)S(1)}, f32[2,5,32,384]{3,2,1,0:T(8,128)S(1)}, u32[]{:S(2)}, u32[]{:S(2)}) collective-permute-start(f32[2,5,32,384]{3,2,1,0:T(8,128)S(1)} %get-tuple-element.132), channel_id=1, source_target_pairs={{0,4},{1,5},{2,6},{3,7},{4,0},{5,1},{6,2},{7,3},{8,12},{9,13},{10,... | collective-permute-start | bytes 1474568 | tf_op jit(solution)/shard_map/ppermute | solution.py:928
  56.4 0.7 pick_cubes.1
  57.1 0.7 collective-permute-start.9
  57.8 2.5 %collective-permute-start.4 = (f32[5,16,384]{2,1,0:T(8,128)}, f32[5,16,384]{2,1,0:T(8,128)S(1)}, u32[]{:S(2)}, u32[]{:S(2)}) collective-permute-start(f32[5,16,384]{2,1,0:T(8,128)} %get-tuple-element.133), channel_id=1, source_target_pairs={{0,1},{1,0},{2,3},{3,2},{4,5},{5,4},{6,7},{7,6},{8,9},{9,8},{10,11... | collective-permute-start | bytes 368648 | tf_op jit(solution)/shard_map/ppermute | solution.py:934
  60.3 4.3 %collective-permute-start.5 = (f32[5,16,384]{2,1,0:T(8,128)}, f32[5,16,384]{2,1,0:T(8,128)S(1)}, u32[]{:S(2)}, u32[]{:S(2)}) collective-permute-start(f32[5,16,384]{2,1,0:T(8,128)} %copy-done.9), channel_id=1, source_target_pairs={{0,3},{1,2},{2,1},{3,0},{4,7},{5,6},{6,5},{7,4},{8,11},{9,10},{10,... | collective-permute-start | bytes 368648 | tf_op jit(solution)/shard_map/ppermute | solution.py:935
  64.6 0.4 collective-permute-done.4
  65.1 4.1 %collective-permute-done.5 = f32[5,16,384]{2,1,0:T(8,128)S(1)} collective-permute-done((f32[5,16,384]{2,1,0:T(8,128)}, f32[5,16,384]{2,1,0:T(8,128)S(1)}, u32[]{:S(2)}, u32[]{:S(2)}) %collective-permute-start.5) | collective-permute-done | bytes 122912 | tf_op jit(solution)/shard_map/ppermute | solution.py:935
  69.2 9.5 %conditional.3 = (f32[17280]{0:T(1024)S(1)}, f32[540]{0:T(1024)S(1)}, f32[540]{0:T(1024)S(1)}, f32[1,5,16,32,384]{4,3,2,1,0:T(8,128)}) conditional(s32[]{:T(128)} %convert_element_type.10, (s32[]{:T(128)}, f32[17280]{0:T(1024)}, f32[17280]{0:T(1024)S(1)}, s32[6]{0:T(128)S(1)}, f32[16,32,384]{2,1,0:T(8,128)S(1)}, ...), branch_computations={%region_3.4_spmd, %region_4.5_spmd} | conditional | flops 17280 | bytes 345632 | solution.py:1016
  69.2 0.8 dynamic_slice.12
  70.0 0.1 dynamic_slice.13
  70.1 8.6 %evolve_brick.1 = f32[5,16,32,384]{3,2,1,0:T(8,128)} custom-call(s32[6]{0:T(128)S(1)} %get-tuple-element.72.place, f32[16,32,384]{2,1,0:T(8,128)S(1)} %get-tuple-element.73.viscosity, f32[5,16,32,384]{3,2,1,0:T(8,128)} %get-tuple-element.74.fields, f32[2,5,32,384]{3,2,1,0:T(8,128)S(1)} %get-tuple-element.75.x_halo, ...), custom_call_target="tpu_custom_call" | custom-call | tf_op jit(solution)/shard_map/cond/branch_0_fun/evolve_brick/pallas_call | solution.py:596
  78.7 0.7 collective-permute-start.10
  79.4 0.7 collective-permute-start.11
  80.1 1.3 %collective-permute-start.12 = (f32[17280]{0:T(1024)S(1)}, f32[17280]{0:T(1024)S(1)}, u32[]{:S(2)}, u32[]{:S(2)}) collective-permute-start(f32[17280]{0:T(1024)S(1)} %get-tuple-element.145), channel_id=1, source_target_pairs={{24,0},{25,1},{26,2},{27,3},{28,4},{29,5},{30,6},{31,7}} | collective-permute-start | bytes 207368 | tf_op jit(solution)/shard_map/ppermute | solution.py:1020
  81.4 5.4 %collective-permute-done.12 = f32[17280]{0:T(1024)S(1)} collective-permute-done((f32[17280]{0:T(1024)S(1)}, f32[17280]{0:T(1024)S(1)}, u32[]{:S(2)}, u32[]{:S(2)}) %collective-permute-start.12) | collective-permute-done | bytes 69152 | tf_op jit(solution)/shard_map/ppermute | solution.py:1020
  86.8 3.6 %collective-permute-start.13 = (f32[17280]{0:T(1024)S(1)}, f32[17280]{0:T(1024)S(1)}, u32[]{:S(2)}, u32[]{:S(2)}) collective-permute-start(f32[17280]{0:T(1024)S(1)} %add_add_fusion.1), channel_id=1, source_target_pairs={{0,1},{1,0},{2,3},{3,2},{4,5},{5,4},{6,7},{7,6},{8,10},{9,11},{10,... | collective-permute-start | bytes 207368 | tf_op jit(solution)/shard_map/ppermute | solution.py:1031
  90.4 2.5 %collective-permute-start.14 = (f32[17280]{0:T(1024)S(1)}, f32[17280]{0:T(1024)S(1)}, u32[]{:S(2)}, u32[]{:S(2)}) collective-permute-start(f32[17280]{0:T(1024)S(1)} %add_add_fusion.1), channel_id=1, source_target_pairs={{0,5},{1,4},{2,7},{3,6},{4,1},{5,0},{6,3},{7,2},{8,14},{9,15},{10,... | collective-permute-start | bytes 207368 | tf_op jit(solution)/shard_map/ppermute | solution.py:1031
  93.0 4.6 %collective-permute-done.14 = f32[17280]{0:T(1024)S(1)} collective-permute-done((f32[17280]{0:T(1024)S(1)}, f32[17280]{0:T(1024)S(1)}, u32[]{:S(2)}, u32[]{:S(2)}) %collective-permute-start.14) | collective-permute-done | bytes 69152 | tf_op jit(solution)/shard_map/ppermute | solution.py:1031
  97.5 0.1 collective-permute-start.15
  97.6 1.2 %collective-permute-done.15 = f32[17280]{0:T(1024)S(1)} collective-permute-done((f32[17280]{0:T(1024)S(1)}, f32[17280]{0:T(1024)S(1)}, u32[]{:S(2)}, u32[]{:S(2)}) %collective-permute-start.15) | collective-permute-done | bytes 69152 | tf_op jit(solution)/shard_map/ppermute | solution.py:1033
  98.9 0.1 collective-permute-start.16
  99.0 4.3 %collective-permute-done.16 = f32[17280]{0:T(1024)S(1)} collective-permute-done((f32[17280]{0:T(1024)S(1)}, f32[17280]{0:T(1024)S(1)}, u32[]{:S(2)}, u32[]{:S(2)}) %collective-permute-start.16) | collective-permute-done | bytes 69152 | tf_op jit(solution)/shard_map/ppermute | solution.py:1033
  103.2 0.6 multiply_reduce_fusion
  104.6 0.7 multiply_subtract_fusion
  (40 shorter events, 0.2 us)
Async XLA Ops:
  0.7 0.7 copy-start.1
  1.4 10.3 %copy-start.5 = (f32[17280]{0:T(1024)S(1)}, f32[17280]{0:T(1024)}, u32[]{:S(2)}) copy-start(f32[17280]{0:T(1024)} %param.19) | copy-start | bytes 207364
  1.4 10.3 %copy-start.7 = (f32[64,5]{0,1:T(8,128)S(1)}, f32[64,5]{0,1:T(8,128)}, u32[]{:S(2)}) copy-start(f32[64,5]{0,1:T(8,128)} %param.16) | copy-start | bytes 3844
  1.4 10.4 %copy-start.10 = (f32[64]{0:T(128)S(1)}, f32[64]{0:T(128)}, u32[]{:S(2)}) copy-start(f32[64]{0:T(128)} %param.17) | copy-start | bytes 772
  1.4 10.4 %copy-start.2 = (s32[24]{0:T(128)S(1)}, s32[24]{0:T(128)}, u32[]{:S(2)}) copy-start(s32[24]{0:T(128)} %sample_block.5) | copy-start | bytes 292
  4.2 11.7 %copy-start.6 = (f32[64]{0:T(128)S(1)}, f32[64]{0:T(128)}, u32[]{:S(2)}) copy-start(f32[64]{0:T(128)} %param.18) | copy-start | bytes 772
  4.2 15.0 %copy-start = (bf16[256,256]{1,0:T(8,128)(2,1)S(1)}, bf16[256,256]{1,0:T(8,128)(2,1)}, u32[]{:S(2)}) copy-start(bf16[256,256]{1,0:T(8,128)(2,1)} %constant.70.clone.order) | copy-start | bytes 393220
  4.2 14.9 %all-to-all-start = ((f32[8,16,256]{2,1,0:T(8,128)}), f32[8,16,256]{2,1,0:T(8,128)S(1)}, u32[]{:S(2)}, u32[]{:S(2)}) async-start(f32[8,16,256]{2,1,0:T(8,128)} %thin_faces.1), calls=%async_computation | async-start | bytes 262144 | tf_op jit(solution)/shard_map/all_to_all | solution.py:967
  15.5 40.9 %copy-start.8 = (s32[24]{0:T(128)S(1)}, s32[24]{0:T(128)}, u32[]{:S(2)}) copy-start(s32[24]{0:T(128)} %trainer_of.1) | copy-start | bytes 292
  16.2 53.1 %copy-start.3 = (bf16[4,256,240]{2,1,0:T(8,128)(2,1)S(1)}, bf16[4,256,240]{2,1,0:T(8,128)(2,1)}, u32[]{:S(2)}) copy-start(bf16[4,256,240]{2,1,0:T(8,128)(2,1)} %constant.68.clone) | copy-start | bytes 1474564
  16.2 53.1 %copy-start.4 = (bf16[256,256]{1,0:T(8,128)(2,1)S(1)}, bf16[256,256]{1,0:T(8,128)(2,1)}, u32[]{:S(2)}) copy-start(bf16[256,256]{1,0:T(8,128)(2,1)} %constant.69.clone) | copy-start | bytes 393220
  20.8 4.1 %collective-permute-start = (bf16[320,128]{1,0:T(8,128)(2,1)S(1)}, bf16[320,128]{1,0:T(8,128)(2,1)S(1)}, u32[]{:S(2)}, u32[]{:S(2)}) collective-permute-start(bf16[320,128]{1,0:T(8,128)(2,1)S(1)} %cube_change.1), channel_id=1, source_target_pairs={{16,24},{17,25},{18,26},{19,27},{20,28},{21,29},{22,30},{23,31}} | collective-permute-start | bytes 245768 | tf_op jit(solution)/shard_map/ppermute | solution.py:943
  21.4 3.4 %collective-permute-start.1 = (bf16[320,128]{1,0:T(8,128)(2,1)S(1)}, bf16[320,128]{1,0:T(8,128)(2,1)S(1)}, u32[]{:S(2)}, u32[]{:S(2)}) collective-permute-start(bf16[320,128]{1,0:T(8,128)(2,1)S(1)} %cube_change.1), channel_id=1, source_target_pairs={{8,24},{9,25},{10,26},{11,27},{12,28},{13,29},{14,30},{15,31}} | collective-permute-start | bytes 245768 | tf_op jit(solution)/shard_map/ppermute | solution.py:943
  22.1 4.8 %collective-permute-start.2 = (bf16[320,128]{1,0:T(8,128)(2,1)S(1)}, bf16[320,128]{1,0:T(8,128)(2,1)S(1)}, u32[]{:S(2)}, u32[]{:S(2)}) collective-permute-start(bf16[320,128]{1,0:T(8,128)(2,1)S(1)} %cube_change.1), channel_id=1, source_target_pairs={{0,24},{1,25},{2,26},{3,27},{4,28},{5,29},{6,30},{7,31}} | collective-permute-start | bytes 245768 | tf_op jit(solution)/shard_map/ppermute | solution.py:943
  26.9 29.4 %collective-permute-start.6 = (bf16[3,320,128]{2,1,0:T(8,128)(2,1)S(1)}, bf16[3,320,128]{2,1,0:T(8,128)(2,1)S(1)}, u32[]{:S(2)}, u32[]{:S(2)}) collective-permute-start(bf16[3,320,128]{2,1,0:T(8,128)(2,1)S(1)} %pad_maximum_fusion.1.refs_0_), channel_id=1, source_target_pairs={{24,25},{25,24},{26,27},{27,26},{28,29},{29,28},{30,31},{31,30}} | collective-permute-start | bytes 737288 | tf_op jit(solution)/shard_map/ppermute | solution.py:951
  27.6 28.8 %collective-permute-start.7 = (bf16[3,320,128]{2,1,0:T(8,128)(2,1)S(1)}, bf16[3,320,128]{2,1,0:T(8,128)(2,1)S(1)}, u32[]{:S(2)}, u32[]{:S(2)}) collective-permute-start(bf16[3,320,128]{2,1,0:T(8,128)(2,1)S(1)} %pad_maximum_fusion.1.refs_0_), channel_id=1, source_target_pairs={{24,26},{25,27},{26,24},{27,25},{28,30},{29,31},{30,28},{31,29}} | collective-permute-start | bytes 737288 | tf_op jit(solution)/shard_map/ppermute | solution.py:951
  28.3 28.1 %collective-permute-start.8 = (bf16[3,320,128]{2,1,0:T(8,128)(2,1)S(1)}, bf16[3,320,128]{2,1,0:T(8,128)(2,1)S(1)}, u32[]{:S(2)}, u32[]{:S(2)}) collective-permute-start(bf16[3,320,128]{2,1,0:T(8,128)(2,1)S(1)} %pad_maximum_fusion.1.refs_0_), channel_id=1, source_target_pairs={{24,27},{25,26},{26,25},{27,24},{28,31},{29,30},{30,29},{31,28}} | collective-permute-start | bytes 737288 | tf_op jit(solution)/shard_map/ppermute | solution.py:951
  53.9 3.9 %copy-start.9 = (f32[5,16,384]{2,1,0:T(8,128)}, f32[5,16,384]{2,1,0:T(8,128)S(1)}, u32[]{:S(2)}) copy-start(f32[5,16,384]{2,1,0:T(8,128)S(1)} %get-tuple-element.134) | copy-start | bytes 368644
  53.9 15.3 %collective-permute-start.3 = (f32[2,5,32,384]{3,2,1,0:T(8,128)S(1)}, f32[2,5,32,384]{3,2,1,0:T(8,128)S(1)}, u32[]{:S(2)}, u32[]{:S(2)}) collective-permute-start(f32[2,5,32,384]{3,2,1,0:T(8,128)S(1)} %get-tuple-element.132), channel_id=1, source_target_pairs={{0,4},{1,5},{2,6},{3,7},{4,0},{5,1},{6,2},{7,3},{8,12},{9,13},{10,... | collective-permute-start | bytes 1474568 | tf_op jit(solution)/shard_map/ppermute | solution.py:928
  57.1 12.1 %collective-permute-start.9 = (bf16[6,320,128]{2,1,0:T(8,128)(2,1)S(1)}, bf16[6,320,128]{2,1,0:T(8,128)(2,1)S(1)}, u32[]{:S(2)}, u32[]{:S(2)}) collective-permute-start(bf16[6,320,128]{2,1,0:T(8,128)(2,1)S(1)} %pick_cubes.1), channel_id=1, source_target_pairs={{24,28},{25,29},{26,30},{27,31},{28,24},{29,25},{30,26},{31,27}} | collective-permute-start | bytes 1474568 | tf_op jit(solution)/shard_map/ppermute | solution.py:954
  57.8 7.3 %collective-permute-start.4 = (f32[5,16,384]{2,1,0:T(8,128)}, f32[5,16,384]{2,1,0:T(8,128)S(1)}, u32[]{:S(2)}, u32[]{:S(2)}) collective-permute-start(f32[5,16,384]{2,1,0:T(8,128)} %get-tuple-element.133), channel_id=1, source_target_pairs={{0,1},{1,0},{2,3},{3,2},{4,5},{5,4},{6,7},{7,6},{8,9},{9,8},{10,11... | collective-permute-start | bytes 368648 | tf_op jit(solution)/shard_map/ppermute | solution.py:934
  60.3 8.9 %collective-permute-start.5 = (f32[5,16,384]{2,1,0:T(8,128)}, f32[5,16,384]{2,1,0:T(8,128)S(1)}, u32[]{:S(2)}, u32[]{:S(2)}) collective-permute-start(f32[5,16,384]{2,1,0:T(8,128)} %copy-done.9), channel_id=1, source_target_pairs={{0,3},{1,2},{2,1},{3,0},{4,7},{5,6},{6,5},{7,4},{8,11},{9,10},{10,... | collective-permute-start | bytes 368648 | tf_op jit(solution)/shard_map/ppermute | solution.py:935
  78.7 2.6 %collective-permute-start.10 = (f32[17280]{0:T(1024)S(1)}, f32[17280]{0:T(1024)S(1)}, u32[]{:S(2)}, u32[]{:S(2)}) collective-permute-start(f32[17280]{0:T(1024)S(1)} %get-tuple-element.145), channel_id=1, source_target_pairs={{24,16},{25,17},{26,18},{27,19},{28,20},{29,21},{30,22},{31,23}} | collective-permute-start | bytes 207368 | tf_op jit(solution)/shard_map/ppermute | solution.py:1020
  79.4 2.0 %collective-permute-start.11 = (f32[17280]{0:T(1024)S(1)}, f32[17280]{0:T(1024)S(1)}, u32[]{:S(2)}, u32[]{:S(2)}) collective-permute-start(f32[17280]{0:T(1024)S(1)} %get-tuple-element.145), channel_id=1, source_target_pairs={{24,8},{25,9},{26,10},{27,11},{28,12},{29,13},{30,14},{31,15}} | collective-permute-start | bytes 207368 | tf_op jit(solution)/shard_map/ppermute | solution.py:1020
  80.1 6.8 %collective-permute-start.12 = (f32[17280]{0:T(1024)S(1)}, f32[17280]{0:T(1024)S(1)}, u32[]{:S(2)}, u32[]{:S(2)}) collective-permute-start(f32[17280]{0:T(1024)S(1)} %get-tuple-element.145), channel_id=1, source_target_pairs={{24,0},{25,1},{26,2},{27,3},{28,4},{29,5},{30,6},{31,7}} | collective-permute-start | bytes 207368 | tf_op jit(solution)/shard_map/ppermute | solution.py:1020
  86.8 6.1 %collective-permute-start.13 = (f32[17280]{0:T(1024)S(1)}, f32[17280]{0:T(1024)S(1)}, u32[]{:S(2)}, u32[]{:S(2)}) collective-permute-start(f32[17280]{0:T(1024)S(1)} %add_add_fusion.1), channel_id=1, source_target_pairs={{0,1},{1,0},{2,3},{3,2},{4,5},{5,4},{6,7},{7,6},{8,10},{9,11},{10,... | collective-permute-start | bytes 207368 | tf_op jit(solution)/shard_map/ppermute | solution.py:1031
  90.4 7.1 %collective-permute-start.14 = (f32[17280]{0:T(1024)S(1)}, f32[17280]{0:T(1024)S(1)}, u32[]{:S(2)}, u32[]{:S(2)}) collective-permute-start(f32[17280]{0:T(1024)S(1)} %add_add_fusion.1), channel_id=1, source_target_pairs={{0,5},{1,4},{2,7},{3,6},{4,1},{5,0},{6,3},{7,2},{8,14},{9,15},{10,... | collective-permute-start | bytes 207368 | tf_op jit(solution)/shard_map/ppermute | solution.py:1031
  97.5 1.3 %collective-permute-start.15 = (f32[17280]{0:T(1024)S(1)}, f32[17280]{0:T(1024)S(1)}, u32[]{:S(2)}, u32[]{:S(2)}) collective-permute-start(f32[17280]{0:T(1024)S(1)} %add_add_fusion), channel_id=1, source_target_pairs={{0,8},{1,9},{2,10},{3,11},{4,12},{5,13},{6,14},{7,15},{8,0},{9,1},... | collective-permute-start | bytes 207368 | tf_op jit(solution)/shard_map/ppermute | solution.py:1033
  98.9 4.4 %collective-permute-start.16 = (f32[17280]{0:T(1024)S(1)}, f32[17280]{0:T(1024)S(1)}, u32[]{:S(2)}, u32[]{:S(2)}) collective-permute-start(f32[17280]{0:T(1024)S(1)} %add.57), channel_id=1, source_target_pairs={{0,16},{1,17},{2,18},{3,19},{4,20},{5,21},{6,22},{7,23},{8,24},{9,... | collective-permute-start | bytes 207368 | tf_op jit(solution)/shard_map/ppermute | solution.py:1033

commit v19 on v15

--- a/solution.py
+++ b/solution.py
@@ -550,51 +550,45 @@
     row = lax.broadcasted_iota(jnp.int32, (y_cells, z_cells), 0)
     lane = lax.broadcasted_iota(jnp.int32, (y_cells, z_cells), 1)
 
-    x = pl.program_id(0)
-    centre = [fields[f, x] for f in range(F)]
-    below = jnp.maximum(x - 1, 0)
-    above = jnp.minimum(x + 1, x_cells - 1)
-    for f in range(F):
-        value = centre[f]
-        west = jnp.where(x == 0, x_halo[1, f], fields[f, below])
-        east = jnp.where(x == x_cells - 1, x_halo[0, f], fields[f, above])
-        first, second = y_first[f, pl.ds(x, 1), :], y_second[f, pl.ds(x, 1), :]
-        south = jnp.where(
-            row == 0, jnp.where(up_first, second, first), pltpu.roll(value, 1, 0)
-        )
-        north = jnp.where(
-            row == y_cells - 1,
-            jnp.where(up_first, first, second),
-            pltpu.roll(value, y_cells - 1, 0),
-        )
-        lower = jnp.where(lane == 0, 0.0, pltpu.roll(value, 1, 1))
-        upper = jnp.where(lane == z_cells - 1, 0.0, pltpu.roll(value, z_cells - 1, 1))
-        laplacian = east + west + north + south + upper + lower - 6.0 * value
-        advection = (
-            centre[0] * (east - west) + centre[1] * (north - south) + centre[2] * (upper - lower)
-        )
-        tendency = viscosity[0] * laplacian - 0.5 * advection
-        if f == 2:
-            tendency = tendency + buoyancy * centre[3]
-        new_fields[f, 0] = value + time_step * tendency
+    def plane(x, carry):
+        centre = [fields[f, x] for f in range(F)]
+        below = jnp.maximum(x - 1, 0)
+        above = jnp.minimum(x + 1, x_cells - 1)
+        for f in range(F):
+            value = centre[f]
+            west = jnp.where(x == 0, x_halo[1, f], fields[f, below])
+            east = jnp.where(x == x_cells - 1, x_halo[0, f], fields[f, above])
+            first, second = y_first[f, pl.ds(x, 1), :], y_second[f, pl.ds(x, 1), :]
+            south = jnp.where(
+                row == 0, jnp.where(up_first, second, first), pltpu.roll(value, 1, 0)
+            )
+            north = jnp.where(
+                row == y_cells - 1,
+                jnp.where(up_first, first, second),
+                pltpu.roll(value, y_cells - 1, 0),
+            )
+            lower = jnp.where(lane == 0, 0.0, pltpu.roll(value, 1, 1))
+            upper = jnp.where(lane == z_cells - 1, 0.0, pltpu.roll(value, z_cells - 1, 1))
+            laplacian = east + west + north + south + upper + lower - 6.0 * value
+            advection = (
+                centre[0] * (east - west) + centre[1] * (north - south) + centre[2] * (upper - lower)
+            )
+            tendency = viscosity[x] * laplacian - 0.5 * advection
+            if f == 2:
+                tendency = tendency + buoyancy * centre[3]
+            new_fields[f, x] = value + time_step * tendency
+        return carry
+
+    lax.fori_loop(0, x_cells, plane, 0)
 
 
 def evolve(place, viscosity, fields, x_halo, y_first, y_second):
-    count, x_cells, y_cells, z_cells = fields.shape
-
-    def whole(shape):
-        return pl.BlockSpec(shape, lambda x: (0,) * len(shape), pipeline_mode=pl.Buffered(1))
-
+    vmem = pl.BlockSpec(memory_space=pltpu.VMEM)
     return pl.pallas_call(
         evolve_kernel,
         out_shape=jax.ShapeDtypeStruct(fields.shape, fields.dtype),
-        grid=(x_cells,),
-        in_specs=[
-            pl.BlockSpec(memory_space=pltpu.SMEM),
-            pl.BlockSpec((1, y_cells, z_cells), lambda x: (x, 0, 0)),
-            *[whole(array.shape) for array in (fields, x_halo, y_first, y_second)],
-        ],
-        out_specs=pl.BlockSpec((count, 1, y_cells, z_cells), lambda x: (0, x, 0, 0)),
+        in_specs=[pl.BlockSpec(memory_space=pltpu.SMEM)] + [vmem] * 5,
+        out_specs=vmem,
         compiler_params=pltpu.CompilerParams(vmem_limit_bytes=16 * 1024 * 1024),
         name="evolve_brick",
     )(place, viscosity, fields, x_halo, y_first, y_second)

time: 104 us -> 103 us (level)
  Pallas kernels: 44.2 us -> 42.5 us
    ppermute x2, starting transfers between devices: 3.84 us -> 5.59 us  [on_device(): lax.ppermute(final, everyone, [(g * trainers + c, (g ^ apart) * trainers...]
    pallas_call x1, Pallas kernels: 10.4 us -> 8.75 us  [evolve(): pl.pallas_call(evolve_kernel, out_shape=jax.ShapeDtypeStruct(fields.shape...]
    ppermute x2, waiting for transfers between devices: 4.15 us -> 3.11 us  [on_device(): final = final + lax.ppermute(held, everyone, meets)]
where the time goes in v19:
time: 103 us; the launch traced here: 102 us
  Pallas kernels  42.5 us (41%)
  starting transfers between devices  34.1 us (33%)
  waiting for transfers between devices  20.1 us (20%)
  other arithmetic  2.29 us (2%)
  between operations  1.66 us (2%)
  local copies, waits for them, and re-layouts  1.28 us (1%)
    pallas_call x1, Pallas kernels, brick_viscosity(): pl.pallas_call(viscosity_kernel, out_shape=(jax.ShapeDtypeStruct(fields.s...  25 us
    pallas_call x1, Pallas kernels, evolve(): pl.pallas_call(evolve_kernel, out_shape=jax.ShapeDtypeStruct(fields.shape...  8.75 us
    all_to_all x1, starting transfers between devices, on_device(): lax.all_to_all(thin, ('gx', 'gy'), split_axis=0, concat_axis=0, tiled=True)  7.42 us
    ppermute x2, starting transfers between devices, on_device(): lax.ppermute(final, everyone, [(g * trainers + c, (g ^ apart) * trainers...  5.59 us
    ppermute x1, starting transfers between devices, y_neighbours(): lax.ppermute(for_second, everyone, pairs(0, -1))  4.33 us
    ppermute x2, starting transfers between devices, on_device(): final = final + lax.ppermute(held, everyone, meets)  4.11 us
    ppermute x3, waiting for transfers between devices, on_device(): lax.ppermute(delta, everyone, [(first_trainer + c, g * trainers + c) for...  3.77 us
    pallas_call x1, Pallas kernels, sample_cube(): pl.pallas_call(functools.partial(sample_kernel, y_cells, z_cells), out_sh...  3.63 us
  transfers between devices with their start and end apart: 18, of which 9 were waited for; matrix products, arithmetic and copies ran while one was open for 1% of the time, Pallas kernels for 29%

profile of v19, /device:TPU:0, one launch (start us, length us, event | category | flops | bytes accessed | tf_op | source)
XLA Modules:
  0.0 101.9 jit_solution(11361651610100702055)
XLA Ops:
  0.6 0.1 stack.27.place
  0.7 0.7 copy-done.1
  1.4 2.8 %thin_faces.1 = f32[8,16,256]{2,1,0:T(8,128)} custom-call(s32[24]{0:T(128)S(1)} %copy-done.1, s32[6]{0:T(128)S(1)} %stack.27.place, f32[2560,384]{1,0:T(8,128)} %bitcast.23, f32[80,32,384]{2,1,0:T(8,128)} %bitcast.24), custom_call_target="tpu_custom_call" | custom-call | tf_op jit(solution)/shard_map/thin_faces/pallas_call | solution.py:681
  4.2 0.0 copy-start.6
  4.2 0.0 copy-start
  4.2 7.4 %all-to-all-start = ((f32[8,16,256]{2,1,0:T(8,128)}), f32[8,16,256]{2,1,0:T(8,128)S(1)}, u32[]{:S(2)}, u32[]{:S(2)}) async-start(f32[8,16,256]{2,1,0:T(8,128)} %thin_faces.1), calls=%async_computation | async-start | bytes 262144 | tf_op jit(solution)/shard_map/all_to_all | solution.py:958
  11.7 0.1 fusion.1
  11.8 3.6 %sample_cube.1 = (f32[80,256]{1,0:T(8,128)S(1)}, f32[80,256]{1,0:T(8,128)S(1)}, f32[80,256]{1,0:T(8,128)S(1)}, f32[2,16,128]{2,1,0:T(8,128)S(1)}) custom-call(s32[24]{0:T(128)S(1)} %copy-done.2, s32[6]{0:T(128)S(1)} %stack.27.place, f32[2560,384]{1,0:T(8,128)} %bitcast.25), custom_call_target="tpu_custom_call" | custom-call | bytes 16000000 | tf_op jit(solution)/shard_map/sample_cube/pallas_call | solution.py:784
  15.4 0.0 copy-start.8
  15.4 0.1 fusion
  15.6 0.1 copy.15
  15.6 0.1 reshape.34
  15.7 0.2 slice.37
  16.0 0.1 select_maximum_fusion.closure
  16.0 3.1 %all-to-all-done.thin = f32[8,16,256]{2,1,0:T(8,128)S(1)} async-done(((f32[8,16,256]{2,1,0:T(8,128)}), f32[8,16,256]{2,1,0:T(8,128)S(1)}, u32[]{:S(2)}, u32[]{:S(2)}) %all-to-all-start) | async-done | bytes 131104 | tf_op jit(solution)/shard_map/all_to_all | solution.py:958
  19.2 1.6 %cube_change.1 = bf16[320,128]{1,0:T(8,128)(2,1)S(1)} custom-call(s32[24]{0:T(128)S(1)} %copy-done.2, s32[6]{0:T(128)S(1)} %stack.27.place, f32[8,128]{1,0:T(8,128)S(1)} %select_maximum_fusion.closure, bf16[256,256]{1,0:T(8,128)(2,1)S(1)} %copy-done, f32[80,256]{1,0:T(8,128)S(1)} %get-tuple-element.93.centre, f32[80,256]{1,0:T(8,128)S(1)} %get-tuple-element.94.lower, ...), custom_call_target="tpu_custom_call" | custom-call | tf_op jit(solution)/shard_map/cube_change/pallas_call | solution.py:865
  20.8 1.5 %collective-permute-start.2 = (bf16[320,128]{1,0:T(8,128)(2,1)S(1)}, bf16[320,128]{1,0:T(8,128)(2,1)S(1)}, u32[]{:S(2)}, u32[]{:S(2)}) collective-permute-start(bf16[320,128]{1,0:T(8,128)(2,1)S(1)} %cube_change.1), channel_id=1, source_target_pairs={{0,24},{1,25},{2,26},{3,27},{4,28},{5,29},{6,30},{7,31}} | collective-permute-start | bytes 245768 | tf_op jit(solution)/shard_map/ppermute | solution.py:934
  22.2 0.7 collective-permute-start.1
  22.9 0.7 collective-permute-start
  23.6 0.8 collective-permute-done.2
  24.4 0.8 collective-permute-start.8
  25.2 0.7 collective-permute-start.7
  25.9 0.7 collective-permute-start.6
  26.6 25.0 %conditional.2 = ((f32[16,32,384]{2,1,0:T(8,128)S(1)}, f32[2,5,32,384]{3,2,1,0:T(8,128)}, f32[2,5,16,384]{3,2,1,0:T(8,128)S(1)})) conditional(s32[]{:T(128)} %convert_element_type.10, (f32[8,128]{1,0:T(8,128)S(1)}, s32[6]{0:T(128)S(1)}, f32[5,16,32,384]{3,2,1,0:T(8,128)}) %tuple.46, () %tuple.31), branch_computations={%region_1.2_spmd, %region_2.3_spmd} | conditional | bytes 1523756 | solution.py:964
  26.6 25.0 %brick_viscosity.1 = (f32[16,32,384]{2,1,0:T(8,128)S(1)}, f32[2,5,32,384]{3,2,1,0:T(8,128)}, f32[2,5,16,384]{3,2,1,0:T(8,128)S(1)}) custom-call(f32[8,128]{1,0:T(8,128)S(1)} %get-tuple-element.43.closure, s32[6]{0:T(128)S(1)} %get-tuple-element.44.place, f32[5,16,32,384]{3,2,1,0:T(8,128)} %get-tuple-element.45.fields), custom_call_target="tpu_custom_call" | custom-call | tf_op jit(solution)/shard_map/cond/branch_0_fun/brick_viscosity/pallas_call | solution.py:520
  51.6 2.5 %collective-permute-start.3 = (f32[2,5,32,384]{3,2,1,0:T(8,128)}, f32[2,5,32,384]{3,2,1,0:T(8,128)S(1)}, u32[]{:S(2)}, u32[]{:S(2)}) collective-permute-start(f32[2,5,32,384]{3,2,1,0:T(8,128)} %get-tuple-element.99), channel_id=1, source_target_pairs={{0,4},{1,5},{2,6},{3,7},{4,0},{5,1},{6,2},{7,3},{8,12},{9,13},{10,... | collective-permute-start | bytes 1474568 | tf_op jit(solution)/shard_map/ppermute | solution.py:919
  54.1 0.7 pick_cubes.1
  54.8 0.7 collective-permute-start.9
  55.5 4.3 %collective-permute-start.5 = (f32[5,16,384]{2,1,0:T(8,128)S(1)}, f32[5,16,384]{2,1,0:T(8,128)S(1)}, u32[]{:S(2)}, u32[]{:S(2)}) collective-permute-start(f32[5,16,384]{2,1,0:T(8,128)S(1)} %get-tuple-element.112), channel_id=1, source_target_pairs={{0,3},{1,2},{2,1},{3,0},{4,7},{5,6},{6,5},{7,4},{8,11},{9,10},{10,... | collective-permute-start | bytes 368648 | tf_op jit(solution)/shard_map/ppermute | solution.py:926
  59.9 1.9 %collective-permute-start.4 = (f32[5,16,384]{2,1,0:T(8,128)S(1)}, f32[5,16,384]{2,1,0:T(8,128)S(1)}, u32[]{:S(2)}, u32[]{:S(2)}) collective-permute-start(f32[5,16,384]{2,1,0:T(8,128)S(1)} %get-tuple-element.113), channel_id=1, source_target_pairs={{0,1},{1,0},{2,3},{3,2},{4,5},{5,4},{6,7},{7,6},{8,9},{9,8},{10,11... | collective-permute-start | bytes 368648 | tf_op jit(solution)/shard_map/ppermute | solution.py:925
  61.8 3.6 %collective-permute-done.5 = f32[5,16,384]{2,1,0:T(8,128)S(1)} collective-permute-done((f32[5,16,384]{2,1,0:T(8,128)S(1)}, f32[5,16,384]{2,1,0:T(8,128)S(1)}, u32[]{:S(2)}, u32[]{:S(2)}) %collective-permute-start.5) | collective-permute-done | bytes 122912 | tf_op jit(solution)/shard_map/ppermute | solution.py:926
  65.4 2.3 %collective-permute-done.4 = f32[5,16,384]{2,1,0:T(8,128)S(1)} collective-permute-done((f32[5,16,384]{2,1,0:T(8,128)S(1)}, f32[5,16,384]{2,1,0:T(8,128)S(1)}, u32[]{:S(2)}, u32[]{:S(2)}) %collective-permute-start.4) | collective-permute-done | bytes 122912 | tf_op jit(solution)/shard_map/ppermute | solution.py:925
  67.7 8.8 %conditional.3 = (f32[17280]{0:T(1024)S(1)}, f32[1,5,16,32,384]{4,3,2,1,0:T(8,128)}) conditional(s32[]{:T(128)} %convert_element_type.10, (s32[6]{0:T(128)S(1)}, f32[16,32,384]{2,1,0:T(8,128)S(1)}, f32[5,16,32,384]{3,2,1,0:T(8,128)}, f32[2,5,32,384]{3,2,1,0:T(8,128)S(1)}, f32[5,16,384]{2,1,0:T(8,128)S(1)}, ...), branch_computations={%region_3.4_spmd, %region_4.5_spmd} | conditional | flops 17280 | bytes 345616 | solution.py:994
  67.8 8.8 %evolve_brick.1 = f32[5,16,32,384]{3,2,1,0:T(8,128)} custom-call(s32[6]{0:T(128)S(1)} %get-tuple-element.46.place, f32[16,32,384]{2,1,0:T(8,128)S(1)} %get-tuple-element.47.viscosity, f32[5,16,32,384]{3,2,1,0:T(8,128)} %get-tuple-element.48.fields, f32[2,5,32,384]{3,2,1,0:T(8,128)S(1)} %get-tuple-element.49.x_halo, ...), custom_call_target="tpu_custom_call" | custom-call | tf_op jit(solution)/shard_map/cond/branch_0_fun/evolve_brick/pallas_call | solution.py:587
  76.5 1.3 %collective-permute-start.12 = (f32[17280]{0:T(1024)S(1)}, f32[17280]{0:T(1024)S(1)}, u32[]{:S(2)}, u32[]{:S(2)}) collective-permute-start(f32[17280]{0:T(1024)S(1)} %get-tuple-element.107), channel_id=1, source_target_pairs={{24,0},{25,1},{26,2},{27,3},{28,4},{29,5},{30,6},{31,7}} | collective-permute-start | bytes 207368 | tf_op jit(solution)/shard_map/ppermute | solution.py:998
  77.8 0.7 collective-permute-start.11
  78.5 0.7 collective-permute-start.10
  79.2 3.8 %collective-permute-done.12 = f32[17280]{0:T(1024)S(1)} collective-permute-done((f32[17280]{0:T(1024)S(1)}, f32[17280]{0:T(1024)S(1)}, u32[]{:S(2)}, u32[]{:S(2)}) %collective-permute-start.12) | collective-permute-done | bytes 69152 | tf_op jit(solution)/shard_map/ppermute | solution.py:998
  83.0 2.1 %collective-permute-start.14 = (f32[17280]{0:T(1024)S(1)}, f32[17280]{0:T(1024)S(1)}, u32[]{:S(2)}, u32[]{:S(2)}) collective-permute-start(f32[17280]{0:T(1024)S(1)} %add_add_fusion.1), channel_id=1, source_target_pairs={{0,5},{1,4},{2,7},{3,6},{4,1},{5,0},{6,3},{7,2},{8,14},{9,15},{10,... | collective-permute-start | bytes 207368 | tf_op jit(solution)/shard_map/ppermute | solution.py:1009
  85.1 2.0 %collective-permute-start.13 = (f32[17280]{0:T(1024)S(1)}, f32[17280]{0:T(1024)S(1)}, u32[]{:S(2)}, u32[]{:S(2)}) collective-permute-start(f32[17280]{0:T(1024)S(1)} %add_add_fusion.1), channel_id=1, source_target_pairs={{0,1},{1,0},{2,3},{3,2},{4,5},{5,4},{6,7},{7,6},{8,10},{9,11},{10,... | collective-permute-start | bytes 207368 | tf_op jit(solution)/shard_map/ppermute | solution.py:1009
  87.1 3.0 %collective-permute-done.14 = f32[17280]{0:T(1024)S(1)} collective-permute-done((f32[17280]{0:T(1024)S(1)}, f32[17280]{0:T(1024)S(1)}, u32[]{:S(2)}, u32[]{:S(2)}) %collective-permute-start.14) | collective-permute-done | bytes 69152 | tf_op jit(solution)/shard_map/ppermute | solution.py:1009
  90.1 0.1 collective-permute-done.13
  90.2 1.3 %collective-permute-start.15 = (f32[17280]{0:T(1024)S(1)}, f32[17280]{0:T(1024)S(1)}, u32[]{:S(2)}, u32[]{:S(2)}) collective-permute-start(f32[17280]{0:T(1024)S(1)} %add_add_fusion), channel_id=1, source_target_pairs={{0,8},{1,9},{2,10},{3,11},{4,12},{5,13},{6,14},{7,15},{8,0},{9,1},... | collective-permute-start | bytes 207368 | tf_op jit(solution)/shard_map/ppermute | solution.py:1011
  91.5 0.9 collective-permute-done.15
  92.4 4.3 %collective-permute-start.16 = (f32[17280]{0:T(1024)S(1)}, f32[17280]{0:T(1024)S(1)}, u32[]{:S(2)}, u32[]{:S(2)}) collective-permute-start(f32[17280]{0:T(1024)S(1)} %add.52), channel_id=1, source_target_pairs={{0,16},{1,17},{2,18},{3,19},{4,20},{5,21},{6,22},{7,23},{8,24},{9,... | collective-permute-start | bytes 207368 | tf_op jit(solution)/shard_map/ppermute | solution.py:1011
  96.7 2.5 %collective-permute-done.16 = f32[17280]{0:T(1024)S(1)} collective-permute-done((f32[17280]{0:T(1024)S(1)}, f32[17280]{0:T(1024)S(1)}, u32[]{:S(2)}, u32[]{:S(2)}) %collective-permute-start.16) | collective-permute-done | bytes 69152 | tf_op jit(solution)/shard_map/ppermute | solution.py:1011
  99.2 0.6 multiply_reduce_fusion
  100.5 1.4 %multiply_subtract_fusion = (f32[540]{0:T(1024)}, f32[540]{0:T(1024)}) fusion(f32[17280]{0:T(1024)S(1)} %copy-done.5, s32[]{:T(128)S(6)} %select_n.2, f32[]{:T(128)S(6)} %sqrt.3, f32[17280]{0:T(1024)S(1)} %get-tuple-element.111, f32[17280]{0:T(1024)} %param.20), kind=kLoop, calls=%fused_computation.14 | loop fusion | flops 2700 | bytes 10808 | tf_op jit(solution)/shard_map/sub | solution.py:1024
  (35 shorter events, 0.2 us)
Async XLA Ops:
  0.7 0.7 copy-start.1
  1.4 10.3 %copy-start.7 = (f32[64,5]{0,1:T(8,128)S(1)}, f32[64,5]{0,1:T(8,128)}, u32[]{:S(2)}) copy-start(f32[64,5]{0,1:T(8,128)} %param.16) | copy-start | bytes 3844
  1.4 10.3 %copy-start.5 = (f32[17280]{0:T(1024)S(1)}, f32[17280]{0:T(1024)}, u32[]{:S(2)}) copy-start(f32[17280]{0:T(1024)} %param.19) | copy-start | bytes 207364
  1.4 10.4 %copy-start.9 = (f32[64]{0:T(128)S(1)}, f32[64]{0:T(128)}, u32[]{:S(2)}) copy-start(f32[64]{0:T(128)} %param.17) | copy-start | bytes 772
  1.4 10.4 %copy-start.2 = (s32[24]{0:T(128)S(1)}, s32[24]{0:T(128)}, u32[]{:S(2)}) copy-start(s32[24]{0:T(128)} %sample_block.5) | copy-start | bytes 292
  4.2 11.2 %copy-start.6 = (f32[64]{0:T(128)S(1)}, f32[64]{0:T(128)}, u32[]{:S(2)}) copy-start(f32[64]{0:T(128)} %param.18) | copy-start | bytes 772
  4.2 15.0 %copy-start = (bf16[256,256]{1,0:T(8,128)(2,1)S(1)}, bf16[256,256]{1,0:T(8,128)(2,1)}, u32[]{:S(2)}) copy-start(bf16[256,256]{1,0:T(8,128)(2,1)} %constant.60.clone.order) | copy-start | bytes 393220
  4.2 14.9 %all-to-all-start = ((f32[8,16,256]{2,1,0:T(8,128)}), f32[8,16,256]{2,1,0:T(8,128)S(1)}, u32[]{:S(2)}, u32[]{:S(2)}) async-start(f32[8,16,256]{2,1,0:T(8,128)} %thin_faces.1), calls=%async_computation | async-start | bytes 262144 | tf_op jit(solution)/shard_map/all_to_all | solution.py:958
  15.4 38.7 %copy-start.8 = (s32[24]{0:T(128)S(1)}, s32[24]{0:T(128)}, u32[]{:S(2)}) copy-start(s32[24]{0:T(128)} %trainer_of.1) | copy-start | bytes 292
  20.8 3.6 %collective-permute-start.2 = (bf16[320,128]{1,0:T(8,128)(2,1)S(1)}, bf16[320,128]{1,0:T(8,128)(2,1)S(1)}, u32[]{:S(2)}, u32[]{:S(2)}) collective-permute-start(bf16[320,128]{1,0:T(8,128)(2,1)S(1)} %cube_change.1), channel_id=1, source_target_pairs={{0,24},{1,25},{2,26},{3,27},{4,28},{5,29},{6,30},{7,31}} | collective-permute-start | bytes 245768 | tf_op jit(solution)/shard_map/ppermute | solution.py:934
  22.2 2.1 %collective-permute-start.1 = (bf16[320,128]{1,0:T(8,128)(2,1)S(1)}, bf16[320,128]{1,0:T(8,128)(2,1)S(1)}, u32[]{:S(2)}, u32[]{:S(2)}) collective-permute-start(bf16[320,128]{1,0:T(8,128)(2,1)S(1)} %cube_change.1), channel_id=1, source_target_pairs={{8,24},{9,25},{10,26},{11,27},{12,28},{13,29},{14,30},{15,31}} | collective-permute-start | bytes 245768 | tf_op jit(solution)/shard_map/ppermute | solution.py:934
  22.9 1.5 %collective-permute-start = (bf16[320,128]{1,0:T(8,128)(2,1)S(1)}, bf16[320,128]{1,0:T(8,128)(2,1)S(1)}, u32[]{:S(2)}, u32[]{:S(2)}) collective-permute-start(bf16[320,128]{1,0:T(8,128)(2,1)S(1)} %cube_change.1), channel_id=1, source_target_pairs={{16,24},{17,25},{18,26},{19,27},{20,28},{21,29},{22,30},{23,31}} | collective-permute-start | bytes 245768 | tf_op jit(solution)/shard_map/ppermute | solution.py:934
  24.4 43.4 %copy-start.3 = (bf16[4,256,240]{2,1,0:T(8,128)(2,1)S(1)}, bf16[4,256,240]{2,1,0:T(8,128)(2,1)}, u32[]{:S(2)}) copy-start(bf16[4,256,240]{2,1,0:T(8,128)(2,1)} %constant.59.clone) | copy-start | bytes 1474564
  24.4 43.4 %copy-start.4 = (bf16[4,256,240]{2,1,0:T(8,128)(2,1)S(1)}, bf16[4,256,240]{2,1,0:T(8,128)(2,1)}, u32[]{:S(2)}) copy-start(bf16[4,256,240]{2,1,0:T(8,128)(2,1)} %constant.58.clone) | copy-start | bytes 1474564
  24.4 29.7 %collective-permute-start.8 = (bf16[3,320,128]{2,1,0:T(8,128)(2,1)S(1)}, bf16[3,320,128]{2,1,0:T(8,128)(2,1)S(1)}, u32[]{:S(2)}, u32[]{:S(2)}) collective-permute-start(bf16[3,320,128]{2,1,0:T(8,128)(2,1)S(1)} %pad_maximum_fusion.1.refs_0_), channel_id=1, source_target_pairs={{24,27},{25,26},{26,25},{27,24},{28,31},{29,30},{30,29},{31,28}} | collective-permute-start | bytes 737288 | tf_op jit(solution)/shard_map/ppermute | solution.py:942
  25.2 28.9 %collective-permute-start.7 = (bf16[3,320,128]{2,1,0:T(8,128)(2,1)S(1)}, bf16[3,320,128]{2,1,0:T(8,128)(2,1)S(1)}, u32[]{:S(2)}, u32[]{:S(2)}) collective-permute-start(bf16[3,320,128]{2,1,0:T(8,128)(2,1)S(1)} %pad_maximum_fusion.1.refs_0_), channel_id=1, source_target_pairs={{24,26},{25,27},{26,24},{27,25},{28,30},{29,31},{30,28},{31,29}} | collective-permute-start | bytes 737288 | tf_op jit(solution)/shard_map/ppermute | solution.py:942
  25.9 28.2 %collective-permute-start.6 = (bf16[3,320,128]{2,1,0:T(8,128)(2,1)S(1)}, bf16[3,320,128]{2,1,0:T(8,128)(2,1)S(1)}, u32[]{:S(2)}, u32[]{:S(2)}) collective-permute-start(bf16[3,320,128]{2,1,0:T(8,128)(2,1)S(1)} %pad_maximum_fusion.1.refs_0_), channel_id=1, source_target_pairs={{24,25},{25,24},{26,27},{27,26},{28,29},{29,28},{30,31},{31,30}} | collective-permute-start | bytes 737288 | tf_op jit(solution)/shard_map/ppermute | solution.py:942
  51.6 16.1 %collective-permute-start.3 = (f32[2,5,32,384]{3,2,1,0:T(8,128)}, f32[2,5,32,384]{3,2,1,0:T(8,128)S(1)}, u32[]{:S(2)}, u32[]{:S(2)}) collective-permute-start(f32[2,5,32,384]{3,2,1,0:T(8,128)} %get-tuple-element.99), channel_id=1, source_target_pairs={{0,4},{1,5},{2,6},{3,7},{4,0},{5,1},{6,2},{7,3},{8,12},{9,13},{10,... | collective-permute-start | bytes 1474568 | tf_op jit(solution)/shard_map/ppermute | solution.py:919
  54.8 12.9 %collective-permute-start.9 = (bf16[6,320,128]{2,1,0:T(8,128)(2,1)S(1)}, bf16[6,320,128]{2,1,0:T(8,128)(2,1)S(1)}, u32[]{:S(2)}, u32[]{:S(2)}) collective-permute-start(bf16[6,320,128]{2,1,0:T(8,128)(2,1)S(1)} %pick_cubes.1), channel_id=1, source_target_pairs={{24,28},{25,29},{26,30},{27,31},{28,24},{29,25},{30,26},{31,27}} | collective-permute-start | bytes 1474568 | tf_op jit(solution)/shard_map/ppermute | solution.py:945
  55.5 9.9 %collective-permute-start.5 = (f32[5,16,384]{2,1,0:T(8,128)S(1)}, f32[5,16,384]{2,1,0:T(8,128)S(1)}, u32[]{:S(2)}, u32[]{:S(2)}) collective-permute-start(f32[5,16,384]{2,1,0:T(8,128)S(1)} %get-tuple-element.112), channel_id=1, source_target_pairs={{0,3},{1,2},{2,1},{3,0},{4,7},{5,6},{6,5},{7,4},{8,11},{9,10},{10,... | collective-permute-start | bytes 368648 | tf_op jit(solution)/shard_map/ppermute | solution.py:926
  59.9 7.8 %collective-permute-start.4 = (f32[5,16,384]{2,1,0:T(8,128)S(1)}, f32[5,16,384]{2,1,0:T(8,128)S(1)}, u32[]{:S(2)}, u32[]{:S(2)}) collective-permute-start(f32[5,16,384]{2,1,0:T(8,128)S(1)} %get-tuple-element.113), channel_id=1, source_target_pairs={{0,1},{1,0},{2,3},{3,2},{4,5},{5,4},{6,7},{7,6},{8,9},{9,8},{10,11... | collective-permute-start | bytes 368648 | tf_op jit(solution)/shard_map/ppermute | solution.py:925
  76.5 6.4 %collective-permute-start.12 = (f32[17280]{0:T(1024)S(1)}, f32[17280]{0:T(1024)S(1)}, u32[]{:S(2)}, u32[]{:S(2)}) collective-permute-start(f32[17280]{0:T(1024)S(1)} %get-tuple-element.107), channel_id=1, source_target_pairs={{24,0},{25,1},{26,2},{27,3},{28,4},{29,5},{30,6},{31,7}} | collective-permute-start | bytes 207368 | tf_op jit(solution)/shard_map/ppermute | solution.py:998
  77.8 5.1 %collective-permute-start.11 = (f32[17280]{0:T(1024)S(1)}, f32[17280]{0:T(1024)S(1)}, u32[]{:S(2)}, u32[]{:S(2)}) collective-permute-start(f32[17280]{0:T(1024)S(1)} %get-tuple-element.107), channel_id=1, source_target_pairs={{24,8},{25,9},{26,10},{27,11},{28,12},{29,13},{30,14},{31,15}} | collective-permute-start | bytes 207368 | tf_op jit(solution)/shard_map/ppermute | solution.py:998
  78.5 4.4 %collective-permute-start.10 = (f32[17280]{0:T(1024)S(1)}, f32[17280]{0:T(1024)S(1)}, u32[]{:S(2)}, u32[]{:S(2)}) collective-permute-start(f32[17280]{0:T(1024)S(1)} %get-tuple-element.107), channel_id=1, source_target_pairs={{24,16},{25,17},{26,18},{27,19},{28,20},{29,21},{30,22},{31,23}} | collective-permute-start | bytes 207368 | tf_op jit(solution)/shard_map/ppermute | solution.py:998
  83.0 7.1 %collective-permute-start.14 = (f32[17280]{0:T(1024)S(1)}, f32[17280]{0:T(1024)S(1)}, u32[]{:S(2)}, u32[]{:S(2)}) collective-permute-start(f32[17280]{0:T(1024)S(1)} %add_add_fusion.1), channel_id=1, source_target_pairs={{0,5},{1,4},{2,7},{3,6},{4,1},{5,0},{6,3},{7,2},{8,14},{9,15},{10,... | collective-permute-start | bytes 207368 | tf_op jit(solution)/shard_map/ppermute | solution.py:1009
  85.1 5.1 %collective-permute-start.13 = (f32[17280]{0:T(1024)S(1)}, f32[17280]{0:T(1024)S(1)}, u32[]{:S(2)}, u32[]{:S(2)}) collective-permute-start(f32[17280]{0:T(1024)S(1)} %add_add_fusion.1), channel_id=1, source_target_pairs={{0,1},{1,0},{2,3},{3,2},{4,5},{5,4},{6,7},{7,6},{8,10},{9,11},{10,... | collective-permute-start | bytes 207368 | tf_op jit(solution)/shard_map/ppermute | solution.py:1009
  90.2 2.2 %collective-permute-start.15 = (f32[17280]{0:T(1024)S(1)}, f32[17280]{0:T(1024)S(1)}, u32[]{:S(2)}, u32[]{:S(2)}) collective-permute-start(f32[17280]{0:T(1024)S(1)} %add_add_fusion), channel_id=1, source_target_pairs={{0,8},{1,9},{2,10},{3,11},{4,12},{5,13},{6,14},{7,15},{8,0},{9,1},... | collective-permute-start | bytes 207368 | tf_op jit(solution)/shard_map/ppermute | solution.py:1011
  92.4 6.8 %collective-permute-start.16 = (f32[17280]{0:T(1024)S(1)}, f32[17280]{0:T(1024)S(1)}, u32[]{:S(2)}, u32[]{:S(2)}) collective-permute-start(f32[17280]{0:T(1024)S(1)} %add.52), channel_id=1, source_target_pairs={{0,16},{1,17},{2,18},{3,19},{4,20},{5,21},{6,22},{7,23},{8,24},{9,... | collective-permute-start | bytes 207368 | tf_op jit(solution)/shard_map/ppermute | solution.py:1011
